TPU v7x, 32 devices: a whole 2x2x4 slice. The times are simulated.
32 devices in a mesh: row: 16 (over z, x, core), col: 2 (over y).
Axes of the slice: x: 2, y: 2, z: 4, core: 2. Of those that a mesh axis runs over, the one named last changes fastest.
Arguments:
- rhs: float32 [1015808], P(('row', 'col')), may hold values from -6 to 6
- blocks: float32 [16, 2, 64, 128, 128], P('row', 'col'), may hold values from -0.5 to 0.5
- blk_row: int32 [16, 2, 64], P('row', 'col'), may hold values from 0 to 495
- blk_col: int32 [16, 2, 64], P('row', 'col'), may hold values from 0 to 511
Outputs:
- solution: float32 [131072], P(('col', 'row'))
- rel_residual: float32 [], replicated
Inputs may be any that keep to these rules, and one draw needn't show every extreme that they name: `blk_row`: each device holds 64 blocks; blocks listed twice at the same place are added.
All inputs are finite; a program needn't handle non-finite values.
Results may differ from a plain program's by a relative error of at most 0.00013.
Values sent between devices are 32-bit elements; how exact they have to be, the bound alone decides.
No kernel may reach another device: no remote copies, remote signals or barrier semaphores. Data moves between devices by JAX's collectives and lax.ppermute only.
A program may use at most 64 MiB of HBM per device.

v0:
```python
import jax
import jax.numpy as jnp
from jax import lax
from jax.sharding import PartitionSpec as P

BLK = 128
ROWB_DEV = 496
COLB_DEV = 512
NB_DEV = 64
ITERS = 3


def on_device(rhs, blocks, blk_row, blk_col):
    tiles = blocks.reshape(NB_DEV, BLK, BLK)
    rows_at = blk_row.reshape(NB_DEV)
    cols_at = blk_col.reshape(NB_DEV)

    def fwd_local(whole):
        picked = whole.reshape(COLB_DEV, BLK)[cols_at]
        prod = jnp.einsum("nij,nj->ni", tiles, picked, precision=lax.Precision.HIGHEST)
        total = jnp.zeros((ROWB_DEV, BLK), jnp.float32).at[rows_at].add(prod)
        return total.reshape(ROWB_DEV * BLK)

    def back_local(whole):
        picked = whole.reshape(ROWB_DEV, BLK)[rows_at]
        prod = jnp.einsum("nij,ni->nj", tiles, picked, precision=lax.Precision.HIGHEST)
        total = jnp.zeros((COLB_DEV, BLK), jnp.float32).at[cols_at].add(prod)
        return total.reshape(COLB_DEV * BLK)

    def forward(vec):
        whole = lax.all_gather(vec, "row", axis=0, tiled=True)
        return lax.psum_scatter(fwd_local(whole), "col", scatter_dimension=0, tiled=True)

    def backward(vec):
        whole = lax.all_gather(vec, "col", axis=0, tiled=True)
        return lax.psum_scatter(back_local(whole), "row", scatter_dimension=0, tiled=True)

    def u_length(vec):
        return jnp.sqrt(lax.psum(jnp.sum(vec * vec), ("row", "col")))

    def settle_u(raw):
        beta = u_length(raw)
        unit = raw / beta
        return (unit, beta, backward(unit))

    def settle_v(raw, needed):
        alpha = u_length(raw)
        unit = raw / alpha
        front = forward(unit) if needed else None
        return (unit, alpha, front)

    u, beta_first, back = settle_u(rhs)
    v, alpha, front = settle_v(back, True)
    w = v
    solution = jnp.zeros_like(v)
    phibar = beta_first
    rhobar = alpha
    for step in range(ITERS):
        u, beta, back = settle_u(front - alpha * u)
        v, alpha, front = settle_v(back - beta * v, step + 1 < ITERS)
        rho = jnp.sqrt(rhobar * rhobar + beta * beta)
        cosine = rhobar / rho
        sine = beta / rho
        theta = sine * alpha
        rhobar = -cosine * alpha
        phi = cosine * phibar
        phibar = sine * phibar
        solution = solution + phi / rho * w
        w = v - theta / rho * w
    return (solution, phibar / beta_first)


def solution(mesh):
    return jax.shard_map(
        on_device,
        mesh=mesh,
        in_specs=(
            P(("row", "col")),
            P("row", "col", None, None, None),
            P("row", "col", None),
            P("row", "col", None),
        ),
        out_specs=(P(("col", "row")), P()),
        check_vma=False,
    )
```

profile of v0, /device:TPU:0, one launch (start us, length us, event | category | flops | bytes accessed | tf_op | source)
XLA Modules:
  0.0 786.1 jit_solution(13914044966287152403)
XLA Ops:
  7.2 1.5 multiply_reduce_fusion.2
  8.8 42.2 %psum.49 = f32[]{:T(128)} all-reduce(f32[]{:T(128)} %multiply_reduce_fusion.2), channel_id=1, replica_groups=mesh['row'=16,'col'=2] {'row','col'}, use_global_device_ids=true, to_apply=%region_1.0 | all-reduce | flops 1 | bytes 8 | tf_op jit(solution)/shard_map/psum | solution.py:39
  51.7 0.9 broadcast_divide_fusion.2
  52.6 6.0 all_gather.18
  58.6 0.7 fusion.27
  59.3 0.7 fusion.26
  60.5 5.3 fusion.10
  65.9 1.5 scatter_custom_fusion
  68.7 87.3 %all-reduce.13.cloned.1.call-done = f32[65536]{0:T(1024)} async-done(((f32[65536]{0:T(1024)}), f32[65536]{0:T(1024)}) %all-reduce.13.cloned.1.call-update) | async-done | bytes 262160
  155.9 1.3 multiply_reduce_fusion.5
  157.3 40.9 %psum.50 = f32[]{:T(128)} all-reduce(f32[]{:T(128)} %multiply_reduce_fusion.5), channel_id=1, replica_groups=mesh['row'=16,'col'=2] {'row','col'}, use_global_device_ids=true, to_apply=%region_5.0 | all-reduce | flops 1 | bytes 8 | tf_op jit(solution)/shard_map/psum | solution.py:39
  198.9 0.7 dynamic-slice_divide_fusion
  199.6 21.8 %all_gather.19 = f32[65536]{0:T(1024)S(1)} all-gather(f32[4096]{0:T(1024)S(1)} %dynamic-slice_divide_fusion), channel_id=1, replica_groups=mesh['row'=16,'col'=2] {'row'}, dimensions={0}, use_global_device_ids=true | all-gather | bytes 278528 | tf_op jit(solution)/shard_map/all_gather | solution.py:31
  222.0 8.3 %fusion.8 = f32[64,1,128]{2,1,0:T(1,128)S(1)} fusion(f32[64,128,1]{1,2,0:T(1,128)S(1)} %bitcast.86, f32[1,1,64,128,128]{4,3,2,1,0:T(8,128)} %param.5), kind=kOutput, calls=%fused_computation.20 | convolution fusion | flops 12582912 | bytes 4259840 | tf_op jit(solution)/shard_map/nij,nj->ni/dot_general | solution.py:20
  230.3 1.5 scatter_custom_fusion.1
  233.1 18.6 %all-reduce.15.cloned.1.call-done = f32[63488]{0:T(1024)} async-done(((f32[63488]{0:T(1024)}), f32[63488]{0:T(1024)}) %all-reduce.15.cloned.1.call-update) | async-done | bytes 253968
  251.7 1.5 multiply_reduce_fusion.1
  253.3 39.6 %psum.51 = f32[]{:T(128)} all-reduce(f32[]{:T(128)} %multiply_reduce_fusion.1), channel_id=1, replica_groups=mesh['row'=16,'col'=2] {'row','col'}, use_global_device_ids=true, to_apply=%region_9.0 | all-reduce | flops 1 | bytes 8 | tf_op jit(solution)/shard_map/psum | solution.py:39
  293.6 0.9 broadcast_divide_fusion.1
  294.5 6.0 all_gather.20
  301.1 5.3 fusion.6
  306.4 1.5 scatter_custom_fusion.2
  308.0 89.3 %all-reduce.17.cloned.1.call-done = f32[65536]{0:T(1024)} async-done(((f32[65536]{0:T(1024)}), f32[65536]{0:T(1024)}) %all-reduce.17.cloned.1.call-update) | async-done | bytes 262160
  397.2 1.4 multiply_reduce_fusion.4
  398.6 40.9 %psum.52 = f32[]{:T(128)} all-reduce(f32[]{:T(128)} %multiply_reduce_fusion.4), channel_id=1, replica_groups=mesh['row'=16,'col'=2] {'row','col'}, use_global_device_ids=true, to_apply=%region_13.0 | all-reduce | flops 1 | bytes 8 | tf_op jit(solution)/shard_map/psum | solution.py:39
  440.2 0.7 broadcast_divide_fusion.4
  441.0 22.0 %all_gather.21 = f32[65536]{0:T(1024)S(1)} all-gather(f32[4096]{0:T(1024)S(1)} %broadcast_divide_fusion.4), channel_id=1, replica_groups=mesh['row'=16,'col'=2] {'row'}, dimensions={0}, use_global_device_ids=true | all-gather | bytes 278528 | tf_op jit(solution)/shard_map/all_gather | solution.py:31
  463.5 8.3 %fusion.4 = f32[64,1,128]{2,1,0:T(1,128)S(1)} fusion(f32[64,128,1]{1,2,0:T(1,128)S(1)} %bitcast.88, f32[1,1,64,128,128]{4,3,2,1,0:T(8,128)} %param.5), kind=kOutput, calls=%fused_computation.16 | convolution fusion | flops 12582912 | bytes 4259840 | tf_op jit(solution)/shard_map/nij,nj->ni/dot_general | solution.py:20
  471.9 1.5 scatter_custom_fusion.3
  473.4 19.8 %all-reduce.19.cloned.1.call-done = f32[63488]{0:T(1024)} async-done(((f32[63488]{0:T(1024)}), f32[63488]{0:T(1024)}) %all-reduce.19.cloned.1.call-update) | async-done | bytes 253968
  493.3 1.5 multiply_reduce_fusion
  494.8 39.6 %psum.53 = f32[]{:T(128)} all-reduce(f32[]{:T(128)} %multiply_reduce_fusion), channel_id=1, replica_groups=mesh['row'=16,'col'=2] {'row','col'}, use_global_device_ids=true, to_apply=%region_17.0 | all-reduce | flops 1 | bytes 8 | tf_op jit(solution)/shard_map/psum | solution.py:39
  535.1 0.9 broadcast_divide_fusion
  536.1 6.0 all_gather.22
  542.1 0.6 gather_fusion.4
  542.7 5.3 fusion.2
  548.0 1.5 scatter_custom_fusion.4
  549.5 89.3 %all-reduce.21.cloned.1.call-done = f32[65536]{0:T(1024)} async-done(((f32[65536]{0:T(1024)}), f32[65536]{0:T(1024)}) %all-reduce.21.cloned.1.call-update) | async-done | bytes 262160
  638.8 1.3 multiply_reduce_fusion.3
  640.2 40.9 %psum.54 = f32[]{:T(128)} all-reduce(f32[]{:T(128)} %multiply_reduce_fusion.3), channel_id=1, replica_groups=mesh['row'=16,'col'=2] {'row','col'}, use_global_device_ids=true, to_apply=%region_21.0 | all-reduce | flops 1 | bytes 8 | tf_op jit(solution)/shard_map/psum | solution.py:39
  681.8 0.7 broadcast_divide_fusion.3
  682.5 21.8 %all_gather.23 = f32[65536]{0:T(1024)S(1)} all-gather(f32[4096]{0:T(1024)S(1)} %broadcast_divide_fusion.3), channel_id=1, replica_groups=mesh['row'=16,'col'=2] {'row'}, dimensions={0}, use_global_device_ids=true | all-gather | bytes 278528 | tf_op jit(solution)/shard_map/all_gather | solution.py:31
  704.9 8.3 %fusion = f32[64,1,128]{2,1,0:T(1,128)S(1)} fusion(f32[64,128,1]{1,2,0:T(1,128)S(1)} %bitcast.84, f32[1,1,64,128,128]{4,3,2,1,0:T(8,128)} %param.5), kind=kOutput, calls=%fused_computation.12 | convolution fusion | flops 12582912 | bytes 4259840 | tf_op jit(solution)/shard_map/nij,nj->ni/dot_general | solution.py:20
  713.2 1.5 scatter_custom_fusion.5
  715.1 19.5 %all-reduce.23.cloned.1.call-done = f32[63488]{0:T(1024)} async-done(((f32[63488]{0:T(1024)}), f32[63488]{0:T(1024)}) %all-reduce.23.cloned.1.call-update) | async-done | bytes 253968
  734.6 1.5 fusion.19
  736.2 39.7 %psum.55 = f32[]{:T(128)} all-reduce(f32[]{:T(128)} %fusion.19), channel_id=1, replica_groups=mesh['row'=16,'col'=2] {'row','col'}, use_global_device_ids=true, to_apply=%region_25.0 | all-reduce | flops 1 | bytes 8 | tf_op jit(solution)/shard_map/psum | solution.py:39
  776.8 1.3 multiply_add_fusion
  (27 shorter events, 4.5 us)
Async XLA Ops:
  7.2 60.3 %copy-start.2 = (u32[32]{0:T(128)S(1)}, u32[32]{0:T(128)}, u32[]{:S(2)}) copy-start(u32[32]{0:T(128)} %constant.15) | copy-start | bytes 388
  7.2 148.8 %all-reduce.13.cloned.1.call-start = ((), (), s32[]{:S(2)}) async-start(), calls=%async_computation | async-start | bytes 524288
  60.5 171.4 %copy-start.1 = (u32[32]{0:T(128)S(1)}, u32[32]{0:T(128)}, u32[]{:S(2)}) copy-start(u32[32]{0:T(128)} %constant.19) | copy-start | bytes 388
  60.5 191.2 %copy-start = (f32[31744]{0:T(1024)S(1)}, f32[31744]{0:T(1024)}, u32[]{:S(2)}) copy-start(f32[31744]{0:T(1024)} %param.4) | copy-start | bytes 380932
  67.4 184.3 %all-reduce.15.cloned.1.call-start = ((), (), s32[]{:S(2)}) async-start(), calls=%async_computation.1 | async-start | bytes 507904
  231.8 165.4 %all-reduce.17.cloned.1.call-start = ((), (), s32[]{:S(2)}) async-start(), calls=%async_computation.2 | async-start | bytes 524288
  307.9 185.3 %all-reduce.19.cloned.1.call-start = ((), (), s32[]{:S(2)}) async-start(), calls=%async_computation.3 | async-start | bytes 507904
  473.4 165.5 %all-reduce.21.cloned.1.call-start = ((), (), s32[]{:S(2)}) async-start(), calls=%async_computation.4 | async-start | bytes 524288
  549.5 185.1 %all-reduce.23.cloned.1.call-start = ((), (), s32[]{:S(2)}) async-start(), calls=%async_computation.5 | async-start | bytes 507904
Sparse Core Ops, SparseCore 0:
  67.5 88.4 all-reduce.12
  232.0 19.7 all-reduce.14
  308.0 89.1 all-reduce.16
  473.5 19.7 all-reduce.18
  549.6 89.1 all-reduce.20
  714.8 19.7 all-reduce.22
where the time goes:
time: 789 us; the launch traced here: 786 us
  blocking collectives  368 us (47%)
  waiting for transfers between devices  324 us (41%)
  matrix products  40.8 us (5%)
  other arithmetic  26.8 us (3%)
  between operations  22.1 us (3%)
    unnamed x12, waiting for transfers between devices  324 us
    psum x7, blocking collectives, u_length(): return jnp.sqrt(lax.psum(jnp.sum(vec * vec), ('row', 'col')))  284 us
    all_gather x3, blocking collectives, forward(): whole = lax.all_gather(vec, 'row', axis=0, tiled=True)  65.6 us
    dot_general x3, matrix products, fwd_local(): jnp.einsum('nij,nj->ni', tiles, picked, precision=lax.Precision.HIGHEST)  24.9 us
    all_gather x3, blocking collectives, backward(): whole = lax.all_gather(vec, 'col', axis=0, tiled=True)  18.1 us
    dot_general x3, matrix products, back_local(): jnp.einsum('nij,ni->nj', tiles, picked, precision=lax.Precision.HIGHEST)  15.9 us
  transfers between devices with their start and end apart: 6, of which 6 were waited for; matrix products, arithmetic and copies ran while one was open for 0% of the time, Pallas kernels for 0%

commit v1 on v0

v1 whole, which is shorter than its diff:
```python
import functools

import jax
import jax.numpy as jnp
from jax import lax
from jax.experimental import pallas as pl
from jax.experimental.pallas import tpu as pltpu
from jax.sharding import PartitionSpec as P

BLK = 128
ROWB_DEV = 496
COLB_DEV = 512
NB_DEV = 64
ITERS = 3
MSG = NB_DEV + 8
VMEM_LIMIT = 24 * 1024 * 1024

f32 = jnp.float32
bf16 = jnp.bfloat16


def total(x):
    s = jnp.sum(jnp.sum(x, axis=0, keepdims=True), axis=1, keepdims=True)
    return jnp.broadcast_to(s, (1, BLK))


def place_sum(index_row, parts, rows):
    k = parts.shape[0]
    at = lax.broadcasted_iota(jnp.int32, (rows, k), 0).astype(f32)
    hot = jnp.where(at == index_row, 1.0, 0.0).astype(bf16)
    high = parts.astype(bf16)
    rest = parts - high.astype(f32)
    mid = rest.astype(bf16)
    low = (rest - mid.astype(f32)).astype(bf16)
    three = jnp.concatenate([high, mid, low], axis=1)
    out = jnp.dot(hot, three, preferred_element_type=f32)
    return out[:, :BLK] + (out[:, BLK : 2 * BLK] + out[:, 2 * BLK :])


def write_message(msg, index_row, square):
    msg[NB_DEV : NB_DEV + 1, :] = index_row
    msg[NB_DEV + 1 : NB_DEV + 2, :] = square
    msg[NB_DEV + 2 :, :] = jnp.zeros((MSG - NB_DEV - 2, BLK), f32)


def times_blocks_t(blocks, picked, msg):
    cols = picked[...].T
    for n in range(NB_DEV):
        prod = blocks[n * BLK : (n + 1) * BLK, :] * cols[:, n : n + 1]
        msg[n : n + 1, :] = jnp.sum(prod, axis=0, keepdims=True)


def times_blocks(blocks, at, vec, msg):
    lane = lax.broadcasted_iota(jnp.int32, (BLK, BLK), 1)
    acc = jnp.zeros((BLK, BLK), f32)
    for n in range(NB_DEV):
        prod = blocks[n * BLK : (n + 1) * BLK, :] * vec[pl.ds(at[n], 1), :]
        acc = jnp.where(lane == n, jnp.sum(prod, axis=1, keepdims=True), acc)
    msg[:NB_DEV, :] = acc.T[:NB_DEV, :]


def first_kernel(rows_at, u_raw, blocks, col_row, msg, picked):
    for n in range(NB_DEV):
        picked[n : n + 1, :] = u_raw[pl.ds(rows_at[n], 1), :]
    u = u_raw[...]
    times_blocks_t(blocks, picked, msg)
    write_message(msg, col_row[...], total(u * u))


def gather_sum_kernel(slot, is_first, own, *refs):
    *others, out = refs
    first = is_first[0] > 0
    lane = lax.broadcasted_iota(jnp.int32, (1, BLK), 1)
    parts, index, square = [], [], jnp.zeros((1, BLK), f32)
    for k, other in enumerate(others):
        m = jnp.where(first, own[...], other[...]) if k == slot else other[...]
        a, b = m[:MSG], m[MSG:]
        parts += [a[:NB_DEV], b[:NB_DEV]]
        index.append(jnp.where(lane < NB_DEV, a[NB_DEV : NB_DEV + 1], b[NB_DEV : NB_DEV + 1]))
        square = square + (a[NB_DEV + 1 : NB_DEV + 2] + b[NB_DEV + 1 : NB_DEV + 2])
    out[:COLB_DEV, :] = place_sum(jnp.concatenate(index, axis=1), jnp.concatenate(parts, axis=0), COLB_DEV)
    out[COLB_DEV:, :] = jnp.broadcast_to(square, (8, BLK))


def v_kernel(has_before, cols_at, half, other, *refs):
    if has_before:
        v_raw_before, alpha, blocks, v_raw, msg, beta_out = refs
    else:
        blocks, v_raw, msg, beta_out = refs
    beta = jnp.sqrt(half[COLB_DEV : COLB_DEV + 1, :] + other[COLB_DEV : COLB_DEV + 1, :])
    v = (half[:COLB_DEV, :] + other[:COLB_DEV, :]) / beta
    if has_before:
        v = v - v_raw_before[...] * (beta / alpha[:1, :])
    v_raw[...] = v
    beta_out[...] = jnp.broadcast_to(beta, (8, BLK))
    write_message(msg, jnp.zeros((1, BLK), f32), total(v * v))
    times_blocks(blocks, cols_at, v_raw, msg)


def u_kernel(n_col, last, rows_at, row_index, u_raw_before, beta, *refs):
    pieces, refs = refs[:n_col], refs[n_col:]
    if last:
        square_out, alpha_out = refs
    else:
        blocks, col_row, u_raw, msg, alpha_out, picked = refs
    square = pieces[0][NB_DEV + 1 : NB_DEV + 2, :]
    for piece in pieces[1:]:
        square = square + piece[NB_DEV + 1 : NB_DEV + 2, :]
    alpha = jnp.sqrt(square)
    alpha_out[...] = jnp.broadcast_to(alpha, (8, BLK))
    prods = jnp.concatenate([piece[:NB_DEV, :] for piece in pieces], axis=0)
    front = place_sum(row_index[...], prods, ROWB_DEV)
    u = front / alpha - u_raw_before[...] * (alpha / beta[:1, :])
    square = total(u * u)
    if last:
        square_out[...] = jnp.broadcast_to(square, (8, BLK))
        return
    u_raw[...] = u
    for n in range(NB_DEV):
        picked[n : n + 1, :] = u_raw[pl.ds(rows_at[n], 1), :]
    times_blocks_t(blocks, picked, msg)
    write_message(msg, col_row[...], square)


def end_kernel(square, *refs):
    v_raws, alphas, betas = refs[:ITERS], refs[ITERS : 2 * ITERS], refs[2 * ITERS : 3 * ITERS]
    out, residual = refs[3 * ITERS :]
    alpha = [a[:1, :] for a in alphas]
    beta = [b[:1, :] for b in betas] + [jnp.sqrt(square[:1, :])]
    phibar, rhobar = beta[0], alpha[0]
    x = None
    for k in range(ITERS):
        v = v_raws[k][...] / alpha[k]
        w = v if k == 0 else v - turn * w
        rho = jnp.sqrt(rhobar * rhobar + beta[k + 1] * beta[k + 1])
        cosine, sine = rhobar / rho, beta[k + 1] / rho
        phi = cosine * phibar
        phibar = sine * phibar
        step = phi / rho * w
        x = step if x is None else x + step
        if k + 1 < ITERS:
            turn = sine * alpha[k + 1] / rho
            rhobar = -cosine * alpha[k + 1]
    out[...] = x
    residual[...] = jnp.broadcast_to(phibar / beta[0], (8, BLK))


def call(body, ins, outs, smem=0, scratch=()):
    specs = [pl.BlockSpec(memory_space=pltpu.SMEM)] * smem
    specs += [pl.BlockSpec(memory_space=pltpu.VMEM)] * (len(ins) - smem)
    return pl.pallas_call(
        body,
        out_shape=[jax.ShapeDtypeStruct(s, f32) for s in outs],
        in_specs=specs,
        out_specs=[pl.BlockSpec(memory_space=pltpu.VMEM)] * len(outs),
        scratch_shapes=list(scratch),
        compiler_params=pltpu.CompilerParams(vmem_limit_bytes=VMEM_LIMIT),
    )(*ins)


def chip_steps(chips):
    if chips == 8:
        return [(1, 4), (3, 3), (2, 6), (5, 7)], 1
    steps = [(m, m + 1) for m in range(1, chips - 1, 2)] + [(chips - 1, chips - 1)]
    return steps, len(steps) - 1


def on_device(n_row, n_col, rhs, blocks, blk_row, blk_col):
    chips = n_row // 2
    steps, twice = chip_steps(chips)
    per_rhs = rhs.shape[0] // BLK
    per_out = COLB_DEV // n_row
    row, col = lax.axis_index("row"), lax.axis_index("col")
    is_first = (row % 2 == 0).astype(jnp.int32).reshape(1)

    def swap(x):
        return lax.ppermute(x, "row", [(r, r ^ 1) for r in range(n_row)])

    def to_chips(x):
        return [
            lax.ppermute(x, "row", [(r, r ^ (2 * step[r % 2])) for r in range(n_row)]) for step in steps
        ]

    def around_col(x):
        return [x] + [
            lax.ppermute(x, "col", [(i, (i - s) % n_col) for i in range(n_col)]) for s in range(1, n_col)
        ]

    tiles = blocks.reshape(NB_DEV * BLK, BLK)
    cols_at = blk_col.reshape(NB_DEV)
    rows_here = blk_row.reshape(NB_DEV)
    col_row = jnp.concatenate([cols_at, cols_at]).astype(f32).reshape(1, BLK)
    row_row = jnp.concatenate([rows_here, rows_here]).astype(f32).reshape(1, BLK)

    first = jnp.concatenate([rhs.reshape(per_rhs, BLK), jnp.broadcast_to(row_row, (8, BLK))])
    got = around_col(first)
    u_raw = jnp.concatenate([g[:per_rhs] for g in got])
    index = jnp.concatenate([g[per_rhs, :NB_DEV] for g in got]).astype(jnp.int32)
    row_index = jnp.remainder(index - col * per_rhs, ROWB_DEV).astype(f32).reshape(1, n_col * NB_DEV)
    rows_at = jnp.remainder(rows_here - col * per_rhs, ROWB_DEV)

    picked = [pltpu.VMEM((NB_DEV, BLK), f32)]

    def gather(msg):
        both = jnp.concatenate([msg, swap(msg)])
        others = to_chips(both)
        (half,) = call(
            functools.partial(gather_sum_kernel, twice), [is_first, both] + others, [(COLB_DEV + 8, BLK)], smem=1
        )
        return half, swap(half)

    (msg,) = call(first_kernel, [rows_at, u_raw, tiles, col_row], [(MSG, BLK)], smem=1, scratch=picked)
    alphas, betas, v_raws = [], [], []
    for step in range(ITERS):
        half, other = gather(msg)
        before = [v_raws[-1], alphas[-1]] if step else []
        v_raw, msg, beta = call(
            functools.partial(v_kernel, step > 0),
            [cols_at, half, other] + before + [tiles],
            [(COLB_DEV, BLK), (MSG, BLK), (8, BLK)],
            smem=1,
        )
        v_raws.append(v_raw)
        betas.append(beta)
        last = step + 1 == ITERS
        ins = [rows_at, row_index, u_raw, beta] + around_col(msg)
        body = functools.partial(u_kernel, n_col, last)
        if last:
            square, alpha = call(body, ins, [(8, BLK), (8, BLK)], smem=1)
        else:
            u_raw, msg, alpha = call(
                body,
                ins + [tiles, col_row],
                [(ROWB_DEV, BLK), (MSG, BLK), (8, BLK)],
                smem=1,
                scratch=picked,
            )
        alphas.append(alpha)

    both = square + swap(square)
    parts = to_chips(both)
    parts[twice] = jnp.where(is_first[0] > 0, both, parts[twice])
    half = functools.reduce(lambda a, b: a + b, parts)
    square = half + swap(half)
    mine = [lax.dynamic_slice_in_dim(v, row * per_out, per_out) for v in v_raws]
    out, residual = call(end_kernel, [square] + mine + alphas + betas, [(per_out, BLK), (8, BLK)])
    return out.reshape(per_out * BLK), residual[0, 0]


def solution(mesh):
    return jax.shard_map(
        functools.partial(on_device, mesh.shape["row"], mesh.shape["col"]),
        mesh=mesh,
        in_specs=(
            P(("row", "col")),
            P("row", "col", None, None, None),
            P("row", "col", None),
            P("row", "col", None),
        ),
        out_specs=(P(("col", "row")), P()),
        check_vma=False,
    )
```

time: 789 us -> 94.5 us (0.12)
  blocking collectives: 368 us -> 0 us
  waiting for transfers between devices: 324 us -> 38.9 us
  matrix products: 40.8 us -> 0 us
  starting transfers between devices: 0.25 us -> 30.2 us
  other arithmetic: 26.8 us -> 4.31 us
  between operations: 22.1 us -> 0.8 us
  Pallas kernels: 0 us -> 15.1 us
    unnamed x12 -> x0, waiting for transfers between devices: 324 us -> none
    psum x7 -> x0, blocking collectives: 284 us -> none  [u_length(): return jnp.sqrt(lax.psum(jnp.sum(vec * vec), ('row', 'col')))]
    all_gather x6 -> x0, blocking collectives: 83.7 us -> none  [the longest x3 65.6 us: forward(): whole = lax.all_gather(vec, 'row', axis=0, tiled=True)]
    dot_general x6 -> x0, matrix products: 40.8 us -> none  [the longest x3 24.9 us: fwd_local(): jnp.einsum('nij,nj->ni', tiles, picked, precision=lax.Precision.HIGHEST)]
    ppermute x0 -> x28, waiting for transfers between devices: none -> 38.9 us  [the longest x16 19.6 us: to_chips(): lax.ppermute(x, 'row', [(r, r ^ 2 * step[r % 2]) for r in range(n_row)])]
    ppermute x0 -> x28, starting transfers between devices: none -> 30.2 us  [the longest x16 21.6 us: to_chips(): lax.ppermute(x, 'row', [(r, r ^ 2 * step[r % 2]) for r in range(n_row)])]
    pallas_call x0 -> x11, Pallas kernels: none -> 15.1 us  [call(): pl.pallas_call(body, out_shape=[jax.ShapeDtypeStruct(s, f32) for s in out...]
    reduce_sum x7 -> x0, other arithmetic: 10.2 us -> none  [u_length(): return jnp.sqrt(lax.psum(jnp.sum(vec * vec), ('row', 'col')))]
  transfers between devices with their start and end apart: 6 -> 28, of which waited for: 6 -> 22; matrix products, arithmetic and copies ran while one was open for 0% -> 2% of each run, Pallas kernels for 0% -> 0%
where the time goes in v1:
time: 94.5 us; the launch traced here: 94.3 us
  waiting for transfers between devices  38.9 us (41%)
  starting transfers between devices  30.2 us (32%)
  Pallas kernels  15.1 us (16%)
  local copies, waits for them, and re-layouts  4.95 us (5%)
  other arithmetic  4.31 us (5%)
    ppermute x16, starting transfers between devices, to_chips(): lax.ppermute(x, 'row', [(r, r ^ 2 * step[r % 2]) for r in range(n_row)])  21.6 us
    ppermute x16, waiting for transfers between devices, to_chips(): lax.ppermute(x, 'row', [(r, r ^ 2 * step[r % 2]) for r in range(n_row)])  19.6 us
    pallas_call x11, Pallas kernels, call(): pl.pallas_call(body, out_shape=[jax.ShapeDtypeStruct(s, f32) for s in out...  15.1 us
    ppermute x8, waiting for transfers between devices, swap(): return lax.ppermute(x, 'row', [(r, r ^ 1) for r in range(n_row)])  10.1 us
    ppermute x4, waiting for transfers between devices, around_col(): lax.ppermute(x, 'col', [(i, (i - s) % n_col) for i in range(n_col)])  9.17 us
    ppermute x4, starting transfers between devices, around_col(): lax.ppermute(x, 'col', [(i, (i - s) % n_col) for i in range(n_col)])  7.82 us
    unnamed x12, local copies, waits for them, and re-layouts  4.4 us
  transfers between devices with their start and end apart: 28, of which 22 were waited for; matrix products, arithmetic and copies ran while one was open for 2% of the time, Pallas kernels for 0%

profile of v1, /device:TPU:0, one launch (start us, length us, event | category | flops | bytes accessed | tf_op | source)
XLA Modules:
  0.0 94.3 jit_solution(7156325154708026119)
XLA Ops:
  0.7 0.8 add_convert_fusion.1
  1.5 0.9 pad_maximum_fusion.1
  2.4 3.0 %collective-permute-start = (f32[256,128]{1,0:T(8,128)S(1)}, f32[256,128]{1,0:T(8,128)S(1)}, u32[]{:S(2)}, u32[]{:S(2)}) collective-permute-start(f32[256,128]{1,0:T(8,128)S(1)} %pad_maximum_fusion.1), channel_id=1, source_target_pairs={{0,1},{1,0},{2,3},{3,2},{4,5},{5,4},{6,7},{7,6},{8,9},{9,8},{10,11... | collective-permute-start | bytes 393224 | tf_op jit(solution)/shard_map/ppermute | solution.py:186
  6.9 2.0 %collective-permute-done = f32[256,128]{1,0:T(8,128)S(1)} collective-permute-done((f32[256,128]{1,0:T(8,128)S(1)}, f32[256,128]{1,0:T(8,128)S(1)}, u32[]{:S(2)}, u32[]{:S(2)}) %collective-permute-start) | collective-permute-done | bytes 131104 | tf_op jit(solution)/shard_map/ppermute | solution.py:186
  8.9 0.9 pad_maximum_fusion.u_raw.u_raw_before
  9.9 2.2 %copy-done = f32[1,1,64,128,128]{4,3,2,1,0:T(8,128)S(1)} copy-done((f32[1,1,64,128,128]{4,3,2,1,0:T(8,128)S(1)}, f32[1,1,64,128,128]{4,3,2,1,0:T(8,128)}, u32[]{:S(2)}) %copy-start) | copy-done | bytes 4194328
  12.1 2.0 %shard_map.59 = f32[72,128]{1,0:T(8,128)S(1)} custom-call(s32[64]{0:T(128)S(1)} %and_select_fusion.1.rows_at, f32[496,128]{1,0:T(8,128)S(1)} %pad_maximum_fusion.u_raw.u_raw_before, f32[8192,128]{1,0:T(8,128)S(1)} %bitcast.11, f32[1,128]{1,0:T(1,128)S(1)} %add_convert_fusion.2.col_row.refs_3_), custom_call_target="tpu_custom_call" | custom-call | tf_op jit(solution)/shard_map/pallas_call | solution.py:151
  14.1 1.2 %collective-permute-done.1 = f32[72,128]{1,0:T(8,128)S(1)} collective-permute-done((f32[72,128]{1,0:T(8,128)S(1)}, f32[72,128]{1,0:T(8,128)S(1)}, u32[]{:S(2)}, u32[]{:S(2)}) %collective-permute-start.1) | collective-permute-done | bytes 36896 | tf_op jit(solution)/shard_map/ppermute | solution.py:177
  15.3 3.7 %collective-permute-start.5 = (f32[144,128]{1,0:T(8,128)S(1)}, f32[144,128]{1,0:T(8,128)S(1)}, u32[]{:S(2)}, u32[]{:S(2)}) collective-permute-start(f32[144,128]{1,0:T(8,128)S(1)} %pad_maximum_fusion.2.own), channel_id=1, source_target_pairs={{0,20},{2,30},{4,16},{6,26},{8,28},{10,22},{12,24},{14,18},{16,4},... | collective-permute-start | bytes 221192 | tf_op jit(solution)/shard_map/ppermute | solution.py:181
  19.0 1.6 %collective-permute-start.4 = (f32[144,128]{1,0:T(8,128)S(1)}, f32[144,128]{1,0:T(8,128)S(1)}, u32[]{:S(2)}, u32[]{:S(2)}) collective-permute-start(f32[144,128]{1,0:T(8,128)S(1)} %pad_maximum_fusion.2.own), channel_id=1, source_target_pairs={{0,8},{2,26},{4,12},{6,30},{8,0},{10,18},{12,4},{14,22},{16,24},{1... | collective-permute-start | bytes 221192 | tf_op jit(solution)/shard_map/ppermute | solution.py:181
  21.0 1.5 %collective-permute-start.2 = (f32[144,128]{1,0:T(8,128)S(1)}, f32[144,128]{1,0:T(8,128)S(1)}, u32[]{:S(2)}, u32[]{:S(2)}) collective-permute-start(f32[144,128]{1,0:T(8,128)S(1)} %pad_maximum_fusion.2.own), channel_id=1, source_target_pairs={{0,4},{2,18},{4,0},{6,22},{8,12},{10,26},{12,8},{14,30},{16,20},{1... | collective-permute-start | bytes 221192 | tf_op jit(solution)/shard_map/ppermute | solution.py:181
  22.5 1.2 %collective-permute-done.5.refs_3_ = f32[144,128]{1,0:T(8,128)S(1)} collective-permute-done((f32[144,128]{1,0:T(8,128)S(1)}, f32[144,128]{1,0:T(8,128)S(1)}, u32[]{:S(2)}, u32[]{:S(2)}) %collective-permute-start.5) | collective-permute-done | bytes 73760 | tf_op jit(solution)/shard_map/ppermute | solution.py:181
  23.8 2.7 %collective-permute-done.4.refs_2_ = f32[144,128]{1,0:T(8,128)S(1)} collective-permute-done((f32[144,128]{1,0:T(8,128)S(1)}, f32[144,128]{1,0:T(8,128)S(1)}, u32[]{:S(2)}, u32[]{:S(2)}) %collective-permute-start.4) | collective-permute-done | bytes 73760 | tf_op jit(solution)/shard_map/ppermute | solution.py:181
  27.7 1.4 %collective-permute-done.6.other = f32[520,128]{1,0:T(8,128)S(1)} collective-permute-done((f32[520,128]{1,0:T(8,128)S(1)}, f32[520,128]{1,0:T(8,128)S(1)}, u32[]{:S(2)}, u32[]{:S(2)}) %collective-permute-start.6) | collective-permute-done | bytes 266272 | tf_op jit(solution)/shard_map/ppermute | solution.py:177
  29.1 2.2 %copy-done.1 = f32[1,1,64,128,128]{4,3,2,1,0:T(8,128)S(1)} copy-done((f32[1,1,64,128,128]{4,3,2,1,0:T(8,128)S(1)}, f32[1,1,64,128,128]{4,3,2,1,0:T(8,128)}, u32[]{:S(2)}) %copy-start.1) | copy-done | bytes 4194328
  31.3 1.8 %shard_map.61 = (f32[512,128]{1,0:T(8,128)S(1)}, f32[72,128]{1,0:T(8,128)S(1)}, f32[8,128]{1,0:T(8,128)S(1)}) custom-call(s32[64]{0:T(128)S(1)} %bitcast.18, f32[520,128]{1,0:T(8,128)S(1)} %shard_map.60.half, f32[520,128]{1,0:T(8,128)S(1)} %collective-permute-done.6.other, f32[8192,128]{1,0:T(8,128)S(1)} %bitcast.12), custom_call_target="tpu_custom_call" | custom-call | tf_op jit(solution)/shard_map/pallas_call | solution.py:151
  33.1 1.7 %collective-permute-start.7 = (f32[72,128]{1,0:T(8,128)S(1)}, f32[72,128]{1,0:T(8,128)S(1)}, u32[]{:S(2)}, u32[]{:S(2)}) collective-permute-start(f32[72,128]{1,0:T(8,128)S(1)} %get-tuple-element.22.refs_0_), channel_id=1, source_target_pairs={{0,1},{1,0},{2,3},{3,2},{4,5},{5,4},{6,7},{7,6},{8,9},{9,8},{10,11... | collective-permute-start | bytes 110600 | tf_op jit(solution)/shard_map/ppermute | solution.py:186
  34.8 2.2 %collective-permute-done.7.refs_1_ = f32[72,128]{1,0:T(8,128)S(1)} collective-permute-done((f32[72,128]{1,0:T(8,128)S(1)}, f32[72,128]{1,0:T(8,128)S(1)}, u32[]{:S(2)}, u32[]{:S(2)}) %collective-permute-start.7) | collective-permute-done | bytes 36896 | tf_op jit(solution)/shard_map/ppermute | solution.py:186
  37.1 2.4 %shard_map.62 = (f32[496,128]{1,0:T(8,128)S(1)}, f32[72,128]{1,0:T(8,128)S(1)}, f32[8,128]{1,0:T(8,128)S(1)}) custom-call(s32[64]{0:T(128)S(1)} %and_select_fusion.1.rows_at, f32[1,128]{1,0:T(1,128)S(1)} %fusion.row_index, f32[496,128]{1,0:T(8,128)S(1)} %pad_maximum_fusion.u_raw.u_raw_before, f32[8,128]{1,0:T(8,128)S(1)} %get-tuple-element.21.beta.refs_6_, ...), custom_call_target="tpu_custom_call" | custom-call | tf_op jit(solution)/shard_map/pallas_call | solution.py:151
  39.6 1.2 %collective-permute-done.8 = f32[72,128]{1,0:T(8,128)S(1)} collective-permute-done((f32[72,128]{1,0:T(8,128)S(1)}, f32[72,128]{1,0:T(8,128)S(1)}, u32[]{:S(2)}, u32[]{:S(2)}) %collective-permute-start.8) | collective-permute-done | bytes 36896 | tf_op jit(solution)/shard_map/ppermute | solution.py:177
  40.8 1.4 %collective-permute-start.12 = (f32[144,128]{1,0:T(8,128)S(1)}, f32[144,128]{1,0:T(8,128)S(1)}, u32[]{:S(2)}, u32[]{:S(2)}) collective-permute-start(f32[144,128]{1,0:T(8,128)S(1)} %constant_dynamic-update-slice_fusion.own), channel_id=1, source_target_pairs={{0,20},{2,30},{4,16},{6,26},{8,28},{10,22},{12,24},{14,18},{16,4},... | collective-permute-start | bytes 221192 | tf_op jit(solution)/shard_map/ppermute | solution.py:181
  42.2 2.0 %collective-permute-start.11 = (f32[144,128]{1,0:T(8,128)S(1)}, f32[144,128]{1,0:T(8,128)S(1)}, u32[]{:S(2)}, u32[]{:S(2)}) collective-permute-start(f32[144,128]{1,0:T(8,128)S(1)} %constant_dynamic-update-slice_fusion.own), channel_id=1, source_target_pairs={{0,8},{2,26},{4,12},{6,30},{8,0},{10,18},{12,4},{14,22},{16,24},{1... | collective-permute-start | bytes 221192 | tf_op jit(solution)/shard_map/ppermute | solution.py:181
  44.2 1.0 %collective-permute-start.10 = (f32[144,128]{1,0:T(8,128)S(1)}, f32[144,128]{1,0:T(8,128)S(1)}, u32[]{:S(2)}, u32[]{:S(2)}) collective-permute-start(f32[144,128]{1,0:T(8,128)S(1)} %constant_dynamic-update-slice_fusion.own), channel_id=1, source_target_pairs={{0,12},{2,14},{4,8},{6,10},{8,4},{10,6},{12,0},{14,2},{16,28},{18,... | collective-permute-start | bytes 221192 | tf_op jit(solution)/shard_map/ppermute | solution.py:181
  45.7 4.1 %collective-permute-done.12.refs_3_ = f32[144,128]{1,0:T(8,128)S(1)} collective-permute-done((f32[144,128]{1,0:T(8,128)S(1)}, f32[144,128]{1,0:T(8,128)S(1)}, u32[]{:S(2)}, u32[]{:S(2)}) %collective-permute-start.12) | collective-permute-done | bytes 73760 | tf_op jit(solution)/shard_map/ppermute | solution.py:181
  49.8 2.3 %collective-permute-done.10.refs_1_ = f32[144,128]{1,0:T(8,128)S(1)} collective-permute-done((f32[144,128]{1,0:T(8,128)S(1)}, f32[144,128]{1,0:T(8,128)S(1)}, u32[]{:S(2)}, u32[]{:S(2)}) %collective-permute-start.10) | collective-permute-done | bytes 73760 | tf_op jit(solution)/shard_map/ppermute | solution.py:181
  52.7 1.4 %collective-permute-done.13.other = f32[520,128]{1,0:T(8,128)S(1)} collective-permute-done((f32[520,128]{1,0:T(8,128)S(1)}, f32[520,128]{1,0:T(8,128)S(1)}, u32[]{:S(2)}, u32[]{:S(2)}) %collective-permute-start.13) | collective-permute-done | bytes 266272 | tf_op jit(solution)/shard_map/ppermute | solution.py:177
  54.1 1.8 %shard_map.64 = (f32[512,128]{1,0:T(8,128)S(1)}, f32[72,128]{1,0:T(8,128)S(1)}, f32[8,128]{1,0:T(8,128)S(1)}) custom-call(s32[64]{0:T(128)S(1)} %bitcast.19, f32[520,128]{1,0:T(8,128)S(1)} %shard_map.63.half, f32[520,128]{1,0:T(8,128)S(1)} %collective-permute-done.13.other, f32[512,128]{1,0:T(8,128)S(1)} %get-tuple-element.25.refs_0_, ...), custom_call_target="tpu_custom_call" | custom-call | tf_op jit(solution)/shard_map/pallas_call | solution.py:151
  55.9 1.6 %collective-permute-start.14 = (f32[72,128]{1,0:T(8,128)S(1)}, f32[72,128]{1,0:T(8,128)S(1)}, u32[]{:S(2)}, u32[]{:S(2)}) collective-permute-start(f32[72,128]{1,0:T(8,128)S(1)} %get-tuple-element.28.refs_0_), channel_id=1, source_target_pairs={{0,1},{1,0},{2,3},{3,2},{4,5},{5,4},{6,7},{7,6},{8,9},{9,8},{10,11... | collective-permute-start | bytes 110600 | tf_op jit(solution)/shard_map/ppermute | solution.py:186
  57.5 2.4 %collective-permute-done.14.refs_1_ = f32[72,128]{1,0:T(8,128)S(1)} collective-permute-done((f32[72,128]{1,0:T(8,128)S(1)}, f32[72,128]{1,0:T(8,128)S(1)}, u32[]{:S(2)}, u32[]{:S(2)}) %collective-permute-start.14) | collective-permute-done | bytes 36896 | tf_op jit(solution)/shard_map/ppermute | solution.py:186
  59.9 2.4 %shard_map.65 = (f32[496,128]{1,0:T(8,128)S(1)}, f32[72,128]{1,0:T(8,128)S(1)}, f32[8,128]{1,0:T(8,128)S(1)}) custom-call(s32[64]{0:T(128)S(1)} %and_select_fusion.1.rows_at, f32[1,128]{1,0:T(1,128)S(1)} %fusion.row_index, f32[496,128]{1,0:T(8,128)S(1)} %get-tuple-element.23.u_raw_before, f32[8,128]{1,0:T(8,128)S(1)} %get-tuple-element.27.beta.refs_7_, ...), custom_call_target="tpu_custom_call" | custom-call | tf_op jit(solution)/shard_map/pallas_call | solution.py:151
  62.4 1.2 %collective-permute-done.15 = f32[72,128]{1,0:T(8,128)S(1)} collective-permute-done((f32[72,128]{1,0:T(8,128)S(1)}, f32[72,128]{1,0:T(8,128)S(1)}, u32[]{:S(2)}, u32[]{:S(2)}) %collective-permute-start.15) | collective-permute-done | bytes 36896 | tf_op jit(solution)/shard_map/ppermute | solution.py:177
  63.6 1.4 %collective-permute-start.19 = (f32[144,128]{1,0:T(8,128)S(1)}, f32[144,128]{1,0:T(8,128)S(1)}, u32[]{:S(2)}, u32[]{:S(2)}) collective-permute-start(f32[144,128]{1,0:T(8,128)S(1)} %constant_dynamic-update-slice_fusion.2.own), channel_id=1, source_target_pairs={{0,20},{2,30},{4,16},{6,26},{8,28},{10,22},{12,24},{14,18},{16,4},... | collective-permute-start | bytes 221192 | tf_op jit(solution)/shard_map/ppermute | solution.py:181
  65.0 2.0 %collective-permute-start.18 = (f32[144,128]{1,0:T(8,128)S(1)}, f32[144,128]{1,0:T(8,128)S(1)}, u32[]{:S(2)}, u32[]{:S(2)}) collective-permute-start(f32[144,128]{1,0:T(8,128)S(1)} %constant_dynamic-update-slice_fusion.2.own), channel_id=1, source_target_pairs={{0,8},{2,26},{4,12},{6,30},{8,0},{10,18},{12,4},{14,22},{16,24},{1... | collective-permute-start | bytes 221192 | tf_op jit(solution)/shard_map/ppermute | solution.py:181
  67.1 1.4 %collective-permute-start.16 = (f32[144,128]{1,0:T(8,128)S(1)}, f32[144,128]{1,0:T(8,128)S(1)}, u32[]{:S(2)}, u32[]{:S(2)}) collective-permute-start(f32[144,128]{1,0:T(8,128)S(1)} %constant_dynamic-update-slice_fusion.2.own), channel_id=1, source_target_pairs={{0,4},{2,18},{4,0},{6,22},{8,12},{10,26},{12,8},{14,30},{16,20},{1... | collective-permute-start | bytes 221192 | tf_op jit(solution)/shard_map/ppermute | solution.py:181
  68.5 2.8 %collective-permute-done.19.refs_3_ = f32[144,128]{1,0:T(8,128)S(1)} collective-permute-done((f32[144,128]{1,0:T(8,128)S(1)}, f32[144,128]{1,0:T(8,128)S(1)}, u32[]{:S(2)}, u32[]{:S(2)}) %collective-permute-start.19) | collective-permute-done | bytes 73760 | tf_op jit(solution)/shard_map/ppermute | solution.py:181
  71.3 1.4 %collective-permute-done.18.refs_2_ = f32[144,128]{1,0:T(8,128)S(1)} collective-permute-done((f32[144,128]{1,0:T(8,128)S(1)}, f32[144,128]{1,0:T(8,128)S(1)}, u32[]{:S(2)}, u32[]{:S(2)}) %collective-permute-start.18) | collective-permute-done | bytes 73760 | tf_op jit(solution)/shard_map/ppermute | solution.py:181
  72.7 1.5 %collective-permute-done.17.refs_1_ = f32[144,128]{1,0:T(8,128)S(1)} collective-permute-done((f32[144,128]{1,0:T(8,128)S(1)}, f32[144,128]{1,0:T(8,128)S(1)}, u32[]{:S(2)}, u32[]{:S(2)}) %collective-permute-start.17) | collective-permute-done | bytes 73760 | tf_op jit(solution)/shard_map/ppermute | solution.py:181
  74.8 1.5 %collective-permute-done.20.other = f32[520,128]{1,0:T(8,128)S(1)} collective-permute-done((f32[520,128]{1,0:T(8,128)S(1)}, f32[520,128]{1,0:T(8,128)S(1)}, u32[]{:S(2)}, u32[]{:S(2)}) %collective-permute-start.20) | collective-permute-done | bytes 266272 | tf_op jit(solution)/shard_map/ppermute | solution.py:177
  76.3 1.8 %shard_map.67 = (f32[512,128]{1,0:T(8,128)S(1)}, f32[72,128]{1,0:T(8,128)S(1)}, f32[8,128]{1,0:T(8,128)S(1)}) custom-call(s32[64]{0:T(128)S(1)} %bitcast.20, f32[520,128]{1,0:T(8,128)S(1)} %shard_map.66.half, f32[520,128]{1,0:T(8,128)S(1)} %collective-permute-done.20.other, f32[512,128]{1,0:T(8,128)S(1)} %get-tuple-element.31.refs_0_, ...), custom_call_target="tpu_custom_call" | custom-call | tf_op jit(solution)/shard_map/pallas_call | solution.py:151
  78.1 1.5 %collective-permute-start.21 = (f32[72,128]{1,0:T(8,128)S(1)}, f32[72,128]{1,0:T(8,128)S(1)}, u32[]{:S(2)}, u32[]{:S(2)}) collective-permute-start(f32[72,128]{1,0:T(8,128)S(1)} %get-tuple-element.34.refs_0_), channel_id=1, source_target_pairs={{0,1},{1,0},{2,3},{3,2},{4,5},{5,4},{6,7},{7,6},{8,9},{9,8},{10,11... | collective-permute-start | bytes 110600 | tf_op jit(solution)/shard_map/ppermute | solution.py:186
  79.6 2.5 %collective-permute-done.21.refs_1_ = f32[72,128]{1,0:T(8,128)S(1)} collective-permute-done((f32[72,128]{1,0:T(8,128)S(1)}, f32[72,128]{1,0:T(8,128)S(1)}, u32[]{:S(2)}, u32[]{:S(2)}) %collective-permute-start.21) | collective-permute-done | bytes 36896 | tf_op jit(solution)/shard_map/ppermute | solution.py:186
  82.1 0.9 shard_map.68
  83.0 1.1 %collective-permute-done.22 = f32[8,128]{1,0:T(8,128)S(1)} collective-permute-done((f32[8,128]{1,0:T(8,128)S(1)}, f32[8,128]{1,0:T(8,128)S(1)}, u32[]{:S(2)}, u32[]{:S(2)}) %collective-permute-start.22) | collective-permute-done | bytes 4128 | tf_op jit(solution)/shard_map/ppermute | solution.py:177
  84.2 1.1 %collective-permute-start.26 = (f32[8,128]{1,0:T(8,128)S(1)}, f32[8,128]{1,0:T(8,128)S(1)}, u32[]{:S(2)}, u32[]{:S(2)}) collective-permute-start(f32[8,128]{1,0:T(8,128)S(1)} %add.46), channel_id=1, source_target_pairs={{0,20},{2,30},{4,16},{6,26},{8,28},{10,22},{12,24},{14,18},{16,4},... | collective-permute-start | bytes 12296 | tf_op jit(solution)/shard_map/ppermute | solution.py:181
  85.3 2.0 %collective-permute-start.25 = (f32[8,128]{1,0:T(8,128)S(1)}, f32[8,128]{1,0:T(8,128)S(1)}, u32[]{:S(2)}, u32[]{:S(2)}) collective-permute-start(f32[8,128]{1,0:T(8,128)S(1)} %add.46), channel_id=1, source_target_pairs={{0,8},{2,26},{4,12},{6,30},{8,0},{10,18},{12,4},{14,22},{16,24},{1... | collective-permute-start | bytes 12296 | tf_op jit(solution)/shard_map/ppermute | solution.py:181
  87.9 0.9 collective-permute-start.23
  89.6 2.2 %collective-permute-done.24 = f32[8,128]{1,0:T(8,128)S(1)} collective-permute-done((f32[8,128]{1,0:T(8,128)S(1)}, f32[8,128]{1,0:T(8,128)S(1)}, u32[]{:S(2)}, u32[]{:S(2)}) %collective-permute-start.24) | collective-permute-done | bytes 4128 | tf_op jit(solution)/shard_map/ppermute | solution.py:181
  92.0 1.0 %collective-permute-done.27 = f32[8,128]{1,0:T(8,128)S(1)} collective-permute-done((f32[8,128]{1,0:T(8,128)S(1)}, f32[8,128]{1,0:T(8,128)S(1)}, u32[]{:S(2)}, u32[]{:S(2)}) %collective-permute-start.27) | collective-permute-done | bytes 4128 | tf_op jit(solution)/shard_map/ppermute | solution.py:177
  (51 shorter events, 8.1 us)
Async XLA Ops:
  0.6 26.9 %copy-start.4 = (s32[1,1,64]{2,1,0:T(1,128)S(1)}, s32[1,1,64]{2,1,0:T(1,128)}, u32[]{:S(2)}) copy-start(s32[1,1,64]{2,1,0:T(1,128)} %param.6) | copy-start | bytes 772
  0.6 28.5 %copy-start.3 = (s32[1,1,64]{2,1,0:T(1,128)S(1)}, s32[1,1,64]{2,1,0:T(1,128)}, u32[]{:S(2)}) copy-start(s32[1,1,64]{2,1,0:T(1,128)} %param.7) | copy-start | bytes 772
  2.4 6.5 %collective-permute-start = (f32[256,128]{1,0:T(8,128)S(1)}, f32[256,128]{1,0:T(8,128)S(1)}, u32[]{:S(2)}, u32[]{:S(2)}) collective-permute-start(f32[256,128]{1,0:T(8,128)S(1)} %pad_maximum_fusion.1), channel_id=1, source_target_pairs={{0,1},{1,0},{2,3},{3,2},{4,5},{5,4},{6,7},{7,6},{8,9},{9,8},{10,11... | collective-permute-start | bytes 393224 | tf_op jit(solution)/shard_map/ppermute | solution.py:186
  9.9 2.2 %copy-start = (f32[1,1,64,128,128]{4,3,2,1,0:T(8,128)S(1)}, f32[1,1,64,128,128]{4,3,2,1,0:T(8,128)}, u32[]{:S(2)}) copy-start(f32[1,1,64,128,128]{4,3,2,1,0:T(8,128)} %param.5) | copy-start | bytes 12582916
  14.0 1.3 %collective-permute-start.1 = (f32[72,128]{1,0:T(8,128)S(1)}, f32[72,128]{1,0:T(8,128)S(1)}, u32[]{:S(2)}, u32[]{:S(2)}) collective-permute-start(f32[72,128]{1,0:T(8,128)S(1)} %shard_map.59), channel_id=1, source_target_pairs={{0,2},{2,0},{4,6},{6,4},{8,10},{10,8},{12,14},{14,12},{16,18},{18,... | collective-permute-start | bytes 110600 | tf_op jit(solution)/shard_map/ppermute | solution.py:177
  15.3 8.4 %collective-permute-start.5 = (f32[144,128]{1,0:T(8,128)S(1)}, f32[144,128]{1,0:T(8,128)S(1)}, u32[]{:S(2)}, u32[]{:S(2)}) collective-permute-start(f32[144,128]{1,0:T(8,128)S(1)} %pad_maximum_fusion.2.own), channel_id=1, source_target_pairs={{0,20},{2,30},{4,16},{6,26},{8,28},{10,22},{12,24},{14,18},{16,4},... | collective-permute-start | bytes 221192 | tf_op jit(solution)/shard_map/ppermute | solution.py:181
  19.0 7.4 %collective-permute-start.4 = (f32[144,128]{1,0:T(8,128)S(1)}, f32[144,128]{1,0:T(8,128)S(1)}, u32[]{:S(2)}, u32[]{:S(2)}) collective-permute-start(f32[144,128]{1,0:T(8,128)S(1)} %pad_maximum_fusion.2.own), channel_id=1, source_target_pairs={{0,8},{2,26},{4,12},{6,30},{8,0},{10,18},{12,4},{14,22},{16,24},{1... | collective-permute-start | bytes 221192 | tf_op jit(solution)/shard_map/ppermute | solution.py:181
  20.6 6.4 %collective-permute-start.3 = (f32[144,128]{1,0:T(8,128)S(1)}, f32[144,128]{1,0:T(8,128)S(1)}, u32[]{:S(2)}, u32[]{:S(2)}) collective-permute-start(f32[144,128]{1,0:T(8,128)S(1)} %pad_maximum_fusion.2.own), channel_id=1, source_target_pairs={{0,12},{2,14},{4,8},{6,10},{8,4},{10,6},{12,0},{14,2},{16,28},{18,... | collective-permute-start | bytes 221192 | tf_op jit(solution)/shard_map/ppermute | solution.py:181
  21.0 6.0 %collective-permute-start.2 = (f32[144,128]{1,0:T(8,128)S(1)}, f32[144,128]{1,0:T(8,128)S(1)}, u32[]{:S(2)}, u32[]{:S(2)}) collective-permute-start(f32[144,128]{1,0:T(8,128)S(1)} %pad_maximum_fusion.2.own), channel_id=1, source_target_pairs={{0,4},{2,18},{4,0},{6,22},{8,12},{10,26},{12,8},{14,30},{16,20},{1... | collective-permute-start | bytes 221192 | tf_op jit(solution)/shard_map/ppermute | solution.py:181
  27.5 1.6 %collective-permute-start.6 = (f32[520,128]{1,0:T(8,128)S(1)}, f32[520,128]{1,0:T(8,128)S(1)}, u32[]{:S(2)}, u32[]{:S(2)}) collective-permute-start(f32[520,128]{1,0:T(8,128)S(1)} %shard_map.60.half), channel_id=1, source_target_pairs={{0,2},{2,0},{4,6},{6,4},{8,10},{10,8},{12,14},{14,12},{16,18},{18,... | collective-permute-start | bytes 798728 | tf_op jit(solution)/shard_map/ppermute | solution.py:177
  29.1 2.2 %copy-start.1 = (f32[1,1,64,128,128]{4,3,2,1,0:T(8,128)S(1)}, f32[1,1,64,128,128]{4,3,2,1,0:T(8,128)}, u32[]{:S(2)}) copy-start(f32[1,1,64,128,128]{4,3,2,1,0:T(8,128)} %param.5) | copy-start | bytes 12582916
  31.3 5.8 %copy-start.2 = (f32[1,1,64,128,128]{4,3,2,1,0:T(8,128)S(1)}, f32[1,1,64,128,128]{4,3,2,1,0:T(8,128)}, u32[]{:S(2)}) copy-start(f32[1,1,64,128,128]{4,3,2,1,0:T(8,128)} %param.5) | copy-start | bytes 12582916
  33.1 4.0 %collective-permute-start.7 = (f32[72,128]{1,0:T(8,128)S(1)}, f32[72,128]{1,0:T(8,128)S(1)}, u32[]{:S(2)}, u32[]{:S(2)}) collective-permute-start(f32[72,128]{1,0:T(8,128)S(1)} %get-tuple-element.22.refs_0_), channel_id=1, source_target_pairs={{0,1},{1,0},{2,3},{3,2},{4,5},{5,4},{6,7},{7,6},{8,9},{9,8},{10,11... | collective-permute-start | bytes 110600 | tf_op jit(solution)/shard_map/ppermute | solution.py:186
  39.5 1.3 %collective-permute-start.8 = (f32[72,128]{1,0:T(8,128)S(1)}, f32[72,128]{1,0:T(8,128)S(1)}, u32[]{:S(2)}, u32[]{:S(2)}) collective-permute-start(f32[72,128]{1,0:T(8,128)S(1)} %get-tuple-element.24), channel_id=1, source_target_pairs={{0,2},{2,0},{4,6},{6,4},{8,10},{10,8},{12,14},{14,12},{16,18},{18,... | collective-permute-start | bytes 110600 | tf_op jit(solution)/shard_map/ppermute | solution.py:177
  40.8 9.0 %collective-permute-start.12 = (f32[144,128]{1,0:T(8,128)S(1)}, f32[144,128]{1,0:T(8,128)S(1)}, u32[]{:S(2)}, u32[]{:S(2)}) collective-permute-start(f32[144,128]{1,0:T(8,128)S(1)} %constant_dynamic-update-slice_fusion.own), channel_id=1, source_target_pairs={{0,20},{2,30},{4,16},{6,26},{8,28},{10,22},{12,24},{14,18},{16,4},... | collective-permute-start | bytes 221192 | tf_op jit(solution)/shard_map/ppermute | solution.py:181
  42.2 7.6 %collective-permute-start.11 = (f32[144,128]{1,0:T(8,128)S(1)}, f32[144,128]{1,0:T(8,128)S(1)}, u32[]{:S(2)}, u32[]{:S(2)}) collective-permute-start(f32[144,128]{1,0:T(8,128)S(1)} %constant_dynamic-update-slice_fusion.own), channel_id=1, source_target_pairs={{0,8},{2,26},{4,12},{6,30},{8,0},{10,18},{12,4},{14,22},{16,24},{1... | collective-permute-start | bytes 221192 | tf_op jit(solution)/shard_map/ppermute | solution.py:181
  44.2 7.9 %collective-permute-start.10 = (f32[144,128]{1,0:T(8,128)S(1)}, f32[144,128]{1,0:T(8,128)S(1)}, u32[]{:S(2)}, u32[]{:S(2)}) collective-permute-start(f32[144,128]{1,0:T(8,128)S(1)} %constant_dynamic-update-slice_fusion.own), channel_id=1, source_target_pairs={{0,12},{2,14},{4,8},{6,10},{8,4},{10,6},{12,0},{14,2},{16,28},{18,... | collective-permute-start | bytes 221192 | tf_op jit(solution)/shard_map/ppermute | solution.py:181
  45.2 6.9 %collective-permute-start.9 = (f32[144,128]{1,0:T(8,128)S(1)}, f32[144,128]{1,0:T(8,128)S(1)}, u32[]{:S(2)}, u32[]{:S(2)}) collective-permute-start(f32[144,128]{1,0:T(8,128)S(1)} %constant_dynamic-update-slice_fusion.own), channel_id=1, source_target_pairs={{0,4},{2,18},{4,0},{6,22},{8,12},{10,26},{12,8},{14,30},{16,20},{1... | collective-permute-start | bytes 221192 | tf_op jit(solution)/shard_map/ppermute | solution.py:181
  52.5 1.6 %collective-permute-start.13 = (f32[520,128]{1,0:T(8,128)S(1)}, f32[520,128]{1,0:T(8,128)S(1)}, u32[]{:S(2)}, u32[]{:S(2)}) collective-permute-start(f32[520,128]{1,0:T(8,128)S(1)} %shard_map.63.half), channel_id=1, source_target_pairs={{0,2},{2,0},{4,6},{6,4},{8,10},{10,8},{12,14},{14,12},{16,18},{18,... | collective-permute-start | bytes 798728 | tf_op jit(solution)/shard_map/ppermute | solution.py:177
  55.9 4.0 %collective-permute-start.14 = (f32[72,128]{1,0:T(8,128)S(1)}, f32[72,128]{1,0:T(8,128)S(1)}, u32[]{:S(2)}, u32[]{:S(2)}) collective-permute-start(f32[72,128]{1,0:T(8,128)S(1)} %get-tuple-element.28.refs_0_), channel_id=1, source_target_pairs={{0,1},{1,0},{2,3},{3,2},{4,5},{5,4},{6,7},{7,6},{8,9},{9,8},{10,11... | collective-permute-start | bytes 110600 | tf_op jit(solution)/shard_map/ppermute | solution.py:186
  62.3 1.3 %collective-permute-start.15 = (f32[72,128]{1,0:T(8,128)S(1)}, f32[72,128]{1,0:T(8,128)S(1)}, u32[]{:S(2)}, u32[]{:S(2)}) collective-permute-start(f32[72,128]{1,0:T(8,128)S(1)} %get-tuple-element.30), channel_id=1, source_target_pairs={{0,2},{2,0},{4,6},{6,4},{8,10},{10,8},{12,14},{14,12},{16,18},{18,... | collective-permute-start | bytes 110600 | tf_op jit(solution)/shard_map/ppermute | solution.py:177
  63.6 7.7 %collective-permute-start.19 = (f32[144,128]{1,0:T(8,128)S(1)}, f32[144,128]{1,0:T(8,128)S(1)}, u32[]{:S(2)}, u32[]{:S(2)}) collective-permute-start(f32[144,128]{1,0:T(8,128)S(1)} %constant_dynamic-update-slice_fusion.2.own), channel_id=1, source_target_pairs={{0,20},{2,30},{4,16},{6,26},{8,28},{10,22},{12,24},{14,18},{16,4},... | collective-permute-start | bytes 221192 | tf_op jit(solution)/shard_map/ppermute | solution.py:181
  65.0 7.7 %collective-permute-start.18 = (f32[144,128]{1,0:T(8,128)S(1)}, f32[144,128]{1,0:T(8,128)S(1)}, u32[]{:S(2)}, u32[]{:S(2)}) collective-permute-start(f32[144,128]{1,0:T(8,128)S(1)} %constant_dynamic-update-slice_fusion.2.own), channel_id=1, source_target_pairs={{0,8},{2,26},{4,12},{6,30},{8,0},{10,18},{12,4},{14,22},{16,24},{1... | collective-permute-start | bytes 221192 | tf_op jit(solution)/shard_map/ppermute | solution.py:181
  67.0 7.2 %collective-permute-start.17 = (f32[144,128]{1,0:T(8,128)S(1)}, f32[144,128]{1,0:T(8,128)S(1)}, u32[]{:S(2)}, u32[]{:S(2)}) collective-permute-start(f32[144,128]{1,0:T(8,128)S(1)} %constant_dynamic-update-slice_fusion.2.own), channel_id=1, source_target_pairs={{0,12},{2,14},{4,8},{6,10},{8,4},{10,6},{12,0},{14,2},{16,28},{18,... | collective-permute-start | bytes 221192 | tf_op jit(solution)/shard_map/ppermute | solution.py:181
  67.1 7.1 %collective-permute-start.16 = (f32[144,128]{1,0:T(8,128)S(1)}, f32[144,128]{1,0:T(8,128)S(1)}, u32[]{:S(2)}, u32[]{:S(2)}) collective-permute-start(f32[144,128]{1,0:T(8,128)S(1)} %constant_dynamic-update-slice_fusion.2.own), channel_id=1, source_target_pairs={{0,4},{2,18},{4,0},{6,22},{8,12},{10,26},{12,8},{14,30},{16,20},{1... | collective-permute-start | bytes 221192 | tf_op jit(solution)/shard_map/ppermute | solution.py:181
  74.7 1.6 %collective-permute-start.20 = (f32[520,128]{1,0:T(8,128)S(1)}, f32[520,128]{1,0:T(8,128)S(1)}, u32[]{:S(2)}, u32[]{:S(2)}) collective-permute-start(f32[520,128]{1,0:T(8,128)S(1)} %shard_map.66.half), channel_id=1, source_target_pairs={{0,2},{2,0},{4,6},{6,4},{8,10},{10,8},{12,14},{14,12},{16,18},{18,... | collective-permute-start | bytes 798728 | tf_op jit(solution)/shard_map/ppermute | solution.py:177
  78.1 4.0 %collective-permute-start.21 = (f32[72,128]{1,0:T(8,128)S(1)}, f32[72,128]{1,0:T(8,128)S(1)}, u32[]{:S(2)}, u32[]{:S(2)}) collective-permute-start(f32[72,128]{1,0:T(8,128)S(1)} %get-tuple-element.34.refs_0_), channel_id=1, source_target_pairs={{0,1},{1,0},{2,3},{3,2},{4,5},{5,4},{6,7},{7,6},{8,9},{9,8},{10,11... | collective-permute-start | bytes 110600 | tf_op jit(solution)/shard_map/ppermute | solution.py:186
  83.0 1.2 %collective-permute-start.22 = (f32[8,128]{1,0:T(8,128)S(1)}, f32[8,128]{1,0:T(8,128)S(1)}, u32[]{:S(2)}, u32[]{:S(2)}) collective-permute-start(f32[8,128]{1,0:T(8,128)S(1)} %get-tuple-element.35), channel_id=1, source_target_pairs={{0,2},{2,0},{4,6},{6,4},{8,10},{10,8},{12,14},{14,12},{16,18},{18,... | collective-permute-start | bytes 12296 | tf_op jit(solution)/shard_map/ppermute | solution.py:177
  84.2 5.4 %collective-permute-start.26 = (f32[8,128]{1,0:T(8,128)S(1)}, f32[8,128]{1,0:T(8,128)S(1)}, u32[]{:S(2)}, u32[]{:S(2)}) collective-permute-start(f32[8,128]{1,0:T(8,128)S(1)} %add.46), channel_id=1, source_target_pairs={{0,20},{2,30},{4,16},{6,26},{8,28},{10,22},{12,24},{14,18},{16,4},... | collective-permute-start | bytes 12296 | tf_op jit(solution)/shard_map/ppermute | solution.py:181
  85.3 4.3 %collective-permute-start.25 = (f32[8,128]{1,0:T(8,128)S(1)}, f32[8,128]{1,0:T(8,128)S(1)}, u32[]{:S(2)}, u32[]{:S(2)}) collective-permute-start(f32[8,128]{1,0:T(8,128)S(1)} %add.46), channel_id=1, source_target_pairs={{0,8},{2,26},{4,12},{6,30},{8,0},{10,18},{12,4},{14,22},{16,24},{1... | collective-permute-start | bytes 12296 | tf_op jit(solution)/shard_map/ppermute | solution.py:181
  87.3 4.5 %collective-permute-start.24 = (f32[8,128]{1,0:T(8,128)S(1)}, f32[8,128]{1,0:T(8,128)S(1)}, u32[]{:S(2)}, u32[]{:S(2)}) collective-permute-start(f32[8,128]{1,0:T(8,128)S(1)} %add.46), channel_id=1, source_target_pairs={{0,12},{2,14},{4,8},{6,10},{8,4},{10,6},{12,0},{14,2},{16,28},{18,... | collective-permute-start | bytes 12296 | tf_op jit(solution)/shard_map/ppermute | solution.py:181
  87.9 4.0 %collective-permute-start.23 = (f32[8,128]{1,0:T(8,128)S(1)}, f32[8,128]{1,0:T(8,128)S(1)}, u32[]{:S(2)}, u32[]{:S(2)}) collective-permute-start(f32[8,128]{1,0:T(8,128)S(1)} %add.46), channel_id=1, source_target_pairs={{0,4},{2,18},{4,0},{6,22},{8,12},{10,26},{12,8},{14,30},{16,20},{1... | collective-permute-start | bytes 12296 | tf_op jit(solution)/shard_map/ppermute | solution.py:181
  91.8 1.2 %collective-permute-start.27 = (f32[8,128]{1,0:T(8,128)S(1)}, f32[8,128]{1,0:T(8,128)S(1)}, u32[]{:S(2)}, u32[]{:S(2)}) collective-permute-start(f32[8,128]{1,0:T(8,128)S(1)} %add_add_fusion), channel_id=1, source_target_pairs={{0,2},{2,0},{4,6},{6,4},{8,10},{10,8},{12,14},{14,12},{16,18},{18,... | collective-permute-start | bytes 12296 | tf_op jit(solution)/shard_map/ppermute | solution.py:177

commit v2 on v1

v2 whole, which is shorter than its diff:
```python
import functools

import jax
import jax.numpy as jnp
from jax import lax
from jax.experimental import pallas as pl
from jax.experimental.pallas import tpu as pltpu
from jax.sharding import PartitionSpec as P

BLK = 128
ROWB_DEV = 496
COLB_DEV = 512
NB_DEV = 64
ITERS = 3
MSG = NB_DEV + 8
INDEX, SQUARE = NB_DEV, NB_DEV + 1
COL_ROW, ROW_ROW, SHIFT, IS_FIRST = (slice(k, k + 1) for k in range(4))
ROWS_HELD = 512
PARTS = 8
VMEM_LIMIT = 16 * 1024 * 1024

f32 = jnp.float32
bf16 = jnp.bfloat16


def total(x):
    s = jnp.sum(jnp.sum(x, axis=0, keepdims=True), axis=1, keepdims=True)
    return jnp.broadcast_to(s, (1, BLK))


def halves(x):
    high = x.astype(bf16)
    return high, (x - high.astype(f32)).astype(bf16)


def place_sum(index_row, parts, rows):
    k = parts.shape[0]
    at = lax.broadcasted_iota(jnp.int32, (rows, k), 0).astype(f32)
    hot = jnp.where(at == index_row, 1.0, 0.0).astype(bf16)
    high = parts.astype(bf16)
    rest = parts - high.astype(f32)
    mid = rest.astype(bf16)
    low = (rest - mid.astype(f32)).astype(bf16)
    three = jnp.concatenate([high, mid, low], axis=1)
    out = jnp.dot(hot, three, preferred_element_type=f32)
    return out[:, :BLK] + (out[:, BLK : 2 * BLK] + out[:, 2 * BLK :])


def pick(at, x):
    rows = x.shape[0]
    lane = lax.broadcasted_iota(jnp.int32, (NB_DEV, rows), 1).astype(f32)
    hot = jnp.where(lane == jnp.concatenate([at] * (rows // BLK), axis=1), 1.0, 0.0).astype(bf16)
    return jnp.dot(hot, jnp.concatenate(halves(x), axis=1), preferred_element_type=f32)


def times_tiles(tiles, first, picked, msg):
    per = 8
    row = lax.broadcasted_iota(jnp.int32, (2 * per, BLK), 0)
    for g in range(0, NB_DEV, per):
        both = jnp.concatenate([picked[g : g + per, :BLK], picked[g : g + per, BLK:]], axis=0)
        lhs = jnp.concatenate([jnp.where(row % per == t, both, 0.0) for t in range(per)], axis=1).astype(bf16)
        out = jnp.dot(lhs, tiles[(first + g) * BLK : (first + g + per) * BLK, :], preferred_element_type=f32)
        out = out[:, :BLK] + out[:, BLK:]
        msg[g : g + per, :] = out[:per] + out[per:]


def write_end(msg, index_row, square):
    row = lax.broadcasted_iota(jnp.int32, (MSG - NB_DEV, BLK), 0)
    msg[NB_DEV:, :] = jnp.where(row == 0, index_row, jnp.where(row == 1, square, 0.0))


def tiles_kernel(blocks, out, held, sems):
    per = held.shape[0] // PARTS
    parts = [
        pltpu.make_async_copy(blocks.at[pl.ds(k * per, per)], held.at[pl.ds(k * per, per)], sems.at[k])
        for k in range(PARTS)
    ]
    for part in parts:
        part.start()
    for k, part in enumerate(parts):
        part.wait()
        for at in range(k * per, (k + 1) * per, BLK):
            block = held[at : at + BLK, :]
            for where, x in ((at, block), (held.shape[0] + at, block.T)):
                high, low = halves(x)
                out[where : where + BLK, :BLK] = high
                out[where : where + BLK, BLK:] = low


def first_kernel(n_col, tiles, *refs):
    pieces, (consts, ats, u_raw, msg, consts_out, ats_out) = refs[:n_col], refs[n_col:]
    consts_out[...] = consts[...]
    ats_out[...] = ats[...]
    per = pieces[0].shape[0]
    for k, piece in enumerate(pieces):
        u_raw[k * per : (k + 1) * per, :] = piece[...]
    u_raw[ROWB_DEV:, :] = jnp.zeros((ROWS_HELD - ROWB_DEV, BLK), f32)
    u = u_raw[...]
    times_tiles(tiles, 0, pick(ats[:NB_DEV, :], u), msg)
    write_end(msg, consts[COL_ROW, :], total(u * u))


def gather_sum_kernel(slot, tiles, consts, own, *refs):
    *others, out = refs
    first = consts[IS_FIRST, :] > 0
    n = 2 * NB_DEV
    parts, index, square = [], [], jnp.zeros((1, BLK), f32)
    for k, other in enumerate(others):
        m = jnp.where(first, own[...], other[...]) if k == slot else other[...]
        parts.append(m[:n])
        index.append(m[n : n + 1])
        square = square + m[n + 1 : n + 2]
    out[:COLB_DEV, :] = place_sum(jnp.concatenate(index, axis=1), jnp.concatenate(parts, axis=0), COLB_DEV)
    out[COLB_DEV:, :] = jnp.broadcast_to(square, (8, BLK))


def v_kernel(has_before, tiles, half, other, *refs):
    if has_before:
        v_raw_before, alpha, consts, ats, v_raw, msg, beta_out = refs
    else:
        consts, ats, v_raw, msg, beta_out = refs
    beta = jnp.sqrt(half[COLB_DEV : COLB_DEV + 1, :] + other[COLB_DEV : COLB_DEV + 1, :])
    v = (half[:COLB_DEV, :] + other[:COLB_DEV, :]) / beta
    if has_before:
        v = v - v_raw_before[...] * (beta / alpha[:1, :])
    v_raw[...] = v
    beta_out[...] = jnp.broadcast_to(beta, (8, BLK))
    times_tiles(tiles, NB_DEV, pick(ats[NB_DEV:, :], v), msg)
    write_end(msg, consts[ROW_ROW, :], total(v * v))


def u_kernel(n_col, last, *refs):
    if not last:
        tiles, *refs = refs
    consts, u_raw_before, beta, *refs = refs
    pieces, refs = refs[:n_col], refs[n_col:]
    if last:
        square_out, alpha_out = refs
    else:
        ats, u_raw, msg, alpha_out = refs
    square = pieces[0][SQUARE : SQUARE + 1, :]
    for piece in pieces[1:]:
        square = square + piece[SQUARE : SQUARE + 1, :]
    alpha = jnp.sqrt(square)
    alpha_out[...] = jnp.broadcast_to(alpha, (8, BLK))
    lane = lax.broadcasted_iota(jnp.int32, (1, BLK), 1)
    index = [
        jnp.where(lane < NB_DEV, a[INDEX : INDEX + 1, :], b[INDEX : INDEX + 1, :])
        for a, b in zip(pieces[::2], pieces[1::2])
    ]
    index = jnp.concatenate([i - consts[SHIFT, :] for i in index], axis=1)
    index = jnp.where(index < 0, index + ROWB_DEV, index)
    prods = jnp.concatenate([piece[:NB_DEV, :] for piece in pieces], axis=0)
    front = place_sum(index, prods, ROWS_HELD)
    u = front / alpha - u_raw_before[...] * (alpha / beta[:1, :])
    square = total(u * u)
    if last:
        square_out[...] = jnp.broadcast_to(square, (8, BLK))
        return
    u_raw[...] = u
    times_tiles(tiles, 0, pick(ats[:NB_DEV, :], u), msg)
    write_end(msg, consts[COL_ROW, :], square)


def end_kernel(square, *refs):
    v_raws, alphas, betas = refs[:ITERS], refs[ITERS : 2 * ITERS], refs[2 * ITERS : 3 * ITERS]
    out, residual = refs[3 * ITERS :]
    alpha = [a[:1, :] for a in alphas]
    beta = [b[:1, :] for b in betas] + [jnp.sqrt(square[:1, :])]
    phibar, rhobar = beta[0], alpha[0]
    x = None
    for k in range(ITERS):
        v = v_raws[k][...] / alpha[k]
        w = v if k == 0 else v - turn * w
        rho = jnp.sqrt(rhobar * rhobar + beta[k + 1] * beta[k + 1])
        cosine, sine = rhobar / rho, beta[k + 1] / rho
        phi = cosine * phibar
        phibar = sine * phibar
        step = phi / rho * w
        x = step if x is None else x + step
        if k + 1 < ITERS:
            turn = sine * alpha[k + 1] / rho
            rhobar = -cosine * alpha[k + 1]
    out[...] = x
    residual[...] = (phibar / beta[0])[:, :1]


def split_tiles(blocks):
    rows = blocks.shape[0]
    return pl.pallas_call(
        tiles_kernel,
        out_shape=pltpu.VMEM((2 * rows, 2 * BLK), bf16),
        in_specs=[pl.BlockSpec(memory_space=pl.ANY)],
        out_specs=pl.BlockSpec(memory_space=pltpu.VMEM),
        scratch_shapes=[pltpu.VMEM((rows, BLK), f32), pltpu.SemaphoreType.DMA((PARTS,))],
        compiler_params=pltpu.CompilerParams(vmem_limit_bytes=VMEM_LIMIT),
        cost_estimate=pl.CostEstimate(flops=0, bytes_accessed=4 * rows * BLK, transcendentals=0),
    )(pltpu.with_memory_space_constraint(blocks, pltpu.HBM))


def call(body, tiles, ins, outs):
    if tiles is not None:
        ins = [pltpu.with_memory_space_constraint(tiles, pltpu.VMEM)] + ins
    return pl.pallas_call(
        body,
        out_shape=[jax.ShapeDtypeStruct(s, f32) for s in outs],
        in_specs=[pl.BlockSpec(memory_space=pltpu.VMEM)] * len(ins),
        out_specs=[pl.BlockSpec(memory_space=pltpu.VMEM)] * len(outs),
        compiler_params=pltpu.CompilerParams(vmem_limit_bytes=VMEM_LIMIT),
    )(*ins)


def chip_steps(chips):
    if chips == 8:
        return [(1, 4), (3, 3), (2, 6), (5, 7)], 1
    steps = [(m, m + 1) for m in range(1, chips - 1, 2)] + [(chips - 1, chips - 1)]
    return steps, len(steps) - 1


def on_device(n_row, n_col, rhs, blocks, blk_row, blk_col):
    chips = n_row // 2
    steps, twice = chip_steps(chips)
    per_rhs = rhs.shape[0] // BLK
    per_out = COLB_DEV // n_row
    row, col = lax.axis_index("row"), lax.axis_index("col")

    def swap(x):
        return lax.ppermute(x, "row", [(r, r ^ 1) for r in range(n_row)])

    def to_chips(x):
        return [
            lax.ppermute(x, "row", [(r, r ^ (2 * step[r % 2])) for r in range(n_row)]) for step in steps
        ]

    def around_col(x):
        return [x] + [
            lax.ppermute(x, "col", [(i, (i - s) % n_col) for i in range(n_col)]) for s in range(1, n_col)
        ]

    pieces = around_col(rhs.reshape(per_rhs, BLK))
    shift = col * per_rhs

    blocks = blocks.reshape(NB_DEV * BLK, BLK)
    tiles = split_tiles(blocks)
    cols_here = blk_col.reshape(NB_DEV)
    rows_here = blk_row.reshape(NB_DEV)
    rows_turned = jnp.where(rows_here < shift, rows_here - shift + ROWB_DEV, rows_here - shift)
    consts = jnp.stack(
        [
            jnp.concatenate([cols_here, cols_here]),
            jnp.concatenate([rows_here, rows_here]),
            jnp.full((BLK,), shift),
            jnp.full((BLK,), 1 - row % 2),
        ]
        + [jnp.zeros((BLK,), jnp.int32)] * 4
    ).astype(f32)
    ats = jnp.concatenate([rows_turned, cols_here]).astype(f32)
    ats = jnp.broadcast_to(ats[:, None], (2 * NB_DEV, BLK))
    lane = lax.broadcasted_iota(jnp.int32, (MSG - NB_DEV, BLK), 1)
    end_row = lax.broadcasted_iota(jnp.int32, (MSG - NB_DEV, BLK), 0)

    def gather(msg):
        peer = swap(msg)
        a, b = msg[NB_DEV:], peer[NB_DEV:]
        end = jnp.where(end_row == 0, jnp.where(lane < NB_DEV, a, b), a + b)
        both = jnp.concatenate([msg[:NB_DEV], peer[:NB_DEV], end])
        others = to_chips(both)
        (half,) = call(
            functools.partial(gather_sum_kernel, twice), tiles, [consts, both] + others, [(COLB_DEV + 8, BLK)]
        )
        return half, swap(half)

    u_raw, msg, consts, ats = call(
        functools.partial(first_kernel, n_col),
        tiles,
        pieces + [consts, ats],
        [(ROWS_HELD, BLK), (MSG, BLK), consts.shape, ats.shape],
    )
    alphas, betas, v_raws = [], [], []
    for step in range(ITERS):
        half, other = gather(msg)
        before = [v_raws[-1], alphas[-1]] if step else []
        v_raw, msg, beta = call(
            functools.partial(v_kernel, step > 0),
            tiles,
            [half, other] + before + [consts, ats],
            [(COLB_DEV, BLK), (MSG, BLK), (8, BLK)],
        )
        v_raws.append(v_raw)
        betas.append(beta)
        last = step + 1 == ITERS
        ins = [consts, u_raw, beta] + around_col(msg)
        body = functools.partial(u_kernel, n_col, last)
        if last:
            square, alpha = call(body, None, ins, [(8, BLK), (8, BLK)])
        else:
            u_raw, msg, alpha = call(
                body, tiles, ins + [ats], [(ROWS_HELD, BLK), (MSG, BLK), (8, BLK)]
            )
        alphas.append(alpha)

    both = square + swap(square)
    parts = to_chips(both)
    parts[twice] = jnp.where(row % 2 == 0, both, parts[twice])
    half = functools.reduce(lambda a, b: a + b, parts)
    square = half + swap(half)
    mine = [lax.dynamic_slice_in_dim(v, row * per_out, per_out) for v in v_raws]
    out, residual = call(end_kernel, None, [square] + mine + alphas + betas, [(per_out, BLK), (1, 1)])
    return out.reshape(per_out * BLK), residual.reshape(())


def solution(mesh):
    return jax.shard_map(
        functools.partial(on_device, mesh.shape["row"], mesh.shape["col"]),
        mesh=mesh,
        in_specs=(
            P(("row", "col")),
            P("row", "col", None, None, None),
            P("row", "col", None),
            P("row", "col", None),
        ),
        out_specs=(P(("col", "row")), P()),
        check_vma=False,
    )
```

time: 94.5 us -> 80.2 us (0.85)
  local copies, waits for them, and re-layouts: 4.95 us -> 0.15 us
  Pallas kernels: 15.1 us -> 10.5 us
  starting transfers between devices: 30.2 us -> 27 us
  other arithmetic: 4.31 us -> 2.54 us
    pallas_call x11, Pallas kernels: 15.1 us -> 7.74 us  [call(): pl.pallas_call(body, out_shape=[jax.ShapeDtypeStruct(s, f32) for s in out...]
    unnamed x12 -> x2, local copies, waits for them, and re-layouts: 4.4 us -> 0.01 us
    ppermute x4, starting transfers between devices: 7.82 us -> 4.46 us  [around_col(): lax.ppermute(x, 'col', [(i, (i - s) % n_col) for i in range(n_col)])]
    pallas_call x0 -> x1, Pallas kernels: none -> 2.81 us  [split_tiles(): pl.pallas_call(tiles_kernel, out_shape=pltpu.VMEM((2 * rows, 2 * BLK), bf...]
    concatenate x3, other arithmetic: 1.84 us -> 0.02 us  [gather(): both = jnp.concatenate([msg[:NB_DEV], peer[:NB_DEV], end])]
    ppermute x16, waiting for transfers between devices: 19.6 us -> 18.2 us  [to_chips(): lax.ppermute(x, 'row', [(r, r ^ 2 * step[r % 2]) for r in range(n_row)])]
    ppermute x4, waiting for transfers between devices: 9.17 us -> 10.5 us  [around_col(): lax.ppermute(x, 'col', [(i, (i - s) % n_col) for i in range(n_col)])]
    convert_element_type x4 -> x2, other arithmetic: 1.79 us -> 0.81 us  [the longest x1 0.81 us: on_device(): ats = jnp.concatenate([rows_turned, cols_here]).astype(f32)]
  transfers between devices with their start and end apart: 28 -> 28, of which waited for: 22 -> 21; matrix products, arithmetic and copies ran while one was open for 2% -> 3% of each run, Pallas kernels for 0% -> 4%
where the time goes in v2:
time: 80.2 us; the launch traced here: 80 us
  waiting for transfers between devices  39 us (49%)
  starting transfers between devices  27 us (34%)
  Pallas kernels  10.5 us (13%)
  other arithmetic  2.54 us (3%)
    ppermute x16, starting transfers between devices, to_chips(): lax.ppermute(x, 'row', [(r, r ^ 2 * step[r % 2]) for r in range(n_row)])  22 us
    ppermute x16, waiting for transfers between devices, to_chips(): lax.ppermute(x, 'row', [(r, r ^ 2 * step[r % 2]) for r in range(n_row)])  18.2 us
    ppermute x4, waiting for transfers between devices, around_col(): lax.ppermute(x, 'col', [(i, (i - s) % n_col) for i in range(n_col)])  10.5 us
    ppermute x8, waiting for transfers between devices, swap(): return lax.ppermute(x, 'row', [(r, r ^ 1) for r in range(n_row)])  10.3 us
    pallas_call x11, Pallas kernels, call(): pl.pallas_call(body, out_shape=[jax.ShapeDtypeStruct(s, f32) for s in out...  7.74 us
    ppermute x4, starting transfers between devices, around_col(): lax.ppermute(x, 'col', [(i, (i - s) % n_col) for i in range(n_col)])  4.46 us
    pallas_call x1, Pallas kernels, split_tiles(): pl.pallas_call(tiles_kernel, out_shape=pltpu.VMEM((2 * rows, 2 * BLK), bf...  2.81 us
  transfers between devices with their start and end apart: 28, of which 21 were waited for; matrix products, arithmetic and copies ran while one was open for 3% of the time, Pallas kernels for 4%

profile of v2, /device:TPU:0, one launch (start us, length us, event | category | flops | bytes accessed | tf_op | source)
XLA Modules:
  0.0 80.0 jit_solution(4566663490227852272)
XLA Ops:
  0.6 3.0 %collective-permute-start = (f32[248,128]{1,0:T(8,128)}, f32[248,128]{1,0:T(8,128)S(1)}, u32[]{:S(2)}, u32[]{:S(2)}) collective-permute-start(f32[248,128]{1,0:T(8,128)} %bitcast.11), channel_id=1, source_target_pairs={{0,1},{1,0},{2,3},{3,2},{4,5},{5,4},{6,7},{7,6},{8,9},{9,8},{10,11... | collective-permute-start | bytes 380936 | tf_op jit(solution)/shard_map/ppermute | solution.py:237
  3.7 0.8 %add_bitcast_fusion.1 = s32[1,128]{1,0:T(1,128)S(1)} fusion(s32[64]{0:T(128)} %bitcast.16), kind=kLoop, calls=%fused_computation.12 | loop fusion | flops 128 | bytes 768 | tf_op jit(solution)/shard_map/stack | solution.py:248
  4.5 0.7 compare_select_fusion
  5.1 0.8 %add_convert_fusion = (f32[128]{0:T(128)S(1)}, s32[1,128]{1,0:T(1,128)S(1)}) fusion(s32[64]{0:T(128)S(1)} %compare_select_fusion, s32[64]{0:T(128)} %bitcast.14), kind=kLoop, calls=%fused_computation.13 | loop fusion | flops 384 | bytes 1536 | tf_op jit(solution)/shard_map/convert_element_type | solution.py:257
  6.0 2.8 %shard_map.59.tiles.refs_0_ = bf16[16384,256]{1,0:T(8,128)(2,1)S(1)} custom-call(f32[8192,128]{1,0:T(8,128)} %bitcast.13), custom_call_target="tpu_custom_call" | custom-call | bytes 4194304 | tf_op jit(solution)/shard_map/pallas_call | solution.py:190
  8.9 0.8 shard_map.60
  9.7 1.2 %collective-permute-done.1 = f32[72,128]{1,0:T(8,128)S(1)} collective-permute-done((f32[72,128]{1,0:T(8,128)S(1)}, f32[72,128]{1,0:T(8,128)S(1)}, u32[]{:S(2)}, u32[]{:S(2)}) %collective-permute-start.1) | collective-permute-done | bytes 36896 | tf_op jit(solution)/shard_map/ppermute | solution.py:228
  11.0 3.5 %collective-permute-start.5 = (f32[136,128]{1,0:T(8,128)S(1)}, f32[136,128]{1,0:T(8,128)S(1)}, u32[]{:S(2)}, u32[]{:S(2)}) collective-permute-start(f32[136,128]{1,0:T(8,128)S(1)} %pad_maximum_fusion.own), channel_id=1, source_target_pairs={{0,20},{2,30},{4,16},{6,26},{8,28},{10,22},{12,24},{14,18},{16,4},... | collective-permute-start | bytes 208904 | tf_op jit(solution)/shard_map/ppermute | solution.py:232
  14.6 1.6 %collective-permute-start.4 = (f32[136,128]{1,0:T(8,128)S(1)}, f32[136,128]{1,0:T(8,128)S(1)}, u32[]{:S(2)}, u32[]{:S(2)}) collective-permute-start(f32[136,128]{1,0:T(8,128)S(1)} %pad_maximum_fusion.own), channel_id=1, source_target_pairs={{0,8},{2,26},{4,12},{6,30},{8,0},{10,18},{12,4},{14,22},{16,24},{1... | collective-permute-start | bytes 208904 | tf_op jit(solution)/shard_map/ppermute | solution.py:232
  16.6 1.5 %collective-permute-start.2 = (f32[136,128]{1,0:T(8,128)S(1)}, f32[136,128]{1,0:T(8,128)S(1)}, u32[]{:S(2)}, u32[]{:S(2)}) collective-permute-start(f32[136,128]{1,0:T(8,128)S(1)} %pad_maximum_fusion.own), channel_id=1, source_target_pairs={{0,4},{2,18},{4,0},{6,22},{8,12},{10,26},{12,8},{14,30},{16,20},{1... | collective-permute-start | bytes 208904 | tf_op jit(solution)/shard_map/ppermute | solution.py:232
  18.0 1.2 %collective-permute-done.5.refs_3_ = f32[136,128]{1,0:T(8,128)S(1)} collective-permute-done((f32[136,128]{1,0:T(8,128)S(1)}, f32[136,128]{1,0:T(8,128)S(1)}, u32[]{:S(2)}, u32[]{:S(2)}) %collective-permute-start.5) | collective-permute-done | bytes 69664 | tf_op jit(solution)/shard_map/ppermute | solution.py:232
  19.2 2.5 %collective-permute-done.4.refs_2_ = f32[136,128]{1,0:T(8,128)S(1)} collective-permute-done((f32[136,128]{1,0:T(8,128)S(1)}, f32[136,128]{1,0:T(8,128)S(1)}, u32[]{:S(2)}, u32[]{:S(2)}) %collective-permute-start.4) | collective-permute-done | bytes 69664 | tf_op jit(solution)/shard_map/ppermute | solution.py:232
  21.7 0.7 collective-permute-done.3.refs_1_
  22.9 1.5 %collective-permute-done.6.other = f32[520,128]{1,0:T(8,128)S(1)} collective-permute-done((f32[520,128]{1,0:T(8,128)S(1)}, f32[520,128]{1,0:T(8,128)S(1)}, u32[]{:S(2)}, u32[]{:S(2)}) %collective-permute-start.6) | collective-permute-done | bytes 266272 | tf_op jit(solution)/shard_map/ppermute | solution.py:228
  24.4 0.8 %shard_map.62 = (f32[512,128]{1,0:T(8,128)S(1)}, f32[72,128]{1,0:T(8,128)S(1)}, f32[8,128]{1,0:T(8,128)S(1)}) custom-call(bf16[16384,256]{1,0:T(8,128)(2,1)S(1)} %shard_map.59.tiles.refs_0_, f32[520,128]{1,0:T(8,128)S(1)} %shard_map.61.half, f32[520,128]{1,0:T(8,128)S(1)} %collective-permute-done.6.other, ...), custom_call_target="tpu_custom_call" | custom-call | tf_op jit(solution)/shard_map/pallas_call | solution.py:204
  25.6 3.6 %collective-permute-done.7.refs_5_ = f32[72,128]{1,0:T(8,128)S(1)} collective-permute-done((f32[72,128]{1,0:T(8,128)S(1)}, f32[72,128]{1,0:T(8,128)S(1)}, u32[]{:S(2)}, u32[]{:S(2)}) %collective-permute-start.7) | collective-permute-done | bytes 36896 | tf_op jit(solution)/shard_map/ppermute | solution.py:237
  29.2 1.0 %shard_map.63 = (f32[512,128]{1,0:T(8,128)S(1)}, f32[72,128]{1,0:T(8,128)S(1)}, f32[8,128]{1,0:T(8,128)S(1)}) custom-call(bf16[16384,256]{1,0:T(8,128)(2,1)S(1)} %shard_map.59.tiles.refs_0_, f32[8,128]{1,0:T(8,128)S(1)} %get-tuple-element.25.consts.refs_0_.refs_1_.refs_2_, f32[512,128]{1,0:T(8,128)S(1)} %get-tuple-element.26.refs_2_, ...), custom_call_target="tpu_custom_call" | custom-call | tf_op jit(solution)/shard_map/pallas_call | solution.py:204
  30.3 1.2 %collective-permute-done.8 = f32[72,128]{1,0:T(8,128)S(1)} collective-permute-done((f32[72,128]{1,0:T(8,128)S(1)}, f32[72,128]{1,0:T(8,128)S(1)}, u32[]{:S(2)}, u32[]{:S(2)}) %collective-permute-start.8) | collective-permute-done | bytes 36896 | tf_op jit(solution)/shard_map/ppermute | solution.py:228
  31.5 1.6 %collective-permute-start.12 = (f32[136,128]{1,0:T(8,128)S(1)}, f32[136,128]{1,0:T(8,128)S(1)}, u32[]{:S(2)}, u32[]{:S(2)}) collective-permute-start(f32[136,128]{1,0:T(8,128)S(1)} %pad_maximum_fusion.1.own), channel_id=1, source_target_pairs={{0,20},{2,30},{4,16},{6,26},{8,28},{10,22},{12,24},{14,18},{16,4},... | collective-permute-start | bytes 208904 | tf_op jit(solution)/shard_map/ppermute | solution.py:232
  33.1 1.8 %collective-permute-start.11 = (f32[136,128]{1,0:T(8,128)S(1)}, f32[136,128]{1,0:T(8,128)S(1)}, u32[]{:S(2)}, u32[]{:S(2)}) collective-permute-start(f32[136,128]{1,0:T(8,128)S(1)} %pad_maximum_fusion.1.own), channel_id=1, source_target_pairs={{0,8},{2,26},{4,12},{6,30},{8,0},{10,18},{12,4},{14,22},{16,24},{1... | collective-permute-start | bytes 208904 | tf_op jit(solution)/shard_map/ppermute | solution.py:232
  34.9 1.0 %collective-permute-start.10 = (f32[136,128]{1,0:T(8,128)S(1)}, f32[136,128]{1,0:T(8,128)S(1)}, u32[]{:S(2)}, u32[]{:S(2)}) collective-permute-start(f32[136,128]{1,0:T(8,128)S(1)} %pad_maximum_fusion.1.own), channel_id=1, source_target_pairs={{0,12},{2,14},{4,8},{6,10},{8,4},{10,6},{12,0},{14,2},{16,28},{18,... | collective-permute-start | bytes 208904 | tf_op jit(solution)/shard_map/ppermute | solution.py:232
  35.9 0.7 collective-permute-start.9
  36.6 3.0 %collective-permute-done.12.refs_3_ = f32[136,128]{1,0:T(8,128)S(1)} collective-permute-done((f32[136,128]{1,0:T(8,128)S(1)}, f32[136,128]{1,0:T(8,128)S(1)}, u32[]{:S(2)}, u32[]{:S(2)}) %collective-permute-start.12) | collective-permute-done | bytes 69664 | tf_op jit(solution)/shard_map/ppermute | solution.py:232
  39.7 2.7 %collective-permute-done.10.refs_1_ = f32[136,128]{1,0:T(8,128)S(1)} collective-permute-done((f32[136,128]{1,0:T(8,128)S(1)}, f32[136,128]{1,0:T(8,128)S(1)}, u32[]{:S(2)}, u32[]{:S(2)}) %collective-permute-start.10) | collective-permute-done | bytes 69664 | tf_op jit(solution)/shard_map/ppermute | solution.py:232
  43.0 1.4 %collective-permute-done.13.other = f32[520,128]{1,0:T(8,128)S(1)} collective-permute-done((f32[520,128]{1,0:T(8,128)S(1)}, f32[520,128]{1,0:T(8,128)S(1)}, u32[]{:S(2)}, u32[]{:S(2)}) %collective-permute-start.13) | collective-permute-done | bytes 266272 | tf_op jit(solution)/shard_map/ppermute | solution.py:228
  44.5 0.8 %shard_map.65 = (f32[512,128]{1,0:T(8,128)S(1)}, f32[72,128]{1,0:T(8,128)S(1)}, f32[8,128]{1,0:T(8,128)S(1)}) custom-call(bf16[16384,256]{1,0:T(8,128)(2,1)S(1)} %shard_map.59.tiles.refs_0_, f32[520,128]{1,0:T(8,128)S(1)} %shard_map.64.half, f32[520,128]{1,0:T(8,128)S(1)} %collective-permute-done.13.other, f32[512,128]{1,0:T(8,128)S(1)} %get-tuple-element.33.refs_0_, ...), custom_call_target="tpu_custom_call" | custom-call | tf_op jit(solution)/shard_map/pallas_call | solution.py:204
  45.3 0.5 collective-permute-start.14
  45.8 3.5 %collective-permute-done.14.refs_5_ = f32[72,128]{1,0:T(8,128)S(1)} collective-permute-done((f32[72,128]{1,0:T(8,128)S(1)}, f32[72,128]{1,0:T(8,128)S(1)}, u32[]{:S(2)}, u32[]{:S(2)}) %collective-permute-start.14) | collective-permute-done | bytes 36896 | tf_op jit(solution)/shard_map/ppermute | solution.py:237
  49.3 1.0 %shard_map.66 = (f32[512,128]{1,0:T(8,128)S(1)}, f32[72,128]{1,0:T(8,128)S(1)}, f32[8,128]{1,0:T(8,128)S(1)}) custom-call(bf16[16384,256]{1,0:T(8,128)(2,1)S(1)} %shard_map.59.tiles.refs_0_, f32[8,128]{1,0:T(8,128)S(1)} %get-tuple-element.25.consts.refs_0_.refs_1_.refs_2_, f32[512,128]{1,0:T(8,128)S(1)} %get-tuple-element.31.refs_2_, ...), custom_call_target="tpu_custom_call" | custom-call | tf_op jit(solution)/shard_map/pallas_call | solution.py:204
  50.3 1.2 %collective-permute-done.15 = f32[72,128]{1,0:T(8,128)S(1)} collective-permute-done((f32[72,128]{1,0:T(8,128)S(1)}, f32[72,128]{1,0:T(8,128)S(1)}, u32[]{:S(2)}, u32[]{:S(2)}) %collective-permute-start.15) | collective-permute-done | bytes 36896 | tf_op jit(solution)/shard_map/ppermute | solution.py:228
  51.6 1.5 %collective-permute-start.19 = (f32[136,128]{1,0:T(8,128)S(1)}, f32[136,128]{1,0:T(8,128)S(1)}, u32[]{:S(2)}, u32[]{:S(2)}) collective-permute-start(f32[136,128]{1,0:T(8,128)S(1)} %pad_maximum_fusion.2.own), channel_id=1, source_target_pairs={{0,20},{2,30},{4,16},{6,26},{8,28},{10,22},{12,24},{14,18},{16,4},... | collective-permute-start | bytes 208904 | tf_op jit(solution)/shard_map/ppermute | solution.py:232
  53.1 2.0 %collective-permute-start.18 = (f32[136,128]{1,0:T(8,128)S(1)}, f32[136,128]{1,0:T(8,128)S(1)}, u32[]{:S(2)}, u32[]{:S(2)}) collective-permute-start(f32[136,128]{1,0:T(8,128)S(1)} %pad_maximum_fusion.2.own), channel_id=1, source_target_pairs={{0,8},{2,26},{4,12},{6,30},{8,0},{10,18},{12,4},{14,22},{16,24},{1... | collective-permute-start | bytes 208904 | tf_op jit(solution)/shard_map/ppermute | solution.py:232
  55.4 1.3 %collective-permute-start.16 = (f32[136,128]{1,0:T(8,128)S(1)}, f32[136,128]{1,0:T(8,128)S(1)}, u32[]{:S(2)}, u32[]{:S(2)}) collective-permute-start(f32[136,128]{1,0:T(8,128)S(1)} %pad_maximum_fusion.2.own), channel_id=1, source_target_pairs={{0,4},{2,18},{4,0},{6,22},{8,12},{10,26},{12,8},{14,30},{16,20},{1... | collective-permute-start | bytes 208904 | tf_op jit(solution)/shard_map/ppermute | solution.py:232
  56.6 2.4 %collective-permute-done.19.refs_3_ = f32[136,128]{1,0:T(8,128)S(1)} collective-permute-done((f32[136,128]{1,0:T(8,128)S(1)}, f32[136,128]{1,0:T(8,128)S(1)}, u32[]{:S(2)}, u32[]{:S(2)}) %collective-permute-start.19) | collective-permute-done | bytes 69664 | tf_op jit(solution)/shard_map/ppermute | solution.py:232
  59.0 1.6 %collective-permute-done.18.refs_2_ = f32[136,128]{1,0:T(8,128)S(1)} collective-permute-done((f32[136,128]{1,0:T(8,128)S(1)}, f32[136,128]{1,0:T(8,128)S(1)}, u32[]{:S(2)}, u32[]{:S(2)}) %collective-permute-start.18) | collective-permute-done | bytes 69664 | tf_op jit(solution)/shard_map/ppermute | solution.py:232
  60.7 1.5 %collective-permute-done.17.refs_1_ = f32[136,128]{1,0:T(8,128)S(1)} collective-permute-done((f32[136,128]{1,0:T(8,128)S(1)}, f32[136,128]{1,0:T(8,128)S(1)}, u32[]{:S(2)}, u32[]{:S(2)}) %collective-permute-start.17) | collective-permute-done | bytes 69664 | tf_op jit(solution)/shard_map/ppermute | solution.py:232
  62.7 1.5 %collective-permute-done.20.other = f32[520,128]{1,0:T(8,128)S(1)} collective-permute-done((f32[520,128]{1,0:T(8,128)S(1)}, f32[520,128]{1,0:T(8,128)S(1)}, u32[]{:S(2)}, u32[]{:S(2)}) %collective-permute-start.20) | collective-permute-done | bytes 266272 | tf_op jit(solution)/shard_map/ppermute | solution.py:228
  64.2 0.8 %shard_map.68 = (f32[512,128]{1,0:T(8,128)S(1)}, f32[72,128]{1,0:T(8,128)S(1)}, f32[8,128]{1,0:T(8,128)S(1)}) custom-call(bf16[16384,256]{1,0:T(8,128)(2,1)S(1)} %shard_map.59.tiles.refs_0_, f32[520,128]{1,0:T(8,128)S(1)} %shard_map.67.half, f32[520,128]{1,0:T(8,128)S(1)} %collective-permute-done.20.other, f32[512,128]{1,0:T(8,128)S(1)} %get-tuple-element.39.refs_0_, ...), custom_call_target="tpu_custom_call" | custom-call | tf_op jit(solution)/shard_map/pallas_call | solution.py:204
  65.6 3.5 %collective-permute-done.21.refs_4_ = f32[72,128]{1,0:T(8,128)S(1)} collective-permute-done((f32[72,128]{1,0:T(8,128)S(1)}, f32[72,128]{1,0:T(8,128)S(1)}, u32[]{:S(2)}, u32[]{:S(2)}) %collective-permute-start.21) | collective-permute-done | bytes 36896 | tf_op jit(solution)/shard_map/ppermute | solution.py:237
  69.4 1.1 %collective-permute-done.22 = f32[8,128]{1,0:T(8,128)S(1)} collective-permute-done((f32[8,128]{1,0:T(8,128)S(1)}, f32[8,128]{1,0:T(8,128)S(1)}, u32[]{:S(2)}, u32[]{:S(2)}) %collective-permute-start.22) | collective-permute-done | bytes 4128 | tf_op jit(solution)/shard_map/ppermute | solution.py:228
  70.5 1.3 %collective-permute-start.26 = (f32[8,128]{1,0:T(8,128)S(1)}, f32[8,128]{1,0:T(8,128)S(1)}, u32[]{:S(2)}, u32[]{:S(2)}) collective-permute-start(f32[8,128]{1,0:T(8,128)S(1)} %add.48), channel_id=1, source_target_pairs={{0,20},{2,30},{4,16},{6,26},{8,28},{10,22},{12,24},{14,18},{16,4},... | collective-permute-start | bytes 12296 | tf_op jit(solution)/shard_map/ppermute | solution.py:232
  71.9 1.7 %collective-permute-start.25 = (f32[8,128]{1,0:T(8,128)S(1)}, f32[8,128]{1,0:T(8,128)S(1)}, u32[]{:S(2)}, u32[]{:S(2)}) collective-permute-start(f32[8,128]{1,0:T(8,128)S(1)} %add.48), channel_id=1, source_target_pairs={{0,8},{2,26},{4,12},{6,30},{8,0},{10,18},{12,4},{14,22},{16,24},{1... | collective-permute-start | bytes 12296 | tf_op jit(solution)/shard_map/ppermute | solution.py:232
  73.6 0.5 collective-permute-start.24
  74.1 1.3 %collective-permute-start.23 = (f32[8,128]{1,0:T(8,128)S(1)}, f32[8,128]{1,0:T(8,128)S(1)}, u32[]{:S(2)}, u32[]{:S(2)}) collective-permute-start(f32[8,128]{1,0:T(8,128)S(1)} %add.48), channel_id=1, source_target_pairs={{0,4},{2,18},{4,0},{6,22},{8,12},{10,26},{12,8},{14,30},{16,20},{1... | collective-permute-start | bytes 12296 | tf_op jit(solution)/shard_map/ppermute | solution.py:232
  75.4 0.6 collective-permute-done.26
  76.0 2.1 %collective-permute-done.24 = f32[8,128]{1,0:T(8,128)S(1)} collective-permute-done((f32[8,128]{1,0:T(8,128)S(1)}, f32[8,128]{1,0:T(8,128)S(1)}, u32[]{:S(2)}, u32[]{:S(2)}) %collective-permute-start.24) | collective-permute-done | bytes 4128 | tf_op jit(solution)/shard_map/ppermute | solution.py:232
  78.3 1.0 %collective-permute-done.27 = f32[8,128]{1,0:T(8,128)S(1)} collective-permute-done((f32[8,128]{1,0:T(8,128)S(1)}, f32[8,128]{1,0:T(8,128)S(1)}, u32[]{:S(2)}, u32[]{:S(2)}) %collective-permute-start.27) | collective-permute-done | bytes 4128 | tf_op jit(solution)/shard_map/ppermute | solution.py:228
  79.3 0.7 shard_map.70
  (51 shorter events, 4.2 us)
Async XLA Ops:
  0.6 8.3 %copy-start = (f32[31744]{0:T(1024)S(1)}, f32[31744]{0:T(1024)}, u32[]{:S(2)}) copy-start(f32[31744]{0:T(1024)} %param.4) | copy-start | bytes 380932
  0.6 8.2 %collective-permute-start = (f32[248,128]{1,0:T(8,128)}, f32[248,128]{1,0:T(8,128)S(1)}, u32[]{:S(2)}, u32[]{:S(2)}) collective-permute-start(f32[248,128]{1,0:T(8,128)} %bitcast.11), channel_id=1, source_target_pairs={{0,1},{1,0},{2,3},{3,2},{4,5},{5,4},{6,7},{7,6},{8,9},{9,8},{10,11... | collective-permute-start | bytes 380936 | tf_op jit(solution)/shard_map/ppermute | solution.py:237
  9.7 1.2 %collective-permute-start.1 = (f32[72,128]{1,0:T(8,128)S(1)}, f32[72,128]{1,0:T(8,128)S(1)}, u32[]{:S(2)}, u32[]{:S(2)}) collective-permute-start(f32[72,128]{1,0:T(8,128)S(1)} %get-tuple-element.27), channel_id=1, source_target_pairs={{0,2},{2,0},{4,6},{6,4},{8,10},{10,8},{12,14},{14,12},{16,18},{18,... | collective-permute-start | bytes 110600 | tf_op jit(solution)/shard_map/ppermute | solution.py:228
  11.0 8.2 %collective-permute-start.5 = (f32[136,128]{1,0:T(8,128)S(1)}, f32[136,128]{1,0:T(8,128)S(1)}, u32[]{:S(2)}, u32[]{:S(2)}) collective-permute-start(f32[136,128]{1,0:T(8,128)S(1)} %pad_maximum_fusion.own), channel_id=1, source_target_pairs={{0,20},{2,30},{4,16},{6,26},{8,28},{10,22},{12,24},{14,18},{16,4},... | collective-permute-start | bytes 208904 | tf_op jit(solution)/shard_map/ppermute | solution.py:232
  14.6 7.1 %collective-permute-start.4 = (f32[136,128]{1,0:T(8,128)S(1)}, f32[136,128]{1,0:T(8,128)S(1)}, u32[]{:S(2)}, u32[]{:S(2)}) collective-permute-start(f32[136,128]{1,0:T(8,128)S(1)} %pad_maximum_fusion.own), channel_id=1, source_target_pairs={{0,8},{2,26},{4,12},{6,30},{8,0},{10,18},{12,4},{14,22},{16,24},{1... | collective-permute-start | bytes 208904 | tf_op jit(solution)/shard_map/ppermute | solution.py:232
  16.1 6.2 %collective-permute-start.3 = (f32[136,128]{1,0:T(8,128)S(1)}, f32[136,128]{1,0:T(8,128)S(1)}, u32[]{:S(2)}, u32[]{:S(2)}) collective-permute-start(f32[136,128]{1,0:T(8,128)S(1)} %pad_maximum_fusion.own), channel_id=1, source_target_pairs={{0,12},{2,14},{4,8},{6,10},{8,4},{10,6},{12,0},{14,2},{16,28},{18,... | collective-permute-start | bytes 208904 | tf_op jit(solution)/shard_map/ppermute | solution.py:232
  16.6 5.8 %collective-permute-start.2 = (f32[136,128]{1,0:T(8,128)S(1)}, f32[136,128]{1,0:T(8,128)S(1)}, u32[]{:S(2)}, u32[]{:S(2)}) collective-permute-start(f32[136,128]{1,0:T(8,128)S(1)} %pad_maximum_fusion.own), channel_id=1, source_target_pairs={{0,4},{2,18},{4,0},{6,22},{8,12},{10,26},{12,8},{14,30},{16,20},{1... | collective-permute-start | bytes 208904 | tf_op jit(solution)/shard_map/ppermute | solution.py:232
  22.8 1.6 %collective-permute-start.6 = (f32[520,128]{1,0:T(8,128)S(1)}, f32[520,128]{1,0:T(8,128)S(1)}, u32[]{:S(2)}, u32[]{:S(2)}) collective-permute-start(f32[520,128]{1,0:T(8,128)S(1)} %shard_map.61.half), channel_id=1, source_target_pairs={{0,2},{2,0},{4,6},{6,4},{8,10},{10,8},{12,14},{14,12},{16,18},{18,... | collective-permute-start | bytes 798728 | tf_op jit(solution)/shard_map/ppermute | solution.py:228
  25.2 4.0 %collective-permute-start.7 = (f32[72,128]{1,0:T(8,128)S(1)}, f32[72,128]{1,0:T(8,128)S(1)}, u32[]{:S(2)}, u32[]{:S(2)}) collective-permute-start(f32[72,128]{1,0:T(8,128)S(1)} %get-tuple-element.30.refs_4_), channel_id=1, source_target_pairs={{0,1},{1,0},{2,3},{3,2},{4,5},{5,4},{6,7},{7,6},{8,9},{9,8},{10,11... | collective-permute-start | bytes 110600 | tf_op jit(solution)/shard_map/ppermute | solution.py:237
  30.2 1.2 %collective-permute-start.8 = (f32[72,128]{1,0:T(8,128)S(1)}, f32[72,128]{1,0:T(8,128)S(1)}, u32[]{:S(2)}, u32[]{:S(2)}) collective-permute-start(f32[72,128]{1,0:T(8,128)S(1)} %get-tuple-element.32), channel_id=1, source_target_pairs={{0,2},{2,0},{4,6},{6,4},{8,10},{10,8},{12,14},{14,12},{16,18},{18,... | collective-permute-start | bytes 110600 | tf_op jit(solution)/shard_map/ppermute | solution.py:228
  31.5 8.1 %collective-permute-start.12 = (f32[136,128]{1,0:T(8,128)S(1)}, f32[136,128]{1,0:T(8,128)S(1)}, u32[]{:S(2)}, u32[]{:S(2)}) collective-permute-start(f32[136,128]{1,0:T(8,128)S(1)} %pad_maximum_fusion.1.own), channel_id=1, source_target_pairs={{0,20},{2,30},{4,16},{6,26},{8,28},{10,22},{12,24},{14,18},{16,4},... | collective-permute-start | bytes 208904 | tf_op jit(solution)/shard_map/ppermute | solution.py:232
  33.1 6.5 %collective-permute-start.11 = (f32[136,128]{1,0:T(8,128)S(1)}, f32[136,128]{1,0:T(8,128)S(1)}, u32[]{:S(2)}, u32[]{:S(2)}) collective-permute-start(f32[136,128]{1,0:T(8,128)S(1)} %pad_maximum_fusion.1.own), channel_id=1, source_target_pairs={{0,8},{2,26},{4,12},{6,30},{8,0},{10,18},{12,4},{14,22},{16,24},{1... | collective-permute-start | bytes 208904 | tf_op jit(solution)/shard_map/ppermute | solution.py:232
  34.9 7.5 %collective-permute-start.10 = (f32[136,128]{1,0:T(8,128)S(1)}, f32[136,128]{1,0:T(8,128)S(1)}, u32[]{:S(2)}, u32[]{:S(2)}) collective-permute-start(f32[136,128]{1,0:T(8,128)S(1)} %pad_maximum_fusion.1.own), channel_id=1, source_target_pairs={{0,12},{2,14},{4,8},{6,10},{8,4},{10,6},{12,0},{14,2},{16,28},{18,... | collective-permute-start | bytes 208904 | tf_op jit(solution)/shard_map/ppermute | solution.py:232
  35.9 6.5 %collective-permute-start.9 = (f32[136,128]{1,0:T(8,128)S(1)}, f32[136,128]{1,0:T(8,128)S(1)}, u32[]{:S(2)}, u32[]{:S(2)}) collective-permute-start(f32[136,128]{1,0:T(8,128)S(1)} %pad_maximum_fusion.1.own), channel_id=1, source_target_pairs={{0,4},{2,18},{4,0},{6,22},{8,12},{10,26},{12,8},{14,30},{16,20},{1... | collective-permute-start | bytes 208904 | tf_op jit(solution)/shard_map/ppermute | solution.py:232
  42.8 1.6 %collective-permute-start.13 = (f32[520,128]{1,0:T(8,128)S(1)}, f32[520,128]{1,0:T(8,128)S(1)}, u32[]{:S(2)}, u32[]{:S(2)}) collective-permute-start(f32[520,128]{1,0:T(8,128)S(1)} %shard_map.64.half), channel_id=1, source_target_pairs={{0,2},{2,0},{4,6},{6,4},{8,10},{10,8},{12,14},{14,12},{16,18},{18,... | collective-permute-start | bytes 798728 | tf_op jit(solution)/shard_map/ppermute | solution.py:228
  45.3 4.0 %collective-permute-start.14 = (f32[72,128]{1,0:T(8,128)S(1)}, f32[72,128]{1,0:T(8,128)S(1)}, u32[]{:S(2)}, u32[]{:S(2)}) collective-permute-start(f32[72,128]{1,0:T(8,128)S(1)} %get-tuple-element.36.refs_4_), channel_id=1, source_target_pairs={{0,1},{1,0},{2,3},{3,2},{4,5},{5,4},{6,7},{7,6},{8,9},{9,8},{10,11... | collective-permute-start | bytes 110600 | tf_op jit(solution)/shard_map/ppermute | solution.py:237
  50.3 1.2 %collective-permute-start.15 = (f32[72,128]{1,0:T(8,128)S(1)}, f32[72,128]{1,0:T(8,128)S(1)}, u32[]{:S(2)}, u32[]{:S(2)}) collective-permute-start(f32[72,128]{1,0:T(8,128)S(1)} %get-tuple-element.38), channel_id=1, source_target_pairs={{0,2},{2,0},{4,6},{6,4},{8,10},{10,8},{12,14},{14,12},{16,18},{18,... | collective-permute-start | bytes 110600 | tf_op jit(solution)/shard_map/ppermute | solution.py:228
  51.6 7.4 %collective-permute-start.19 = (f32[136,128]{1,0:T(8,128)S(1)}, f32[136,128]{1,0:T(8,128)S(1)}, u32[]{:S(2)}, u32[]{:S(2)}) collective-permute-start(f32[136,128]{1,0:T(8,128)S(1)} %pad_maximum_fusion.2.own), channel_id=1, source_target_pairs={{0,20},{2,30},{4,16},{6,26},{8,28},{10,22},{12,24},{14,18},{16,4},... | collective-permute-start | bytes 208904 | tf_op jit(solution)/shard_map/ppermute | solution.py:232
  53.1 7.5 %collective-permute-start.18 = (f32[136,128]{1,0:T(8,128)S(1)}, f32[136,128]{1,0:T(8,128)S(1)}, u32[]{:S(2)}, u32[]{:S(2)}) collective-permute-start(f32[136,128]{1,0:T(8,128)S(1)} %pad_maximum_fusion.2.own), channel_id=1, source_target_pairs={{0,8},{2,26},{4,12},{6,30},{8,0},{10,18},{12,4},{14,22},{16,24},{1... | collective-permute-start | bytes 208904 | tf_op jit(solution)/shard_map/ppermute | solution.py:232
  55.1 7.0 %collective-permute-start.17 = (f32[136,128]{1,0:T(8,128)S(1)}, f32[136,128]{1,0:T(8,128)S(1)}, u32[]{:S(2)}, u32[]{:S(2)}) collective-permute-start(f32[136,128]{1,0:T(8,128)S(1)} %pad_maximum_fusion.2.own), channel_id=1, source_target_pairs={{0,12},{2,14},{4,8},{6,10},{8,4},{10,6},{12,0},{14,2},{16,28},{18,... | collective-permute-start | bytes 208904 | tf_op jit(solution)/shard_map/ppermute | solution.py:232
  55.4 6.8 %collective-permute-start.16 = (f32[136,128]{1,0:T(8,128)S(1)}, f32[136,128]{1,0:T(8,128)S(1)}, u32[]{:S(2)}, u32[]{:S(2)}) collective-permute-start(f32[136,128]{1,0:T(8,128)S(1)} %pad_maximum_fusion.2.own), channel_id=1, source_target_pairs={{0,4},{2,18},{4,0},{6,22},{8,12},{10,26},{12,8},{14,30},{16,20},{1... | collective-permute-start | bytes 208904 | tf_op jit(solution)/shard_map/ppermute | solution.py:232
  62.6 1.6 %collective-permute-start.20 = (f32[520,128]{1,0:T(8,128)S(1)}, f32[520,128]{1,0:T(8,128)S(1)}, u32[]{:S(2)}, u32[]{:S(2)}) collective-permute-start(f32[520,128]{1,0:T(8,128)S(1)} %shard_map.67.half), channel_id=1, source_target_pairs={{0,2},{2,0},{4,6},{6,4},{8,10},{10,8},{12,14},{14,12},{16,18},{18,... | collective-permute-start | bytes 798728 | tf_op jit(solution)/shard_map/ppermute | solution.py:228
  65.0 4.0 %collective-permute-start.21 = (f32[72,128]{1,0:T(8,128)S(1)}, f32[72,128]{1,0:T(8,128)S(1)}, u32[]{:S(2)}, u32[]{:S(2)}) collective-permute-start(f32[72,128]{1,0:T(8,128)S(1)} %get-tuple-element.42.refs_3_), channel_id=1, source_target_pairs={{0,1},{1,0},{2,3},{3,2},{4,5},{5,4},{6,7},{7,6},{8,9},{9,8},{10,11... | collective-permute-start | bytes 110600 | tf_op jit(solution)/shard_map/ppermute | solution.py:237
  69.4 1.2 %collective-permute-start.22 = (f32[8,128]{1,0:T(8,128)S(1)}, f32[8,128]{1,0:T(8,128)S(1)}, u32[]{:S(2)}, u32[]{:S(2)}) collective-permute-start(f32[8,128]{1,0:T(8,128)S(1)} %get-tuple-element.43), channel_id=1, source_target_pairs={{0,2},{2,0},{4,6},{6,4},{8,10},{10,8},{12,14},{14,12},{16,18},{18,... | collective-permute-start | bytes 12296 | tf_op jit(solution)/shard_map/ppermute | solution.py:228
  70.5 5.4 %collective-permute-start.26 = (f32[8,128]{1,0:T(8,128)S(1)}, f32[8,128]{1,0:T(8,128)S(1)}, u32[]{:S(2)}, u32[]{:S(2)}) collective-permute-start(f32[8,128]{1,0:T(8,128)S(1)} %add.48), channel_id=1, source_target_pairs={{0,20},{2,30},{4,16},{6,26},{8,28},{10,22},{12,24},{14,18},{16,4},... | collective-permute-start | bytes 12296 | tf_op jit(solution)/shard_map/ppermute | solution.py:232
  71.9 4.1 %collective-permute-start.25 = (f32[8,128]{1,0:T(8,128)S(1)}, f32[8,128]{1,0:T(8,128)S(1)}, u32[]{:S(2)}, u32[]{:S(2)}) collective-permute-start(f32[8,128]{1,0:T(8,128)S(1)} %add.48), channel_id=1, source_target_pairs={{0,8},{2,26},{4,12},{6,30},{8,0},{10,18},{12,4},{14,22},{16,24},{1... | collective-permute-start | bytes 12296 | tf_op jit(solution)/shard_map/ppermute | solution.py:232
  73.6 4.5 %collective-permute-start.24 = (f32[8,128]{1,0:T(8,128)S(1)}, f32[8,128]{1,0:T(8,128)S(1)}, u32[]{:S(2)}, u32[]{:S(2)}) collective-permute-start(f32[8,128]{1,0:T(8,128)S(1)} %add.48), channel_id=1, source_target_pairs={{0,12},{2,14},{4,8},{6,10},{8,4},{10,6},{12,0},{14,2},{16,28},{18,... | collective-permute-start | bytes 12296 | tf_op jit(solution)/shard_map/ppermute | solution.py:232
  74.1 4.0 %collective-permute-start.23 = (f32[8,128]{1,0:T(8,128)S(1)}, f32[8,128]{1,0:T(8,128)S(1)}, u32[]{:S(2)}, u32[]{:S(2)}) collective-permute-start(f32[8,128]{1,0:T(8,128)S(1)} %add.48), channel_id=1, source_target_pairs={{0,4},{2,18},{4,0},{6,22},{8,12},{10,26},{12,8},{14,30},{16,20},{1... | collective-permute-start | bytes 12296 | tf_op jit(solution)/shard_map/ppermute | solution.py:232
  78.1 1.2 %collective-permute-start.27 = (f32[8,128]{1,0:T(8,128)S(1)}, f32[8,128]{1,0:T(8,128)S(1)}, u32[]{:S(2)}, u32[]{:S(2)}) collective-permute-start(f32[8,128]{1,0:T(8,128)S(1)} %add_add_fusion), channel_id=1, source_target_pairs={{0,2},{2,0},{4,6},{6,4},{8,10},{10,8},{12,14},{14,12},{16,18},{18,... | collective-permute-start | bytes 12296 | tf_op jit(solution)/shard_map/ppermute | solution.py:228

commit v3 on v2

--- a/solution.py
+++ b/solution.py
@@ -14,7 +14,7 @@
 ITERS = 3
 MSG = NB_DEV + 8
 INDEX, SQUARE = NB_DEV, NB_DEV + 1
-COL_ROW, ROW_ROW, SHIFT, IS_FIRST = (slice(k, k + 1) for k in range(4))
+COL_ROW, ROW_ROW, SHIFT = (slice(k, k + 1) for k in range(3))
 ROWS_HELD = 512
 PARTS = 8
 VMEM_LIMIT = 16 * 1024 * 1024
@@ -37,13 +37,8 @@
     k = parts.shape[0]
     at = lax.broadcasted_iota(jnp.int32, (rows, k), 0).astype(f32)
     hot = jnp.where(at == index_row, 1.0, 0.0).astype(bf16)
-    high = parts.astype(bf16)
-    rest = parts - high.astype(f32)
-    mid = rest.astype(bf16)
-    low = (rest - mid.astype(f32)).astype(bf16)
-    three = jnp.concatenate([high, mid, low], axis=1)
-    out = jnp.dot(hot, three, preferred_element_type=f32)
-    return out[:, :BLK] + (out[:, BLK : 2 * BLK] + out[:, 2 * BLK :])
+    out = jnp.dot(hot, jnp.concatenate(halves(parts), axis=1), preferred_element_type=f32)
+    return out[:, :BLK] + out[:, BLK:]
 
 
 def pick(at, x):
@@ -69,28 +64,39 @@
     msg[NB_DEV:, :] = jnp.where(row == 0, index_row, jnp.where(row == 1, square, 0.0))
 
 
-def tiles_kernel(blocks, out, held, sems):
+def tiles_kernel(blocks, blk_row, blk_col, rhs, place, out, consts, ats, mine, held, rows_held, cols_held, sems):
     per = held.shape[0] // PARTS
+    few = [
+        pltpu.make_async_copy(a, b, sems.at[PARTS + k])
+        for k, (a, b) in enumerate(((blk_row, rows_held), (blk_col, cols_held), (rhs, mine)))
+    ]
     parts = [
         pltpu.make_async_copy(blocks.at[pl.ds(k * per, per)], held.at[pl.ds(k * per, per)], sems.at[k])
         for k in range(PARTS)
     ]
-    for part in parts:
+    for part in few + parts:
         part.start()
+    for part in few:
+        part.wait()
+    rows, cols = rows_held[...].astype(f32), cols_held[...].astype(f32)
+    shift = place[:1, :]
+    consts[COL_ROW, :] = jnp.concatenate([cols, cols], axis=1)
+    consts[ROW_ROW, :] = jnp.concatenate([rows, rows], axis=1)
+    consts[SHIFT, :] = shift
+    consts[3:, :] = jnp.zeros((5, BLK), f32)
+    turned = rows - shift[:, :NB_DEV]
+    turned = jnp.where(turned < 0, turned + ROWB_DEV, turned)
+    ats[...] = jnp.broadcast_to(jnp.concatenate([turned, cols], axis=1), (2 * NB_DEV, BLK)).T
     for k, part in enumerate(parts):
         part.wait()
         for at in range(k * per, (k + 1) * per, BLK):
-            block = held[at : at + BLK, :]
-            for where, x in ((at, block), (held.shape[0] + at, block.T)):
-                high, low = halves(x)
-                out[where : where + BLK, :BLK] = high
-                out[where : where + BLK, BLK:] = low
+            for lane, half in zip((0, BLK), halves(held[at : at + BLK, :])):
+                out[at : at + BLK, lane : lane + BLK] = half
+                out[held.shape[0] + at : held.shape[0] + at + BLK, lane : lane + BLK] = half.T
 
 
 def first_kernel(n_col, tiles, *refs):
-    pieces, (consts, ats, u_raw, msg, consts_out, ats_out) = refs[:n_col], refs[n_col:]
-    consts_out[...] = consts[...]
-    ats_out[...] = ats[...]
+    pieces, (consts, ats, u_raw, msg) = refs[:n_col], refs[n_col:]
     per = pieces[0].shape[0]
     for k, piece in enumerate(pieces):
         u_raw[k * per : (k + 1) * per, :] = piece[...]
@@ -100,16 +106,17 @@
     write_end(msg, consts[COL_ROW, :], total(u * u))
 
 
-def gather_sum_kernel(slot, tiles, consts, own, *refs):
-    *others, out = refs
-    first = consts[IS_FIRST, :] > 0
+def gather_sum_kernel(tiles, own, near, *refs):
+    *chips, out = refs
+    lane = lax.broadcasted_iota(jnp.int32, (1, BLK), 1)
+    parts = [own[:NB_DEV], near[:NB_DEV]]
+    index = [jnp.where(lane < NB_DEV, own[INDEX : INDEX + 1], near[INDEX : INDEX + 1])]
+    square = own[SQUARE : SQUARE + 1] + near[SQUARE : SQUARE + 1]
     n = 2 * NB_DEV
-    parts, index, square = [], [], jnp.zeros((1, BLK), f32)
-    for k, other in enumerate(others):
-        m = jnp.where(first, own[...], other[...]) if k == slot else other[...]
-        parts.append(m[:n])
-        index.append(m[n : n + 1])
-        square = square + m[n + 1 : n + 2]
+    for chip in chips:
+        parts.append(chip[:n])
+        index.append(chip[n : n + 1])
+        square = square + chip[n + 1 : n + 2]
     out[:COLB_DEV, :] = place_sum(jnp.concatenate(index, axis=1), jnp.concatenate(parts, axis=0), COLB_DEV)
     out[COLB_DEV:, :] = jnp.broadcast_to(square, (8, BLK))
 
@@ -162,40 +169,59 @@
     write_end(msg, consts[COL_ROW, :], square)
 
 
-def end_kernel(square, *refs):
+def before_end_kernel(*refs):
     v_raws, alphas, betas = refs[:ITERS], refs[ITERS : 2 * ITERS], refs[2 * ITERS : 3 * ITERS]
-    out, residual = refs[3 * ITERS :]
+    x_out, w_out, scalars = refs[3 * ITERS :]
     alpha = [a[:1, :] for a in alphas]
-    beta = [b[:1, :] for b in betas] + [jnp.sqrt(square[:1, :])]
+    beta = [b[:1, :] for b in betas]
     phibar, rhobar = beta[0], alpha[0]
-    x = None
-    for k in range(ITERS):
-        v = v_raws[k][...] / alpha[k]
-        w = v if k == 0 else v - turn * w
-        rho = jnp.sqrt(rhobar * rhobar + beta[k + 1] * beta[k + 1])
-        cosine, sine = rhobar / rho, beta[k + 1] / rho
+    x = jnp.zeros(x_out.shape, f32)
+    w = v_raws[0][...] / alpha[0]
+    for k in range(1, ITERS):
+        rho = jnp.sqrt(rhobar * rhobar + beta[k] * beta[k])
+        cosine, sine = rhobar / rho, beta[k] / rho
         phi = cosine * phibar
         phibar = sine * phibar
-        step = phi / rho * w
-        x = step if x is None else x + step
-        if k + 1 < ITERS:
-            turn = sine * alpha[k + 1] / rho
-            rhobar = -cosine * alpha[k + 1]
-    out[...] = x
-    residual[...] = (phibar / beta[0])[:, :1]
-
-
-def split_tiles(blocks):
+        x = x + phi / rho * w
+        w = v_raws[k][...] / alpha[k] - sine * alpha[k] / rho * w
+        rhobar = -cosine * alpha[k]
+    x_out[...] = x
+    w_out[...] = w
+    row = lax.broadcasted_iota(jnp.int32, (8, BLK), 0)
+    scalars[...] = jnp.where(row == 0, phibar, jnp.where(row == 1, rhobar, beta[0]))
+
+
+def end_kernel(half, other, x, w, scalars, out, residual):
+    beta = jnp.sqrt(half[:1, :] + other[:1, :])
+    phibar, rhobar, beta_first = scalars[:1, :], scalars[1:2, :], scalars[2:3, :]
+    rho = jnp.sqrt(rhobar * rhobar + beta * beta)
+    out[...] = x[...] + rhobar / rho * phibar / rho * w[...]
+    residual[...] = (beta / rho * phibar / beta_first)[:, :1]
+
+
+def split_tiles(blocks, blk_row, blk_col, rhs, place):
     rows = blocks.shape[0]
+    vmem = pl.BlockSpec(memory_space=pltpu.VMEM)
+    there = [pltpu.with_memory_space_constraint(x, pltpu.HBM) for x in (blocks, blk_row, blk_col, rhs)]
     return pl.pallas_call(
         tiles_kernel,
-        out_shape=pltpu.VMEM((2 * rows, 2 * BLK), bf16),
-        in_specs=[pl.BlockSpec(memory_space=pl.ANY)],
-        out_specs=pl.BlockSpec(memory_space=pltpu.VMEM),
-        scratch_shapes=[pltpu.VMEM((rows, BLK), f32), pltpu.SemaphoreType.DMA((PARTS,))],
+        out_shape=[
+            pltpu.VMEM((2 * rows, 2 * BLK), bf16),
+            jax.ShapeDtypeStruct((8, BLK), f32),
+            jax.ShapeDtypeStruct((2 * NB_DEV, BLK), f32),
+            jax.ShapeDtypeStruct(rhs.shape, f32),
+        ],
+        in_specs=[pl.BlockSpec(memory_space=pl.ANY)] * 4 + [vmem],
+        out_specs=[vmem] * 4,
+        scratch_shapes=[
+            pltpu.VMEM((rows, BLK), f32),
+            pltpu.VMEM((1, NB_DEV), jnp.int32),
+            pltpu.VMEM((1, NB_DEV), jnp.int32),
+            pltpu.SemaphoreType.DMA((PARTS + 3,)),
+        ],
         compiler_params=pltpu.CompilerParams(vmem_limit_bytes=VMEM_LIMIT),
         cost_estimate=pl.CostEstimate(flops=0, bytes_accessed=4 * rows * BLK, transcendentals=0),
-    )(pltpu.with_memory_space_constraint(blocks, pltpu.HBM))
+    )(*there, place)
 
 
 def call(body, tiles, ins, outs):
@@ -212,20 +238,22 @@
 
 def chip_steps(chips):
     if chips == 8:
-        return [(1, 4), (3, 3), (2, 6), (5, 7)], 1
-    steps = [(m, m + 1) for m in range(1, chips - 1, 2)] + [(chips - 1, chips - 1)]
-    return steps, len(steps) - 1
+        return 1, [(2, 4), (3, 5), (6, 7)]
+    return 1, [(m, m + 1) for m in range(2, chips, 2)]
 
 
 def on_device(n_row, n_col, rhs, blocks, blk_row, blk_col):
     chips = n_row // 2
-    steps, twice = chip_steps(chips)
+    near, steps = chip_steps(chips)
     per_rhs = rhs.shape[0] // BLK
     per_out = COLB_DEV // n_row
     row, col = lax.axis_index("row"), lax.axis_index("col")
 
     def swap(x):
         return lax.ppermute(x, "row", [(r, r ^ 1) for r in range(n_row)])
+
+    def to_near(x):
+        return lax.ppermute(x, "row", [(r, r ^ (2 * near)) for r in range(n_row)])
 
     def to_chips(x):
         return [
@@ -237,44 +265,28 @@
             lax.ppermute(x, "col", [(i, (i - s) % n_col) for i in range(n_col)]) for s in range(1, n_col)
         ]
 
-    pieces = around_col(rhs.reshape(per_rhs, BLK))
-    shift = col * per_rhs
-
-    blocks = blocks.reshape(NB_DEV * BLK, BLK)
-    tiles = split_tiles(blocks)
-    cols_here = blk_col.reshape(NB_DEV)
-    rows_here = blk_row.reshape(NB_DEV)
-    rows_turned = jnp.where(rows_here < shift, rows_here - shift + ROWB_DEV, rows_here - shift)
-    consts = jnp.stack(
-        [
-            jnp.concatenate([cols_here, cols_here]),
-            jnp.concatenate([rows_here, rows_here]),
-            jnp.full((BLK,), shift),
-            jnp.full((BLK,), 1 - row % 2),
-        ]
-        + [jnp.zeros((BLK,), jnp.int32)] * 4
-    ).astype(f32)
-    ats = jnp.concatenate([rows_turned, cols_here]).astype(f32)
-    ats = jnp.broadcast_to(ats[:, None], (2 * NB_DEV, BLK))
+    rhs = rhs.reshape(per_rhs, BLK)
+    pieces = around_col(rhs)
+    place = jnp.full((8, BLK), col * per_rhs).astype(f32)
+    tiles, consts, ats, pieces[0] = split_tiles(
+        blocks.reshape(NB_DEV * BLK, BLK), blk_row.reshape(1, NB_DEV), blk_col.reshape(1, NB_DEV), rhs, place
+    )
     lane = lax.broadcasted_iota(jnp.int32, (MSG - NB_DEV, BLK), 1)
     end_row = lax.broadcasted_iota(jnp.int32, (MSG - NB_DEV, BLK), 0)
 
     def gather(msg):
-        peer = swap(msg)
+        peer, beside = swap(msg), to_near(msg)
         a, b = msg[NB_DEV:], peer[NB_DEV:]
         end = jnp.where(end_row == 0, jnp.where(lane < NB_DEV, a, b), a + b)
         both = jnp.concatenate([msg[:NB_DEV], peer[:NB_DEV], end])
-        others = to_chips(both)
-        (half,) = call(
-            functools.partial(gather_sum_kernel, twice), tiles, [consts, both] + others, [(COLB_DEV + 8, BLK)]
-        )
+        (half,) = call(gather_sum_kernel, tiles, [msg, beside] + to_chips(both), [(COLB_DEV + 8, BLK)])
         return half, swap(half)
 
-    u_raw, msg, consts, ats = call(
+    u_raw, msg = call(
         functools.partial(first_kernel, n_col),
         tiles,
         pieces + [consts, ats],
-        [(ROWS_HELD, BLK), (MSG, BLK), consts.shape, ats.shape],
+        [(ROWS_HELD, BLK), (MSG, BLK)],
     )
     alphas, betas, v_raws = [], [], []
     for step in range(ITERS):
@@ -299,13 +311,11 @@
             )
         alphas.append(alpha)
 
-    both = square + swap(square)
-    parts = to_chips(both)
-    parts[twice] = jnp.where(row % 2 == 0, both, parts[twice])
-    half = functools.reduce(lambda a, b: a + b, parts)
-    square = half + swap(half)
     mine = [lax.dynamic_slice_in_dim(v, row * per_out, per_out) for v in v_raws]
-    out, residual = call(end_kernel, None, [square] + mine + alphas + betas, [(per_out, BLK), (1, 1)])
+    held = call(before_end_kernel, None, mine + alphas + betas, [(per_out, BLK), (per_out, BLK), (8, BLK)])
+    beside = to_near(square)
+    half = functools.reduce(lambda a, b: a + b, to_chips(square + swap(square)), square + beside)
+    out, residual = call(end_kernel, None, [half, swap(half), *held], [(per_out, BLK), (1, 1)])
     return out.reshape(per_out * BLK), residual.reshape(())
 
 

time: 80.2 us -> 74.2 us (0.925)
  waiting for transfers between devices: 39 us -> 32.1 us
  starting transfers between devices: 27 us -> 30.7 us
  other arithmetic: 2.54 us -> 0.26 us
    ppermute x16 -> x12, waiting for transfers between devices: 18.2 us -> 3.23 us  [to_chips(): lax.ppermute(x, 'row', [(r, r ^ 2 * step[r % 2]) for r in range(n_row)])]
    ppermute x0 -> x4, waiting for transfers between devices: none -> 11.3 us  [to_near(): return lax.ppermute(x, 'row', [(r, r ^ 2 * near) for r in range(n_row)])]
    ppermute x0 -> x4, starting transfers between devices: none -> 4.31 us  [to_near(): return lax.ppermute(x, 'row', [(r, r ^ 2 * near) for r in range(n_row)])]
    ppermute x16 -> x12, starting transfers between devices: 22 us -> 18.4 us  [to_chips(): lax.ppermute(x, 'row', [(r, r ^ 2 * step[r % 2]) for r in range(n_row)])]
    ppermute x4, starting transfers between devices: 4.46 us -> 7.62 us  [around_col(): lax.ppermute(x, 'col', [(i, (i - s) % n_col) for i in range(n_col)])]
    ppermute x4, waiting for transfers between devices: 10.5 us -> 8.03 us  [around_col(): lax.ppermute(x, 'col', [(i, (i - s) % n_col) for i in range(n_col)])]
    convert_element_type x2 -> x0, other arithmetic: 0.81 us -> none  [the longest x1 0.81 us: on_device(): ats = jnp.concatenate([rows_turned, cols_here]).astype(f32)]
    another operation x1 -> x0, other arithmetic: 0.8 us -> none  [on_device(): jnp.stack([jnp.concatenate([cols_here, cols_here]), jnp.concatenate([rows...]
  transfers between devices with their start and end apart: 28 -> 28, of which waited for: 21 -> 20; matrix products, arithmetic and copies ran while one was open for 3% -> 0% of each run, Pallas kernels for 4% -> 4%
where the time goes in v3:
time: 74.2 us; the launch traced here: 74.1 us
  waiting for transfers between devices  32.1 us (43%)
  starting transfers between devices  30.7 us (41%)
  Pallas kernels  10.1 us (14%)
  between operations  0.78 us (1%)
    ppermute x12, starting transfers between devices, to_chips(): lax.ppermute(x, 'row', [(r, r ^ 2 * step[r % 2]) for r in range(n_row)])  18.4 us
    ppermute x4, waiting for transfers between devices, to_near(): return lax.ppermute(x, 'row', [(r, r ^ 2 * near) for r in range(n_row)])  11.3 us
    ppermute x8, waiting for transfers between devices, swap(): return lax.ppermute(x, 'row', [(r, r ^ 1) for r in range(n_row)])  9.53 us
    ppermute x4, waiting for transfers between devices, around_col(): lax.ppermute(x, 'col', [(i, (i - s) % n_col) for i in range(n_col)])  8.03 us
    ppermute x4, starting transfers between devices, around_col(): lax.ppermute(x, 'col', [(i, (i - s) % n_col) for i in range(n_col)])  7.62 us
    pallas_call x12, Pallas kernels, call(): pl.pallas_call(body, out_shape=[jax.ShapeDtypeStruct(s, f32) for s in out...  7.23 us
    ppermute x4, starting transfers between devices, to_near(): return lax.ppermute(x, 'row', [(r, r ^ 2 * near) for r in range(n_row)])  4.31 us
    ppermute x12, waiting for transfers between devices, to_chips(): lax.ppermute(x, 'row', [(r, r ^ 2 * step[r % 2]) for r in range(n_row)])  3.23 us
  transfers between devices with their start and end apart: 28, of which 20 were waited for; matrix products, arithmetic and copies ran while one was open for 0% of the time, Pallas kernels for 4%

profile of v3, /device:TPU:0, one launch (start us, length us, event | category | flops | bytes accessed | tf_op | source)
XLA Modules:
  0.0 74.1 jit_solution(15965095063093772235)
XLA Ops:
  0.6 3.0 %collective-permute-start = (f32[248,128]{1,0:T(8,128)}, f32[248,128]{1,0:T(8,128)S(1)}, u32[]{:S(2)}, u32[]{:S(2)}) collective-permute-start(f32[248,128]{1,0:T(8,128)} %bitcast.7), channel_id=1, source_target_pairs={{0,1},{1,0},{2,3},{3,2},{4,5},{5,4},{6,7},{7,6},{8,9},{9,8},{10,11... | collective-permute-start | bytes 380936 | tf_op jit(solution)/shard_map/ppermute | solution.py:265
  3.7 2.9 %shard_map.59 = (bf16[16384,256]{1,0:T(8,128)(2,1)S(1)}, f32[8,128]{1,0:T(8,128)S(1)}, f32[128,128]{1,0:T(8,128)S(1)}, f32[248,128]{1,0:T(8,128)S(1)}) custom-call(f32[8192,128]{1,0:T(8,128)} %bitcast.6, s32[1,64]{1,0:T(1,128)} %bitcast.9, s32[1,64]{1,0:T(1,128)} %bitcast.10, f32[248,128]{1,0:T(8,128)} %bitcast.8, f32[8,128]{1,0:T(8,128)S(1)} %broadcast_in_dim.3.place), custom_call_target="tpu_custom_call" | custom-call | bytes 4194304 | tf_op jit(solution)/shard_map/pallas_call | solution.py:206
  6.6 0.7 collective-permute-done.refs_1_
  7.3 0.8 %shard_map.60 = (f32[512,128]{1,0:T(8,128)S(1)}, f32[72,128]{1,0:T(8,128)S(1)}) custom-call(bf16[16384,256]{1,0:T(8,128)(2,1)S(1)} %get-tuple-element.31.tiles.refs_0_, f32[248,128]{1,0:T(8,128)S(1)} %get-tuple-element.32.refs_0_, f32[248,128]{1,0:T(8,128)S(1)} %collective-permute-done.refs_1_, f32[8,128]{1,0:T(8,128)S(1)} %get-tuple-element.30.refs_2_.refs_0_.refs_1_, ...), custom_call_target="tpu_custom_call" | custom-call | tf_op jit(solution)/shard_map/pallas_call | solution.py:230
  8.1 1.2 %collective-permute-done.2 = f32[72,128]{1,0:T(8,128)S(1)} collective-permute-done((f32[72,128]{1,0:T(8,128)S(1)}, f32[72,128]{1,0:T(8,128)S(1)}, u32[]{:S(2)}, u32[]{:S(2)}) %collective-permute-start.2) | collective-permute-done | bytes 36896 | tf_op jit(solution)/shard_map/ppermute | solution.py:253
  9.4 3.9 %collective-permute-start.5 = (f32[136,128]{1,0:T(8,128)S(1)}, f32[136,128]{1,0:T(8,128)S(1)}, u32[]{:S(2)}, u32[]{:S(2)}) collective-permute-start(f32[136,128]{1,0:T(8,128)S(1)} %pad_maximum_fusion), channel_id=1, source_target_pairs={{0,24},{2,30},{4,28},{6,26},{8,16},{10,22},{12,20},{14,18},{16,8},... | collective-permute-start | bytes 208904 | tf_op jit(solution)/shard_map/ppermute | solution.py:260
  13.2 0.5 collective-permute-start.4
  13.7 2.5 %collective-permute-start.3 = (f32[136,128]{1,0:T(8,128)S(1)}, f32[136,128]{1,0:T(8,128)S(1)}, u32[]{:S(2)}, u32[]{:S(2)}) collective-permute-start(f32[136,128]{1,0:T(8,128)S(1)} %pad_maximum_fusion), channel_id=1, source_target_pairs={{0,8},{2,18},{4,12},{6,22},{8,0},{10,26},{12,4},{14,30},{16,24},{1... | collective-permute-start | bytes 208904 | tf_op jit(solution)/shard_map/ppermute | solution.py:260
  16.2 0.5 collective-permute-start.1
  16.7 3.7 %collective-permute-done.1.near = f32[72,128]{1,0:T(8,128)S(1)} collective-permute-done((f32[72,128]{1,0:T(8,128)S(1)}, f32[72,128]{1,0:T(8,128)S(1)}, u32[]{:S(2)}, u32[]{:S(2)}) %collective-permute-start.1) | collective-permute-done | bytes 36896 | tf_op jit(solution)/shard_map/ppermute | solution.py:256
  20.4 0.3 collective-permute-done.3.refs_0_
  20.7 0.3 shard_map.61.half
  21.1 1.5 %collective-permute-done.6.other = f32[520,128]{1,0:T(8,128)S(1)} collective-permute-done((f32[520,128]{1,0:T(8,128)S(1)}, f32[520,128]{1,0:T(8,128)S(1)}, u32[]{:S(2)}, u32[]{:S(2)}) %collective-permute-start.6) | collective-permute-done | bytes 266272 | tf_op jit(solution)/shard_map/ppermute | solution.py:253
  22.6 0.8 %shard_map.62 = (f32[512,128]{1,0:T(8,128)S(1)}, f32[72,128]{1,0:T(8,128)S(1)}, f32[8,128]{1,0:T(8,128)S(1)}) custom-call(bf16[16384,256]{1,0:T(8,128)(2,1)S(1)} %get-tuple-element.31.tiles.refs_0_, f32[520,128]{1,0:T(8,128)S(1)} %shard_map.61.half, f32[520,128]{1,0:T(8,128)S(1)} %collective-permute-done.6.other, ...), custom_call_target="tpu_custom_call" | custom-call | tf_op jit(solution)/shard_map/pallas_call | solution.py:230
  23.4 1.5 %collective-permute-start.7 = (f32[72,128]{1,0:T(8,128)S(1)}, f32[72,128]{1,0:T(8,128)S(1)}, u32[]{:S(2)}, u32[]{:S(2)}) collective-permute-start(f32[72,128]{1,0:T(8,128)S(1)} %get-tuple-element.37.refs_4_), channel_id=1, source_target_pairs={{0,1},{1,0},{2,3},{3,2},{4,5},{5,4},{6,7},{7,6},{8,9},{9,8},{10,11... | collective-permute-start | bytes 110600 | tf_op jit(solution)/shard_map/ppermute | solution.py:265
  25.0 2.4 %collective-permute-done.7.refs_5_ = f32[72,128]{1,0:T(8,128)S(1)} collective-permute-done((f32[72,128]{1,0:T(8,128)S(1)}, f32[72,128]{1,0:T(8,128)S(1)}, u32[]{:S(2)}, u32[]{:S(2)}) %collective-permute-start.7) | collective-permute-done | bytes 36896 | tf_op jit(solution)/shard_map/ppermute | solution.py:265
  27.4 1.0 %shard_map.63 = (f32[512,128]{1,0:T(8,128)S(1)}, f32[72,128]{1,0:T(8,128)S(1)}, f32[8,128]{1,0:T(8,128)S(1)}) custom-call(bf16[16384,256]{1,0:T(8,128)(2,1)S(1)} %get-tuple-element.31.tiles.refs_0_, f32[8,128]{1,0:T(8,128)S(1)} %get-tuple-element.30.refs_2_.refs_0_.refs_1_, f32[512,128]{1,0:T(8,128)S(1)} %get-tuple-element.34.refs_2_, ...), custom_call_target="tpu_custom_call" | custom-call | tf_op jit(solution)/shard_map/pallas_call | solution.py:230
  28.4 1.2 %collective-permute-done.9 = f32[72,128]{1,0:T(8,128)S(1)} collective-permute-done((f32[72,128]{1,0:T(8,128)S(1)}, f32[72,128]{1,0:T(8,128)S(1)}, u32[]{:S(2)}, u32[]{:S(2)}) %collective-permute-start.9) | collective-permute-done | bytes 36896 | tf_op jit(solution)/shard_map/ppermute | solution.py:253
  29.7 1.8 %collective-permute-start.12 = (f32[136,128]{1,0:T(8,128)S(1)}, f32[136,128]{1,0:T(8,128)S(1)}, u32[]{:S(2)}, u32[]{:S(2)}) collective-permute-start(f32[136,128]{1,0:T(8,128)S(1)} %pad_maximum_fusion.1), channel_id=1, source_target_pairs={{0,24},{2,30},{4,28},{6,26},{8,16},{10,22},{12,20},{14,18},{16,8},... | collective-permute-start | bytes 208904 | tf_op jit(solution)/shard_map/ppermute | solution.py:260
  31.5 1.8 %collective-permute-start.10 = (f32[136,128]{1,0:T(8,128)S(1)}, f32[136,128]{1,0:T(8,128)S(1)}, u32[]{:S(2)}, u32[]{:S(2)}) collective-permute-start(f32[136,128]{1,0:T(8,128)S(1)} %pad_maximum_fusion.1), channel_id=1, source_target_pairs={{0,8},{2,18},{4,12},{6,22},{8,0},{10,26},{12,4},{14,30},{16,24},{1... | collective-permute-start | bytes 208904 | tf_op jit(solution)/shard_map/ppermute | solution.py:260
  33.3 1.7 %collective-permute-start.8 = (f32[72,128]{1,0:T(8,128)S(1)}, f32[72,128]{1,0:T(8,128)S(1)}, u32[]{:S(2)}, u32[]{:S(2)}) collective-permute-start(f32[72,128]{1,0:T(8,128)S(1)} %get-tuple-element.39.own), channel_id=1, source_target_pairs={{0,4},{2,6},{4,0},{6,2},{8,12},{10,14},{12,8},{14,10},{16,20},{18,... | collective-permute-start | bytes 110600 | tf_op jit(solution)/shard_map/ppermute | solution.py:256
  35.0 3.8 %collective-permute-done.8.near = f32[72,128]{1,0:T(8,128)S(1)} collective-permute-done((f32[72,128]{1,0:T(8,128)S(1)}, f32[72,128]{1,0:T(8,128)S(1)}, u32[]{:S(2)}, u32[]{:S(2)}) %collective-permute-start.8) | collective-permute-done | bytes 36896 | tf_op jit(solution)/shard_map/ppermute | solution.py:256
  39.0 0.3 shard_map.64.half
  39.5 1.5 %collective-permute-done.13.other = f32[520,128]{1,0:T(8,128)S(1)} collective-permute-done((f32[520,128]{1,0:T(8,128)S(1)}, f32[520,128]{1,0:T(8,128)S(1)}, u32[]{:S(2)}, u32[]{:S(2)}) %collective-permute-start.13) | collective-permute-done | bytes 266272 | tf_op jit(solution)/shard_map/ppermute | solution.py:253
  40.9 0.8 %shard_map.65 = (f32[512,128]{1,0:T(8,128)S(1)}, f32[72,128]{1,0:T(8,128)S(1)}, f32[8,128]{1,0:T(8,128)S(1)}) custom-call(bf16[16384,256]{1,0:T(8,128)(2,1)S(1)} %get-tuple-element.31.tiles.refs_0_, f32[520,128]{1,0:T(8,128)S(1)} %shard_map.64.half, f32[520,128]{1,0:T(8,128)S(1)} %collective-permute-done.13.other, f32[512,128]{1,0:T(8,128)S(1)} %get-tuple-element.40.refs_0_, ...), custom_call_target="tpu_custom_call" | custom-call | tf_op jit(solution)/shard_map/pallas_call | solution.py:230
  41.8 1.5 %collective-permute-start.14 = (f32[72,128]{1,0:T(8,128)S(1)}, f32[72,128]{1,0:T(8,128)S(1)}, u32[]{:S(2)}, u32[]{:S(2)}) collective-permute-start(f32[72,128]{1,0:T(8,128)S(1)} %get-tuple-element.43.refs_4_), channel_id=1, source_target_pairs={{0,1},{1,0},{2,3},{3,2},{4,5},{5,4},{6,7},{7,6},{8,9},{9,8},{10,11... | collective-permute-start | bytes 110600 | tf_op jit(solution)/shard_map/ppermute | solution.py:265
  43.3 2.4 %collective-permute-done.14.refs_5_ = f32[72,128]{1,0:T(8,128)S(1)} collective-permute-done((f32[72,128]{1,0:T(8,128)S(1)}, f32[72,128]{1,0:T(8,128)S(1)}, u32[]{:S(2)}, u32[]{:S(2)}) %collective-permute-start.14) | collective-permute-done | bytes 36896 | tf_op jit(solution)/shard_map/ppermute | solution.py:265
  45.7 1.0 %shard_map.66 = (f32[512,128]{1,0:T(8,128)S(1)}, f32[72,128]{1,0:T(8,128)S(1)}, f32[8,128]{1,0:T(8,128)S(1)}) custom-call(bf16[16384,256]{1,0:T(8,128)(2,1)S(1)} %get-tuple-element.31.tiles.refs_0_, f32[8,128]{1,0:T(8,128)S(1)} %get-tuple-element.30.refs_2_.refs_0_.refs_1_, f32[512,128]{1,0:T(8,128)S(1)} %get-tuple-element.38.refs_2_, ...), custom_call_target="tpu_custom_call" | custom-call | tf_op jit(solution)/shard_map/pallas_call | solution.py:230
  46.8 1.2 %collective-permute-done.16 = f32[72,128]{1,0:T(8,128)S(1)} collective-permute-done((f32[72,128]{1,0:T(8,128)S(1)}, f32[72,128]{1,0:T(8,128)S(1)}, u32[]{:S(2)}, u32[]{:S(2)}) %collective-permute-start.16) | collective-permute-done | bytes 36896 | tf_op jit(solution)/shard_map/ppermute | solution.py:253
  48.1 1.8 %collective-permute-start.19 = (f32[136,128]{1,0:T(8,128)S(1)}, f32[136,128]{1,0:T(8,128)S(1)}, u32[]{:S(2)}, u32[]{:S(2)}) collective-permute-start(f32[136,128]{1,0:T(8,128)S(1)} %pad_maximum_fusion.2), channel_id=1, source_target_pairs={{0,24},{2,30},{4,28},{6,26},{8,16},{10,22},{12,20},{14,18},{16,8},... | collective-permute-start | bytes 208904 | tf_op jit(solution)/shard_map/ppermute | solution.py:260
  50.0 2.2 %collective-permute-start.17 = (f32[136,128]{1,0:T(8,128)S(1)}, f32[136,128]{1,0:T(8,128)S(1)}, u32[]{:S(2)}, u32[]{:S(2)}) collective-permute-start(f32[136,128]{1,0:T(8,128)S(1)} %pad_maximum_fusion.2), channel_id=1, source_target_pairs={{0,8},{2,18},{4,12},{6,22},{8,0},{10,26},{12,4},{14,30},{16,24},{1... | collective-permute-start | bytes 208904 | tf_op jit(solution)/shard_map/ppermute | solution.py:260
  52.1 1.2 %collective-permute-start.15 = (f32[72,128]{1,0:T(8,128)S(1)}, f32[72,128]{1,0:T(8,128)S(1)}, u32[]{:S(2)}, u32[]{:S(2)}) collective-permute-start(f32[72,128]{1,0:T(8,128)S(1)} %get-tuple-element.45.own), channel_id=1, source_target_pairs={{0,4},{2,6},{4,0},{6,2},{8,12},{10,14},{12,8},{14,10},{16,20},{18,... | collective-permute-start | bytes 110600 | tf_op jit(solution)/shard_map/ppermute | solution.py:256
  53.4 3.9 %collective-permute-done.15.near = f32[72,128]{1,0:T(8,128)S(1)} collective-permute-done((f32[72,128]{1,0:T(8,128)S(1)}, f32[72,128]{1,0:T(8,128)S(1)}, u32[]{:S(2)}, u32[]{:S(2)}) %collective-permute-start.15) | collective-permute-done | bytes 36896 | tf_op jit(solution)/shard_map/ppermute | solution.py:256
  57.3 0.6 collective-permute-done.17.refs_0_
  57.9 0.3 shard_map.67.half
  58.3 1.5 %collective-permute-done.20.other = f32[520,128]{1,0:T(8,128)S(1)} collective-permute-done((f32[520,128]{1,0:T(8,128)S(1)}, f32[520,128]{1,0:T(8,128)S(1)}, u32[]{:S(2)}, u32[]{:S(2)}) %collective-permute-start.20) | collective-permute-done | bytes 266272 | tf_op jit(solution)/shard_map/ppermute | solution.py:253
  59.8 0.8 %shard_map.68 = (f32[512,128]{1,0:T(8,128)S(1)}, f32[72,128]{1,0:T(8,128)S(1)}, f32[8,128]{1,0:T(8,128)S(1)}) custom-call(bf16[16384,256]{1,0:T(8,128)(2,1)S(1)} %get-tuple-element.31.tiles.refs_0_, f32[520,128]{1,0:T(8,128)S(1)} %shard_map.67.half, f32[520,128]{1,0:T(8,128)S(1)} %collective-permute-done.20.other, f32[512,128]{1,0:T(8,128)S(1)} %get-tuple-element.46.refs_0_, ...), custom_call_target="tpu_custom_call" | custom-call | tf_op jit(solution)/shard_map/pallas_call | solution.py:230
  60.6 1.5 %collective-permute-start.21 = (f32[72,128]{1,0:T(8,128)S(1)}, f32[72,128]{1,0:T(8,128)S(1)}, u32[]{:S(2)}, u32[]{:S(2)}) collective-permute-start(f32[72,128]{1,0:T(8,128)S(1)} %get-tuple-element.49.refs_3_), channel_id=1, source_target_pairs={{0,1},{1,0},{2,3},{3,2},{4,5},{5,4},{6,7},{7,6},{8,9},{9,8},{10,11... | collective-permute-start | bytes 110600 | tf_op jit(solution)/shard_map/ppermute | solution.py:265
  62.1 2.4 %collective-permute-done.21.refs_4_ = f32[72,128]{1,0:T(8,128)S(1)} collective-permute-done((f32[72,128]{1,0:T(8,128)S(1)}, f32[72,128]{1,0:T(8,128)S(1)}, u32[]{:S(2)}, u32[]{:S(2)}) %collective-permute-start.21) | collective-permute-done | bytes 36896 | tf_op jit(solution)/shard_map/ppermute | solution.py:265
  64.6 0.3 shard_map.69
  64.9 0.8 %collective-permute-start.22 = (f32[8,128]{1,0:T(8,128)S(1)}, f32[8,128]{1,0:T(8,128)S(1)}, u32[]{:S(2)}, u32[]{:S(2)}) collective-permute-start(f32[8,128]{1,0:T(8,128)S(1)} %get-tuple-element.50), channel_id=1, source_target_pairs={{0,4},{2,6},{4,0},{6,2},{8,12},{10,14},{12,8},{14,10},{16,20},{18,... | collective-permute-start | bytes 12296 | tf_op jit(solution)/shard_map/ppermute | solution.py:256
  65.8 0.3 collective-permute-done.23
  66.1 1.6 %collective-permute-start.26 = (f32[8,128]{1,0:T(8,128)S(1)}, f32[8,128]{1,0:T(8,128)S(1)}, u32[]{:S(2)}, u32[]{:S(2)}) collective-permute-start(f32[8,128]{1,0:T(8,128)S(1)} %add.33), channel_id=1, source_target_pairs={{0,24},{2,30},{4,28},{6,26},{8,16},{10,22},{12,20},{14,18},{16,8},... | collective-permute-start | bytes 12296 | tf_op jit(solution)/shard_map/ppermute | solution.py:260
  67.7 2.4 %collective-permute-start.24 = (f32[8,128]{1,0:T(8,128)S(1)}, f32[8,128]{1,0:T(8,128)S(1)}, u32[]{:S(2)}, u32[]{:S(2)}) collective-permute-start(f32[8,128]{1,0:T(8,128)S(1)} %add.33), channel_id=1, source_target_pairs={{0,8},{2,18},{4,12},{6,22},{8,0},{10,26},{12,4},{14,30},{16,24},{1... | collective-permute-start | bytes 12296 | tf_op jit(solution)/shard_map/ppermute | solution.py:260
  70.1 1.4 %collective-permute-done.26 = f32[8,128]{1,0:T(8,128)S(1)} collective-permute-done((f32[8,128]{1,0:T(8,128)S(1)}, f32[8,128]{1,0:T(8,128)S(1)}, u32[]{:S(2)}, u32[]{:S(2)}) %collective-permute-start.26) | collective-permute-done | bytes 4128 | tf_op jit(solution)/shard_map/ppermute | solution.py:260
  71.5 0.7 collective-permute-done.25
  72.4 1.1 %collective-permute-done.27.other = f32[8,128]{1,0:T(8,128)S(1)} collective-permute-done((f32[8,128]{1,0:T(8,128)S(1)}, f32[8,128]{1,0:T(8,128)S(1)}, u32[]{:S(2)}, u32[]{:S(2)}) %collective-permute-start.27) | collective-permute-done | bytes 4128 | tf_op jit(solution)/shard_map/ppermute | solution.py:253
  73.4 0.6 shard_map.71
  (41 shorter events, 1.1 us)
Async XLA Ops:
  0.6 6.7 %collective-permute-start = (f32[248,128]{1,0:T(8,128)}, f32[248,128]{1,0:T(8,128)S(1)}, u32[]{:S(2)}, u32[]{:S(2)}) collective-permute-start(f32[248,128]{1,0:T(8,128)} %bitcast.7), channel_id=1, source_target_pairs={{0,1},{1,0},{2,3},{3,2},{4,5},{5,4},{6,7},{7,6},{8,9},{9,8},{10,11... | collective-permute-start | bytes 380936 | tf_op jit(solution)/shard_map/ppermute | solution.py:265
  8.1 1.2 %collective-permute-start.2 = (f32[72,128]{1,0:T(8,128)S(1)}, f32[72,128]{1,0:T(8,128)S(1)}, u32[]{:S(2)}, u32[]{:S(2)}) collective-permute-start(f32[72,128]{1,0:T(8,128)S(1)} %get-tuple-element.35.own), channel_id=1, source_target_pairs={{0,2},{2,0},{4,6},{6,4},{8,10},{10,8},{12,14},{14,12},{16,18},{18,... | collective-permute-start | bytes 110600 | tf_op jit(solution)/shard_map/ppermute | solution.py:253
  9.4 11.0 %collective-permute-start.5 = (f32[136,128]{1,0:T(8,128)S(1)}, f32[136,128]{1,0:T(8,128)S(1)}, u32[]{:S(2)}, u32[]{:S(2)}) collective-permute-start(f32[136,128]{1,0:T(8,128)S(1)} %pad_maximum_fusion), channel_id=1, source_target_pairs={{0,24},{2,30},{4,28},{6,26},{8,16},{10,22},{12,20},{14,18},{16,8},... | collective-permute-start | bytes 208904 | tf_op jit(solution)/shard_map/ppermute | solution.py:260
  13.2 7.1 %collective-permute-start.4 = (f32[136,128]{1,0:T(8,128)S(1)}, f32[136,128]{1,0:T(8,128)S(1)}, u32[]{:S(2)}, u32[]{:S(2)}) collective-permute-start(f32[136,128]{1,0:T(8,128)S(1)} %pad_maximum_fusion), channel_id=1, source_target_pairs={{0,12},{2,22},{4,8},{6,18},{8,4},{10,30},{12,0},{14,26},{16,28},{1... | collective-permute-start | bytes 208904 | tf_op jit(solution)/shard_map/ppermute | solution.py:260
  13.7 7.0 %collective-permute-start.3 = (f32[136,128]{1,0:T(8,128)S(1)}, f32[136,128]{1,0:T(8,128)S(1)}, u32[]{:S(2)}, u32[]{:S(2)}) collective-permute-start(f32[136,128]{1,0:T(8,128)S(1)} %pad_maximum_fusion), channel_id=1, source_target_pairs={{0,8},{2,18},{4,12},{6,22},{8,0},{10,26},{12,4},{14,30},{16,24},{1... | collective-permute-start | bytes 208904 | tf_op jit(solution)/shard_map/ppermute | solution.py:260
  16.2 4.2 %collective-permute-start.1 = (f32[72,128]{1,0:T(8,128)S(1)}, f32[72,128]{1,0:T(8,128)S(1)}, u32[]{:S(2)}, u32[]{:S(2)}) collective-permute-start(f32[72,128]{1,0:T(8,128)S(1)} %get-tuple-element.35.own), channel_id=1, source_target_pairs={{0,4},{2,6},{4,0},{6,2},{8,12},{10,14},{12,8},{14,10},{16,20},{18,... | collective-permute-start | bytes 110600 | tf_op jit(solution)/shard_map/ppermute | solution.py:256
  21.0 1.6 %collective-permute-start.6 = (f32[520,128]{1,0:T(8,128)S(1)}, f32[520,128]{1,0:T(8,128)S(1)}, u32[]{:S(2)}, u32[]{:S(2)}) collective-permute-start(f32[520,128]{1,0:T(8,128)S(1)} %shard_map.61.half), channel_id=1, source_target_pairs={{0,2},{2,0},{4,6},{6,4},{8,10},{10,8},{12,14},{14,12},{16,18},{18,... | collective-permute-start | bytes 798728 | tf_op jit(solution)/shard_map/ppermute | solution.py:253
  23.4 4.0 %collective-permute-start.7 = (f32[72,128]{1,0:T(8,128)S(1)}, f32[72,128]{1,0:T(8,128)S(1)}, u32[]{:S(2)}, u32[]{:S(2)}) collective-permute-start(f32[72,128]{1,0:T(8,128)S(1)} %get-tuple-element.37.refs_4_), channel_id=1, source_target_pairs={{0,1},{1,0},{2,3},{3,2},{4,5},{5,4},{6,7},{7,6},{8,9},{9,8},{10,11... | collective-permute-start | bytes 110600 | tf_op jit(solution)/shard_map/ppermute | solution.py:265
  28.4 1.2 %collective-permute-start.9 = (f32[72,128]{1,0:T(8,128)S(1)}, f32[72,128]{1,0:T(8,128)S(1)}, u32[]{:S(2)}, u32[]{:S(2)}) collective-permute-start(f32[72,128]{1,0:T(8,128)S(1)} %get-tuple-element.39.own), channel_id=1, source_target_pairs={{0,2},{2,0},{4,6},{6,4},{8,10},{10,8},{12,14},{14,12},{16,18},{18,... | collective-permute-start | bytes 110600 | tf_op jit(solution)/shard_map/ppermute | solution.py:253
  29.7 9.1 %collective-permute-start.12 = (f32[136,128]{1,0:T(8,128)S(1)}, f32[136,128]{1,0:T(8,128)S(1)}, u32[]{:S(2)}, u32[]{:S(2)}) collective-permute-start(f32[136,128]{1,0:T(8,128)S(1)} %pad_maximum_fusion.1), channel_id=1, source_target_pairs={{0,24},{2,30},{4,28},{6,26},{8,16},{10,22},{12,20},{14,18},{16,8},... | collective-permute-start | bytes 208904 | tf_op jit(solution)/shard_map/ppermute | solution.py:260
  31.5 7.3 %collective-permute-start.11 = (f32[136,128]{1,0:T(8,128)S(1)}, f32[136,128]{1,0:T(8,128)S(1)}, u32[]{:S(2)}, u32[]{:S(2)}) collective-permute-start(f32[136,128]{1,0:T(8,128)S(1)} %pad_maximum_fusion.1), channel_id=1, source_target_pairs={{0,12},{2,22},{4,8},{6,18},{8,4},{10,30},{12,0},{14,26},{16,28},{1... | collective-permute-start | bytes 208904 | tf_op jit(solution)/shard_map/ppermute | solution.py:260
  31.5 7.5 %collective-permute-start.10 = (f32[136,128]{1,0:T(8,128)S(1)}, f32[136,128]{1,0:T(8,128)S(1)}, u32[]{:S(2)}, u32[]{:S(2)}) collective-permute-start(f32[136,128]{1,0:T(8,128)S(1)} %pad_maximum_fusion.1), channel_id=1, source_target_pairs={{0,8},{2,18},{4,12},{6,22},{8,0},{10,26},{12,4},{14,30},{16,24},{1... | collective-permute-start | bytes 208904 | tf_op jit(solution)/shard_map/ppermute | solution.py:260
  33.3 5.5 %collective-permute-start.8 = (f32[72,128]{1,0:T(8,128)S(1)}, f32[72,128]{1,0:T(8,128)S(1)}, u32[]{:S(2)}, u32[]{:S(2)}) collective-permute-start(f32[72,128]{1,0:T(8,128)S(1)} %get-tuple-element.39.own), channel_id=1, source_target_pairs={{0,4},{2,6},{4,0},{6,2},{8,12},{10,14},{12,8},{14,10},{16,20},{18,... | collective-permute-start | bytes 110600 | tf_op jit(solution)/shard_map/ppermute | solution.py:256
  39.3 1.6 %collective-permute-start.13 = (f32[520,128]{1,0:T(8,128)S(1)}, f32[520,128]{1,0:T(8,128)S(1)}, u32[]{:S(2)}, u32[]{:S(2)}) collective-permute-start(f32[520,128]{1,0:T(8,128)S(1)} %shard_map.64.half), channel_id=1, source_target_pairs={{0,2},{2,0},{4,6},{6,4},{8,10},{10,8},{12,14},{14,12},{16,18},{18,... | collective-permute-start | bytes 798728 | tf_op jit(solution)/shard_map/ppermute | solution.py:253
  41.8 4.0 %collective-permute-start.14 = (f32[72,128]{1,0:T(8,128)S(1)}, f32[72,128]{1,0:T(8,128)S(1)}, u32[]{:S(2)}, u32[]{:S(2)}) collective-permute-start(f32[72,128]{1,0:T(8,128)S(1)} %get-tuple-element.43.refs_4_), channel_id=1, source_target_pairs={{0,1},{1,0},{2,3},{3,2},{4,5},{5,4},{6,7},{7,6},{8,9},{9,8},{10,11... | collective-permute-start | bytes 110600 | tf_op jit(solution)/shard_map/ppermute | solution.py:265
  46.8 1.2 %collective-permute-start.16 = (f32[72,128]{1,0:T(8,128)S(1)}, f32[72,128]{1,0:T(8,128)S(1)}, u32[]{:S(2)}, u32[]{:S(2)}) collective-permute-start(f32[72,128]{1,0:T(8,128)S(1)} %get-tuple-element.45.own), channel_id=1, source_target_pairs={{0,2},{2,0},{4,6},{6,4},{8,10},{10,8},{12,14},{14,12},{16,18},{18,... | collective-permute-start | bytes 110600 | tf_op jit(solution)/shard_map/ppermute | solution.py:253
  48.1 9.2 %collective-permute-start.19 = (f32[136,128]{1,0:T(8,128)S(1)}, f32[136,128]{1,0:T(8,128)S(1)}, u32[]{:S(2)}, u32[]{:S(2)}) collective-permute-start(f32[136,128]{1,0:T(8,128)S(1)} %pad_maximum_fusion.2), channel_id=1, source_target_pairs={{0,24},{2,30},{4,28},{6,26},{8,16},{10,22},{12,20},{14,18},{16,8},... | collective-permute-start | bytes 208904 | tf_op jit(solution)/shard_map/ppermute | solution.py:260
  49.9 7.4 %collective-permute-start.18 = (f32[136,128]{1,0:T(8,128)S(1)}, f32[136,128]{1,0:T(8,128)S(1)}, u32[]{:S(2)}, u32[]{:S(2)}) collective-permute-start(f32[136,128]{1,0:T(8,128)S(1)} %pad_maximum_fusion.2), channel_id=1, source_target_pairs={{0,12},{2,22},{4,8},{6,18},{8,4},{10,30},{12,0},{14,26},{16,28},{1... | collective-permute-start | bytes 208904 | tf_op jit(solution)/shard_map/ppermute | solution.py:260
  50.0 7.9 %collective-permute-start.17 = (f32[136,128]{1,0:T(8,128)S(1)}, f32[136,128]{1,0:T(8,128)S(1)}, u32[]{:S(2)}, u32[]{:S(2)}) collective-permute-start(f32[136,128]{1,0:T(8,128)S(1)} %pad_maximum_fusion.2), channel_id=1, source_target_pairs={{0,8},{2,18},{4,12},{6,22},{8,0},{10,26},{12,4},{14,30},{16,24},{1... | collective-permute-start | bytes 208904 | tf_op jit(solution)/shard_map/ppermute | solution.py:260
  52.1 5.1 %collective-permute-start.15 = (f32[72,128]{1,0:T(8,128)S(1)}, f32[72,128]{1,0:T(8,128)S(1)}, u32[]{:S(2)}, u32[]{:S(2)}) collective-permute-start(f32[72,128]{1,0:T(8,128)S(1)} %get-tuple-element.45.own), channel_id=1, source_target_pairs={{0,4},{2,6},{4,0},{6,2},{8,12},{10,14},{12,8},{14,10},{16,20},{18,... | collective-permute-start | bytes 110600 | tf_op jit(solution)/shard_map/ppermute | solution.py:256
  58.2 1.6 %collective-permute-start.20 = (f32[520,128]{1,0:T(8,128)S(1)}, f32[520,128]{1,0:T(8,128)S(1)}, u32[]{:S(2)}, u32[]{:S(2)}) collective-permute-start(f32[520,128]{1,0:T(8,128)S(1)} %shard_map.67.half), channel_id=1, source_target_pairs={{0,2},{2,0},{4,6},{6,4},{8,10},{10,8},{12,14},{14,12},{16,18},{18,... | collective-permute-start | bytes 798728 | tf_op jit(solution)/shard_map/ppermute | solution.py:253
  60.6 4.0 %collective-permute-start.21 = (f32[72,128]{1,0:T(8,128)S(1)}, f32[72,128]{1,0:T(8,128)S(1)}, u32[]{:S(2)}, u32[]{:S(2)}) collective-permute-start(f32[72,128]{1,0:T(8,128)S(1)} %get-tuple-element.49.refs_3_), channel_id=1, source_target_pairs={{0,1},{1,0},{2,3},{3,2},{4,5},{5,4},{6,7},{7,6},{8,9},{9,8},{10,11... | collective-permute-start | bytes 110600 | tf_op jit(solution)/shard_map/ppermute | solution.py:265
  64.9 1.2 %collective-permute-start.23 = (f32[8,128]{1,0:T(8,128)S(1)}, f32[8,128]{1,0:T(8,128)S(1)}, u32[]{:S(2)}, u32[]{:S(2)}) collective-permute-start(f32[8,128]{1,0:T(8,128)S(1)} %get-tuple-element.50), channel_id=1, source_target_pairs={{0,2},{2,0},{4,6},{6,4},{8,10},{10,8},{12,14},{14,12},{16,18},{18,... | collective-permute-start | bytes 12296 | tf_op jit(solution)/shard_map/ppermute | solution.py:253
  64.9 5.2 %collective-permute-start.22 = (f32[8,128]{1,0:T(8,128)S(1)}, f32[8,128]{1,0:T(8,128)S(1)}, u32[]{:S(2)}, u32[]{:S(2)}) collective-permute-start(f32[8,128]{1,0:T(8,128)S(1)} %get-tuple-element.50), channel_id=1, source_target_pairs={{0,4},{2,6},{4,0},{6,2},{8,12},{10,14},{12,8},{14,10},{16,20},{18,... | collective-permute-start | bytes 12296 | tf_op jit(solution)/shard_map/ppermute | solution.py:256
  66.1 5.4 %collective-permute-start.26 = (f32[8,128]{1,0:T(8,128)S(1)}, f32[8,128]{1,0:T(8,128)S(1)}, u32[]{:S(2)}, u32[]{:S(2)}) collective-permute-start(f32[8,128]{1,0:T(8,128)S(1)} %add.33), channel_id=1, source_target_pairs={{0,24},{2,30},{4,28},{6,26},{8,16},{10,22},{12,20},{14,18},{16,8},... | collective-permute-start | bytes 12296 | tf_op jit(solution)/shard_map/ppermute | solution.py:260
  67.7 4.5 %collective-permute-start.25 = (f32[8,128]{1,0:T(8,128)S(1)}, f32[8,128]{1,0:T(8,128)S(1)}, u32[]{:S(2)}, u32[]{:S(2)}) collective-permute-start(f32[8,128]{1,0:T(8,128)S(1)} %add.33), channel_id=1, source_target_pairs={{0,12},{2,22},{4,8},{6,18},{8,4},{10,30},{12,0},{14,26},{16,28},{1... | collective-permute-start | bytes 12296 | tf_op jit(solution)/shard_map/ppermute | solution.py:260
  67.7 4.5 %collective-permute-start.24 = (f32[8,128]{1,0:T(8,128)S(1)}, f32[8,128]{1,0:T(8,128)S(1)}, u32[]{:S(2)}, u32[]{:S(2)}) collective-permute-start(f32[8,128]{1,0:T(8,128)S(1)} %add.33), channel_id=1, source_target_pairs={{0,8},{2,18},{4,12},{6,22},{8,0},{10,26},{12,4},{14,30},{16,24},{1... | collective-permute-start | bytes 12296 | tf_op jit(solution)/shard_map/ppermute | solution.py:260
  72.2 1.2 %collective-permute-start.27 = (f32[8,128]{1,0:T(8,128)S(1)}, f32[8,128]{1,0:T(8,128)S(1)}, u32[]{:S(2)}, u32[]{:S(2)}) collective-permute-start(f32[8,128]{1,0:T(8,128)S(1)} %add_add_fusion.half), channel_id=1, source_target_pairs={{0,2},{2,0},{4,6},{6,4},{8,10},{10,8},{12,14},{14,12},{16,18},{18,... | collective-permute-start | bytes 12296 | tf_op jit(solution)/shard_map/ppermute | solution.py:253

commit v4 on v3

--- a/solution.py
+++ b/solution.py
@@ -238,13 +238,14 @@
 
 def chip_steps(chips):
     if chips == 8:
-        return 1, [(2, 4), (3, 5), (6, 7)]
-    return 1, [(m, m + 1) for m in range(2, chips, 2)]
+        return (2, [(1, 7), (3, 5), (6, 4)]), (1, [(2, 4), (3, 5), (6, 7)])
+    steps = 1, [(m, m + 1) for m in range(2, chips, 2)]
+    return steps, steps
 
 
 def on_device(n_row, n_col, rhs, blocks, blk_row, blk_col):
     chips = n_row // 2
-    near, steps = chip_steps(chips)
+    gather_steps, sum_steps = chip_steps(chips)
     per_rhs = rhs.shape[0] // BLK
     per_out = COLB_DEV // n_row
     row, col = lax.axis_index("row"), lax.axis_index("col")
@@ -252,13 +253,11 @@
     def swap(x):
         return lax.ppermute(x, "row", [(r, r ^ 1) for r in range(n_row)])
 
-    def to_near(x):
-        return lax.ppermute(x, "row", [(r, r ^ (2 * near)) for r in range(n_row)])
-
-    def to_chips(x):
-        return [
-            lax.ppermute(x, "row", [(r, r ^ (2 * step[r % 2])) for r in range(n_row)]) for step in steps
-        ]
+    def to_near(x, steps):
+        return lax.ppermute(x, "row", [(r, r ^ (2 * steps[0])) for r in range(n_row)])
+
+    def to_chips(x, steps):
+        return [lax.ppermute(x, "row", [(r, r ^ (2 * step[r % 2])) for r in range(n_row)]) for step in steps[1]]
 
     def around_col(x):
         return [x] + [
@@ -275,11 +274,11 @@
     end_row = lax.broadcasted_iota(jnp.int32, (MSG - NB_DEV, BLK), 0)
 
     def gather(msg):
-        peer, beside = swap(msg), to_near(msg)
+        peer, beside = swap(msg), to_near(jnp.pad(msg, ((0, MSG), (0, 0))), gather_steps)
         a, b = msg[NB_DEV:], peer[NB_DEV:]
         end = jnp.where(end_row == 0, jnp.where(lane < NB_DEV, a, b), a + b)
         both = jnp.concatenate([msg[:NB_DEV], peer[:NB_DEV], end])
-        (half,) = call(gather_sum_kernel, tiles, [msg, beside] + to_chips(both), [(COLB_DEV + 8, BLK)])
+        (half,) = call(gather_sum_kernel, tiles, [msg, beside] + to_chips(both, gather_steps), [(COLB_DEV + 8, BLK)])
         return half, swap(half)
 
     u_raw, msg = call(
@@ -313,8 +312,8 @@
 
     mine = [lax.dynamic_slice_in_dim(v, row * per_out, per_out) for v in v_raws]
     held = call(before_end_kernel, None, mine + alphas + betas, [(per_out, BLK), (per_out, BLK), (8, BLK)])
-    beside = to_near(square)
-    half = functools.reduce(lambda a, b: a + b, to_chips(square + swap(square)), square + beside)
+    beside = to_near(square, sum_steps)
+    half = functools.reduce(lambda a, b: a + b, to_chips(square + swap(square), sum_steps), square + beside)
     out, residual = call(end_kernel, None, [half, swap(half), *held], [(per_out, BLK), (1, 1)])
     return out.reshape(per_out * BLK), residual.reshape(())
 

time: 74.2 us -> 73.6 us (level)
  waiting for transfers between devices: 32.1 us -> 30.1 us
  starting transfers between devices: 30.7 us -> 32.1 us
    ppermute x12, waiting for transfers between devices: 3.23 us -> 16.3 us  [to_chips(): lax.ppermute(x, 'row', [(r, r ^ 2 * step[r % 2]) for r in range(n_row)])]
    ppermute x4, waiting for transfers between devices: 11.3 us -> 0.01 us  [to_near(): return lax.ppermute(x, 'row', [(r, r ^ 2 * steps[0]) for r in range(n_row)])]
    ppermute x8, waiting for transfers between devices: 9.53 us -> 5.72 us  [swap(): return lax.ppermute(x, 'row', [(r, r ^ 1) for r in range(n_row)])]
    ppermute x8, starting transfers between devices: 0.38 us -> 3.12 us  [swap(): return lax.ppermute(x, 'row', [(r, r ^ 1) for r in range(n_row)])]
    ppermute x12, starting transfers between devices: 18.4 us -> 16.5 us  [to_chips(): lax.ppermute(x, 'row', [(r, r ^ 2 * step[r % 2]) for r in range(n_row)])]
where the time goes in v4:
time: 73.6 us; the launch traced here: 73.4 us
  starting transfers between devices  32.1 us (44%)
  waiting for transfers between devices  30.1 us (41%)
  Pallas kernels  10.1 us (14%)
  between operations  0.79 us (1%)
    ppermute x12, starting transfers between devices, to_chips(): lax.ppermute(x, 'row', [(r, r ^ 2 * step[r % 2]) for r in range(n_row)])  16.5 us
    ppermute x12, waiting for transfers between devices, to_chips(): lax.ppermute(x, 'row', [(r, r ^ 2 * step[r % 2]) for r in range(n_row)])  16.3 us
    ppermute x4, waiting for transfers between devices, around_col(): lax.ppermute(x, 'col', [(i, (i - s) % n_col) for i in range(n_col)])  8.03 us
    ppermute x4, starting transfers between devices, around_col(): lax.ppermute(x, 'col', [(i, (i - s) % n_col) for i in range(n_col)])  7.65 us
    pallas_call x12, Pallas kernels, call(): pl.pallas_call(body, out_shape=[jax.ShapeDtypeStruct(s, f32) for s in out...  7.23 us
    ppermute x8, waiting for transfers between devices, swap(): return lax.ppermute(x, 'row', [(r, r ^ 1) for r in range(n_row)])  5.72 us
    ppermute x4, starting transfers between devices, to_near(): return lax.ppermute(x, 'row', [(r, r ^ 2 * steps[0]) for r in range(n_row)])  4.79 us
    ppermute x8, starting transfers between devices, swap(): return lax.ppermute(x, 'row', [(r, r ^ 1) for r in range(n_row)])  3.12 us
  transfers between devices with their start and end apart: 28, of which 20 were waited for; matrix products, arithmetic and copies ran while one was open for 0% of the time, Pallas kernels for 4%

profile of v4, /device:TPU:0, one launch (start us, length us, event | category | flops | bytes accessed | tf_op | source)
XLA Modules:
  0.0 73.4 jit_solution(16405371542851938736)
XLA Ops:
  0.6 3.0 %collective-permute-start = (f32[248,128]{1,0:T(8,128)}, f32[248,128]{1,0:T(8,128)S(1)}, u32[]{:S(2)}, u32[]{:S(2)}) collective-permute-start(f32[248,128]{1,0:T(8,128)} %bitcast.7), channel_id=1, source_target_pairs={{0,1},{1,0},{2,3},{3,2},{4,5},{5,4},{6,7},{7,6},{8,9},{9,8},{10,11... | collective-permute-start | bytes 380936 | tf_op jit(solution)/shard_map/ppermute | solution.py:264
  3.7 2.9 %shard_map.59 = (bf16[16384,256]{1,0:T(8,128)(2,1)S(1)}, f32[8,128]{1,0:T(8,128)S(1)}, f32[128,128]{1,0:T(8,128)S(1)}, f32[248,128]{1,0:T(8,128)S(1)}) custom-call(f32[8192,128]{1,0:T(8,128)} %bitcast.6, s32[1,64]{1,0:T(1,128)} %bitcast.9, s32[1,64]{1,0:T(1,128)} %bitcast.10, f32[248,128]{1,0:T(8,128)} %bitcast.8, f32[8,128]{1,0:T(8,128)S(1)} %broadcast_in_dim.3.place), custom_call_target="tpu_custom_call" | custom-call | bytes 4194304 | tf_op jit(solution)/shard_map/pallas_call | solution.py:206
  6.6 0.7 collective-permute-done.refs_1_
  7.3 0.8 %shard_map.60 = (f32[512,128]{1,0:T(8,128)S(1)}, f32[72,128]{1,0:T(8,128)S(1)}) custom-call(bf16[16384,256]{1,0:T(8,128)(2,1)S(1)} %get-tuple-element.31.tiles.refs_0_, f32[248,128]{1,0:T(8,128)S(1)} %get-tuple-element.32.refs_0_, f32[248,128]{1,0:T(8,128)S(1)} %collective-permute-done.refs_1_, f32[8,128]{1,0:T(8,128)S(1)} %get-tuple-element.30.refs_2_.refs_0_.refs_1_, ...), custom_call_target="tpu_custom_call" | custom-call | tf_op jit(solution)/shard_map/pallas_call | solution.py:230
  8.1 1.9 %collective-permute-start.1 = (f32[144,128]{1,0:T(8,128)S(1)}, f32[144,128]{1,0:T(8,128)S(1)}, u32[]{:S(2)}, u32[]{:S(2)}) collective-permute-start(f32[144,128]{1,0:T(8,128)S(1)} %pad.10), channel_id=1, source_target_pairs={{0,8},{2,10},{4,12},{6,14},{8,0},{10,2},{12,4},{14,6},{16,24},{18,... | collective-permute-start | bytes 221192 | tf_op jit(solution)/shard_map/ppermute | solution.py:257
  10.1 3.2 %collective-permute-start.5 = (f32[136,128]{1,0:T(8,128)S(1)}, f32[136,128]{1,0:T(8,128)S(1)}, u32[]{:S(2)}, u32[]{:S(2)}) collective-permute-start(f32[136,128]{1,0:T(8,128)S(1)} %pad_maximum_fusion), channel_id=1, source_target_pairs={{0,24},{2,18},{4,28},{6,22},{8,16},{10,26},{12,20},{14,30},{16,8},... | collective-permute-start | bytes 208904 | tf_op jit(solution)/shard_map/ppermute | solution.py:260
  13.2 0.9 %collective-permute-start.4 = (f32[136,128]{1,0:T(8,128)S(1)}, f32[136,128]{1,0:T(8,128)S(1)}, u32[]{:S(2)}, u32[]{:S(2)}) collective-permute-start(f32[136,128]{1,0:T(8,128)S(1)} %pad_maximum_fusion), channel_id=1, source_target_pairs={{0,12},{2,22},{4,8},{6,18},{8,4},{10,30},{12,0},{14,26},{16,28},{1... | collective-permute-start | bytes 208904 | tf_op jit(solution)/shard_map/ppermute | solution.py:260
  14.2 0.5 collective-permute-start.3
  14.7 2.0 %collective-permute-done.5.refs_2_ = f32[136,128]{1,0:T(8,128)S(1)} collective-permute-done((f32[136,128]{1,0:T(8,128)S(1)}, f32[136,128]{1,0:T(8,128)S(1)}, u32[]{:S(2)}, u32[]{:S(2)}) %collective-permute-start.5) | collective-permute-done | bytes 69664 | tf_op jit(solution)/shard_map/ppermute | solution.py:260
  16.7 2.4 %collective-permute-done.4.refs_1_ = f32[136,128]{1,0:T(8,128)S(1)} collective-permute-done((f32[136,128]{1,0:T(8,128)S(1)}, f32[136,128]{1,0:T(8,128)S(1)}, u32[]{:S(2)}, u32[]{:S(2)}) %collective-permute-start.4) | collective-permute-done | bytes 69664 | tf_op jit(solution)/shard_map/ppermute | solution.py:260
  19.1 1.6 %collective-permute-done.3.refs_0_ = f32[136,128]{1,0:T(8,128)S(1)} collective-permute-done((f32[136,128]{1,0:T(8,128)S(1)}, f32[136,128]{1,0:T(8,128)S(1)}, u32[]{:S(2)}, u32[]{:S(2)}) %collective-permute-start.3) | collective-permute-done | bytes 69664 | tf_op jit(solution)/shard_map/ppermute | solution.py:260
  21.1 1.5 %collective-permute-done.6.other = f32[520,128]{1,0:T(8,128)S(1)} collective-permute-done((f32[520,128]{1,0:T(8,128)S(1)}, f32[520,128]{1,0:T(8,128)S(1)}, u32[]{:S(2)}, u32[]{:S(2)}) %collective-permute-start.6) | collective-permute-done | bytes 266272 | tf_op jit(solution)/shard_map/ppermute | solution.py:254
  22.6 0.8 %shard_map.62 = (f32[512,128]{1,0:T(8,128)S(1)}, f32[72,128]{1,0:T(8,128)S(1)}, f32[8,128]{1,0:T(8,128)S(1)}) custom-call(bf16[16384,256]{1,0:T(8,128)(2,1)S(1)} %get-tuple-element.31.tiles.refs_0_, f32[520,128]{1,0:T(8,128)S(1)} %shard_map.61.half, f32[520,128]{1,0:T(8,128)S(1)} %collective-permute-done.6.other, ...), custom_call_target="tpu_custom_call" | custom-call | tf_op jit(solution)/shard_map/pallas_call | solution.py:230
  23.4 1.5 %collective-permute-start.7 = (f32[72,128]{1,0:T(8,128)S(1)}, f32[72,128]{1,0:T(8,128)S(1)}, u32[]{:S(2)}, u32[]{:S(2)}) collective-permute-start(f32[72,128]{1,0:T(8,128)S(1)} %get-tuple-element.37.refs_4_), channel_id=1, source_target_pairs={{0,1},{1,0},{2,3},{3,2},{4,5},{5,4},{6,7},{7,6},{8,9},{9,8},{10,11... | collective-permute-start | bytes 110600 | tf_op jit(solution)/shard_map/ppermute | solution.py:264
  24.9 2.4 %collective-permute-done.7.refs_5_ = f32[72,128]{1,0:T(8,128)S(1)} collective-permute-done((f32[72,128]{1,0:T(8,128)S(1)}, f32[72,128]{1,0:T(8,128)S(1)}, u32[]{:S(2)}, u32[]{:S(2)}) %collective-permute-start.7) | collective-permute-done | bytes 36896 | tf_op jit(solution)/shard_map/ppermute | solution.py:264
  27.4 1.0 %shard_map.63 = (f32[512,128]{1,0:T(8,128)S(1)}, f32[72,128]{1,0:T(8,128)S(1)}, f32[8,128]{1,0:T(8,128)S(1)}) custom-call(bf16[16384,256]{1,0:T(8,128)(2,1)S(1)} %get-tuple-element.31.tiles.refs_0_, f32[8,128]{1,0:T(8,128)S(1)} %get-tuple-element.30.refs_2_.refs_0_.refs_1_, f32[512,128]{1,0:T(8,128)S(1)} %get-tuple-element.34.refs_2_, ...), custom_call_target="tpu_custom_call" | custom-call | tf_op jit(solution)/shard_map/pallas_call | solution.py:230
  28.4 0.8 %collective-permute-start.8 = (f32[144,128]{1,0:T(8,128)S(1)}, f32[144,128]{1,0:T(8,128)S(1)}, u32[]{:S(2)}, u32[]{:S(2)}) collective-permute-start(f32[144,128]{1,0:T(8,128)S(1)} %pad.11), channel_id=1, source_target_pairs={{0,8},{2,10},{4,12},{6,14},{8,0},{10,2},{12,4},{14,6},{16,24},{18,... | collective-permute-start | bytes 221192 | tf_op jit(solution)/shard_map/ppermute | solution.py:257
  29.2 0.4 collective-permute-done.9
  29.7 2.1 %collective-permute-start.12 = (f32[136,128]{1,0:T(8,128)S(1)}, f32[136,128]{1,0:T(8,128)S(1)}, u32[]{:S(2)}, u32[]{:S(2)}) collective-permute-start(f32[136,128]{1,0:T(8,128)S(1)} %pad_maximum_fusion.1), channel_id=1, source_target_pairs={{0,24},{2,18},{4,28},{6,22},{8,16},{10,26},{12,20},{14,30},{16,8},... | collective-permute-start | bytes 208904 | tf_op jit(solution)/shard_map/ppermute | solution.py:260
  32.0 1.5 %collective-permute-start.10 = (f32[136,128]{1,0:T(8,128)S(1)}, f32[136,128]{1,0:T(8,128)S(1)}, u32[]{:S(2)}, u32[]{:S(2)}) collective-permute-start(f32[136,128]{1,0:T(8,128)S(1)} %pad_maximum_fusion.1), channel_id=1, source_target_pairs={{0,4},{2,30},{4,0},{6,26},{8,12},{10,22},{12,8},{14,18},{16,20},{1... | collective-permute-start | bytes 208904 | tf_op jit(solution)/shard_map/ppermute | solution.py:260
  33.5 3.1 %collective-permute-done.12.refs_2_ = f32[136,128]{1,0:T(8,128)S(1)} collective-permute-done((f32[136,128]{1,0:T(8,128)S(1)}, f32[136,128]{1,0:T(8,128)S(1)}, u32[]{:S(2)}, u32[]{:S(2)}) %collective-permute-start.12) | collective-permute-done | bytes 69664 | tf_op jit(solution)/shard_map/ppermute | solution.py:260
  36.6 0.7 collective-permute-done.11.refs_1_
  37.6 1.4 %collective-permute-start.13 = (f32[520,128]{1,0:T(8,128)S(1)}, f32[520,128]{1,0:T(8,128)S(1)}, u32[]{:S(2)}, u32[]{:S(2)}) collective-permute-start(f32[520,128]{1,0:T(8,128)S(1)} %shard_map.64.half), channel_id=1, source_target_pairs={{0,2},{2,0},{4,6},{6,4},{8,10},{10,8},{12,14},{14,12},{16,18},{18,... | collective-permute-start | bytes 798728 | tf_op jit(solution)/shard_map/ppermute | solution.py:254
  39.0 1.2 %collective-permute-done.13.other = f32[520,128]{1,0:T(8,128)S(1)} collective-permute-done((f32[520,128]{1,0:T(8,128)S(1)}, f32[520,128]{1,0:T(8,128)S(1)}, u32[]{:S(2)}, u32[]{:S(2)}) %collective-permute-start.13) | collective-permute-done | bytes 266272 | tf_op jit(solution)/shard_map/ppermute | solution.py:254
  40.1 0.8 %shard_map.65 = (f32[512,128]{1,0:T(8,128)S(1)}, f32[72,128]{1,0:T(8,128)S(1)}, f32[8,128]{1,0:T(8,128)S(1)}) custom-call(bf16[16384,256]{1,0:T(8,128)(2,1)S(1)} %get-tuple-element.31.tiles.refs_0_, f32[520,128]{1,0:T(8,128)S(1)} %shard_map.64.half, f32[520,128]{1,0:T(8,128)S(1)} %collective-permute-done.13.other, f32[512,128]{1,0:T(8,128)S(1)} %get-tuple-element.40.refs_0_, ...), custom_call_target="tpu_custom_call" | custom-call | tf_op jit(solution)/shard_map/pallas_call | solution.py:230
  41.0 1.5 %collective-permute-start.14 = (f32[72,128]{1,0:T(8,128)S(1)}, f32[72,128]{1,0:T(8,128)S(1)}, u32[]{:S(2)}, u32[]{:S(2)}) collective-permute-start(f32[72,128]{1,0:T(8,128)S(1)} %get-tuple-element.43.refs_4_), channel_id=1, source_target_pairs={{0,1},{1,0},{2,3},{3,2},{4,5},{5,4},{6,7},{7,6},{8,9},{9,8},{10,11... | collective-permute-start | bytes 110600 | tf_op jit(solution)/shard_map/ppermute | solution.py:264
  42.5 2.4 %collective-permute-done.14.refs_5_ = f32[72,128]{1,0:T(8,128)S(1)} collective-permute-done((f32[72,128]{1,0:T(8,128)S(1)}, f32[72,128]{1,0:T(8,128)S(1)}, u32[]{:S(2)}, u32[]{:S(2)}) %collective-permute-start.14) | collective-permute-done | bytes 36896 | tf_op jit(solution)/shard_map/ppermute | solution.py:264
  45.0 1.0 %shard_map.66 = (f32[512,128]{1,0:T(8,128)S(1)}, f32[72,128]{1,0:T(8,128)S(1)}, f32[8,128]{1,0:T(8,128)S(1)}) custom-call(bf16[16384,256]{1,0:T(8,128)(2,1)S(1)} %get-tuple-element.31.tiles.refs_0_, f32[8,128]{1,0:T(8,128)S(1)} %get-tuple-element.30.refs_2_.refs_0_.refs_1_, f32[512,128]{1,0:T(8,128)S(1)} %get-tuple-element.38.refs_2_, ...), custom_call_target="tpu_custom_call" | custom-call | tf_op jit(solution)/shard_map/pallas_call | solution.py:230
  46.0 1.4 %collective-permute-start.15 = (f32[144,128]{1,0:T(8,128)S(1)}, f32[144,128]{1,0:T(8,128)S(1)}, u32[]{:S(2)}, u32[]{:S(2)}) collective-permute-start(f32[144,128]{1,0:T(8,128)S(1)} %pad.12), channel_id=1, source_target_pairs={{0,8},{2,10},{4,12},{6,14},{8,0},{10,2},{12,4},{14,6},{16,24},{18,... | collective-permute-start | bytes 221192 | tf_op jit(solution)/shard_map/ppermute | solution.py:257
  47.5 2.0 %collective-permute-start.19 = (f32[136,128]{1,0:T(8,128)S(1)}, f32[136,128]{1,0:T(8,128)S(1)}, u32[]{:S(2)}, u32[]{:S(2)}) collective-permute-start(f32[136,128]{1,0:T(8,128)S(1)} %pad_maximum_fusion.2), channel_id=1, source_target_pairs={{0,24},{2,18},{4,28},{6,22},{8,16},{10,26},{12,20},{14,30},{16,8},... | collective-permute-start | bytes 208904 | tf_op jit(solution)/shard_map/ppermute | solution.py:260
  49.4 1.1 %collective-permute-start.18 = (f32[136,128]{1,0:T(8,128)S(1)}, f32[136,128]{1,0:T(8,128)S(1)}, u32[]{:S(2)}, u32[]{:S(2)}) collective-permute-start(f32[136,128]{1,0:T(8,128)S(1)} %pad_maximum_fusion.2), channel_id=1, source_target_pairs={{0,12},{2,22},{4,8},{6,18},{8,4},{10,30},{12,0},{14,26},{16,28},{1... | collective-permute-start | bytes 208904 | tf_op jit(solution)/shard_map/ppermute | solution.py:260
  50.6 0.5 collective-permute-start.17
  51.1 2.5 %collective-permute-done.19.refs_2_ = f32[136,128]{1,0:T(8,128)S(1)} collective-permute-done((f32[136,128]{1,0:T(8,128)S(1)}, f32[136,128]{1,0:T(8,128)S(1)}, u32[]{:S(2)}, u32[]{:S(2)}) %collective-permute-start.19) | collective-permute-done | bytes 69664 | tf_op jit(solution)/shard_map/ppermute | solution.py:260
  53.7 1.7 %collective-permute-done.18.refs_1_ = f32[136,128]{1,0:T(8,128)S(1)} collective-permute-done((f32[136,128]{1,0:T(8,128)S(1)}, f32[136,128]{1,0:T(8,128)S(1)}, u32[]{:S(2)}, u32[]{:S(2)}) %collective-permute-start.18) | collective-permute-done | bytes 69664 | tf_op jit(solution)/shard_map/ppermute | solution.py:260
  55.9 1.5 %collective-permute-start.20 = (f32[520,128]{1,0:T(8,128)S(1)}, f32[520,128]{1,0:T(8,128)S(1)}, u32[]{:S(2)}, u32[]{:S(2)}) collective-permute-start(f32[520,128]{1,0:T(8,128)S(1)} %shard_map.67.half), channel_id=1, source_target_pairs={{0,2},{2,0},{4,6},{6,4},{8,10},{10,8},{12,14},{14,12},{16,18},{18,... | collective-permute-start | bytes 798728 | tf_op jit(solution)/shard_map/ppermute | solution.py:254
  57.4 1.2 %collective-permute-done.20.other = f32[520,128]{1,0:T(8,128)S(1)} collective-permute-done((f32[520,128]{1,0:T(8,128)S(1)}, f32[520,128]{1,0:T(8,128)S(1)}, u32[]{:S(2)}, u32[]{:S(2)}) %collective-permute-start.20) | collective-permute-done | bytes 266272 | tf_op jit(solution)/shard_map/ppermute | solution.py:254
  58.6 0.8 %shard_map.68 = (f32[512,128]{1,0:T(8,128)S(1)}, f32[72,128]{1,0:T(8,128)S(1)}, f32[8,128]{1,0:T(8,128)S(1)}) custom-call(bf16[16384,256]{1,0:T(8,128)(2,1)S(1)} %get-tuple-element.31.tiles.refs_0_, f32[520,128]{1,0:T(8,128)S(1)} %shard_map.67.half, f32[520,128]{1,0:T(8,128)S(1)} %collective-permute-done.20.other, f32[512,128]{1,0:T(8,128)S(1)} %get-tuple-element.46.refs_0_, ...), custom_call_target="tpu_custom_call" | custom-call | tf_op jit(solution)/shard_map/pallas_call | solution.py:230
  59.5 1.5 %collective-permute-start.21 = (f32[72,128]{1,0:T(8,128)S(1)}, f32[72,128]{1,0:T(8,128)S(1)}, u32[]{:S(2)}, u32[]{:S(2)}) collective-permute-start(f32[72,128]{1,0:T(8,128)S(1)} %get-tuple-element.49.refs_3_), channel_id=1, source_target_pairs={{0,1},{1,0},{2,3},{3,2},{4,5},{5,4},{6,7},{7,6},{8,9},{9,8},{10,11... | collective-permute-start | bytes 110600 | tf_op jit(solution)/shard_map/ppermute | solution.py:264
  61.0 2.4 %collective-permute-done.21.refs_4_ = f32[72,128]{1,0:T(8,128)S(1)} collective-permute-done((f32[72,128]{1,0:T(8,128)S(1)}, f32[72,128]{1,0:T(8,128)S(1)}, u32[]{:S(2)}, u32[]{:S(2)}) %collective-permute-start.21) | collective-permute-done | bytes 36896 | tf_op jit(solution)/shard_map/ppermute | solution.py:264
  63.8 0.8 %collective-permute-start.22 = (f32[8,128]{1,0:T(8,128)S(1)}, f32[8,128]{1,0:T(8,128)S(1)}, u32[]{:S(2)}, u32[]{:S(2)}) collective-permute-start(f32[8,128]{1,0:T(8,128)S(1)} %get-tuple-element.50), channel_id=1, source_target_pairs={{0,4},{2,6},{4,0},{6,2},{8,12},{10,14},{12,8},{14,10},{16,20},{18,... | collective-permute-start | bytes 12296 | tf_op jit(solution)/shard_map/ppermute | solution.py:257
  64.6 0.4 collective-permute-done.23
  64.9 2.1 %collective-permute-start.26 = (f32[8,128]{1,0:T(8,128)S(1)}, f32[8,128]{1,0:T(8,128)S(1)}, u32[]{:S(2)}, u32[]{:S(2)}) collective-permute-start(f32[8,128]{1,0:T(8,128)S(1)} %add.39), channel_id=1, source_target_pairs={{0,24},{2,30},{4,28},{6,26},{8,16},{10,22},{12,20},{14,18},{16,8},... | collective-permute-start | bytes 12296 | tf_op jit(solution)/shard_map/ppermute | solution.py:260
  67.0 0.8 %collective-permute-start.25 = (f32[8,128]{1,0:T(8,128)S(1)}, f32[8,128]{1,0:T(8,128)S(1)}, u32[]{:S(2)}, u32[]{:S(2)}) collective-permute-start(f32[8,128]{1,0:T(8,128)S(1)} %add.39), channel_id=1, source_target_pairs={{0,12},{2,22},{4,8},{6,18},{8,4},{10,30},{12,0},{14,26},{16,28},{1... | collective-permute-start | bytes 12296 | tf_op jit(solution)/shard_map/ppermute | solution.py:260
  67.8 1.6 %collective-permute-start.24 = (f32[8,128]{1,0:T(8,128)S(1)}, f32[8,128]{1,0:T(8,128)S(1)}, u32[]{:S(2)}, u32[]{:S(2)}) collective-permute-start(f32[8,128]{1,0:T(8,128)S(1)} %add.39), channel_id=1, source_target_pairs={{0,8},{2,18},{4,12},{6,22},{8,0},{10,26},{12,4},{14,30},{16,24},{1... | collective-permute-start | bytes 12296 | tf_op jit(solution)/shard_map/ppermute | solution.py:260
  69.4 0.9 %collective-permute-done.26 = f32[8,128]{1,0:T(8,128)S(1)} collective-permute-done((f32[8,128]{1,0:T(8,128)S(1)}, f32[8,128]{1,0:T(8,128)S(1)}, u32[]{:S(2)}, u32[]{:S(2)}) %collective-permute-start.26) | collective-permute-done | bytes 4128 | tf_op jit(solution)/shard_map/ppermute | solution.py:260
  70.3 1.2 %collective-permute-done.25 = f32[8,128]{1,0:T(8,128)S(1)} collective-permute-done((f32[8,128]{1,0:T(8,128)S(1)}, f32[8,128]{1,0:T(8,128)S(1)}, u32[]{:S(2)}, u32[]{:S(2)}) %collective-permute-start.25) | collective-permute-done | bytes 4128 | tf_op jit(solution)/shard_map/ppermute | solution.py:260
  71.7 1.1 %collective-permute-done.27.other = f32[8,128]{1,0:T(8,128)S(1)} collective-permute-done((f32[8,128]{1,0:T(8,128)S(1)}, f32[8,128]{1,0:T(8,128)S(1)}, u32[]{:S(2)}, u32[]{:S(2)}) %collective-permute-start.27) | collective-permute-done | bytes 4128 | tf_op jit(solution)/shard_map/ppermute | solution.py:254
  72.8 0.6 shard_map.71
  (44 shorter events, 2.3 us)
Async XLA Ops:
  0.6 6.7 %collective-permute-start = (f32[248,128]{1,0:T(8,128)}, f32[248,128]{1,0:T(8,128)S(1)}, u32[]{:S(2)}, u32[]{:S(2)}) collective-permute-start(f32[248,128]{1,0:T(8,128)} %bitcast.7), channel_id=1, source_target_pairs={{0,1},{1,0},{2,3},{3,2},{4,5},{5,4},{6,7},{7,6},{8,9},{9,8},{10,11... | collective-permute-start | bytes 380936 | tf_op jit(solution)/shard_map/ppermute | solution.py:264
  8.1 1.9 %collective-permute-start.2 = (f32[72,128]{1,0:T(8,128)S(1)}, f32[72,128]{1,0:T(8,128)S(1)}, u32[]{:S(2)}, u32[]{:S(2)}) collective-permute-start(f32[72,128]{1,0:T(8,128)S(1)} %get-tuple-element.35.own), channel_id=1, source_target_pairs={{0,2},{2,0},{4,6},{6,4},{8,10},{10,8},{12,14},{14,12},{16,18},{18,... | collective-permute-start | bytes 110600 | tf_op jit(solution)/shard_map/ppermute | solution.py:254
  8.1 6.6 %collective-permute-start.1 = (f32[144,128]{1,0:T(8,128)S(1)}, f32[144,128]{1,0:T(8,128)S(1)}, u32[]{:S(2)}, u32[]{:S(2)}) collective-permute-start(f32[144,128]{1,0:T(8,128)S(1)} %pad.10), channel_id=1, source_target_pairs={{0,8},{2,10},{4,12},{6,14},{8,0},{10,2},{12,4},{14,6},{16,24},{18,... | collective-permute-start | bytes 221192 | tf_op jit(solution)/shard_map/ppermute | solution.py:257
  10.1 6.6 %collective-permute-start.5 = (f32[136,128]{1,0:T(8,128)S(1)}, f32[136,128]{1,0:T(8,128)S(1)}, u32[]{:S(2)}, u32[]{:S(2)}) collective-permute-start(f32[136,128]{1,0:T(8,128)S(1)} %pad_maximum_fusion), channel_id=1, source_target_pairs={{0,24},{2,18},{4,28},{6,22},{8,16},{10,26},{12,20},{14,30},{16,8},... | collective-permute-start | bytes 208904 | tf_op jit(solution)/shard_map/ppermute | solution.py:260
  13.2 5.9 %collective-permute-start.4 = (f32[136,128]{1,0:T(8,128)S(1)}, f32[136,128]{1,0:T(8,128)S(1)}, u32[]{:S(2)}, u32[]{:S(2)}) collective-permute-start(f32[136,128]{1,0:T(8,128)S(1)} %pad_maximum_fusion), channel_id=1, source_target_pairs={{0,12},{2,22},{4,8},{6,18},{8,4},{10,30},{12,0},{14,26},{16,28},{1... | collective-permute-start | bytes 208904 | tf_op jit(solution)/shard_map/ppermute | solution.py:260
  14.2 6.5 %collective-permute-start.3 = (f32[136,128]{1,0:T(8,128)S(1)}, f32[136,128]{1,0:T(8,128)S(1)}, u32[]{:S(2)}, u32[]{:S(2)}) collective-permute-start(f32[136,128]{1,0:T(8,128)S(1)} %pad_maximum_fusion), channel_id=1, source_target_pairs={{0,4},{2,30},{4,0},{6,26},{8,12},{10,22},{12,8},{14,18},{16,20},{1... | collective-permute-start | bytes 208904 | tf_op jit(solution)/shard_map/ppermute | solution.py:260
  21.0 1.6 %collective-permute-start.6 = (f32[520,128]{1,0:T(8,128)S(1)}, f32[520,128]{1,0:T(8,128)S(1)}, u32[]{:S(2)}, u32[]{:S(2)}) collective-permute-start(f32[520,128]{1,0:T(8,128)S(1)} %shard_map.61.half), channel_id=1, source_target_pairs={{0,2},{2,0},{4,6},{6,4},{8,10},{10,8},{12,14},{14,12},{16,18},{18,... | collective-permute-start | bytes 798728 | tf_op jit(solution)/shard_map/ppermute | solution.py:254
  23.4 4.0 %collective-permute-start.7 = (f32[72,128]{1,0:T(8,128)S(1)}, f32[72,128]{1,0:T(8,128)S(1)}, u32[]{:S(2)}, u32[]{:S(2)}) collective-permute-start(f32[72,128]{1,0:T(8,128)S(1)} %get-tuple-element.37.refs_4_), channel_id=1, source_target_pairs={{0,1},{1,0},{2,3},{3,2},{4,5},{5,4},{6,7},{7,6},{8,9},{9,8},{10,11... | collective-permute-start | bytes 110600 | tf_op jit(solution)/shard_map/ppermute | solution.py:264
  28.4 1.2 %collective-permute-start.9 = (f32[72,128]{1,0:T(8,128)S(1)}, f32[72,128]{1,0:T(8,128)S(1)}, u32[]{:S(2)}, u32[]{:S(2)}) collective-permute-start(f32[72,128]{1,0:T(8,128)S(1)} %get-tuple-element.39.own), channel_id=1, source_target_pairs={{0,2},{2,0},{4,6},{6,4},{8,10},{10,8},{12,14},{14,12},{16,18},{18,... | collective-permute-start | bytes 110600 | tf_op jit(solution)/shard_map/ppermute | solution.py:254
  28.4 5.0 %collective-permute-start.8 = (f32[144,128]{1,0:T(8,128)S(1)}, f32[144,128]{1,0:T(8,128)S(1)}, u32[]{:S(2)}, u32[]{:S(2)}) collective-permute-start(f32[144,128]{1,0:T(8,128)S(1)} %pad.11), channel_id=1, source_target_pairs={{0,8},{2,10},{4,12},{6,14},{8,0},{10,2},{12,4},{14,6},{16,24},{18,... | collective-permute-start | bytes 221192 | tf_op jit(solution)/shard_map/ppermute | solution.py:257
  29.7 6.9 %collective-permute-start.12 = (f32[136,128]{1,0:T(8,128)S(1)}, f32[136,128]{1,0:T(8,128)S(1)}, u32[]{:S(2)}, u32[]{:S(2)}) collective-permute-start(f32[136,128]{1,0:T(8,128)S(1)} %pad_maximum_fusion.1), channel_id=1, source_target_pairs={{0,24},{2,18},{4,28},{6,22},{8,16},{10,26},{12,20},{14,30},{16,8},... | collective-permute-start | bytes 208904 | tf_op jit(solution)/shard_map/ppermute | solution.py:260
  31.8 5.5 %collective-permute-start.11 = (f32[136,128]{1,0:T(8,128)S(1)}, f32[136,128]{1,0:T(8,128)S(1)}, u32[]{:S(2)}, u32[]{:S(2)}) collective-permute-start(f32[136,128]{1,0:T(8,128)S(1)} %pad_maximum_fusion.1), channel_id=1, source_target_pairs={{0,12},{2,22},{4,8},{6,18},{8,4},{10,30},{12,0},{14,26},{16,28},{1... | collective-permute-start | bytes 208904 | tf_op jit(solution)/shard_map/ppermute | solution.py:260
  32.0 5.3 %collective-permute-start.10 = (f32[136,128]{1,0:T(8,128)S(1)}, f32[136,128]{1,0:T(8,128)S(1)}, u32[]{:S(2)}, u32[]{:S(2)}) collective-permute-start(f32[136,128]{1,0:T(8,128)S(1)} %pad_maximum_fusion.1), channel_id=1, source_target_pairs={{0,4},{2,30},{4,0},{6,26},{8,12},{10,22},{12,8},{14,18},{16,20},{1... | collective-permute-start | bytes 208904 | tf_op jit(solution)/shard_map/ppermute | solution.py:260
  37.6 2.6 %collective-permute-start.13 = (f32[520,128]{1,0:T(8,128)S(1)}, f32[520,128]{1,0:T(8,128)S(1)}, u32[]{:S(2)}, u32[]{:S(2)}) collective-permute-start(f32[520,128]{1,0:T(8,128)S(1)} %shard_map.64.half), channel_id=1, source_target_pairs={{0,2},{2,0},{4,6},{6,4},{8,10},{10,8},{12,14},{14,12},{16,18},{18,... | collective-permute-start | bytes 798728 | tf_op jit(solution)/shard_map/ppermute | solution.py:254
  41.0 4.0 %collective-permute-start.14 = (f32[72,128]{1,0:T(8,128)S(1)}, f32[72,128]{1,0:T(8,128)S(1)}, u32[]{:S(2)}, u32[]{:S(2)}) collective-permute-start(f32[72,128]{1,0:T(8,128)S(1)} %get-tuple-element.43.refs_4_), channel_id=1, source_target_pairs={{0,1},{1,0},{2,3},{3,2},{4,5},{5,4},{6,7},{7,6},{8,9},{9,8},{10,11... | collective-permute-start | bytes 110600 | tf_op jit(solution)/shard_map/ppermute | solution.py:264
  46.0 1.4 %collective-permute-start.16 = (f32[72,128]{1,0:T(8,128)S(1)}, f32[72,128]{1,0:T(8,128)S(1)}, u32[]{:S(2)}, u32[]{:S(2)}) collective-permute-start(f32[72,128]{1,0:T(8,128)S(1)} %get-tuple-element.45.own), channel_id=1, source_target_pairs={{0,2},{2,0},{4,6},{6,4},{8,10},{10,8},{12,14},{14,12},{16,18},{18,... | collective-permute-start | bytes 110600 | tf_op jit(solution)/shard_map/ppermute | solution.py:254
  46.0 5.1 %collective-permute-start.15 = (f32[144,128]{1,0:T(8,128)S(1)}, f32[144,128]{1,0:T(8,128)S(1)}, u32[]{:S(2)}, u32[]{:S(2)}) collective-permute-start(f32[144,128]{1,0:T(8,128)S(1)} %pad.12), channel_id=1, source_target_pairs={{0,8},{2,10},{4,12},{6,14},{8,0},{10,2},{12,4},{14,6},{16,24},{18,... | collective-permute-start | bytes 221192 | tf_op jit(solution)/shard_map/ppermute | solution.py:257
  47.5 6.2 %collective-permute-start.19 = (f32[136,128]{1,0:T(8,128)S(1)}, f32[136,128]{1,0:T(8,128)S(1)}, u32[]{:S(2)}, u32[]{:S(2)}) collective-permute-start(f32[136,128]{1,0:T(8,128)S(1)} %pad_maximum_fusion.2), channel_id=1, source_target_pairs={{0,24},{2,18},{4,28},{6,22},{8,16},{10,26},{12,20},{14,30},{16,8},... | collective-permute-start | bytes 208904 | tf_op jit(solution)/shard_map/ppermute | solution.py:260
  49.4 5.9 %collective-permute-start.18 = (f32[136,128]{1,0:T(8,128)S(1)}, f32[136,128]{1,0:T(8,128)S(1)}, u32[]{:S(2)}, u32[]{:S(2)}) collective-permute-start(f32[136,128]{1,0:T(8,128)S(1)} %pad_maximum_fusion.2), channel_id=1, source_target_pairs={{0,12},{2,22},{4,8},{6,18},{8,4},{10,30},{12,0},{14,26},{16,28},{1... | collective-permute-start | bytes 208904 | tf_op jit(solution)/shard_map/ppermute | solution.py:260
  50.6 5.0 %collective-permute-start.17 = (f32[136,128]{1,0:T(8,128)S(1)}, f32[136,128]{1,0:T(8,128)S(1)}, u32[]{:S(2)}, u32[]{:S(2)}) collective-permute-start(f32[136,128]{1,0:T(8,128)S(1)} %pad_maximum_fusion.2), channel_id=1, source_target_pairs={{0,4},{2,30},{4,0},{6,26},{8,12},{10,22},{12,8},{14,18},{16,20},{1... | collective-permute-start | bytes 208904 | tf_op jit(solution)/shard_map/ppermute | solution.py:260
  55.9 2.7 %collective-permute-start.20 = (f32[520,128]{1,0:T(8,128)S(1)}, f32[520,128]{1,0:T(8,128)S(1)}, u32[]{:S(2)}, u32[]{:S(2)}) collective-permute-start(f32[520,128]{1,0:T(8,128)S(1)} %shard_map.67.half), channel_id=1, source_target_pairs={{0,2},{2,0},{4,6},{6,4},{8,10},{10,8},{12,14},{14,12},{16,18},{18,... | collective-permute-start | bytes 798728 | tf_op jit(solution)/shard_map/ppermute | solution.py:254
  59.5 4.0 %collective-permute-start.21 = (f32[72,128]{1,0:T(8,128)S(1)}, f32[72,128]{1,0:T(8,128)S(1)}, u32[]{:S(2)}, u32[]{:S(2)}) collective-permute-start(f32[72,128]{1,0:T(8,128)S(1)} %get-tuple-element.49.refs_3_), channel_id=1, source_target_pairs={{0,1},{1,0},{2,3},{3,2},{4,5},{5,4},{6,7},{7,6},{8,9},{9,8},{10,11... | collective-permute-start | bytes 110600 | tf_op jit(solution)/shard_map/ppermute | solution.py:264
  63.8 1.2 %collective-permute-start.23 = (f32[8,128]{1,0:T(8,128)S(1)}, f32[8,128]{1,0:T(8,128)S(1)}, u32[]{:S(2)}, u32[]{:S(2)}) collective-permute-start(f32[8,128]{1,0:T(8,128)S(1)} %get-tuple-element.50), channel_id=1, source_target_pairs={{0,2},{2,0},{4,6},{6,4},{8,10},{10,8},{12,14},{14,12},{16,18},{18,... | collective-permute-start | bytes 12296 | tf_op jit(solution)/shard_map/ppermute | solution.py:254
  63.8 5.6 %collective-permute-start.22 = (f32[8,128]{1,0:T(8,128)S(1)}, f32[8,128]{1,0:T(8,128)S(1)}, u32[]{:S(2)}, u32[]{:S(2)}) collective-permute-start(f32[8,128]{1,0:T(8,128)S(1)} %get-tuple-element.50), channel_id=1, source_target_pairs={{0,4},{2,6},{4,0},{6,2},{8,12},{10,14},{12,8},{14,10},{16,20},{18,... | collective-permute-start | bytes 12296 | tf_op jit(solution)/shard_map/ppermute | solution.py:257
  64.9 5.4 %collective-permute-start.26 = (f32[8,128]{1,0:T(8,128)S(1)}, f32[8,128]{1,0:T(8,128)S(1)}, u32[]{:S(2)}, u32[]{:S(2)}) collective-permute-start(f32[8,128]{1,0:T(8,128)S(1)} %add.39), channel_id=1, source_target_pairs={{0,24},{2,30},{4,28},{6,26},{8,16},{10,22},{12,20},{14,18},{16,8},... | collective-permute-start | bytes 12296 | tf_op jit(solution)/shard_map/ppermute | solution.py:260
  67.0 4.5 %collective-permute-start.25 = (f32[8,128]{1,0:T(8,128)S(1)}, f32[8,128]{1,0:T(8,128)S(1)}, u32[]{:S(2)}, u32[]{:S(2)}) collective-permute-start(f32[8,128]{1,0:T(8,128)S(1)} %add.39), channel_id=1, source_target_pairs={{0,12},{2,22},{4,8},{6,18},{8,4},{10,30},{12,0},{14,26},{16,28},{1... | collective-permute-start | bytes 12296 | tf_op jit(solution)/shard_map/ppermute | solution.py:260
  67.8 3.7 %collective-permute-start.24 = (f32[8,128]{1,0:T(8,128)S(1)}, f32[8,128]{1,0:T(8,128)S(1)}, u32[]{:S(2)}, u32[]{:S(2)}) collective-permute-start(f32[8,128]{1,0:T(8,128)S(1)} %add.39), channel_id=1, source_target_pairs={{0,8},{2,18},{4,12},{6,22},{8,0},{10,26},{12,4},{14,30},{16,24},{1... | collective-permute-start | bytes 12296 | tf_op jit(solution)/shard_map/ppermute | solution.py:260
  71.5 1.2 %collective-permute-start.27 = (f32[8,128]{1,0:T(8,128)S(1)}, f32[8,128]{1,0:T(8,128)S(1)}, u32[]{:S(2)}, u32[]{:S(2)}) collective-permute-start(f32[8,128]{1,0:T(8,128)S(1)} %add_add_fusion.half), channel_id=1, source_target_pairs={{0,2},{2,0},{4,6},{6,4},{8,10},{10,8},{12,14},{14,12},{16,18},{18,... | collective-permute-start | bytes 12296 | tf_op jit(solution)/shard_map/ppermute | solution.py:254

commit v5 on v4

--- a/solution.py
+++ b/solution.py
@@ -106,28 +106,38 @@
     write_end(msg, consts[COL_ROW, :], total(u * u))
 
 
-def gather_sum_kernel(tiles, own, near, *refs):
-    *chips, out = refs
+def sum_messages(cores, chips):
     lane = lax.broadcasted_iota(jnp.int32, (1, BLK), 1)
-    parts = [own[:NB_DEV], near[:NB_DEV]]
-    index = [jnp.where(lane < NB_DEV, own[INDEX : INDEX + 1], near[INDEX : INDEX + 1])]
-    square = own[SQUARE : SQUARE + 1] + near[SQUARE : SQUARE + 1]
     n = 2 * NB_DEV
+    parts, index, square = [], [], jnp.zeros((1, BLK), f32)
+    for a, b in zip(cores[::2], cores[1::2]):
+        parts += [a[:NB_DEV], b[:NB_DEV]]
+        index.append(jnp.where(lane < NB_DEV, a[INDEX : INDEX + 1], b[INDEX : INDEX + 1]))
+        square = square + (a[SQUARE : SQUARE + 1] + b[SQUARE : SQUARE + 1])
     for chip in chips:
         parts.append(chip[:n])
         index.append(chip[n : n + 1])
         square = square + chip[n + 1 : n + 2]
-    out[:COLB_DEV, :] = place_sum(jnp.concatenate(index, axis=1), jnp.concatenate(parts, axis=0), COLB_DEV)
+    return place_sum(jnp.concatenate(index, axis=1), jnp.concatenate(parts, axis=0), COLB_DEV), square
+
+
+def early_kernel(n_cores, *refs):
+    *msgs, out = refs
+    back, square = sum_messages(msgs[:n_cores], msgs[n_cores:])
+    out[:COLB_DEV, :] = back
     out[COLB_DEV:, :] = jnp.broadcast_to(square, (8, BLK))
 
 
-def v_kernel(has_before, tiles, half, other, *refs):
+def v_kernel(has_before, n_msgs, tiles, *refs):
+    msgs, refs = refs[:n_msgs], refs[n_msgs:]
     if has_before:
         v_raw_before, alpha, consts, ats, v_raw, msg, beta_out = refs
     else:
         consts, ats, v_raw, msg, beta_out = refs
-    beta = jnp.sqrt(half[COLB_DEV : COLB_DEV + 1, :] + other[COLB_DEV : COLB_DEV + 1, :])
-    v = (half[:COLB_DEV, :] + other[:COLB_DEV, :]) / beta
+    early, *chips = msgs
+    back, square = sum_messages([], chips)
+    beta = jnp.sqrt(early[COLB_DEV : COLB_DEV + 1, :] + square)
+    v = (early[:COLB_DEV, :] + back) / beta
     if has_before:
         v = v - v_raw_before[...] * (beta / alpha[:1, :])
     v_raw[...] = v
@@ -278,8 +288,13 @@
         a, b = msg[NB_DEV:], peer[NB_DEV:]
         end = jnp.where(end_row == 0, jnp.where(lane < NB_DEV, a, b), a + b)
         both = jnp.concatenate([msg[:NB_DEV], peer[:NB_DEV], end])
-        (half,) = call(gather_sum_kernel, tiles, [msg, beside] + to_chips(both, gather_steps), [(COLB_DEV + 8, BLK)])
-        return half, swap(half)
+        chips = to_chips(both, gather_steps)
+        chips = [(c, swap(c)) for c in chips]
+        late, soon = sum(chips[:1], ()), sum(chips[1:], ())
+        (early,) = call(
+            functools.partial(early_kernel, 4), None, [msg, peer, beside, swap(beside), *soon], [(COLB_DEV + 8, BLK)]
+        )
+        return [early, *late]
 
     u_raw, msg = call(
         functools.partial(first_kernel, n_col),
@@ -289,12 +304,12 @@
     )
     alphas, betas, v_raws = [], [], []
     for step in range(ITERS):
-        half, other = gather(msg)
+        msgs = gather(msg)
         before = [v_raws[-1], alphas[-1]] if step else []
         v_raw, msg, beta = call(
-            functools.partial(v_kernel, step > 0),
+            functools.partial(v_kernel, step > 0, len(msgs)),
             tiles,
-            [half, other] + before + [consts, ats],
+            msgs + before + [consts, ats],
             [(COLB_DEV, BLK), (MSG, BLK), (8, BLK)],
         )
         v_raws.append(v_raw)

time: 73.6 us -> 73 us (level)
  waiting for transfers between devices: 30.1 us -> 22.6 us
  starting transfers between devices: 32.1 us -> 38 us
  Pallas kernels: 10.1 us -> 11 us
    ppermute x12, waiting for transfers between devices: 16.3 us -> 9.84 us  [to_chips(): lax.ppermute(x, 'row', [(r, r ^ 2 * step[r % 2]) for r in range(n_row)])]
    ppermute x8 -> x17, starting transfers between devices: 3.12 us -> 9.33 us  [swap(): return lax.ppermute(x, 'row', [(r, r ^ 1) for r in range(n_row)])]
    ppermute x8 -> x17, waiting for transfers between devices: 5.72 us -> 4.75 us  [swap(): return lax.ppermute(x, 'row', [(r, r ^ 1) for r in range(n_row)])]
    pallas_call x12, Pallas kernels: 7.23 us -> 8.1 us  [call(): pl.pallas_call(body, out_shape=[jax.ShapeDtypeStruct(s, f32) for s in out...]
  transfers between devices with their start and end apart: 28 -> 37, of which waited for: 20 -> 21; matrix products, arithmetic and copies ran while one was open for 0% -> 0% of each run, Pallas kernels for 4% -> 6%
where the time goes in v5:
time: 73 us; the launch traced here: 72.8 us
  starting transfers between devices  38 us (52%)
  waiting for transfers between devices  22.6 us (31%)
  Pallas kernels  11 us (15%)
  between operations  0.83 us (1%)
    ppermute x12, starting transfers between devices, to_chips(): lax.ppermute(x, 'row', [(r, r ^ 2 * step[r % 2]) for r in range(n_row)])  16.7 us
    ppermute x12, waiting for transfers between devices, to_chips(): lax.ppermute(x, 'row', [(r, r ^ 2 * step[r % 2]) for r in range(n_row)])  9.84 us
    ppermute x17, starting transfers between devices, swap(): return lax.ppermute(x, 'row', [(r, r ^ 1) for r in range(n_row)])  9.33 us
    pallas_call x12, Pallas kernels, call(): pl.pallas_call(body, out_shape=[jax.ShapeDtypeStruct(s, f32) for s in out...  8.1 us
    ppermute x4, waiting for transfers between devices, around_col(): lax.ppermute(x, 'col', [(i, (i - s) % n_col) for i in range(n_col)])  8.05 us
    ppermute x4, starting transfers between devices, around_col(): lax.ppermute(x, 'col', [(i, (i - s) % n_col) for i in range(n_col)])  7.61 us
    ppermute x17, waiting for transfers between devices, swap(): return lax.ppermute(x, 'row', [(r, r ^ 1) for r in range(n_row)])  4.75 us
    ppermute x4, starting transfers between devices, to_near(): return lax.ppermute(x, 'row', [(r, r ^ 2 * steps[0]) for r in range(n_row)])  4.37 us
  transfers between devices with their start and end apart: 37, of which 21 were waited for; matrix products, arithmetic and copies ran while one was open for 0% of the time, Pallas kernels for 6%

profile of v5, /device:TPU:0, one launch (start us, length us, event | category | flops | bytes accessed | tf_op | source)
XLA Modules:
  0.0 72.8 jit_solution(11999923449429082844)
XLA Ops:
  0.6 3.0 %collective-permute-start = (f32[248,128]{1,0:T(8,128)}, f32[248,128]{1,0:T(8,128)S(1)}, u32[]{:S(2)}, u32[]{:S(2)}) collective-permute-start(f32[248,128]{1,0:T(8,128)} %bitcast.7), channel_id=1, source_target_pairs={{0,1},{1,0},{2,3},{3,2},{4,5},{5,4},{6,7},{7,6},{8,9},{9,8},{10,11... | collective-permute-start | bytes 380936 | tf_op jit(solution)/shard_map/ppermute | solution.py:274
  3.7 2.9 %shard_map.59 = (bf16[16384,256]{1,0:T(8,128)(2,1)S(1)}, f32[8,128]{1,0:T(8,128)S(1)}, f32[128,128]{1,0:T(8,128)S(1)}, f32[248,128]{1,0:T(8,128)S(1)}) custom-call(f32[8192,128]{1,0:T(8,128)} %bitcast.6, s32[1,64]{1,0:T(1,128)} %bitcast.9, s32[1,64]{1,0:T(1,128)} %bitcast.10, f32[248,128]{1,0:T(8,128)} %bitcast.8, f32[8,128]{1,0:T(8,128)S(1)} %broadcast_in_dim.3.place), custom_call_target="tpu_custom_call" | custom-call | bytes 4194304 | tf_op jit(solution)/shard_map/pallas_call | solution.py:216
  6.6 0.7 collective-permute-done.refs_1_
  7.3 0.8 %shard_map.60 = (f32[512,128]{1,0:T(8,128)S(1)}, f32[72,128]{1,0:T(8,128)S(1)}) custom-call(bf16[16384,256]{1,0:T(8,128)(2,1)S(1)} %get-tuple-element.31.tiles.refs_0_, f32[248,128]{1,0:T(8,128)S(1)} %get-tuple-element.32.refs_0_, f32[248,128]{1,0:T(8,128)S(1)} %collective-permute-done.refs_1_, ...), custom_call_target="tpu_custom_call" | custom-call | tf_op jit(solution)/shard_map/pallas_call | solution.py:240
  8.1 1.9 %collective-permute-start.2 = (f32[144,128]{1,0:T(8,128)S(1)}, f32[144,128]{1,0:T(8,128)S(1)}, u32[]{:S(2)}, u32[]{:S(2)}) collective-permute-start(f32[144,128]{1,0:T(8,128)S(1)} %pad.10), channel_id=1, source_target_pairs={{0,8},{2,10},{4,12},{6,14},{8,0},{10,2},{12,4},{14,6},{16,24},{18,... | collective-permute-start | bytes 221192 | tf_op jit(solution)/shard_map/ppermute | solution.py:267
  10.1 3.2 %collective-permute-start.6 = (f32[136,128]{1,0:T(8,128)S(1)}, f32[136,128]{1,0:T(8,128)S(1)}, u32[]{:S(2)}, u32[]{:S(2)}) collective-permute-start(f32[136,128]{1,0:T(8,128)S(1)} %pad_maximum_fusion), channel_id=1, source_target_pairs={{0,24},{2,18},{4,28},{6,22},{8,16},{10,26},{12,20},{14,30},{16,8},... | collective-permute-start | bytes 208904 | tf_op jit(solution)/shard_map/ppermute | solution.py:270
  13.2 0.9 %collective-permute-start.4 = (f32[136,128]{1,0:T(8,128)S(1)}, f32[136,128]{1,0:T(8,128)S(1)}, u32[]{:S(2)}, u32[]{:S(2)}) collective-permute-start(f32[136,128]{1,0:T(8,128)S(1)} %pad_maximum_fusion), channel_id=1, source_target_pairs={{0,12},{2,22},{4,8},{6,18},{8,4},{10,30},{12,0},{14,26},{16,28},{1... | collective-permute-start | bytes 208904 | tf_op jit(solution)/shard_map/ppermute | solution.py:270
  14.2 0.5 collective-permute-start.8
  14.7 1.7 %collective-permute-start.3 = (f32[144,128]{1,0:T(8,128)S(1)}, f32[144,128]{1,0:T(8,128)S(1)}, u32[]{:S(2)}, u32[]{:S(2)}) collective-permute-start(f32[144,128]{1,0:T(8,128)S(1)} %collective-permute-done.2.refs_2_), channel_id=1, source_target_pairs={{0,2},{2,0},{4,6},{6,4},{8,10},{10,8},{12,14},{14,12},{16,18},{18,... | collective-permute-start | bytes 221192 | tf_op jit(solution)/shard_map/ppermute | solution.py:264
  16.7 2.4 %collective-permute-done.4.refs_4_ = f32[136,128]{1,0:T(8,128)S(1)} collective-permute-done((f32[136,128]{1,0:T(8,128)S(1)}, f32[136,128]{1,0:T(8,128)S(1)}, u32[]{:S(2)}, u32[]{:S(2)}) %collective-permute-start.4) | collective-permute-done | bytes 69664 | tf_op jit(solution)/shard_map/ppermute | solution.py:270
  19.1 0.7 %collective-permute-start.5 = (f32[136,128]{1,0:T(8,128)S(1)}, f32[136,128]{1,0:T(8,128)S(1)}, u32[]{:S(2)}, u32[]{:S(2)}) collective-permute-start(f32[136,128]{1,0:T(8,128)S(1)} %collective-permute-done.4.refs_4_), channel_id=1, source_target_pairs={{0,2},{2,0},{4,6},{6,4},{8,10},{10,8},{12,14},{14,12},{16,18},{18,... | collective-permute-start | bytes 208904 | tf_op jit(solution)/shard_map/ppermute | solution.py:264
  19.9 0.8 %collective-permute-done.8.refs_1_ = f32[136,128]{1,0:T(8,128)S(1)} collective-permute-done((f32[136,128]{1,0:T(8,128)S(1)}, f32[136,128]{1,0:T(8,128)S(1)}, u32[]{:S(2)}, u32[]{:S(2)}) %collective-permute-start.8) | collective-permute-done | bytes 69664 | tf_op jit(solution)/shard_map/ppermute | solution.py:270
  21.1 0.8 %collective-permute-done.9.refs_2_ = f32[136,128]{1,0:T(8,128)S(1)} collective-permute-done((f32[136,128]{1,0:T(8,128)S(1)}, f32[136,128]{1,0:T(8,128)S(1)}, u32[]{:S(2)}, u32[]{:S(2)}) %collective-permute-start.9) | collective-permute-done | bytes 69664 | tf_op jit(solution)/shard_map/ppermute | solution.py:264
  21.9 1.0 %shard_map.62 = (f32[512,128]{1,0:T(8,128)S(1)}, f32[72,128]{1,0:T(8,128)S(1)}, f32[8,128]{1,0:T(8,128)S(1)}) custom-call(bf16[16384,256]{1,0:T(8,128)(2,1)S(1)} %get-tuple-element.31.tiles.refs_0_, f32[520,128]{1,0:T(8,128)S(1)} %shard_map.61.refs_0_, f32[136,128]{1,0:T(8,128)S(1)} %collective-permute-done.8.refs_1_, ...), custom_call_target="tpu_custom_call" | custom-call | tf_op jit(solution)/shard_map/pallas_call | solution.py:240
  23.0 1.5 %collective-permute-start.10 = (f32[72,128]{1,0:T(8,128)S(1)}, f32[72,128]{1,0:T(8,128)S(1)}, u32[]{:S(2)}, u32[]{:S(2)}) collective-permute-start(f32[72,128]{1,0:T(8,128)S(1)} %get-tuple-element.37.refs_4_), channel_id=1, source_target_pairs={{0,1},{1,0},{2,3},{3,2},{4,5},{5,4},{6,7},{7,6},{8,9},{9,8},{10,11... | collective-permute-start | bytes 110600 | tf_op jit(solution)/shard_map/ppermute | solution.py:274
  24.5 2.4 %collective-permute-done.10.refs_5_ = f32[72,128]{1,0:T(8,128)S(1)} collective-permute-done((f32[72,128]{1,0:T(8,128)S(1)}, f32[72,128]{1,0:T(8,128)S(1)}, u32[]{:S(2)}, u32[]{:S(2)}) %collective-permute-start.10) | collective-permute-done | bytes 36896 | tf_op jit(solution)/shard_map/ppermute | solution.py:274
  26.9 1.0 %shard_map.63 = (f32[512,128]{1,0:T(8,128)S(1)}, f32[72,128]{1,0:T(8,128)S(1)}, f32[8,128]{1,0:T(8,128)S(1)}) custom-call(bf16[16384,256]{1,0:T(8,128)(2,1)S(1)} %get-tuple-element.31.tiles.refs_0_, f32[8,128]{1,0:T(8,128)S(1)} %get-tuple-element.30.refs_2_.refs_3_.refs_1_.refs_5_.refs_0_, f32[512,128]{1,0:T(8,128)S(1)} %get-tuple-element.34.refs_2_, ...), custom_call_target="tpu_custom_call" | custom-call | tf_op jit(solution)/shard_map/pallas_call | solution.py:240
  28.0 0.8 %collective-permute-start.12 = (f32[144,128]{1,0:T(8,128)S(1)}, f32[144,128]{1,0:T(8,128)S(1)}, u32[]{:S(2)}, u32[]{:S(2)}) collective-permute-start(f32[144,128]{1,0:T(8,128)S(1)} %pad.11), channel_id=1, source_target_pairs={{0,8},{2,10},{4,12},{6,14},{8,0},{10,2},{12,4},{14,6},{16,24},{18,... | collective-permute-start | bytes 221192 | tf_op jit(solution)/shard_map/ppermute | solution.py:267
  29.3 2.3 %collective-permute-start.16 = (f32[136,128]{1,0:T(8,128)S(1)}, f32[136,128]{1,0:T(8,128)S(1)}, u32[]{:S(2)}, u32[]{:S(2)}) collective-permute-start(f32[136,128]{1,0:T(8,128)S(1)} %pad_maximum_fusion.1), channel_id=1, source_target_pairs={{0,24},{2,18},{4,28},{6,22},{8,16},{10,26},{12,20},{14,30},{16,8},... | collective-permute-start | bytes 208904 | tf_op jit(solution)/shard_map/ppermute | solution.py:270
  31.6 1.5 %collective-permute-start.18 = (f32[136,128]{1,0:T(8,128)S(1)}, f32[136,128]{1,0:T(8,128)S(1)}, u32[]{:S(2)}, u32[]{:S(2)}) collective-permute-start(f32[136,128]{1,0:T(8,128)S(1)} %pad_maximum_fusion.1), channel_id=1, source_target_pairs={{0,4},{2,30},{4,0},{6,26},{8,12},{10,22},{12,8},{14,18},{16,20},{1... | collective-permute-start | bytes 208904 | tf_op jit(solution)/shard_map/ppermute | solution.py:270
  33.0 1.7 %collective-permute-start.13 = (f32[144,128]{1,0:T(8,128)S(1)}, f32[144,128]{1,0:T(8,128)S(1)}, u32[]{:S(2)}, u32[]{:S(2)}) collective-permute-start(f32[144,128]{1,0:T(8,128)S(1)} %collective-permute-done.12.refs_2_), channel_id=1, source_target_pairs={{0,2},{2,0},{4,6},{6,4},{8,10},{10,8},{12,14},{14,12},{16,18},{18,... | collective-permute-start | bytes 221192 | tf_op jit(solution)/shard_map/ppermute | solution.py:264
  34.7 1.3 %collective-permute-done.16.refs_6_ = f32[136,128]{1,0:T(8,128)S(1)} collective-permute-done((f32[136,128]{1,0:T(8,128)S(1)}, f32[136,128]{1,0:T(8,128)S(1)}, u32[]{:S(2)}, u32[]{:S(2)}) %collective-permute-start.16) | collective-permute-done | bytes 69664 | tf_op jit(solution)/shard_map/ppermute | solution.py:270
  36.0 0.6 collective-permute-start.17
  37.0 1.2 %collective-permute-start.15 = (f32[136,128]{1,0:T(8,128)S(1)}, f32[136,128]{1,0:T(8,128)S(1)}, u32[]{:S(2)}, u32[]{:S(2)}) collective-permute-start(f32[136,128]{1,0:T(8,128)S(1)} %collective-permute-done.14.refs_4_), channel_id=1, source_target_pairs={{0,2},{2,0},{4,6},{6,4},{8,10},{10,8},{12,14},{14,12},{16,18},{18,... | collective-permute-start | bytes 208904 | tf_op jit(solution)/shard_map/ppermute | solution.py:264
  38.2 0.9 %collective-permute-done.15.refs_5_ = f32[136,128]{1,0:T(8,128)S(1)} collective-permute-done((f32[136,128]{1,0:T(8,128)S(1)}, f32[136,128]{1,0:T(8,128)S(1)}, u32[]{:S(2)}, u32[]{:S(2)}) %collective-permute-start.15) | collective-permute-done | bytes 69664 | tf_op jit(solution)/shard_map/ppermute | solution.py:264
  39.5 1.0 %shard_map.65 = (f32[512,128]{1,0:T(8,128)S(1)}, f32[72,128]{1,0:T(8,128)S(1)}, f32[8,128]{1,0:T(8,128)S(1)}) custom-call(bf16[16384,256]{1,0:T(8,128)(2,1)S(1)} %get-tuple-element.31.tiles.refs_0_, f32[520,128]{1,0:T(8,128)S(1)} %shard_map.64.refs_0_, f32[136,128]{1,0:T(8,128)S(1)} %collective-permute-done.18.refs_1_, ...), custom_call_target="tpu_custom_call" | custom-call | tf_op jit(solution)/shard_map/pallas_call | solution.py:240
  40.5 1.5 %collective-permute-start.20 = (f32[72,128]{1,0:T(8,128)S(1)}, f32[72,128]{1,0:T(8,128)S(1)}, u32[]{:S(2)}, u32[]{:S(2)}) collective-permute-start(f32[72,128]{1,0:T(8,128)S(1)} %get-tuple-element.43.refs_4_), channel_id=1, source_target_pairs={{0,1},{1,0},{2,3},{3,2},{4,5},{5,4},{6,7},{7,6},{8,9},{9,8},{10,11... | collective-permute-start | bytes 110600 | tf_op jit(solution)/shard_map/ppermute | solution.py:274
  42.0 2.4 %collective-permute-done.20.refs_5_ = f32[72,128]{1,0:T(8,128)S(1)} collective-permute-done((f32[72,128]{1,0:T(8,128)S(1)}, f32[72,128]{1,0:T(8,128)S(1)}, u32[]{:S(2)}, u32[]{:S(2)}) %collective-permute-start.20) | collective-permute-done | bytes 36896 | tf_op jit(solution)/shard_map/ppermute | solution.py:274
  44.5 1.0 %shard_map.66 = (f32[512,128]{1,0:T(8,128)S(1)}, f32[72,128]{1,0:T(8,128)S(1)}, f32[8,128]{1,0:T(8,128)S(1)}) custom-call(bf16[16384,256]{1,0:T(8,128)(2,1)S(1)} %get-tuple-element.31.tiles.refs_0_, f32[8,128]{1,0:T(8,128)S(1)} %get-tuple-element.30.refs_2_.refs_3_.refs_1_.refs_5_.refs_0_, f32[512,128]{1,0:T(8,128)S(1)} %get-tuple-element.38.refs_2_, ...), custom_call_target="tpu_custom_call" | custom-call | tf_op jit(solution)/shard_map/pallas_call | solution.py:240
  45.5 1.0 %collective-permute-start.22 = (f32[144,128]{1,0:T(8,128)S(1)}, f32[144,128]{1,0:T(8,128)S(1)}, u32[]{:S(2)}, u32[]{:S(2)}) collective-permute-start(f32[144,128]{1,0:T(8,128)S(1)} %pad.12), channel_id=1, source_target_pairs={{0,8},{2,10},{4,12},{6,14},{8,0},{10,2},{12,4},{14,6},{16,24},{18,... | collective-permute-start | bytes 221192 | tf_op jit(solution)/shard_map/ppermute | solution.py:267
  46.8 2.1 %collective-permute-start.26 = (f32[136,128]{1,0:T(8,128)S(1)}, f32[136,128]{1,0:T(8,128)S(1)}, u32[]{:S(2)}, u32[]{:S(2)}) collective-permute-start(f32[136,128]{1,0:T(8,128)S(1)} %pad_maximum_fusion.2), channel_id=1, source_target_pairs={{0,24},{2,18},{4,28},{6,22},{8,16},{10,26},{12,20},{14,30},{16,8},... | collective-permute-start | bytes 208904 | tf_op jit(solution)/shard_map/ppermute | solution.py:270
  48.9 0.9 %collective-permute-start.24 = (f32[136,128]{1,0:T(8,128)S(1)}, f32[136,128]{1,0:T(8,128)S(1)}, u32[]{:S(2)}, u32[]{:S(2)}) collective-permute-start(f32[136,128]{1,0:T(8,128)S(1)} %pad_maximum_fusion.2), channel_id=1, source_target_pairs={{0,12},{2,22},{4,8},{6,18},{8,4},{10,30},{12,0},{14,26},{16,28},{1... | collective-permute-start | bytes 208904 | tf_op jit(solution)/shard_map/ppermute | solution.py:270
  49.9 0.6 collective-permute-start.28
  50.4 1.6 %collective-permute-start.23 = (f32[144,128]{1,0:T(8,128)S(1)}, f32[144,128]{1,0:T(8,128)S(1)}, u32[]{:S(2)}, u32[]{:S(2)}) collective-permute-start(f32[144,128]{1,0:T(8,128)S(1)} %collective-permute-done.22.refs_2_), channel_id=1, source_target_pairs={{0,2},{2,0},{4,6},{6,4},{8,10},{10,8},{12,14},{14,12},{16,18},{18,... | collective-permute-start | bytes 221192 | tf_op jit(solution)/shard_map/ppermute | solution.py:264
  52.1 0.9 %collective-permute-done.26.refs_6_ = f32[136,128]{1,0:T(8,128)S(1)} collective-permute-done((f32[136,128]{1,0:T(8,128)S(1)}, f32[136,128]{1,0:T(8,128)S(1)}, u32[]{:S(2)}, u32[]{:S(2)}) %collective-permute-start.26) | collective-permute-done | bytes 69664 | tf_op jit(solution)/shard_map/ppermute | solution.py:270
  53.1 1.6 %collective-permute-done.24.refs_4_ = f32[136,128]{1,0:T(8,128)S(1)} collective-permute-done((f32[136,128]{1,0:T(8,128)S(1)}, f32[136,128]{1,0:T(8,128)S(1)}, u32[]{:S(2)}, u32[]{:S(2)}) %collective-permute-start.24) | collective-permute-done | bytes 69664 | tf_op jit(solution)/shard_map/ppermute | solution.py:270
  54.7 1.6 %collective-permute-start.25 = (f32[136,128]{1,0:T(8,128)S(1)}, f32[136,128]{1,0:T(8,128)S(1)}, u32[]{:S(2)}, u32[]{:S(2)}) collective-permute-start(f32[136,128]{1,0:T(8,128)S(1)} %collective-permute-done.24.refs_4_), channel_id=1, source_target_pairs={{0,2},{2,0},{4,6},{6,4},{8,10},{10,8},{12,14},{14,12},{16,18},{18,... | collective-permute-start | bytes 208904 | tf_op jit(solution)/shard_map/ppermute | solution.py:264
  56.4 0.9 %collective-permute-done.25.refs_5_ = f32[136,128]{1,0:T(8,128)S(1)} collective-permute-done((f32[136,128]{1,0:T(8,128)S(1)}, f32[136,128]{1,0:T(8,128)S(1)}, u32[]{:S(2)}, u32[]{:S(2)}) %collective-permute-start.25) | collective-permute-done | bytes 69664 | tf_op jit(solution)/shard_map/ppermute | solution.py:264
  57.7 1.0 %shard_map.68 = (f32[512,128]{1,0:T(8,128)S(1)}, f32[72,128]{1,0:T(8,128)S(1)}, f32[8,128]{1,0:T(8,128)S(1)}) custom-call(bf16[16384,256]{1,0:T(8,128)(2,1)S(1)} %get-tuple-element.31.tiles.refs_0_, f32[520,128]{1,0:T(8,128)S(1)} %shard_map.67.refs_0_, f32[136,128]{1,0:T(8,128)S(1)} %collective-permute-done.28.refs_1_, ...), custom_call_target="tpu_custom_call" | custom-call | tf_op jit(solution)/shard_map/pallas_call | solution.py:240
  58.7 1.5 %collective-permute-start.30 = (f32[72,128]{1,0:T(8,128)S(1)}, f32[72,128]{1,0:T(8,128)S(1)}, u32[]{:S(2)}, u32[]{:S(2)}) collective-permute-start(f32[72,128]{1,0:T(8,128)S(1)} %get-tuple-element.49.refs_3_), channel_id=1, source_target_pairs={{0,1},{1,0},{2,3},{3,2},{4,5},{5,4},{6,7},{7,6},{8,9},{9,8},{10,11... | collective-permute-start | bytes 110600 | tf_op jit(solution)/shard_map/ppermute | solution.py:274
  60.2 2.5 %collective-permute-done.30.refs_4_ = f32[72,128]{1,0:T(8,128)S(1)} collective-permute-done((f32[72,128]{1,0:T(8,128)S(1)}, f32[72,128]{1,0:T(8,128)S(1)}, u32[]{:S(2)}, u32[]{:S(2)}) %collective-permute-start.30) | collective-permute-done | bytes 36896 | tf_op jit(solution)/shard_map/ppermute | solution.py:274
  63.0 0.7 %collective-permute-start.31 = (f32[8,128]{1,0:T(8,128)S(1)}, f32[8,128]{1,0:T(8,128)S(1)}, u32[]{:S(2)}, u32[]{:S(2)}) collective-permute-start(f32[8,128]{1,0:T(8,128)S(1)} %get-tuple-element.50), channel_id=1, source_target_pairs={{0,4},{2,6},{4,0},{6,2},{8,12},{10,14},{12,8},{14,10},{16,20},{18,... | collective-permute-start | bytes 12296 | tf_op jit(solution)/shard_map/ppermute | solution.py:267
  64.2 2.2 %collective-permute-start.35 = (f32[8,128]{1,0:T(8,128)S(1)}, f32[8,128]{1,0:T(8,128)S(1)}, u32[]{:S(2)}, u32[]{:S(2)}) collective-permute-start(f32[8,128]{1,0:T(8,128)S(1)} %add.39), channel_id=1, source_target_pairs={{0,24},{2,30},{4,28},{6,26},{8,16},{10,22},{12,20},{14,18},{16,8},... | collective-permute-start | bytes 12296 | tf_op jit(solution)/shard_map/ppermute | solution.py:270
  66.8 2.0 %collective-permute-start.33 = (f32[8,128]{1,0:T(8,128)S(1)}, f32[8,128]{1,0:T(8,128)S(1)}, u32[]{:S(2)}, u32[]{:S(2)}) collective-permute-start(f32[8,128]{1,0:T(8,128)S(1)} %add.39), channel_id=1, source_target_pairs={{0,8},{2,18},{4,12},{6,22},{8,0},{10,26},{12,4},{14,30},{16,24},{1... | collective-permute-start | bytes 12296 | tf_op jit(solution)/shard_map/ppermute | solution.py:270
  68.8 0.8 %collective-permute-done.35 = f32[8,128]{1,0:T(8,128)S(1)} collective-permute-done((f32[8,128]{1,0:T(8,128)S(1)}, f32[8,128]{1,0:T(8,128)S(1)}, u32[]{:S(2)}, u32[]{:S(2)}) %collective-permute-start.35) | collective-permute-done | bytes 4128 | tf_op jit(solution)/shard_map/ppermute | solution.py:270
  69.6 1.3 %collective-permute-done.34 = f32[8,128]{1,0:T(8,128)S(1)} collective-permute-done((f32[8,128]{1,0:T(8,128)S(1)}, f32[8,128]{1,0:T(8,128)S(1)}, u32[]{:S(2)}, u32[]{:S(2)}) %collective-permute-start.34) | collective-permute-done | bytes 4128 | tf_op jit(solution)/shard_map/ppermute | solution.py:270
  71.1 1.1 %collective-permute-done.36.other = f32[8,128]{1,0:T(8,128)S(1)} collective-permute-done((f32[8,128]{1,0:T(8,128)S(1)}, f32[8,128]{1,0:T(8,128)S(1)}, u32[]{:S(2)}, u32[]{:S(2)}) %collective-permute-start.36) | collective-permute-done | bytes 4128 | tf_op jit(solution)/shard_map/ppermute | solution.py:264
  72.2 0.6 shard_map.71
  (62 shorter events, 4.3 us)
Async XLA Ops:
  0.6 6.7 %collective-permute-start = (f32[248,128]{1,0:T(8,128)}, f32[248,128]{1,0:T(8,128)S(1)}, u32[]{:S(2)}, u32[]{:S(2)}) collective-permute-start(f32[248,128]{1,0:T(8,128)} %bitcast.7), channel_id=1, source_target_pairs={{0,1},{1,0},{2,3},{3,2},{4,5},{5,4},{6,7},{7,6},{8,9},{9,8},{10,11... | collective-permute-start | bytes 380936 | tf_op jit(solution)/shard_map/ppermute | solution.py:274
  8.1 1.9 %collective-permute-start.1 = (f32[72,128]{1,0:T(8,128)S(1)}, f32[72,128]{1,0:T(8,128)S(1)}, u32[]{:S(2)}, u32[]{:S(2)}) collective-permute-start(f32[72,128]{1,0:T(8,128)S(1)} %get-tuple-element.35.refs_0_), channel_id=1, source_target_pairs={{0,2},{2,0},{4,6},{6,4},{8,10},{10,8},{12,14},{14,12},{16,18},{18,... | collective-permute-start | bytes 110600 | tf_op jit(solution)/shard_map/ppermute | solution.py:264
  8.1 6.6 %collective-permute-start.2 = (f32[144,128]{1,0:T(8,128)S(1)}, f32[144,128]{1,0:T(8,128)S(1)}, u32[]{:S(2)}, u32[]{:S(2)}) collective-permute-start(f32[144,128]{1,0:T(8,128)S(1)} %pad.10), channel_id=1, source_target_pairs={{0,8},{2,10},{4,12},{6,14},{8,0},{10,2},{12,4},{14,6},{16,24},{18,... | collective-permute-start | bytes 221192 | tf_op jit(solution)/shard_map/ppermute | solution.py:267
  10.1 6.6 %collective-permute-start.6 = (f32[136,128]{1,0:T(8,128)S(1)}, f32[136,128]{1,0:T(8,128)S(1)}, u32[]{:S(2)}, u32[]{:S(2)}) collective-permute-start(f32[136,128]{1,0:T(8,128)S(1)} %pad_maximum_fusion), channel_id=1, source_target_pairs={{0,24},{2,18},{4,28},{6,22},{8,16},{10,26},{12,20},{14,30},{16,8},... | collective-permute-start | bytes 208904 | tf_op jit(solution)/shard_map/ppermute | solution.py:270
  13.2 5.9 %collective-permute-start.4 = (f32[136,128]{1,0:T(8,128)S(1)}, f32[136,128]{1,0:T(8,128)S(1)}, u32[]{:S(2)}, u32[]{:S(2)}) collective-permute-start(f32[136,128]{1,0:T(8,128)S(1)} %pad_maximum_fusion), channel_id=1, source_target_pairs={{0,12},{2,22},{4,8},{6,18},{8,4},{10,30},{12,0},{14,26},{16,28},{1... | collective-permute-start | bytes 208904 | tf_op jit(solution)/shard_map/ppermute | solution.py:270
  14.2 6.5 %collective-permute-start.8 = (f32[136,128]{1,0:T(8,128)S(1)}, f32[136,128]{1,0:T(8,128)S(1)}, u32[]{:S(2)}, u32[]{:S(2)}) collective-permute-start(f32[136,128]{1,0:T(8,128)S(1)} %pad_maximum_fusion), channel_id=1, source_target_pairs={{0,4},{2,30},{4,0},{6,26},{8,12},{10,22},{12,8},{14,18},{16,20},{1... | collective-permute-start | bytes 208904 | tf_op jit(solution)/shard_map/ppermute | solution.py:270
  14.7 6.0 %collective-permute-start.3 = (f32[144,128]{1,0:T(8,128)S(1)}, f32[144,128]{1,0:T(8,128)S(1)}, u32[]{:S(2)}, u32[]{:S(2)}) collective-permute-start(f32[144,128]{1,0:T(8,128)S(1)} %collective-permute-done.2.refs_2_), channel_id=1, source_target_pairs={{0,2},{2,0},{4,6},{6,4},{8,10},{10,8},{12,14},{14,12},{16,18},{18,... | collective-permute-start | bytes 221192 | tf_op jit(solution)/shard_map/ppermute | solution.py:264
  16.7 4.0 %collective-permute-start.7 = (f32[136,128]{1,0:T(8,128)S(1)}, f32[136,128]{1,0:T(8,128)S(1)}, u32[]{:S(2)}, u32[]{:S(2)}) collective-permute-start(f32[136,128]{1,0:T(8,128)S(1)} %collective-permute-done.6.refs_6_), channel_id=1, source_target_pairs={{0,2},{2,0},{4,6},{6,4},{8,10},{10,8},{12,14},{14,12},{16,18},{18,... | collective-permute-start | bytes 208904 | tf_op jit(solution)/shard_map/ppermute | solution.py:264
  19.1 1.6 %collective-permute-start.5 = (f32[136,128]{1,0:T(8,128)S(1)}, f32[136,128]{1,0:T(8,128)S(1)}, u32[]{:S(2)}, u32[]{:S(2)}) collective-permute-start(f32[136,128]{1,0:T(8,128)S(1)} %collective-permute-done.4.refs_4_), channel_id=1, source_target_pairs={{0,2},{2,0},{4,6},{6,4},{8,10},{10,8},{12,14},{14,12},{16,18},{18,... | collective-permute-start | bytes 208904 | tf_op jit(solution)/shard_map/ppermute | solution.py:264
  20.7 1.3 %collective-permute-start.9 = (f32[136,128]{1,0:T(8,128)S(1)}, f32[136,128]{1,0:T(8,128)S(1)}, u32[]{:S(2)}, u32[]{:S(2)}) collective-permute-start(f32[136,128]{1,0:T(8,128)S(1)} %collective-permute-done.8.refs_1_), channel_id=1, source_target_pairs={{0,2},{2,0},{4,6},{6,4},{8,10},{10,8},{12,14},{14,12},{16,18},{18,... | collective-permute-start | bytes 208904 | tf_op jit(solution)/shard_map/ppermute | solution.py:264
  23.0 4.0 %collective-permute-start.10 = (f32[72,128]{1,0:T(8,128)S(1)}, f32[72,128]{1,0:T(8,128)S(1)}, u32[]{:S(2)}, u32[]{:S(2)}) collective-permute-start(f32[72,128]{1,0:T(8,128)S(1)} %get-tuple-element.37.refs_4_), channel_id=1, source_target_pairs={{0,1},{1,0},{2,3},{3,2},{4,5},{5,4},{6,7},{7,6},{8,9},{9,8},{10,11... | collective-permute-start | bytes 110600 | tf_op jit(solution)/shard_map/ppermute | solution.py:274
  28.0 1.2 %collective-permute-start.11 = (f32[72,128]{1,0:T(8,128)S(1)}, f32[72,128]{1,0:T(8,128)S(1)}, u32[]{:S(2)}, u32[]{:S(2)}) collective-permute-start(f32[72,128]{1,0:T(8,128)S(1)} %get-tuple-element.39.refs_0_), channel_id=1, source_target_pairs={{0,2},{2,0},{4,6},{6,4},{8,10},{10,8},{12,14},{14,12},{16,18},{18,... | collective-permute-start | bytes 110600 | tf_op jit(solution)/shard_map/ppermute | solution.py:264
  28.0 5.0 %collective-permute-start.12 = (f32[144,128]{1,0:T(8,128)S(1)}, f32[144,128]{1,0:T(8,128)S(1)}, u32[]{:S(2)}, u32[]{:S(2)}) collective-permute-start(f32[144,128]{1,0:T(8,128)S(1)} %pad.11), channel_id=1, source_target_pairs={{0,8},{2,10},{4,12},{6,14},{8,0},{10,2},{12,4},{14,6},{16,24},{18,... | collective-permute-start | bytes 221192 | tf_op jit(solution)/shard_map/ppermute | solution.py:267
  29.3 6.7 %collective-permute-start.16 = (f32[136,128]{1,0:T(8,128)S(1)}, f32[136,128]{1,0:T(8,128)S(1)}, u32[]{:S(2)}, u32[]{:S(2)}) collective-permute-start(f32[136,128]{1,0:T(8,128)S(1)} %pad_maximum_fusion.1), channel_id=1, source_target_pairs={{0,24},{2,18},{4,28},{6,22},{8,16},{10,26},{12,20},{14,30},{16,8},... | collective-permute-start | bytes 208904 | tf_op jit(solution)/shard_map/ppermute | solution.py:270
  31.6 5.4 %collective-permute-start.14 = (f32[136,128]{1,0:T(8,128)S(1)}, f32[136,128]{1,0:T(8,128)S(1)}, u32[]{:S(2)}, u32[]{:S(2)}) collective-permute-start(f32[136,128]{1,0:T(8,128)S(1)} %pad_maximum_fusion.1), channel_id=1, source_target_pairs={{0,12},{2,22},{4,8},{6,18},{8,4},{10,30},{12,0},{14,26},{16,28},{1... | collective-permute-start | bytes 208904 | tf_op jit(solution)/shard_map/ppermute | solution.py:270
  31.6 6.6 %collective-permute-start.18 = (f32[136,128]{1,0:T(8,128)S(1)}, f32[136,128]{1,0:T(8,128)S(1)}, u32[]{:S(2)}, u32[]{:S(2)}) collective-permute-start(f32[136,128]{1,0:T(8,128)S(1)} %pad_maximum_fusion.1), channel_id=1, source_target_pairs={{0,4},{2,30},{4,0},{6,26},{8,12},{10,22},{12,8},{14,18},{16,20},{1... | collective-permute-start | bytes 208904 | tf_op jit(solution)/shard_map/ppermute | solution.py:270
  33.0 5.1 %collective-permute-start.13 = (f32[144,128]{1,0:T(8,128)S(1)}, f32[144,128]{1,0:T(8,128)S(1)}, u32[]{:S(2)}, u32[]{:S(2)}) collective-permute-start(f32[144,128]{1,0:T(8,128)S(1)} %collective-permute-done.12.refs_2_), channel_id=1, source_target_pairs={{0,2},{2,0},{4,6},{6,4},{8,10},{10,8},{12,14},{14,12},{16,18},{18,... | collective-permute-start | bytes 221192 | tf_op jit(solution)/shard_map/ppermute | solution.py:264
  36.0 2.2 %collective-permute-start.17 = (f32[136,128]{1,0:T(8,128)S(1)}, f32[136,128]{1,0:T(8,128)S(1)}, u32[]{:S(2)}, u32[]{:S(2)}) collective-permute-start(f32[136,128]{1,0:T(8,128)S(1)} %collective-permute-done.16.refs_6_), channel_id=1, source_target_pairs={{0,2},{2,0},{4,6},{6,4},{8,10},{10,8},{12,14},{14,12},{16,18},{18,... | collective-permute-start | bytes 208904 | tf_op jit(solution)/shard_map/ppermute | solution.py:264
  37.0 2.1 %collective-permute-start.15 = (f32[136,128]{1,0:T(8,128)S(1)}, f32[136,128]{1,0:T(8,128)S(1)}, u32[]{:S(2)}, u32[]{:S(2)}) collective-permute-start(f32[136,128]{1,0:T(8,128)S(1)} %collective-permute-done.14.refs_4_), channel_id=1, source_target_pairs={{0,2},{2,0},{4,6},{6,4},{8,10},{10,8},{12,14},{14,12},{16,18},{18,... | collective-permute-start | bytes 208904 | tf_op jit(solution)/shard_map/ppermute | solution.py:264
  38.2 1.3 %collective-permute-start.19 = (f32[136,128]{1,0:T(8,128)S(1)}, f32[136,128]{1,0:T(8,128)S(1)}, u32[]{:S(2)}, u32[]{:S(2)}) collective-permute-start(f32[136,128]{1,0:T(8,128)S(1)} %collective-permute-done.18.refs_1_), channel_id=1, source_target_pairs={{0,2},{2,0},{4,6},{6,4},{8,10},{10,8},{12,14},{14,12},{16,18},{18,... | collective-permute-start | bytes 208904 | tf_op jit(solution)/shard_map/ppermute | solution.py:264
  40.5 4.0 %collective-permute-start.20 = (f32[72,128]{1,0:T(8,128)S(1)}, f32[72,128]{1,0:T(8,128)S(1)}, u32[]{:S(2)}, u32[]{:S(2)}) collective-permute-start(f32[72,128]{1,0:T(8,128)S(1)} %get-tuple-element.43.refs_4_), channel_id=1, source_target_pairs={{0,1},{1,0},{2,3},{3,2},{4,5},{5,4},{6,7},{7,6},{8,9},{9,8},{10,11... | collective-permute-start | bytes 110600 | tf_op jit(solution)/shard_map/ppermute | solution.py:274
  45.5 1.2 %collective-permute-start.21 = (f32[72,128]{1,0:T(8,128)S(1)}, f32[72,128]{1,0:T(8,128)S(1)}, u32[]{:S(2)}, u32[]{:S(2)}) collective-permute-start(f32[72,128]{1,0:T(8,128)S(1)} %get-tuple-element.45.refs_0_), channel_id=1, source_target_pairs={{0,2},{2,0},{4,6},{6,4},{8,10},{10,8},{12,14},{14,12},{16,18},{18,... | collective-permute-start | bytes 110600 | tf_op jit(solution)/shard_map/ppermute | solution.py:264
  45.5 4.9 %collective-permute-start.22 = (f32[144,128]{1,0:T(8,128)S(1)}, f32[144,128]{1,0:T(8,128)S(1)}, u32[]{:S(2)}, u32[]{:S(2)}) collective-permute-start(f32[144,128]{1,0:T(8,128)S(1)} %pad.12), channel_id=1, source_target_pairs={{0,8},{2,10},{4,12},{6,14},{8,0},{10,2},{12,4},{14,6},{16,24},{18,... | collective-permute-start | bytes 221192 | tf_op jit(solution)/shard_map/ppermute | solution.py:267
  46.8 6.2 %collective-permute-start.26 = (f32[136,128]{1,0:T(8,128)S(1)}, f32[136,128]{1,0:T(8,128)S(1)}, u32[]{:S(2)}, u32[]{:S(2)}) collective-permute-start(f32[136,128]{1,0:T(8,128)S(1)} %pad_maximum_fusion.2), channel_id=1, source_target_pairs={{0,24},{2,18},{4,28},{6,22},{8,16},{10,26},{12,20},{14,30},{16,8},... | collective-permute-start | bytes 208904 | tf_op jit(solution)/shard_map/ppermute | solution.py:270
  48.9 5.8 %collective-permute-start.24 = (f32[136,128]{1,0:T(8,128)S(1)}, f32[136,128]{1,0:T(8,128)S(1)}, u32[]{:S(2)}, u32[]{:S(2)}) collective-permute-start(f32[136,128]{1,0:T(8,128)S(1)} %pad_maximum_fusion.2), channel_id=1, source_target_pairs={{0,12},{2,22},{4,8},{6,18},{8,4},{10,30},{12,0},{14,26},{16,28},{1... | collective-permute-start | bytes 208904 | tf_op jit(solution)/shard_map/ppermute | solution.py:270
  49.9 6.5 %collective-permute-start.28 = (f32[136,128]{1,0:T(8,128)S(1)}, f32[136,128]{1,0:T(8,128)S(1)}, u32[]{:S(2)}, u32[]{:S(2)}) collective-permute-start(f32[136,128]{1,0:T(8,128)S(1)} %pad_maximum_fusion.2), channel_id=1, source_target_pairs={{0,4},{2,30},{4,0},{6,26},{8,12},{10,22},{12,8},{14,18},{16,20},{1... | collective-permute-start | bytes 208904 | tf_op jit(solution)/shard_map/ppermute | solution.py:270
  50.4 5.9 %collective-permute-start.23 = (f32[144,128]{1,0:T(8,128)S(1)}, f32[144,128]{1,0:T(8,128)S(1)}, u32[]{:S(2)}, u32[]{:S(2)}) collective-permute-start(f32[144,128]{1,0:T(8,128)S(1)} %collective-permute-done.22.refs_2_), channel_id=1, source_target_pairs={{0,2},{2,0},{4,6},{6,4},{8,10},{10,8},{12,14},{14,12},{16,18},{18,... | collective-permute-start | bytes 221192 | tf_op jit(solution)/shard_map/ppermute | solution.py:264
  53.0 3.4 %collective-permute-start.27 = (f32[136,128]{1,0:T(8,128)S(1)}, f32[136,128]{1,0:T(8,128)S(1)}, u32[]{:S(2)}, u32[]{:S(2)}) collective-permute-start(f32[136,128]{1,0:T(8,128)S(1)} %collective-permute-done.26.refs_6_), channel_id=1, source_target_pairs={{0,2},{2,0},{4,6},{6,4},{8,10},{10,8},{12,14},{14,12},{16,18},{18,... | collective-permute-start | bytes 208904 | tf_op jit(solution)/shard_map/ppermute | solution.py:264
  54.7 2.5 %collective-permute-start.25 = (f32[136,128]{1,0:T(8,128)S(1)}, f32[136,128]{1,0:T(8,128)S(1)}, u32[]{:S(2)}, u32[]{:S(2)}) collective-permute-start(f32[136,128]{1,0:T(8,128)S(1)} %collective-permute-done.24.refs_4_), channel_id=1, source_target_pairs={{0,2},{2,0},{4,6},{6,4},{8,10},{10,8},{12,14},{14,12},{16,18},{18,... | collective-permute-start | bytes 208904 | tf_op jit(solution)/shard_map/ppermute | solution.py:264
  56.4 1.3 %collective-permute-start.29 = (f32[136,128]{1,0:T(8,128)S(1)}, f32[136,128]{1,0:T(8,128)S(1)}, u32[]{:S(2)}, u32[]{:S(2)}) collective-permute-start(f32[136,128]{1,0:T(8,128)S(1)} %collective-permute-done.28.refs_1_), channel_id=1, source_target_pairs={{0,2},{2,0},{4,6},{6,4},{8,10},{10,8},{12,14},{14,12},{16,18},{18,... | collective-permute-start | bytes 208904 | tf_op jit(solution)/shard_map/ppermute | solution.py:264
  58.7 4.0 %collective-permute-start.30 = (f32[72,128]{1,0:T(8,128)S(1)}, f32[72,128]{1,0:T(8,128)S(1)}, u32[]{:S(2)}, u32[]{:S(2)}) collective-permute-start(f32[72,128]{1,0:T(8,128)S(1)} %get-tuple-element.49.refs_3_), channel_id=1, source_target_pairs={{0,1},{1,0},{2,3},{3,2},{4,5},{5,4},{6,7},{7,6},{8,9},{9,8},{10,11... | collective-permute-start | bytes 110600 | tf_op jit(solution)/shard_map/ppermute | solution.py:274
  63.0 1.2 %collective-permute-start.32 = (f32[8,128]{1,0:T(8,128)S(1)}, f32[8,128]{1,0:T(8,128)S(1)}, u32[]{:S(2)}, u32[]{:S(2)}) collective-permute-start(f32[8,128]{1,0:T(8,128)S(1)} %get-tuple-element.50), channel_id=1, source_target_pairs={{0,2},{2,0},{4,6},{6,4},{8,10},{10,8},{12,14},{14,12},{16,18},{18,... | collective-permute-start | bytes 12296 | tf_op jit(solution)/shard_map/ppermute | solution.py:264
  63.0 5.8 %collective-permute-start.31 = (f32[8,128]{1,0:T(8,128)S(1)}, f32[8,128]{1,0:T(8,128)S(1)}, u32[]{:S(2)}, u32[]{:S(2)}) collective-permute-start(f32[8,128]{1,0:T(8,128)S(1)} %get-tuple-element.50), channel_id=1, source_target_pairs={{0,4},{2,6},{4,0},{6,2},{8,12},{10,14},{12,8},{14,10},{16,20},{18,... | collective-permute-start | bytes 12296 | tf_op jit(solution)/shard_map/ppermute | solution.py:267
  64.2 5.4 %collective-permute-start.35 = (f32[8,128]{1,0:T(8,128)S(1)}, f32[8,128]{1,0:T(8,128)S(1)}, u32[]{:S(2)}, u32[]{:S(2)}) collective-permute-start(f32[8,128]{1,0:T(8,128)S(1)} %add.39), channel_id=1, source_target_pairs={{0,24},{2,30},{4,28},{6,26},{8,16},{10,22},{12,20},{14,18},{16,8},... | collective-permute-start | bytes 12296 | tf_op jit(solution)/shard_map/ppermute | solution.py:270
  66.4 4.5 %collective-permute-start.34 = (f32[8,128]{1,0:T(8,128)S(1)}, f32[8,128]{1,0:T(8,128)S(1)}, u32[]{:S(2)}, u32[]{:S(2)}) collective-permute-start(f32[8,128]{1,0:T(8,128)S(1)} %add.39), channel_id=1, source_target_pairs={{0,12},{2,22},{4,8},{6,18},{8,4},{10,30},{12,0},{14,26},{16,28},{1... | collective-permute-start | bytes 12296 | tf_op jit(solution)/shard_map/ppermute | solution.py:270
  66.8 4.1 %collective-permute-start.33 = (f32[8,128]{1,0:T(8,128)S(1)}, f32[8,128]{1,0:T(8,128)S(1)}, u32[]{:S(2)}, u32[]{:S(2)}) collective-permute-start(f32[8,128]{1,0:T(8,128)S(1)} %add.39), channel_id=1, source_target_pairs={{0,8},{2,18},{4,12},{6,22},{8,0},{10,26},{12,4},{14,30},{16,24},{1... | collective-permute-start | bytes 12296 | tf_op jit(solution)/shard_map/ppermute | solution.py:270
  70.9 1.2 %collective-permute-start.36 = (f32[8,128]{1,0:T(8,128)S(1)}, f32[8,128]{1,0:T(8,128)S(1)}, u32[]{:S(2)}, u32[]{:S(2)}) collective-permute-start(f32[8,128]{1,0:T(8,128)S(1)} %add_add_fusion.half), channel_id=1, source_target_pairs={{0,2},{2,0},{4,6},{6,4},{8,10},{10,8},{12,14},{14,12},{16,18},{18,... | collective-permute-start | bytes 12296 | tf_op jit(solution)/shard_map/ppermute | solution.py:264

commit v6 on v5

--- a/solution.py
+++ b/solution.py
@@ -248,7 +248,7 @@
 
 def chip_steps(chips):
     if chips == 8:
-        return (2, [(1, 7), (3, 5), (6, 4)]), (1, [(2, 4), (3, 5), (6, 7)])
+        return (2, [(3, 4), (1, 5), (6, 7)]), (1, [(2, 4), (3, 5), (6, 7)])
     steps = 1, [(m, m + 1) for m in range(2, chips, 2)]
     return steps, steps
 

time: 73 us -> 72.6 us (level)
  waiting for transfers between devices: 22.6 us -> 19.8 us
  starting transfers between devices: 38 us -> 40.5 us
    ppermute x12, waiting for transfers between devices: 9.84 us -> 6.33 us  [to_chips(): lax.ppermute(x, 'row', [(r, r ^ 2 * step[r % 2]) for r in range(n_row)])]
    ppermute x17, starting transfers between devices: 9.33 us -> 12.2 us  [swap(): return lax.ppermute(x, 'row', [(r, r ^ 1) for r in range(n_row)])]
    ppermute x4, starting transfers between devices: 4.37 us -> 3.08 us  [to_near(): return lax.ppermute(x, 'row', [(r, r ^ 2 * steps[0]) for r in range(n_row)])]
    ppermute x12, starting transfers between devices: 16.7 us -> 17.5 us  [to_chips(): lax.ppermute(x, 'row', [(r, r ^ 2 * step[r % 2]) for r in range(n_row)])]
  transfers between devices with their start and end apart: 37 -> 37, of which waited for: 21 -> 19; matrix products, arithmetic and copies ran while one was open for 0% -> 0% of each run, Pallas kernels for 6% -> 6%
where the time goes in v6:
time: 72.6 us; the launch traced here: 72.4 us
  starting transfers between devices  40.5 us (56%)
  waiting for transfers between devices  19.8 us (27%)
  Pallas kernels  11 us (15%)
  between operations  0.81 us (1%)
    ppermute x12, starting transfers between devices, to_chips(): lax.ppermute(x, 'row', [(r, r ^ 2 * step[r % 2]) for r in range(n_row)])  17.5 us
    ppermute x17, starting transfers between devices, swap(): return lax.ppermute(x, 'row', [(r, r ^ 1) for r in range(n_row)])  12.2 us
    pallas_call x12, Pallas kernels, call(): pl.pallas_call(body, out_shape=[jax.ShapeDtypeStruct(s, f32) for s in out...  8.09 us
    ppermute x4, waiting for transfers between devices, around_col(): lax.ppermute(x, 'col', [(i, (i - s) % n_col) for i in range(n_col)])  8.02 us
    ppermute x4, starting transfers between devices, around_col(): lax.ppermute(x, 'col', [(i, (i - s) % n_col) for i in range(n_col)])  7.63 us
    ppermute x12, waiting for transfers between devices, to_chips(): lax.ppermute(x, 'row', [(r, r ^ 2 * step[r % 2]) for r in range(n_row)])  6.33 us
    ppermute x17, waiting for transfers between devices, swap(): return lax.ppermute(x, 'row', [(r, r ^ 1) for r in range(n_row)])  5.46 us
    ppermute x4, starting transfers between devices, to_near(): return lax.ppermute(x, 'row', [(r, r ^ 2 * steps[0]) for r in range(n_row)])  3.08 us
  transfers between devices with their start and end apart: 37, of which 19 were waited for; matrix products, arithmetic and copies ran while one was open for 0% of the time, Pallas kernels for 6%

profile of v6, /device:TPU:0, one launch (start us, length us, event | category | flops | bytes accessed | tf_op | source)
XLA Modules:
  0.0 72.4 jit_solution(18386749904020482891)
XLA Ops:
  0.6 3.0 %collective-permute-start = (f32[248,128]{1,0:T(8,128)}, f32[248,128]{1,0:T(8,128)S(1)}, u32[]{:S(2)}, u32[]{:S(2)}) collective-permute-start(f32[248,128]{1,0:T(8,128)} %bitcast.7), channel_id=1, source_target_pairs={{0,1},{1,0},{2,3},{3,2},{4,5},{5,4},{6,7},{7,6},{8,9},{9,8},{10,11... | collective-permute-start | bytes 380936 | tf_op jit(solution)/shard_map/ppermute | solution.py:274
  3.7 2.9 %shard_map.59 = (bf16[16384,256]{1,0:T(8,128)(2,1)S(1)}, f32[8,128]{1,0:T(8,128)S(1)}, f32[128,128]{1,0:T(8,128)S(1)}, f32[248,128]{1,0:T(8,128)S(1)}) custom-call(f32[8192,128]{1,0:T(8,128)} %bitcast.6, s32[1,64]{1,0:T(1,128)} %bitcast.9, s32[1,64]{1,0:T(1,128)} %bitcast.10, f32[248,128]{1,0:T(8,128)} %bitcast.8, f32[8,128]{1,0:T(8,128)S(1)} %broadcast_in_dim.3.place), custom_call_target="tpu_custom_call" | custom-call | bytes 4194304 | tf_op jit(solution)/shard_map/pallas_call | solution.py:216
  6.6 0.7 collective-permute-done.refs_1_
  7.3 0.8 %shard_map.60 = (f32[512,128]{1,0:T(8,128)S(1)}, f32[72,128]{1,0:T(8,128)S(1)}) custom-call(bf16[16384,256]{1,0:T(8,128)(2,1)S(1)} %get-tuple-element.31.tiles.refs_0_, f32[248,128]{1,0:T(8,128)S(1)} %get-tuple-element.32.refs_0_, f32[248,128]{1,0:T(8,128)S(1)} %collective-permute-done.refs_1_, ...), custom_call_target="tpu_custom_call" | custom-call | tf_op jit(solution)/shard_map/pallas_call | solution.py:240
  8.1 1.9 %collective-permute-start.2 = (f32[144,128]{1,0:T(8,128)S(1)}, f32[144,128]{1,0:T(8,128)S(1)}, u32[]{:S(2)}, u32[]{:S(2)}) collective-permute-start(f32[144,128]{1,0:T(8,128)S(1)} %pad.10), channel_id=1, source_target_pairs={{0,8},{2,10},{4,12},{6,14},{8,0},{10,2},{12,4},{14,6},{16,24},{18,... | collective-permute-start | bytes 221192 | tf_op jit(solution)/shard_map/ppermute | solution.py:267
  10.1 3.2 %collective-permute-start.6 = (f32[136,128]{1,0:T(8,128)S(1)}, f32[136,128]{1,0:T(8,128)S(1)}, u32[]{:S(2)}, u32[]{:S(2)}) collective-permute-start(f32[136,128]{1,0:T(8,128)S(1)} %pad_maximum_fusion), channel_id=1, source_target_pairs={{0,24},{2,30},{4,28},{6,26},{8,16},{10,22},{12,20},{14,18},{16,8},... | collective-permute-start | bytes 208904 | tf_op jit(solution)/shard_map/ppermute | solution.py:270
  13.2 1.5 %collective-permute-start.4 = (f32[136,128]{1,0:T(8,128)S(1)}, f32[136,128]{1,0:T(8,128)S(1)}, u32[]{:S(2)}, u32[]{:S(2)}) collective-permute-start(f32[136,128]{1,0:T(8,128)S(1)} %pad_maximum_fusion), channel_id=1, source_target_pairs={{0,4},{2,22},{4,0},{6,18},{8,12},{10,30},{12,8},{14,26},{16,20},{1... | collective-permute-start | bytes 208904 | tf_op jit(solution)/shard_map/ppermute | solution.py:270
  14.7 1.7 %collective-permute-start.3 = (f32[144,128]{1,0:T(8,128)S(1)}, f32[144,128]{1,0:T(8,128)S(1)}, u32[]{:S(2)}, u32[]{:S(2)}) collective-permute-start(f32[144,128]{1,0:T(8,128)S(1)} %collective-permute-done.2.refs_2_), channel_id=1, source_target_pairs={{0,2},{2,0},{4,6},{6,4},{8,10},{10,8},{12,14},{14,12},{16,18},{18,... | collective-permute-start | bytes 221192 | tf_op jit(solution)/shard_map/ppermute | solution.py:264
  16.4 0.5 collective-permute-done.6.refs_6_
  17.0 0.7 collective-permute-done.4.refs_4_
  17.7 2.4 %collective-permute-start.5 = (f32[136,128]{1,0:T(8,128)S(1)}, f32[136,128]{1,0:T(8,128)S(1)}, u32[]{:S(2)}, u32[]{:S(2)}) collective-permute-start(f32[136,128]{1,0:T(8,128)S(1)} %collective-permute-done.4.refs_4_), channel_id=1, source_target_pairs={{0,2},{2,0},{4,6},{6,4},{8,10},{10,8},{12,14},{14,12},{16,18},{18,... | collective-permute-start | bytes 208904 | tf_op jit(solution)/shard_map/ppermute | solution.py:264
  20.3 0.8 %collective-permute-done.5.refs_5_ = f32[136,128]{1,0:T(8,128)S(1)} collective-permute-done((f32[136,128]{1,0:T(8,128)S(1)}, f32[136,128]{1,0:T(8,128)S(1)}, u32[]{:S(2)}, u32[]{:S(2)}) %collective-permute-start.5) | collective-permute-done | bytes 69664 | tf_op jit(solution)/shard_map/ppermute | solution.py:264
  21.0 0.4 shard_map.61.refs_0_
  21.4 1.0 %shard_map.62 = (f32[512,128]{1,0:T(8,128)S(1)}, f32[72,128]{1,0:T(8,128)S(1)}, f32[8,128]{1,0:T(8,128)S(1)}) custom-call(bf16[16384,256]{1,0:T(8,128)(2,1)S(1)} %get-tuple-element.31.tiles.refs_0_, f32[520,128]{1,0:T(8,128)S(1)} %shard_map.61.refs_0_, f32[136,128]{1,0:T(8,128)S(1)} %collective-permute-done.8.refs_1_, ...), custom_call_target="tpu_custom_call" | custom-call | tf_op jit(solution)/shard_map/pallas_call | solution.py:240
  22.5 1.5 %collective-permute-start.10 = (f32[72,128]{1,0:T(8,128)S(1)}, f32[72,128]{1,0:T(8,128)S(1)}, u32[]{:S(2)}, u32[]{:S(2)}) collective-permute-start(f32[72,128]{1,0:T(8,128)S(1)} %get-tuple-element.37.refs_4_), channel_id=1, source_target_pairs={{0,1},{1,0},{2,3},{3,2},{4,5},{5,4},{6,7},{7,6},{8,9},{9,8},{10,11... | collective-permute-start | bytes 110600 | tf_op jit(solution)/shard_map/ppermute | solution.py:274
  24.0 2.4 %collective-permute-done.10.refs_5_ = f32[72,128]{1,0:T(8,128)S(1)} collective-permute-done((f32[72,128]{1,0:T(8,128)S(1)}, f32[72,128]{1,0:T(8,128)S(1)}, u32[]{:S(2)}, u32[]{:S(2)}) %collective-permute-start.10) | collective-permute-done | bytes 36896 | tf_op jit(solution)/shard_map/ppermute | solution.py:274
  26.4 1.0 %shard_map.63 = (f32[512,128]{1,0:T(8,128)S(1)}, f32[72,128]{1,0:T(8,128)S(1)}, f32[8,128]{1,0:T(8,128)S(1)}) custom-call(bf16[16384,256]{1,0:T(8,128)(2,1)S(1)} %get-tuple-element.31.tiles.refs_0_, f32[8,128]{1,0:T(8,128)S(1)} %get-tuple-element.30.refs_2_.refs_3_.refs_1_.refs_5_.refs_0_, f32[512,128]{1,0:T(8,128)S(1)} %get-tuple-element.34.refs_2_, ...), custom_call_target="tpu_custom_call" | custom-call | tf_op jit(solution)/shard_map/pallas_call | solution.py:240
  27.6 1.1 %collective-permute-done.11.refs_1_ = f32[72,128]{1,0:T(8,128)S(1)} collective-permute-done((f32[72,128]{1,0:T(8,128)S(1)}, f32[72,128]{1,0:T(8,128)S(1)}, u32[]{:S(2)}, u32[]{:S(2)}) %collective-permute-start.11) | collective-permute-done | bytes 36896 | tf_op jit(solution)/shard_map/ppermute | solution.py:264
  28.8 2.5 %collective-permute-start.16 = (f32[136,128]{1,0:T(8,128)S(1)}, f32[136,128]{1,0:T(8,128)S(1)}, u32[]{:S(2)}, u32[]{:S(2)}) collective-permute-start(f32[136,128]{1,0:T(8,128)S(1)} %pad_maximum_fusion.1), channel_id=1, source_target_pairs={{0,24},{2,30},{4,28},{6,26},{8,16},{10,22},{12,20},{14,18},{16,8},... | collective-permute-start | bytes 208904 | tf_op jit(solution)/shard_map/ppermute | solution.py:270
  31.2 1.1 %collective-permute-start.14 = (f32[136,128]{1,0:T(8,128)S(1)}, f32[136,128]{1,0:T(8,128)S(1)}, u32[]{:S(2)}, u32[]{:S(2)}) collective-permute-start(f32[136,128]{1,0:T(8,128)S(1)} %pad_maximum_fusion.1), channel_id=1, source_target_pairs={{0,4},{2,22},{4,0},{6,18},{8,12},{10,30},{12,8},{14,26},{16,20},{1... | collective-permute-start | bytes 208904 | tf_op jit(solution)/shard_map/ppermute | solution.py:270
  32.4 0.4 collective-permute-start.18
  32.7 1.7 %collective-permute-start.13 = (f32[144,128]{1,0:T(8,128)S(1)}, f32[144,128]{1,0:T(8,128)S(1)}, u32[]{:S(2)}, u32[]{:S(2)}) collective-permute-start(f32[144,128]{1,0:T(8,128)S(1)} %collective-permute-done.12.refs_2_), channel_id=1, source_target_pairs={{0,2},{2,0},{4,6},{6,4},{8,10},{10,8},{12,14},{14,12},{16,18},{18,... | collective-permute-start | bytes 221192 | tf_op jit(solution)/shard_map/ppermute | solution.py:264
  34.4 1.2 %collective-permute-done.16.refs_6_ = f32[136,128]{1,0:T(8,128)S(1)} collective-permute-done((f32[136,128]{1,0:T(8,128)S(1)}, f32[136,128]{1,0:T(8,128)S(1)}, u32[]{:S(2)}, u32[]{:S(2)}) %collective-permute-start.16) | collective-permute-done | bytes 69664 | tf_op jit(solution)/shard_map/ppermute | solution.py:270
  36.0 2.0 %collective-permute-start.15 = (f32[136,128]{1,0:T(8,128)S(1)}, f32[136,128]{1,0:T(8,128)S(1)}, u32[]{:S(2)}, u32[]{:S(2)}) collective-permute-start(f32[136,128]{1,0:T(8,128)S(1)} %collective-permute-done.14.refs_4_), channel_id=1, source_target_pairs={{0,2},{2,0},{4,6},{6,4},{8,10},{10,8},{12,14},{14,12},{16,18},{18,... | collective-permute-start | bytes 208904 | tf_op jit(solution)/shard_map/ppermute | solution.py:264
  38.1 0.7 collective-permute-done.15.refs_5_
  38.8 0.4 shard_map.64.refs_0_
  39.2 1.0 %shard_map.65 = (f32[512,128]{1,0:T(8,128)S(1)}, f32[72,128]{1,0:T(8,128)S(1)}, f32[8,128]{1,0:T(8,128)S(1)}) custom-call(bf16[16384,256]{1,0:T(8,128)(2,1)S(1)} %get-tuple-element.31.tiles.refs_0_, f32[520,128]{1,0:T(8,128)S(1)} %shard_map.64.refs_0_, f32[136,128]{1,0:T(8,128)S(1)} %collective-permute-done.18.refs_1_, ...), custom_call_target="tpu_custom_call" | custom-call | tf_op jit(solution)/shard_map/pallas_call | solution.py:240
  40.3 1.5 %collective-permute-start.20 = (f32[72,128]{1,0:T(8,128)S(1)}, f32[72,128]{1,0:T(8,128)S(1)}, u32[]{:S(2)}, u32[]{:S(2)}) collective-permute-start(f32[72,128]{1,0:T(8,128)S(1)} %get-tuple-element.43.refs_4_), channel_id=1, source_target_pairs={{0,1},{1,0},{2,3},{3,2},{4,5},{5,4},{6,7},{7,6},{8,9},{9,8},{10,11... | collective-permute-start | bytes 110600 | tf_op jit(solution)/shard_map/ppermute | solution.py:274
  41.8 2.4 %collective-permute-done.20.refs_5_ = f32[72,128]{1,0:T(8,128)S(1)} collective-permute-done((f32[72,128]{1,0:T(8,128)S(1)}, f32[72,128]{1,0:T(8,128)S(1)}, u32[]{:S(2)}, u32[]{:S(2)}) %collective-permute-start.20) | collective-permute-done | bytes 36896 | tf_op jit(solution)/shard_map/ppermute | solution.py:274
  44.2 1.0 %shard_map.66 = (f32[512,128]{1,0:T(8,128)S(1)}, f32[72,128]{1,0:T(8,128)S(1)}, f32[8,128]{1,0:T(8,128)S(1)}) custom-call(bf16[16384,256]{1,0:T(8,128)(2,1)S(1)} %get-tuple-element.31.tiles.refs_0_, f32[8,128]{1,0:T(8,128)S(1)} %get-tuple-element.30.refs_2_.refs_3_.refs_1_.refs_5_.refs_0_, f32[512,128]{1,0:T(8,128)S(1)} %get-tuple-element.38.refs_2_, ...), custom_call_target="tpu_custom_call" | custom-call | tf_op jit(solution)/shard_map/pallas_call | solution.py:240
  45.4 1.1 %collective-permute-done.21.refs_1_ = f32[72,128]{1,0:T(8,128)S(1)} collective-permute-done((f32[72,128]{1,0:T(8,128)S(1)}, f32[72,128]{1,0:T(8,128)S(1)}, u32[]{:S(2)}, u32[]{:S(2)}) %collective-permute-start.21) | collective-permute-done | bytes 36896 | tf_op jit(solution)/shard_map/ppermute | solution.py:264
  46.6 2.5 %collective-permute-start.26 = (f32[136,128]{1,0:T(8,128)S(1)}, f32[136,128]{1,0:T(8,128)S(1)}, u32[]{:S(2)}, u32[]{:S(2)}) collective-permute-start(f32[136,128]{1,0:T(8,128)S(1)} %pad_maximum_fusion.2), channel_id=1, source_target_pairs={{0,24},{2,30},{4,28},{6,26},{8,16},{10,22},{12,20},{14,18},{16,8},... | collective-permute-start | bytes 208904 | tf_op jit(solution)/shard_map/ppermute | solution.py:270
  49.0 1.1 %collective-permute-start.24 = (f32[136,128]{1,0:T(8,128)S(1)}, f32[136,128]{1,0:T(8,128)S(1)}, u32[]{:S(2)}, u32[]{:S(2)}) collective-permute-start(f32[136,128]{1,0:T(8,128)S(1)} %pad_maximum_fusion.2), channel_id=1, source_target_pairs={{0,4},{2,22},{4,0},{6,18},{8,12},{10,30},{12,8},{14,26},{16,20},{1... | collective-permute-start | bytes 208904 | tf_op jit(solution)/shard_map/ppermute | solution.py:270
  50.5 1.7 %collective-permute-start.23 = (f32[144,128]{1,0:T(8,128)S(1)}, f32[144,128]{1,0:T(8,128)S(1)}, u32[]{:S(2)}, u32[]{:S(2)}) collective-permute-start(f32[144,128]{1,0:T(8,128)S(1)} %collective-permute-done.22.refs_2_), channel_id=1, source_target_pairs={{0,2},{2,0},{4,6},{6,4},{8,10},{10,8},{12,14},{14,12},{16,18},{18,... | collective-permute-start | bytes 221192 | tf_op jit(solution)/shard_map/ppermute | solution.py:264
  52.2 1.2 %collective-permute-done.26.refs_6_ = f32[136,128]{1,0:T(8,128)S(1)} collective-permute-done((f32[136,128]{1,0:T(8,128)S(1)}, f32[136,128]{1,0:T(8,128)S(1)}, u32[]{:S(2)}, u32[]{:S(2)}) %collective-permute-start.26) | collective-permute-done | bytes 69664 | tf_op jit(solution)/shard_map/ppermute | solution.py:270
  53.8 2.0 %collective-permute-start.25 = (f32[136,128]{1,0:T(8,128)S(1)}, f32[136,128]{1,0:T(8,128)S(1)}, u32[]{:S(2)}, u32[]{:S(2)}) collective-permute-start(f32[136,128]{1,0:T(8,128)S(1)} %collective-permute-done.24.refs_4_), channel_id=1, source_target_pairs={{0,2},{2,0},{4,6},{6,4},{8,10},{10,8},{12,14},{14,12},{16,18},{18,... | collective-permute-start | bytes 208904 | tf_op jit(solution)/shard_map/ppermute | solution.py:264
  55.9 0.7 collective-permute-done.25.refs_5_
  56.6 0.4 shard_map.67.refs_0_
  57.0 1.0 %shard_map.68 = (f32[512,128]{1,0:T(8,128)S(1)}, f32[72,128]{1,0:T(8,128)S(1)}, f32[8,128]{1,0:T(8,128)S(1)}) custom-call(bf16[16384,256]{1,0:T(8,128)(2,1)S(1)} %get-tuple-element.31.tiles.refs_0_, f32[520,128]{1,0:T(8,128)S(1)} %shard_map.67.refs_0_, f32[136,128]{1,0:T(8,128)S(1)} %collective-permute-done.28.refs_1_, ...), custom_call_target="tpu_custom_call" | custom-call | tf_op jit(solution)/shard_map/pallas_call | solution.py:240
  58.1 1.5 %collective-permute-start.30 = (f32[72,128]{1,0:T(8,128)S(1)}, f32[72,128]{1,0:T(8,128)S(1)}, u32[]{:S(2)}, u32[]{:S(2)}) collective-permute-start(f32[72,128]{1,0:T(8,128)S(1)} %get-tuple-element.49.refs_3_), channel_id=1, source_target_pairs={{0,1},{1,0},{2,3},{3,2},{4,5},{5,4},{6,7},{7,6},{8,9},{9,8},{10,11... | collective-permute-start | bytes 110600 | tf_op jit(solution)/shard_map/ppermute | solution.py:274
  59.6 2.4 %collective-permute-done.30.refs_4_ = f32[72,128]{1,0:T(8,128)S(1)} collective-permute-done((f32[72,128]{1,0:T(8,128)S(1)}, f32[72,128]{1,0:T(8,128)S(1)}, u32[]{:S(2)}, u32[]{:S(2)}) %collective-permute-start.30) | collective-permute-done | bytes 36896 | tf_op jit(solution)/shard_map/ppermute | solution.py:274
  62.4 1.0 %collective-permute-start.31 = (f32[8,128]{1,0:T(8,128)S(1)}, f32[8,128]{1,0:T(8,128)S(1)}, u32[]{:S(2)}, u32[]{:S(2)}) collective-permute-start(f32[8,128]{1,0:T(8,128)S(1)} %get-tuple-element.50), channel_id=1, source_target_pairs={{0,4},{2,6},{4,0},{6,2},{8,12},{10,14},{12,8},{14,10},{16,20},{18,... | collective-permute-start | bytes 12296 | tf_op jit(solution)/shard_map/ppermute | solution.py:267
  63.6 2.5 %collective-permute-start.35 = (f32[8,128]{1,0:T(8,128)S(1)}, f32[8,128]{1,0:T(8,128)S(1)}, u32[]{:S(2)}, u32[]{:S(2)}) collective-permute-start(f32[8,128]{1,0:T(8,128)S(1)} %add.39), channel_id=1, source_target_pairs={{0,24},{2,30},{4,28},{6,26},{8,16},{10,22},{12,20},{14,18},{16,8},... | collective-permute-start | bytes 12296 | tf_op jit(solution)/shard_map/ppermute | solution.py:270
  66.0 2.5 %collective-permute-start.33 = (f32[8,128]{1,0:T(8,128)S(1)}, f32[8,128]{1,0:T(8,128)S(1)}, u32[]{:S(2)}, u32[]{:S(2)}) collective-permute-start(f32[8,128]{1,0:T(8,128)S(1)} %add.39), channel_id=1, source_target_pairs={{0,8},{2,18},{4,12},{6,22},{8,0},{10,26},{12,4},{14,30},{16,24},{1... | collective-permute-start | bytes 12296 | tf_op jit(solution)/shard_map/ppermute | solution.py:270
  68.6 0.4 collective-permute-done.35
  69.0 1.6 %collective-permute-done.34 = f32[8,128]{1,0:T(8,128)S(1)} collective-permute-done((f32[8,128]{1,0:T(8,128)S(1)}, f32[8,128]{1,0:T(8,128)S(1)}, u32[]{:S(2)}, u32[]{:S(2)}) %collective-permute-start.34) | collective-permute-done | bytes 4128 | tf_op jit(solution)/shard_map/ppermute | solution.py:270
  70.8 1.0 %collective-permute-done.36.other = f32[8,128]{1,0:T(8,128)S(1)} collective-permute-done((f32[8,128]{1,0:T(8,128)S(1)}, f32[8,128]{1,0:T(8,128)S(1)}, u32[]{:S(2)}, u32[]{:S(2)}) %collective-permute-start.36) | collective-permute-done | bytes 4128 | tf_op jit(solution)/shard_map/ppermute | solution.py:264
  71.8 0.6 shard_map.71
  (62 shorter events, 3.1 us)
Async XLA Ops:
  0.6 6.7 %collective-permute-start = (f32[248,128]{1,0:T(8,128)}, f32[248,128]{1,0:T(8,128)S(1)}, u32[]{:S(2)}, u32[]{:S(2)}) collective-permute-start(f32[248,128]{1,0:T(8,128)} %bitcast.7), channel_id=1, source_target_pairs={{0,1},{1,0},{2,3},{3,2},{4,5},{5,4},{6,7},{7,6},{8,9},{9,8},{10,11... | collective-permute-start | bytes 380936 | tf_op jit(solution)/shard_map/ppermute | solution.py:274
  8.1 1.9 %collective-permute-start.1 = (f32[72,128]{1,0:T(8,128)S(1)}, f32[72,128]{1,0:T(8,128)S(1)}, u32[]{:S(2)}, u32[]{:S(2)}) collective-permute-start(f32[72,128]{1,0:T(8,128)S(1)} %get-tuple-element.35.refs_0_), channel_id=1, source_target_pairs={{0,2},{2,0},{4,6},{6,4},{8,10},{10,8},{12,14},{14,12},{16,18},{18,... | collective-permute-start | bytes 110600 | tf_op jit(solution)/shard_map/ppermute | solution.py:264
  8.1 6.6 %collective-permute-start.2 = (f32[144,128]{1,0:T(8,128)S(1)}, f32[144,128]{1,0:T(8,128)S(1)}, u32[]{:S(2)}, u32[]{:S(2)}) collective-permute-start(f32[144,128]{1,0:T(8,128)S(1)} %pad.10), channel_id=1, source_target_pairs={{0,8},{2,10},{4,12},{6,14},{8,0},{10,2},{12,4},{14,6},{16,24},{18,... | collective-permute-start | bytes 221192 | tf_op jit(solution)/shard_map/ppermute | solution.py:267
  10.1 6.8 %collective-permute-start.6 = (f32[136,128]{1,0:T(8,128)S(1)}, f32[136,128]{1,0:T(8,128)S(1)}, u32[]{:S(2)}, u32[]{:S(2)}) collective-permute-start(f32[136,128]{1,0:T(8,128)S(1)} %pad_maximum_fusion), channel_id=1, source_target_pairs={{0,24},{2,30},{4,28},{6,26},{8,16},{10,22},{12,20},{14,18},{16,8},... | collective-permute-start | bytes 208904 | tf_op jit(solution)/shard_map/ppermute | solution.py:270
  13.2 4.5 %collective-permute-start.4 = (f32[136,128]{1,0:T(8,128)S(1)}, f32[136,128]{1,0:T(8,128)S(1)}, u32[]{:S(2)}, u32[]{:S(2)}) collective-permute-start(f32[136,128]{1,0:T(8,128)S(1)} %pad_maximum_fusion), channel_id=1, source_target_pairs={{0,4},{2,22},{4,0},{6,18},{8,12},{10,30},{12,8},{14,26},{16,20},{1... | collective-permute-start | bytes 208904 | tf_op jit(solution)/shard_map/ppermute | solution.py:270
  14.7 5.4 %collective-permute-start.8 = (f32[136,128]{1,0:T(8,128)S(1)}, f32[136,128]{1,0:T(8,128)S(1)}, u32[]{:S(2)}, u32[]{:S(2)}) collective-permute-start(f32[136,128]{1,0:T(8,128)S(1)} %pad_maximum_fusion), channel_id=1, source_target_pairs={{0,12},{2,18},{4,8},{6,22},{8,4},{10,26},{12,0},{14,30},{16,28},{1... | collective-permute-start | bytes 208904 | tf_op jit(solution)/shard_map/ppermute | solution.py:270
  14.7 5.6 %collective-permute-start.3 = (f32[144,128]{1,0:T(8,128)S(1)}, f32[144,128]{1,0:T(8,128)S(1)}, u32[]{:S(2)}, u32[]{:S(2)}) collective-permute-start(f32[144,128]{1,0:T(8,128)S(1)} %collective-permute-done.2.refs_2_), channel_id=1, source_target_pairs={{0,2},{2,0},{4,6},{6,4},{8,10},{10,8},{12,14},{14,12},{16,18},{18,... | collective-permute-start | bytes 221192 | tf_op jit(solution)/shard_map/ppermute | solution.py:264
  16.9 3.4 %collective-permute-start.7 = (f32[136,128]{1,0:T(8,128)S(1)}, f32[136,128]{1,0:T(8,128)S(1)}, u32[]{:S(2)}, u32[]{:S(2)}) collective-permute-start(f32[136,128]{1,0:T(8,128)S(1)} %collective-permute-done.6.refs_6_), channel_id=1, source_target_pairs={{0,2},{2,0},{4,6},{6,4},{8,10},{10,8},{12,14},{14,12},{16,18},{18,... | collective-permute-start | bytes 208904 | tf_op jit(solution)/shard_map/ppermute | solution.py:264
  17.7 3.3 %collective-permute-start.5 = (f32[136,128]{1,0:T(8,128)S(1)}, f32[136,128]{1,0:T(8,128)S(1)}, u32[]{:S(2)}, u32[]{:S(2)}) collective-permute-start(f32[136,128]{1,0:T(8,128)S(1)} %collective-permute-done.4.refs_4_), channel_id=1, source_target_pairs={{0,2},{2,0},{4,6},{6,4},{8,10},{10,8},{12,14},{14,12},{16,18},{18,... | collective-permute-start | bytes 208904 | tf_op jit(solution)/shard_map/ppermute | solution.py:264
  20.2 1.3 %collective-permute-start.9 = (f32[136,128]{1,0:T(8,128)S(1)}, f32[136,128]{1,0:T(8,128)S(1)}, u32[]{:S(2)}, u32[]{:S(2)}) collective-permute-start(f32[136,128]{1,0:T(8,128)S(1)} %collective-permute-done.8.refs_1_), channel_id=1, source_target_pairs={{0,2},{2,0},{4,6},{6,4},{8,10},{10,8},{12,14},{14,12},{16,18},{18,... | collective-permute-start | bytes 208904 | tf_op jit(solution)/shard_map/ppermute | solution.py:264
  22.5 4.0 %collective-permute-start.10 = (f32[72,128]{1,0:T(8,128)S(1)}, f32[72,128]{1,0:T(8,128)S(1)}, u32[]{:S(2)}, u32[]{:S(2)}) collective-permute-start(f32[72,128]{1,0:T(8,128)S(1)} %get-tuple-element.37.refs_4_), channel_id=1, source_target_pairs={{0,1},{1,0},{2,3},{3,2},{4,5},{5,4},{6,7},{7,6},{8,9},{9,8},{10,11... | collective-permute-start | bytes 110600 | tf_op jit(solution)/shard_map/ppermute | solution.py:274
  27.5 1.2 %collective-permute-start.11 = (f32[72,128]{1,0:T(8,128)S(1)}, f32[72,128]{1,0:T(8,128)S(1)}, u32[]{:S(2)}, u32[]{:S(2)}) collective-permute-start(f32[72,128]{1,0:T(8,128)S(1)} %get-tuple-element.39.refs_0_), channel_id=1, source_target_pairs={{0,2},{2,0},{4,6},{6,4},{8,10},{10,8},{12,14},{14,12},{16,18},{18,... | collective-permute-start | bytes 110600 | tf_op jit(solution)/shard_map/ppermute | solution.py:264
  27.5 5.2 %collective-permute-start.12 = (f32[144,128]{1,0:T(8,128)S(1)}, f32[144,128]{1,0:T(8,128)S(1)}, u32[]{:S(2)}, u32[]{:S(2)}) collective-permute-start(f32[144,128]{1,0:T(8,128)S(1)} %pad.11), channel_id=1, source_target_pairs={{0,8},{2,10},{4,12},{6,14},{8,0},{10,2},{12,4},{14,6},{16,24},{18,... | collective-permute-start | bytes 221192 | tf_op jit(solution)/shard_map/ppermute | solution.py:267
  28.8 6.8 %collective-permute-start.16 = (f32[136,128]{1,0:T(8,128)S(1)}, f32[136,128]{1,0:T(8,128)S(1)}, u32[]{:S(2)}, u32[]{:S(2)}) collective-permute-start(f32[136,128]{1,0:T(8,128)S(1)} %pad_maximum_fusion.1), channel_id=1, source_target_pairs={{0,24},{2,30},{4,28},{6,26},{8,16},{10,22},{12,20},{14,18},{16,8},... | collective-permute-start | bytes 208904 | tf_op jit(solution)/shard_map/ppermute | solution.py:270
  31.2 4.7 %collective-permute-start.14 = (f32[136,128]{1,0:T(8,128)S(1)}, f32[136,128]{1,0:T(8,128)S(1)}, u32[]{:S(2)}, u32[]{:S(2)}) collective-permute-start(f32[136,128]{1,0:T(8,128)S(1)} %pad_maximum_fusion.1), channel_id=1, source_target_pairs={{0,4},{2,22},{4,0},{6,18},{8,12},{10,30},{12,8},{14,26},{16,20},{1... | collective-permute-start | bytes 208904 | tf_op jit(solution)/shard_map/ppermute | solution.py:270
  32.4 5.6 %collective-permute-start.18 = (f32[136,128]{1,0:T(8,128)S(1)}, f32[136,128]{1,0:T(8,128)S(1)}, u32[]{:S(2)}, u32[]{:S(2)}) collective-permute-start(f32[136,128]{1,0:T(8,128)S(1)} %pad_maximum_fusion.1), channel_id=1, source_target_pairs={{0,12},{2,18},{4,8},{6,22},{8,4},{10,26},{12,0},{14,30},{16,28},{1... | collective-permute-start | bytes 208904 | tf_op jit(solution)/shard_map/ppermute | solution.py:270
  32.7 5.4 %collective-permute-start.13 = (f32[144,128]{1,0:T(8,128)S(1)}, f32[144,128]{1,0:T(8,128)S(1)}, u32[]{:S(2)}, u32[]{:S(2)}) collective-permute-start(f32[144,128]{1,0:T(8,128)S(1)} %collective-permute-done.12.refs_2_), channel_id=1, source_target_pairs={{0,2},{2,0},{4,6},{6,4},{8,10},{10,8},{12,14},{14,12},{16,18},{18,... | collective-permute-start | bytes 221192 | tf_op jit(solution)/shard_map/ppermute | solution.py:264
  35.6 2.5 %collective-permute-start.17 = (f32[136,128]{1,0:T(8,128)S(1)}, f32[136,128]{1,0:T(8,128)S(1)}, u32[]{:S(2)}, u32[]{:S(2)}) collective-permute-start(f32[136,128]{1,0:T(8,128)S(1)} %collective-permute-done.16.refs_6_), channel_id=1, source_target_pairs={{0,2},{2,0},{4,6},{6,4},{8,10},{10,8},{12,14},{14,12},{16,18},{18,... | collective-permute-start | bytes 208904 | tf_op jit(solution)/shard_map/ppermute | solution.py:264
  36.0 2.9 %collective-permute-start.15 = (f32[136,128]{1,0:T(8,128)S(1)}, f32[136,128]{1,0:T(8,128)S(1)}, u32[]{:S(2)}, u32[]{:S(2)}) collective-permute-start(f32[136,128]{1,0:T(8,128)S(1)} %collective-permute-done.14.refs_4_), channel_id=1, source_target_pairs={{0,2},{2,0},{4,6},{6,4},{8,10},{10,8},{12,14},{14,12},{16,18},{18,... | collective-permute-start | bytes 208904 | tf_op jit(solution)/shard_map/ppermute | solution.py:264
  37.9 1.3 %collective-permute-start.19 = (f32[136,128]{1,0:T(8,128)S(1)}, f32[136,128]{1,0:T(8,128)S(1)}, u32[]{:S(2)}, u32[]{:S(2)}) collective-permute-start(f32[136,128]{1,0:T(8,128)S(1)} %collective-permute-done.18.refs_1_), channel_id=1, source_target_pairs={{0,2},{2,0},{4,6},{6,4},{8,10},{10,8},{12,14},{14,12},{16,18},{18,... | collective-permute-start | bytes 208904 | tf_op jit(solution)/shard_map/ppermute | solution.py:264
  40.3 4.0 %collective-permute-start.20 = (f32[72,128]{1,0:T(8,128)S(1)}, f32[72,128]{1,0:T(8,128)S(1)}, u32[]{:S(2)}, u32[]{:S(2)}) collective-permute-start(f32[72,128]{1,0:T(8,128)S(1)} %get-tuple-element.43.refs_4_), channel_id=1, source_target_pairs={{0,1},{1,0},{2,3},{3,2},{4,5},{5,4},{6,7},{7,6},{8,9},{9,8},{10,11... | collective-permute-start | bytes 110600 | tf_op jit(solution)/shard_map/ppermute | solution.py:274
  45.3 1.2 %collective-permute-start.21 = (f32[72,128]{1,0:T(8,128)S(1)}, f32[72,128]{1,0:T(8,128)S(1)}, u32[]{:S(2)}, u32[]{:S(2)}) collective-permute-start(f32[72,128]{1,0:T(8,128)S(1)} %get-tuple-element.45.refs_0_), channel_id=1, source_target_pairs={{0,2},{2,0},{4,6},{6,4},{8,10},{10,8},{12,14},{14,12},{16,18},{18,... | collective-permute-start | bytes 110600 | tf_op jit(solution)/shard_map/ppermute | solution.py:264
  45.3 5.2 %collective-permute-start.22 = (f32[144,128]{1,0:T(8,128)S(1)}, f32[144,128]{1,0:T(8,128)S(1)}, u32[]{:S(2)}, u32[]{:S(2)}) collective-permute-start(f32[144,128]{1,0:T(8,128)S(1)} %pad.12), channel_id=1, source_target_pairs={{0,8},{2,10},{4,12},{6,14},{8,0},{10,2},{12,4},{14,6},{16,24},{18,... | collective-permute-start | bytes 221192 | tf_op jit(solution)/shard_map/ppermute | solution.py:267
  46.6 6.8 %collective-permute-start.26 = (f32[136,128]{1,0:T(8,128)S(1)}, f32[136,128]{1,0:T(8,128)S(1)}, u32[]{:S(2)}, u32[]{:S(2)}) collective-permute-start(f32[136,128]{1,0:T(8,128)S(1)} %pad_maximum_fusion.2), channel_id=1, source_target_pairs={{0,24},{2,30},{4,28},{6,26},{8,16},{10,22},{12,20},{14,18},{16,8},... | collective-permute-start | bytes 208904 | tf_op jit(solution)/shard_map/ppermute | solution.py:270
  49.0 4.7 %collective-permute-start.24 = (f32[136,128]{1,0:T(8,128)S(1)}, f32[136,128]{1,0:T(8,128)S(1)}, u32[]{:S(2)}, u32[]{:S(2)}) collective-permute-start(f32[136,128]{1,0:T(8,128)S(1)} %pad_maximum_fusion.2), channel_id=1, source_target_pairs={{0,4},{2,22},{4,0},{6,18},{8,12},{10,30},{12,8},{14,26},{16,20},{1... | collective-permute-start | bytes 208904 | tf_op jit(solution)/shard_map/ppermute | solution.py:270
  50.2 5.6 %collective-permute-start.28 = (f32[136,128]{1,0:T(8,128)S(1)}, f32[136,128]{1,0:T(8,128)S(1)}, u32[]{:S(2)}, u32[]{:S(2)}) collective-permute-start(f32[136,128]{1,0:T(8,128)S(1)} %pad_maximum_fusion.2), channel_id=1, source_target_pairs={{0,12},{2,18},{4,8},{6,22},{8,4},{10,26},{12,0},{14,30},{16,28},{1... | collective-permute-start | bytes 208904 | tf_op jit(solution)/shard_map/ppermute | solution.py:270
  50.5 5.4 %collective-permute-start.23 = (f32[144,128]{1,0:T(8,128)S(1)}, f32[144,128]{1,0:T(8,128)S(1)}, u32[]{:S(2)}, u32[]{:S(2)}) collective-permute-start(f32[144,128]{1,0:T(8,128)S(1)} %collective-permute-done.22.refs_2_), channel_id=1, source_target_pairs={{0,2},{2,0},{4,6},{6,4},{8,10},{10,8},{12,14},{14,12},{16,18},{18,... | collective-permute-start | bytes 221192 | tf_op jit(solution)/shard_map/ppermute | solution.py:264
  53.4 2.5 %collective-permute-start.27 = (f32[136,128]{1,0:T(8,128)S(1)}, f32[136,128]{1,0:T(8,128)S(1)}, u32[]{:S(2)}, u32[]{:S(2)}) collective-permute-start(f32[136,128]{1,0:T(8,128)S(1)} %collective-permute-done.26.refs_6_), channel_id=1, source_target_pairs={{0,2},{2,0},{4,6},{6,4},{8,10},{10,8},{12,14},{14,12},{16,18},{18,... | collective-permute-start | bytes 208904 | tf_op jit(solution)/shard_map/ppermute | solution.py:264
  53.8 2.9 %collective-permute-start.25 = (f32[136,128]{1,0:T(8,128)S(1)}, f32[136,128]{1,0:T(8,128)S(1)}, u32[]{:S(2)}, u32[]{:S(2)}) collective-permute-start(f32[136,128]{1,0:T(8,128)S(1)} %collective-permute-done.24.refs_4_), channel_id=1, source_target_pairs={{0,2},{2,0},{4,6},{6,4},{8,10},{10,8},{12,14},{14,12},{16,18},{18,... | collective-permute-start | bytes 208904 | tf_op jit(solution)/shard_map/ppermute | solution.py:264
  55.7 1.3 %collective-permute-start.29 = (f32[136,128]{1,0:T(8,128)S(1)}, f32[136,128]{1,0:T(8,128)S(1)}, u32[]{:S(2)}, u32[]{:S(2)}) collective-permute-start(f32[136,128]{1,0:T(8,128)S(1)} %collective-permute-done.28.refs_1_), channel_id=1, source_target_pairs={{0,2},{2,0},{4,6},{6,4},{8,10},{10,8},{12,14},{14,12},{16,18},{18,... | collective-permute-start | bytes 208904 | tf_op jit(solution)/shard_map/ppermute | solution.py:264
  58.1 4.0 %collective-permute-start.30 = (f32[72,128]{1,0:T(8,128)S(1)}, f32[72,128]{1,0:T(8,128)S(1)}, u32[]{:S(2)}, u32[]{:S(2)}) collective-permute-start(f32[72,128]{1,0:T(8,128)S(1)} %get-tuple-element.49.refs_3_), channel_id=1, source_target_pairs={{0,1},{1,0},{2,3},{3,2},{4,5},{5,4},{6,7},{7,6},{8,9},{9,8},{10,11... | collective-permute-start | bytes 110600 | tf_op jit(solution)/shard_map/ppermute | solution.py:274
  62.4 1.2 %collective-permute-start.32 = (f32[8,128]{1,0:T(8,128)S(1)}, f32[8,128]{1,0:T(8,128)S(1)}, u32[]{:S(2)}, u32[]{:S(2)}) collective-permute-start(f32[8,128]{1,0:T(8,128)S(1)} %get-tuple-element.50), channel_id=1, source_target_pairs={{0,2},{2,0},{4,6},{6,4},{8,10},{10,8},{12,14},{14,12},{16,18},{18,... | collective-permute-start | bytes 12296 | tf_op jit(solution)/shard_map/ppermute | solution.py:264
  62.4 6.2 %collective-permute-start.31 = (f32[8,128]{1,0:T(8,128)S(1)}, f32[8,128]{1,0:T(8,128)S(1)}, u32[]{:S(2)}, u32[]{:S(2)}) collective-permute-start(f32[8,128]{1,0:T(8,128)S(1)} %get-tuple-element.50), channel_id=1, source_target_pairs={{0,4},{2,6},{4,0},{6,2},{8,12},{10,14},{12,8},{14,10},{16,20},{18,... | collective-permute-start | bytes 12296 | tf_op jit(solution)/shard_map/ppermute | solution.py:267
  63.6 5.4 %collective-permute-start.35 = (f32[8,128]{1,0:T(8,128)S(1)}, f32[8,128]{1,0:T(8,128)S(1)}, u32[]{:S(2)}, u32[]{:S(2)}) collective-permute-start(f32[8,128]{1,0:T(8,128)S(1)} %add.39), channel_id=1, source_target_pairs={{0,24},{2,30},{4,28},{6,26},{8,16},{10,22},{12,20},{14,18},{16,8},... | collective-permute-start | bytes 12296 | tf_op jit(solution)/shard_map/ppermute | solution.py:270
  66.0 4.5 %collective-permute-start.34 = (f32[8,128]{1,0:T(8,128)S(1)}, f32[8,128]{1,0:T(8,128)S(1)}, u32[]{:S(2)}, u32[]{:S(2)}) collective-permute-start(f32[8,128]{1,0:T(8,128)S(1)} %add.39), channel_id=1, source_target_pairs={{0,12},{2,22},{4,8},{6,18},{8,4},{10,30},{12,0},{14,26},{16,28},{1... | collective-permute-start | bytes 12296 | tf_op jit(solution)/shard_map/ppermute | solution.py:270
  66.0 4.5 %collective-permute-start.33 = (f32[8,128]{1,0:T(8,128)S(1)}, f32[8,128]{1,0:T(8,128)S(1)}, u32[]{:S(2)}, u32[]{:S(2)}) collective-permute-start(f32[8,128]{1,0:T(8,128)S(1)} %add.39), channel_id=1, source_target_pairs={{0,8},{2,18},{4,12},{6,22},{8,0},{10,26},{12,4},{14,30},{16,24},{1... | collective-permute-start | bytes 12296 | tf_op jit(solution)/shard_map/ppermute | solution.py:270
  70.5 1.2 %collective-permute-start.36 = (f32[8,128]{1,0:T(8,128)S(1)}, f32[8,128]{1,0:T(8,128)S(1)}, u32[]{:S(2)}, u32[]{:S(2)}) collective-permute-start(f32[8,128]{1,0:T(8,128)S(1)} %add_add_fusion.half), channel_id=1, source_target_pairs={{0,2},{2,0},{4,6},{6,4},{8,10},{10,8},{12,14},{14,12},{16,18},{18,... | collective-permute-start | bytes 12296 | tf_op jit(solution)/shard_map/ppermute | solution.py:264

commit v7 on v6

--- a/solution.py
+++ b/solution.py
@@ -248,14 +248,15 @@
 
 def chip_steps(chips):
     if chips == 8:
-        return (2, [(3, 4), (1, 5), (6, 7)]), (1, [(2, 4), (3, 5), (6, 7)])
+        gathers = [(2, [(3, 4), (1, 5), (6, 7)])] * (ITERS - 1) + [(2, [(1, 7), (3, 5), (6, 4)])]
+        return gathers, (1, [(2, 4), (3, 5), (6, 7)])
     steps = 1, [(m, m + 1) for m in range(2, chips, 2)]
-    return steps, steps
+    return [steps] * ITERS, steps
 
 
 def on_device(n_row, n_col, rhs, blocks, blk_row, blk_col):
     chips = n_row // 2
-    gather_steps, sum_steps = chip_steps(chips)
+    all_gather_steps, sum_steps = chip_steps(chips)
     per_rhs = rhs.shape[0] // BLK
     per_out = COLB_DEV // n_row
     row, col = lax.axis_index("row"), lax.axis_index("col")
@@ -283,7 +284,7 @@
     lane = lax.broadcasted_iota(jnp.int32, (MSG - NB_DEV, BLK), 1)
     end_row = lax.broadcasted_iota(jnp.int32, (MSG - NB_DEV, BLK), 0)
 
-    def gather(msg):
+    def gather(msg, gather_steps):
         peer, beside = swap(msg), to_near(jnp.pad(msg, ((0, MSG), (0, 0))), gather_steps)
         a, b = msg[NB_DEV:], peer[NB_DEV:]
         end = jnp.where(end_row == 0, jnp.where(lane < NB_DEV, a, b), a + b)
@@ -304,7 +305,7 @@
     )
     alphas, betas, v_raws = [], [], []
     for step in range(ITERS):
-        msgs = gather(msg)
+        msgs = gather(msg, all_gather_steps[step])
         before = [v_raws[-1], alphas[-1]] if step else []
         v_raw, msg, beta = call(
             functools.partial(v_kernel, step > 0, len(msgs)),

time: 72.6 us -> 72.7 us (level)
  waiting for transfers between devices: 19.8 us -> 21.4 us
  starting transfers between devices: 40.5 us -> 39 us
    ppermute x12, waiting for transfers between devices: 6.33 us -> 7.65 us  [to_chips(): lax.ppermute(x, 'row', [(r, r ^ 2 * step[r % 2]) for r in range(n_row)])]
    ppermute x17, starting transfers between devices: 12.2 us -> 11.1 us  [swap(): return lax.ppermute(x, 'row', [(r, r ^ 1) for r in range(n_row)])]
  transfers between devices with their start and end apart: 37 -> 37, of which waited for: 19 -> 21; matrix products, arithmetic and copies ran while one was open for 0% -> 0% of each run, Pallas kernels for 6% -> 6%
where the time goes in v7:
time: 72.7 us; the launch traced here: 72.5 us
  starting transfers between devices  39 us (54%)
  waiting for transfers between devices  21.4 us (29%)
  Pallas kernels  11 us (15%)
  between operations  0.81 us (1%)
    ppermute x12, starting transfers between devices, to_chips(): lax.ppermute(x, 'row', [(r, r ^ 2 * step[r % 2]) for r in range(n_row)])  17.1 us
    ppermute x17, starting transfers between devices, swap(): return lax.ppermute(x, 'row', [(r, r ^ 1) for r in range(n_row)])  11.1 us
    pallas_call x12, Pallas kernels, call(): pl.pallas_call(body, out_shape=[jax.ShapeDtypeStruct(s, f32) for s in out...  8.09 us
    ppermute x4, waiting for transfers between devices, around_col(): lax.ppermute(x, 'col', [(i, (i - s) % n_col) for i in range(n_col)])  8.03 us
    ppermute x12, waiting for transfers between devices, to_chips(): lax.ppermute(x, 'row', [(r, r ^ 2 * step[r % 2]) for r in range(n_row)])  7.65 us
    ppermute x4, starting transfers between devices, around_col(): lax.ppermute(x, 'col', [(i, (i - s) % n_col) for i in range(n_col)])  7.62 us
    ppermute x17, waiting for transfers between devices, swap(): return lax.ppermute(x, 'row', [(r, r ^ 1) for r in range(n_row)])  5.75 us
    ppermute x4, starting transfers between devices, to_near(): return lax.ppermute(x, 'row', [(r, r ^ 2 * steps[0]) for r in range(n_row)])  3.07 us
  transfers between devices with their start and end apart: 37, of which 21 were waited for; matrix products, arithmetic and copies ran while one was open for 0% of the time, Pallas kernels for 6%

profile of v7, /device:TPU:0, one launch (start us, length us, event | category | flops | bytes accessed | tf_op | source)
XLA Modules:
  0.0 72.5 jit_solution(12254873485870245764)
XLA Ops:
  0.6 3.0 %collective-permute-start = (f32[248,128]{1,0:T(8,128)}, f32[248,128]{1,0:T(8,128)S(1)}, u32[]{:S(2)}, u32[]{:S(2)}) collective-permute-start(f32[248,128]{1,0:T(8,128)} %bitcast.7), channel_id=1, source_target_pairs={{0,1},{1,0},{2,3},{3,2},{4,5},{5,4},{6,7},{7,6},{8,9},{9,8},{10,11... | collective-permute-start | bytes 380936 | tf_op jit(solution)/shard_map/ppermute | solution.py:275
  3.7 2.9 %shard_map.59 = (bf16[16384,256]{1,0:T(8,128)(2,1)S(1)}, f32[8,128]{1,0:T(8,128)S(1)}, f32[128,128]{1,0:T(8,128)S(1)}, f32[248,128]{1,0:T(8,128)S(1)}) custom-call(f32[8192,128]{1,0:T(8,128)} %bitcast.6, s32[1,64]{1,0:T(1,128)} %bitcast.9, s32[1,64]{1,0:T(1,128)} %bitcast.10, f32[248,128]{1,0:T(8,128)} %bitcast.8, f32[8,128]{1,0:T(8,128)S(1)} %broadcast_in_dim.3.place), custom_call_target="tpu_custom_call" | custom-call | bytes 4194304 | tf_op jit(solution)/shard_map/pallas_call | solution.py:216
  6.6 0.7 collective-permute-done.refs_1_
  7.3 0.8 %shard_map.60 = (f32[512,128]{1,0:T(8,128)S(1)}, f32[72,128]{1,0:T(8,128)S(1)}) custom-call(bf16[16384,256]{1,0:T(8,128)(2,1)S(1)} %get-tuple-element.31.tiles.refs_0_, f32[248,128]{1,0:T(8,128)S(1)} %get-tuple-element.32.refs_0_, f32[248,128]{1,0:T(8,128)S(1)} %collective-permute-done.refs_1_, ...), custom_call_target="tpu_custom_call" | custom-call | tf_op jit(solution)/shard_map/pallas_call | solution.py:240
  8.1 1.9 %collective-permute-start.2 = (f32[144,128]{1,0:T(8,128)S(1)}, f32[144,128]{1,0:T(8,128)S(1)}, u32[]{:S(2)}, u32[]{:S(2)}) collective-permute-start(f32[144,128]{1,0:T(8,128)S(1)} %pad.10), channel_id=1, source_target_pairs={{0,8},{2,10},{4,12},{6,14},{8,0},{10,2},{12,4},{14,6},{16,24},{18,... | collective-permute-start | bytes 221192 | tf_op jit(solution)/shard_map/ppermute | solution.py:268
  10.1 3.2 %collective-permute-start.6 = (f32[136,128]{1,0:T(8,128)S(1)}, f32[136,128]{1,0:T(8,128)S(1)}, u32[]{:S(2)}, u32[]{:S(2)}) collective-permute-start(f32[136,128]{1,0:T(8,128)S(1)} %pad_maximum_fusion), channel_id=1, source_target_pairs={{0,24},{2,30},{4,28},{6,26},{8,16},{10,22},{12,20},{14,18},{16,8},... | collective-permute-start | bytes 208904 | tf_op jit(solution)/shard_map/ppermute | solution.py:271
  13.2 1.5 %collective-permute-start.4 = (f32[136,128]{1,0:T(8,128)S(1)}, f32[136,128]{1,0:T(8,128)S(1)}, u32[]{:S(2)}, u32[]{:S(2)}) collective-permute-start(f32[136,128]{1,0:T(8,128)S(1)} %pad_maximum_fusion), channel_id=1, source_target_pairs={{0,4},{2,22},{4,0},{6,18},{8,12},{10,30},{12,8},{14,26},{16,20},{1... | collective-permute-start | bytes 208904 | tf_op jit(solution)/shard_map/ppermute | solution.py:271
  14.7 1.7 %collective-permute-start.3 = (f32[144,128]{1,0:T(8,128)S(1)}, f32[144,128]{1,0:T(8,128)S(1)}, u32[]{:S(2)}, u32[]{:S(2)}) collective-permute-start(f32[144,128]{1,0:T(8,128)S(1)} %collective-permute-done.2.refs_2_), channel_id=1, source_target_pairs={{0,2},{2,0},{4,6},{6,4},{8,10},{10,8},{12,14},{14,12},{16,18},{18,... | collective-permute-start | bytes 221192 | tf_op jit(solution)/shard_map/ppermute | solution.py:265
  16.4 0.5 collective-permute-done.6.refs_6_
  17.0 0.7 collective-permute-done.4.refs_4_
  17.7 2.4 %collective-permute-start.5 = (f32[136,128]{1,0:T(8,128)S(1)}, f32[136,128]{1,0:T(8,128)S(1)}, u32[]{:S(2)}, u32[]{:S(2)}) collective-permute-start(f32[136,128]{1,0:T(8,128)S(1)} %collective-permute-done.4.refs_4_), channel_id=1, source_target_pairs={{0,2},{2,0},{4,6},{6,4},{8,10},{10,8},{12,14},{14,12},{16,18},{18,... | collective-permute-start | bytes 208904 | tf_op jit(solution)/shard_map/ppermute | solution.py:265
  20.3 0.8 %collective-permute-done.5.refs_5_ = f32[136,128]{1,0:T(8,128)S(1)} collective-permute-done((f32[136,128]{1,0:T(8,128)S(1)}, f32[136,128]{1,0:T(8,128)S(1)}, u32[]{:S(2)}, u32[]{:S(2)}) %collective-permute-start.5) | collective-permute-done | bytes 69664 | tf_op jit(solution)/shard_map/ppermute | solution.py:265
  21.4 1.0 %shard_map.62 = (f32[512,128]{1,0:T(8,128)S(1)}, f32[72,128]{1,0:T(8,128)S(1)}, f32[8,128]{1,0:T(8,128)S(1)}) custom-call(bf16[16384,256]{1,0:T(8,128)(2,1)S(1)} %get-tuple-element.31.tiles.refs_0_, f32[520,128]{1,0:T(8,128)S(1)} %shard_map.61.refs_0_, f32[136,128]{1,0:T(8,128)S(1)} %collective-permute-done.8.refs_1_, ...), custom_call_target="tpu_custom_call" | custom-call | tf_op jit(solution)/shard_map/pallas_call | solution.py:240
  22.5 1.5 %collective-permute-start.10 = (f32[72,128]{1,0:T(8,128)S(1)}, f32[72,128]{1,0:T(8,128)S(1)}, u32[]{:S(2)}, u32[]{:S(2)}) collective-permute-start(f32[72,128]{1,0:T(8,128)S(1)} %get-tuple-element.37.refs_4_), channel_id=1, source_target_pairs={{0,1},{1,0},{2,3},{3,2},{4,5},{5,4},{6,7},{7,6},{8,9},{9,8},{10,11... | collective-permute-start | bytes 110600 | tf_op jit(solution)/shard_map/ppermute | solution.py:275
  24.0 2.4 %collective-permute-done.10.refs_5_ = f32[72,128]{1,0:T(8,128)S(1)} collective-permute-done((f32[72,128]{1,0:T(8,128)S(1)}, f32[72,128]{1,0:T(8,128)S(1)}, u32[]{:S(2)}, u32[]{:S(2)}) %collective-permute-start.10) | collective-permute-done | bytes 36896 | tf_op jit(solution)/shard_map/ppermute | solution.py:275
  26.4 1.0 %shard_map.63 = (f32[512,128]{1,0:T(8,128)S(1)}, f32[72,128]{1,0:T(8,128)S(1)}, f32[8,128]{1,0:T(8,128)S(1)}) custom-call(bf16[16384,256]{1,0:T(8,128)(2,1)S(1)} %get-tuple-element.31.tiles.refs_0_, f32[8,128]{1,0:T(8,128)S(1)} %get-tuple-element.30.refs_2_.refs_3_.refs_1_.refs_5_.refs_0_, f32[512,128]{1,0:T(8,128)S(1)} %get-tuple-element.34.refs_2_, ...), custom_call_target="tpu_custom_call" | custom-call | tf_op jit(solution)/shard_map/pallas_call | solution.py:240
  27.6 1.1 %collective-permute-done.11.refs_1_ = f32[72,128]{1,0:T(8,128)S(1)} collective-permute-done((f32[72,128]{1,0:T(8,128)S(1)}, f32[72,128]{1,0:T(8,128)S(1)}, u32[]{:S(2)}, u32[]{:S(2)}) %collective-permute-start.11) | collective-permute-done | bytes 36896 | tf_op jit(solution)/shard_map/ppermute | solution.py:265
  28.8 2.5 %collective-permute-start.16 = (f32[136,128]{1,0:T(8,128)S(1)}, f32[136,128]{1,0:T(8,128)S(1)}, u32[]{:S(2)}, u32[]{:S(2)}) collective-permute-start(f32[136,128]{1,0:T(8,128)S(1)} %pad_maximum_fusion.1), channel_id=1, source_target_pairs={{0,24},{2,30},{4,28},{6,26},{8,16},{10,22},{12,20},{14,18},{16,8},... | collective-permute-start | bytes 208904 | tf_op jit(solution)/shard_map/ppermute | solution.py:271
  31.2 1.1 %collective-permute-start.14 = (f32[136,128]{1,0:T(8,128)S(1)}, f32[136,128]{1,0:T(8,128)S(1)}, u32[]{:S(2)}, u32[]{:S(2)}) collective-permute-start(f32[136,128]{1,0:T(8,128)S(1)} %pad_maximum_fusion.1), channel_id=1, source_target_pairs={{0,4},{2,22},{4,0},{6,18},{8,12},{10,30},{12,8},{14,26},{16,20},{1... | collective-permute-start | bytes 208904 | tf_op jit(solution)/shard_map/ppermute | solution.py:271
  32.7 1.7 %collective-permute-start.13 = (f32[144,128]{1,0:T(8,128)S(1)}, f32[144,128]{1,0:T(8,128)S(1)}, u32[]{:S(2)}, u32[]{:S(2)}) collective-permute-start(f32[144,128]{1,0:T(8,128)S(1)} %collective-permute-done.12.refs_2_), channel_id=1, source_target_pairs={{0,2},{2,0},{4,6},{6,4},{8,10},{10,8},{12,14},{14,12},{16,18},{18,... | collective-permute-start | bytes 221192 | tf_op jit(solution)/shard_map/ppermute | solution.py:265
  34.4 1.2 %collective-permute-done.16.refs_6_ = f32[136,128]{1,0:T(8,128)S(1)} collective-permute-done((f32[136,128]{1,0:T(8,128)S(1)}, f32[136,128]{1,0:T(8,128)S(1)}, u32[]{:S(2)}, u32[]{:S(2)}) %collective-permute-start.16) | collective-permute-done | bytes 69664 | tf_op jit(solution)/shard_map/ppermute | solution.py:271
  36.0 2.0 %collective-permute-start.15 = (f32[136,128]{1,0:T(8,128)S(1)}, f32[136,128]{1,0:T(8,128)S(1)}, u32[]{:S(2)}, u32[]{:S(2)}) collective-permute-start(f32[136,128]{1,0:T(8,128)S(1)} %collective-permute-done.14.refs_4_), channel_id=1, source_target_pairs={{0,2},{2,0},{4,6},{6,4},{8,10},{10,8},{12,14},{14,12},{16,18},{18,... | collective-permute-start | bytes 208904 | tf_op jit(solution)/shard_map/ppermute | solution.py:265
  38.1 0.7 collective-permute-done.15.refs_5_
  39.2 1.0 %shard_map.65 = (f32[512,128]{1,0:T(8,128)S(1)}, f32[72,128]{1,0:T(8,128)S(1)}, f32[8,128]{1,0:T(8,128)S(1)}) custom-call(bf16[16384,256]{1,0:T(8,128)(2,1)S(1)} %get-tuple-element.31.tiles.refs_0_, f32[520,128]{1,0:T(8,128)S(1)} %shard_map.64.refs_0_, f32[136,128]{1,0:T(8,128)S(1)} %collective-permute-done.18.refs_1_, ...), custom_call_target="tpu_custom_call" | custom-call | tf_op jit(solution)/shard_map/pallas_call | solution.py:240
  40.3 1.5 %collective-permute-start.20 = (f32[72,128]{1,0:T(8,128)S(1)}, f32[72,128]{1,0:T(8,128)S(1)}, u32[]{:S(2)}, u32[]{:S(2)}) collective-permute-start(f32[72,128]{1,0:T(8,128)S(1)} %get-tuple-element.43.refs_4_), channel_id=1, source_target_pairs={{0,1},{1,0},{2,3},{3,2},{4,5},{5,4},{6,7},{7,6},{8,9},{9,8},{10,11... | collective-permute-start | bytes 110600 | tf_op jit(solution)/shard_map/ppermute | solution.py:275
  41.8 2.4 %collective-permute-done.20.refs_5_ = f32[72,128]{1,0:T(8,128)S(1)} collective-permute-done((f32[72,128]{1,0:T(8,128)S(1)}, f32[72,128]{1,0:T(8,128)S(1)}, u32[]{:S(2)}, u32[]{:S(2)}) %collective-permute-start.20) | collective-permute-done | bytes 36896 | tf_op jit(solution)/shard_map/ppermute | solution.py:275
  44.2 1.0 %shard_map.66 = (f32[512,128]{1,0:T(8,128)S(1)}, f32[72,128]{1,0:T(8,128)S(1)}, f32[8,128]{1,0:T(8,128)S(1)}) custom-call(bf16[16384,256]{1,0:T(8,128)(2,1)S(1)} %get-tuple-element.31.tiles.refs_0_, f32[8,128]{1,0:T(8,128)S(1)} %get-tuple-element.30.refs_2_.refs_3_.refs_1_.refs_5_.refs_0_, f32[512,128]{1,0:T(8,128)S(1)} %get-tuple-element.38.refs_2_, ...), custom_call_target="tpu_custom_call" | custom-call | tf_op jit(solution)/shard_map/pallas_call | solution.py:240
  45.4 1.1 %collective-permute-done.21.refs_1_ = f32[72,128]{1,0:T(8,128)S(1)} collective-permute-done((f32[72,128]{1,0:T(8,128)S(1)}, f32[72,128]{1,0:T(8,128)S(1)}, u32[]{:S(2)}, u32[]{:S(2)}) %collective-permute-start.21) | collective-permute-done | bytes 36896 | tf_op jit(solution)/shard_map/ppermute | solution.py:265
  46.6 2.5 %collective-permute-start.26 = (f32[136,128]{1,0:T(8,128)S(1)}, f32[136,128]{1,0:T(8,128)S(1)}, u32[]{:S(2)}, u32[]{:S(2)}) collective-permute-start(f32[136,128]{1,0:T(8,128)S(1)} %pad_maximum_fusion.2), channel_id=1, source_target_pairs={{0,24},{2,18},{4,28},{6,22},{8,16},{10,26},{12,20},{14,30},{16,8},... | collective-permute-start | bytes 208904 | tf_op jit(solution)/shard_map/ppermute | solution.py:271
  49.0 0.6 collective-permute-start.24
  49.6 0.9 %collective-permute-start.28 = (f32[136,128]{1,0:T(8,128)S(1)}, f32[136,128]{1,0:T(8,128)S(1)}, u32[]{:S(2)}, u32[]{:S(2)}) collective-permute-start(f32[136,128]{1,0:T(8,128)S(1)} %pad_maximum_fusion.2), channel_id=1, source_target_pairs={{0,4},{2,30},{4,0},{6,26},{8,12},{10,22},{12,8},{14,18},{16,20},{1... | collective-permute-start | bytes 208904 | tf_op jit(solution)/shard_map/ppermute | solution.py:271
  50.5 1.7 %collective-permute-start.23 = (f32[144,128]{1,0:T(8,128)S(1)}, f32[144,128]{1,0:T(8,128)S(1)}, u32[]{:S(2)}, u32[]{:S(2)}) collective-permute-start(f32[144,128]{1,0:T(8,128)S(1)} %collective-permute-done.22.refs_2_), channel_id=1, source_target_pairs={{0,2},{2,0},{4,6},{6,4},{8,10},{10,8},{12,14},{14,12},{16,18},{18,... | collective-permute-start | bytes 221192 | tf_op jit(solution)/shard_map/ppermute | solution.py:265
  52.2 0.7 collective-permute-done.26.refs_6_
  52.9 1.7 %collective-permute-done.24.refs_4_ = f32[136,128]{1,0:T(8,128)S(1)} collective-permute-done((f32[136,128]{1,0:T(8,128)S(1)}, f32[136,128]{1,0:T(8,128)S(1)}, u32[]{:S(2)}, u32[]{:S(2)}) %collective-permute-start.24) | collective-permute-done | bytes 69664 | tf_op jit(solution)/shard_map/ppermute | solution.py:271
  54.6 1.2 %collective-permute-start.25 = (f32[136,128]{1,0:T(8,128)S(1)}, f32[136,128]{1,0:T(8,128)S(1)}, u32[]{:S(2)}, u32[]{:S(2)}) collective-permute-start(f32[136,128]{1,0:T(8,128)S(1)} %collective-permute-done.24.refs_4_), channel_id=1, source_target_pairs={{0,2},{2,0},{4,6},{6,4},{8,10},{10,8},{12,14},{14,12},{16,18},{18,... | collective-permute-start | bytes 208904 | tf_op jit(solution)/shard_map/ppermute | solution.py:265
  55.7 0.4 collective-permute-done.28.refs_1_
  56.2 0.5 collective-permute-done.25.refs_5_
  57.4 1.0 %shard_map.68 = (f32[512,128]{1,0:T(8,128)S(1)}, f32[72,128]{1,0:T(8,128)S(1)}, f32[8,128]{1,0:T(8,128)S(1)}) custom-call(bf16[16384,256]{1,0:T(8,128)(2,1)S(1)} %get-tuple-element.31.tiles.refs_0_, f32[520,128]{1,0:T(8,128)S(1)} %shard_map.67.refs_0_, f32[136,128]{1,0:T(8,128)S(1)} %collective-permute-done.28.refs_1_, ...), custom_call_target="tpu_custom_call" | custom-call | tf_op jit(solution)/shard_map/pallas_call | solution.py:240
  58.5 1.5 %collective-permute-start.30 = (f32[72,128]{1,0:T(8,128)S(1)}, f32[72,128]{1,0:T(8,128)S(1)}, u32[]{:S(2)}, u32[]{:S(2)}) collective-permute-start(f32[72,128]{1,0:T(8,128)S(1)} %get-tuple-element.49.refs_3_), channel_id=1, source_target_pairs={{0,1},{1,0},{2,3},{3,2},{4,5},{5,4},{6,7},{7,6},{8,9},{9,8},{10,11... | collective-permute-start | bytes 110600 | tf_op jit(solution)/shard_map/ppermute | solution.py:275
  60.0 2.4 %collective-permute-done.30.refs_4_ = f32[72,128]{1,0:T(8,128)S(1)} collective-permute-done((f32[72,128]{1,0:T(8,128)S(1)}, f32[72,128]{1,0:T(8,128)S(1)}, u32[]{:S(2)}, u32[]{:S(2)}) %collective-permute-start.30) | collective-permute-done | bytes 36896 | tf_op jit(solution)/shard_map/ppermute | solution.py:275
  62.8 1.0 %collective-permute-start.31 = (f32[8,128]{1,0:T(8,128)S(1)}, f32[8,128]{1,0:T(8,128)S(1)}, u32[]{:S(2)}, u32[]{:S(2)}) collective-permute-start(f32[8,128]{1,0:T(8,128)S(1)} %get-tuple-element.50), channel_id=1, source_target_pairs={{0,4},{2,6},{4,0},{6,2},{8,12},{10,14},{12,8},{14,10},{16,20},{18,... | collective-permute-start | bytes 12296 | tf_op jit(solution)/shard_map/ppermute | solution.py:268
  63.9 2.2 %collective-permute-start.35 = (f32[8,128]{1,0:T(8,128)S(1)}, f32[8,128]{1,0:T(8,128)S(1)}, u32[]{:S(2)}, u32[]{:S(2)}) collective-permute-start(f32[8,128]{1,0:T(8,128)S(1)} %add.39), channel_id=1, source_target_pairs={{0,24},{2,30},{4,28},{6,26},{8,16},{10,22},{12,20},{14,18},{16,8},... | collective-permute-start | bytes 12296 | tf_op jit(solution)/shard_map/ppermute | solution.py:271
  66.1 0.4 collective-permute-start.34
  66.5 2.0 %collective-permute-start.33 = (f32[8,128]{1,0:T(8,128)S(1)}, f32[8,128]{1,0:T(8,128)S(1)}, u32[]{:S(2)}, u32[]{:S(2)}) collective-permute-start(f32[8,128]{1,0:T(8,128)S(1)} %add.39), channel_id=1, source_target_pairs={{0,8},{2,18},{4,12},{6,22},{8,0},{10,26},{12,4},{14,30},{16,24},{1... | collective-permute-start | bytes 12296 | tf_op jit(solution)/shard_map/ppermute | solution.py:271
  68.5 0.8 %collective-permute-done.35 = f32[8,128]{1,0:T(8,128)S(1)} collective-permute-done((f32[8,128]{1,0:T(8,128)S(1)}, f32[8,128]{1,0:T(8,128)S(1)}, u32[]{:S(2)}, u32[]{:S(2)}) %collective-permute-start.35) | collective-permute-done | bytes 4128 | tf_op jit(solution)/shard_map/ppermute | solution.py:271
  69.3 1.3 %collective-permute-done.34 = f32[8,128]{1,0:T(8,128)S(1)} collective-permute-done((f32[8,128]{1,0:T(8,128)S(1)}, f32[8,128]{1,0:T(8,128)S(1)}, u32[]{:S(2)}, u32[]{:S(2)}) %collective-permute-start.34) | collective-permute-done | bytes 4128 | tf_op jit(solution)/shard_map/ppermute | solution.py:271
  70.8 1.1 %collective-permute-done.36.other = f32[8,128]{1,0:T(8,128)S(1)} collective-permute-done((f32[8,128]{1,0:T(8,128)S(1)}, f32[8,128]{1,0:T(8,128)S(1)}, u32[]{:S(2)}, u32[]{:S(2)}) %collective-permute-start.36) | collective-permute-done | bytes 4128 | tf_op jit(solution)/shard_map/ppermute | solution.py:265
  71.9 0.6 shard_map.71
  (62 shorter events, 4.0 us)
Async XLA Ops:
  0.6 6.7 %collective-permute-start = (f32[248,128]{1,0:T(8,128)}, f32[248,128]{1,0:T(8,128)S(1)}, u32[]{:S(2)}, u32[]{:S(2)}) collective-permute-start(f32[248,128]{1,0:T(8,128)} %bitcast.7), channel_id=1, source_target_pairs={{0,1},{1,0},{2,3},{3,2},{4,5},{5,4},{6,7},{7,6},{8,9},{9,8},{10,11... | collective-permute-start | bytes 380936 | tf_op jit(solution)/shard_map/ppermute | solution.py:275
  8.1 1.9 %collective-permute-start.1 = (f32[72,128]{1,0:T(8,128)S(1)}, f32[72,128]{1,0:T(8,128)S(1)}, u32[]{:S(2)}, u32[]{:S(2)}) collective-permute-start(f32[72,128]{1,0:T(8,128)S(1)} %get-tuple-element.35.refs_0_), channel_id=1, source_target_pairs={{0,2},{2,0},{4,6},{6,4},{8,10},{10,8},{12,14},{14,12},{16,18},{18,... | collective-permute-start | bytes 110600 | tf_op jit(solution)/shard_map/ppermute | solution.py:265
  8.1 6.6 %collective-permute-start.2 = (f32[144,128]{1,0:T(8,128)S(1)}, f32[144,128]{1,0:T(8,128)S(1)}, u32[]{:S(2)}, u32[]{:S(2)}) collective-permute-start(f32[144,128]{1,0:T(8,128)S(1)} %pad.10), channel_id=1, source_target_pairs={{0,8},{2,10},{4,12},{6,14},{8,0},{10,2},{12,4},{14,6},{16,24},{18,... | collective-permute-start | bytes 221192 | tf_op jit(solution)/shard_map/ppermute | solution.py:268
  10.1 6.8 %collective-permute-start.6 = (f32[136,128]{1,0:T(8,128)S(1)}, f32[136,128]{1,0:T(8,128)S(1)}, u32[]{:S(2)}, u32[]{:S(2)}) collective-permute-start(f32[136,128]{1,0:T(8,128)S(1)} %pad_maximum_fusion), channel_id=1, source_target_pairs={{0,24},{2,30},{4,28},{6,26},{8,16},{10,22},{12,20},{14,18},{16,8},... | collective-permute-start | bytes 208904 | tf_op jit(solution)/shard_map/ppermute | solution.py:271
  13.2 4.5 %collective-permute-start.4 = (f32[136,128]{1,0:T(8,128)S(1)}, f32[136,128]{1,0:T(8,128)S(1)}, u32[]{:S(2)}, u32[]{:S(2)}) collective-permute-start(f32[136,128]{1,0:T(8,128)S(1)} %pad_maximum_fusion), channel_id=1, source_target_pairs={{0,4},{2,22},{4,0},{6,18},{8,12},{10,30},{12,8},{14,26},{16,20},{1... | collective-permute-start | bytes 208904 | tf_op jit(solution)/shard_map/ppermute | solution.py:271
  14.7 5.4 %collective-permute-start.8 = (f32[136,128]{1,0:T(8,128)S(1)}, f32[136,128]{1,0:T(8,128)S(1)}, u32[]{:S(2)}, u32[]{:S(2)}) collective-permute-start(f32[136,128]{1,0:T(8,128)S(1)} %pad_maximum_fusion), channel_id=1, source_target_pairs={{0,12},{2,18},{4,8},{6,22},{8,4},{10,26},{12,0},{14,30},{16,28},{1... | collective-permute-start | bytes 208904 | tf_op jit(solution)/shard_map/ppermute | solution.py:271
  14.7 5.6 %collective-permute-start.3 = (f32[144,128]{1,0:T(8,128)S(1)}, f32[144,128]{1,0:T(8,128)S(1)}, u32[]{:S(2)}, u32[]{:S(2)}) collective-permute-start(f32[144,128]{1,0:T(8,128)S(1)} %collective-permute-done.2.refs_2_), channel_id=1, source_target_pairs={{0,2},{2,0},{4,6},{6,4},{8,10},{10,8},{12,14},{14,12},{16,18},{18,... | collective-permute-start | bytes 221192 | tf_op jit(solution)/shard_map/ppermute | solution.py:265
  16.9 3.4 %collective-permute-start.7 = (f32[136,128]{1,0:T(8,128)S(1)}, f32[136,128]{1,0:T(8,128)S(1)}, u32[]{:S(2)}, u32[]{:S(2)}) collective-permute-start(f32[136,128]{1,0:T(8,128)S(1)} %collective-permute-done.6.refs_6_), channel_id=1, source_target_pairs={{0,2},{2,0},{4,6},{6,4},{8,10},{10,8},{12,14},{14,12},{16,18},{18,... | collective-permute-start | bytes 208904 | tf_op jit(solution)/shard_map/ppermute | solution.py:265
  17.7 3.3 %collective-permute-start.5 = (f32[136,128]{1,0:T(8,128)S(1)}, f32[136,128]{1,0:T(8,128)S(1)}, u32[]{:S(2)}, u32[]{:S(2)}) collective-permute-start(f32[136,128]{1,0:T(8,128)S(1)} %collective-permute-done.4.refs_4_), channel_id=1, source_target_pairs={{0,2},{2,0},{4,6},{6,4},{8,10},{10,8},{12,14},{14,12},{16,18},{18,... | collective-permute-start | bytes 208904 | tf_op jit(solution)/shard_map/ppermute | solution.py:265
  20.2 1.3 %collective-permute-start.9 = (f32[136,128]{1,0:T(8,128)S(1)}, f32[136,128]{1,0:T(8,128)S(1)}, u32[]{:S(2)}, u32[]{:S(2)}) collective-permute-start(f32[136,128]{1,0:T(8,128)S(1)} %collective-permute-done.8.refs_1_), channel_id=1, source_target_pairs={{0,2},{2,0},{4,6},{6,4},{8,10},{10,8},{12,14},{14,12},{16,18},{18,... | collective-permute-start | bytes 208904 | tf_op jit(solution)/shard_map/ppermute | solution.py:265
  22.5 4.0 %collective-permute-start.10 = (f32[72,128]{1,0:T(8,128)S(1)}, f32[72,128]{1,0:T(8,128)S(1)}, u32[]{:S(2)}, u32[]{:S(2)}) collective-permute-start(f32[72,128]{1,0:T(8,128)S(1)} %get-tuple-element.37.refs_4_), channel_id=1, source_target_pairs={{0,1},{1,0},{2,3},{3,2},{4,5},{5,4},{6,7},{7,6},{8,9},{9,8},{10,11... | collective-permute-start | bytes 110600 | tf_op jit(solution)/shard_map/ppermute | solution.py:275
  27.5 1.2 %collective-permute-start.11 = (f32[72,128]{1,0:T(8,128)S(1)}, f32[72,128]{1,0:T(8,128)S(1)}, u32[]{:S(2)}, u32[]{:S(2)}) collective-permute-start(f32[72,128]{1,0:T(8,128)S(1)} %get-tuple-element.39.refs_0_), channel_id=1, source_target_pairs={{0,2},{2,0},{4,6},{6,4},{8,10},{10,8},{12,14},{14,12},{16,18},{18,... | collective-permute-start | bytes 110600 | tf_op jit(solution)/shard_map/ppermute | solution.py:265
  27.5 5.2 %collective-permute-start.12 = (f32[144,128]{1,0:T(8,128)S(1)}, f32[144,128]{1,0:T(8,128)S(1)}, u32[]{:S(2)}, u32[]{:S(2)}) collective-permute-start(f32[144,128]{1,0:T(8,128)S(1)} %pad.11), channel_id=1, source_target_pairs={{0,8},{2,10},{4,12},{6,14},{8,0},{10,2},{12,4},{14,6},{16,24},{18,... | collective-permute-start | bytes 221192 | tf_op jit(solution)/shard_map/ppermute | solution.py:268
  28.8 6.8 %collective-permute-start.16 = (f32[136,128]{1,0:T(8,128)S(1)}, f32[136,128]{1,0:T(8,128)S(1)}, u32[]{:S(2)}, u32[]{:S(2)}) collective-permute-start(f32[136,128]{1,0:T(8,128)S(1)} %pad_maximum_fusion.1), channel_id=1, source_target_pairs={{0,24},{2,30},{4,28},{6,26},{8,16},{10,22},{12,20},{14,18},{16,8},... | collective-permute-start | bytes 208904 | tf_op jit(solution)/shard_map/ppermute | solution.py:271
  31.2 4.7 %collective-permute-start.14 = (f32[136,128]{1,0:T(8,128)S(1)}, f32[136,128]{1,0:T(8,128)S(1)}, u32[]{:S(2)}, u32[]{:S(2)}) collective-permute-start(f32[136,128]{1,0:T(8,128)S(1)} %pad_maximum_fusion.1), channel_id=1, source_target_pairs={{0,4},{2,22},{4,0},{6,18},{8,12},{10,30},{12,8},{14,26},{16,20},{1... | collective-permute-start | bytes 208904 | tf_op jit(solution)/shard_map/ppermute | solution.py:271
  32.4 5.6 %collective-permute-start.18 = (f32[136,128]{1,0:T(8,128)S(1)}, f32[136,128]{1,0:T(8,128)S(1)}, u32[]{:S(2)}, u32[]{:S(2)}) collective-permute-start(f32[136,128]{1,0:T(8,128)S(1)} %pad_maximum_fusion.1), channel_id=1, source_target_pairs={{0,12},{2,18},{4,8},{6,22},{8,4},{10,26},{12,0},{14,30},{16,28},{1... | collective-permute-start | bytes 208904 | tf_op jit(solution)/shard_map/ppermute | solution.py:271
  32.7 5.4 %collective-permute-start.13 = (f32[144,128]{1,0:T(8,128)S(1)}, f32[144,128]{1,0:T(8,128)S(1)}, u32[]{:S(2)}, u32[]{:S(2)}) collective-permute-start(f32[144,128]{1,0:T(8,128)S(1)} %collective-permute-done.12.refs_2_), channel_id=1, source_target_pairs={{0,2},{2,0},{4,6},{6,4},{8,10},{10,8},{12,14},{14,12},{16,18},{18,... | collective-permute-start | bytes 221192 | tf_op jit(solution)/shard_map/ppermute | solution.py:265
  35.6 2.5 %collective-permute-start.17 = (f32[136,128]{1,0:T(8,128)S(1)}, f32[136,128]{1,0:T(8,128)S(1)}, u32[]{:S(2)}, u32[]{:S(2)}) collective-permute-start(f32[136,128]{1,0:T(8,128)S(1)} %collective-permute-done.16.refs_6_), channel_id=1, source_target_pairs={{0,2},{2,0},{4,6},{6,4},{8,10},{10,8},{12,14},{14,12},{16,18},{18,... | collective-permute-start | bytes 208904 | tf_op jit(solution)/shard_map/ppermute | solution.py:265
  36.0 2.9 %collective-permute-start.15 = (f32[136,128]{1,0:T(8,128)S(1)}, f32[136,128]{1,0:T(8,128)S(1)}, u32[]{:S(2)}, u32[]{:S(2)}) collective-permute-start(f32[136,128]{1,0:T(8,128)S(1)} %collective-permute-done.14.refs_4_), channel_id=1, source_target_pairs={{0,2},{2,0},{4,6},{6,4},{8,10},{10,8},{12,14},{14,12},{16,18},{18,... | collective-permute-start | bytes 208904 | tf_op jit(solution)/shard_map/ppermute | solution.py:265
  37.9 1.3 %collective-permute-start.19 = (f32[136,128]{1,0:T(8,128)S(1)}, f32[136,128]{1,0:T(8,128)S(1)}, u32[]{:S(2)}, u32[]{:S(2)}) collective-permute-start(f32[136,128]{1,0:T(8,128)S(1)} %collective-permute-done.18.refs_1_), channel_id=1, source_target_pairs={{0,2},{2,0},{4,6},{6,4},{8,10},{10,8},{12,14},{14,12},{16,18},{18,... | collective-permute-start | bytes 208904 | tf_op jit(solution)/shard_map/ppermute | solution.py:265
  40.3 4.0 %collective-permute-start.20 = (f32[72,128]{1,0:T(8,128)S(1)}, f32[72,128]{1,0:T(8,128)S(1)}, u32[]{:S(2)}, u32[]{:S(2)}) collective-permute-start(f32[72,128]{1,0:T(8,128)S(1)} %get-tuple-element.43.refs_4_), channel_id=1, source_target_pairs={{0,1},{1,0},{2,3},{3,2},{4,5},{5,4},{6,7},{7,6},{8,9},{9,8},{10,11... | collective-permute-start | bytes 110600 | tf_op jit(solution)/shard_map/ppermute | solution.py:275
  45.3 1.2 %collective-permute-start.21 = (f32[72,128]{1,0:T(8,128)S(1)}, f32[72,128]{1,0:T(8,128)S(1)}, u32[]{:S(2)}, u32[]{:S(2)}) collective-permute-start(f32[72,128]{1,0:T(8,128)S(1)} %get-tuple-element.45.refs_0_), channel_id=1, source_target_pairs={{0,2},{2,0},{4,6},{6,4},{8,10},{10,8},{12,14},{14,12},{16,18},{18,... | collective-permute-start | bytes 110600 | tf_op jit(solution)/shard_map/ppermute | solution.py:265
  45.3 5.2 %collective-permute-start.22 = (f32[144,128]{1,0:T(8,128)S(1)}, f32[144,128]{1,0:T(8,128)S(1)}, u32[]{:S(2)}, u32[]{:S(2)}) collective-permute-start(f32[144,128]{1,0:T(8,128)S(1)} %pad.12), channel_id=1, source_target_pairs={{0,8},{2,10},{4,12},{6,14},{8,0},{10,2},{12,4},{14,6},{16,24},{18,... | collective-permute-start | bytes 221192 | tf_op jit(solution)/shard_map/ppermute | solution.py:268
  46.6 6.3 %collective-permute-start.26 = (f32[136,128]{1,0:T(8,128)S(1)}, f32[136,128]{1,0:T(8,128)S(1)}, u32[]{:S(2)}, u32[]{:S(2)}) collective-permute-start(f32[136,128]{1,0:T(8,128)S(1)} %pad_maximum_fusion.2), channel_id=1, source_target_pairs={{0,24},{2,18},{4,28},{6,22},{8,16},{10,26},{12,20},{14,30},{16,8},... | collective-permute-start | bytes 208904 | tf_op jit(solution)/shard_map/ppermute | solution.py:271
  49.0 5.5 %collective-permute-start.24 = (f32[136,128]{1,0:T(8,128)S(1)}, f32[136,128]{1,0:T(8,128)S(1)}, u32[]{:S(2)}, u32[]{:S(2)}) collective-permute-start(f32[136,128]{1,0:T(8,128)S(1)} %pad_maximum_fusion.2), channel_id=1, source_target_pairs={{0,12},{2,22},{4,8},{6,18},{8,4},{10,30},{12,0},{14,26},{16,28},{1... | collective-permute-start | bytes 208904 | tf_op jit(solution)/shard_map/ppermute | solution.py:271
  49.6 6.5 %collective-permute-start.28 = (f32[136,128]{1,0:T(8,128)S(1)}, f32[136,128]{1,0:T(8,128)S(1)}, u32[]{:S(2)}, u32[]{:S(2)}) collective-permute-start(f32[136,128]{1,0:T(8,128)S(1)} %pad_maximum_fusion.2), channel_id=1, source_target_pairs={{0,4},{2,30},{4,0},{6,26},{8,12},{10,22},{12,8},{14,18},{16,20},{1... | collective-permute-start | bytes 208904 | tf_op jit(solution)/shard_map/ppermute | solution.py:271
  50.5 5.6 %collective-permute-start.23 = (f32[144,128]{1,0:T(8,128)S(1)}, f32[144,128]{1,0:T(8,128)S(1)}, u32[]{:S(2)}, u32[]{:S(2)}) collective-permute-start(f32[144,128]{1,0:T(8,128)S(1)} %collective-permute-done.22.refs_2_), channel_id=1, source_target_pairs={{0,2},{2,0},{4,6},{6,4},{8,10},{10,8},{12,14},{14,12},{16,18},{18,... | collective-permute-start | bytes 221192 | tf_op jit(solution)/shard_map/ppermute | solution.py:265
  52.9 3.3 %collective-permute-start.27 = (f32[136,128]{1,0:T(8,128)S(1)}, f32[136,128]{1,0:T(8,128)S(1)}, u32[]{:S(2)}, u32[]{:S(2)}) collective-permute-start(f32[136,128]{1,0:T(8,128)S(1)} %collective-permute-done.26.refs_6_), channel_id=1, source_target_pairs={{0,2},{2,0},{4,6},{6,4},{8,10},{10,8},{12,14},{14,12},{16,18},{18,... | collective-permute-start | bytes 208904 | tf_op jit(solution)/shard_map/ppermute | solution.py:265
  54.6 2.1 %collective-permute-start.25 = (f32[136,128]{1,0:T(8,128)S(1)}, f32[136,128]{1,0:T(8,128)S(1)}, u32[]{:S(2)}, u32[]{:S(2)}) collective-permute-start(f32[136,128]{1,0:T(8,128)S(1)} %collective-permute-done.24.refs_4_), channel_id=1, source_target_pairs={{0,2},{2,0},{4,6},{6,4},{8,10},{10,8},{12,14},{14,12},{16,18},{18,... | collective-permute-start | bytes 208904 | tf_op jit(solution)/shard_map/ppermute | solution.py:265
  56.2 1.3 %collective-permute-start.29 = (f32[136,128]{1,0:T(8,128)S(1)}, f32[136,128]{1,0:T(8,128)S(1)}, u32[]{:S(2)}, u32[]{:S(2)}) collective-permute-start(f32[136,128]{1,0:T(8,128)S(1)} %collective-permute-done.28.refs_1_), channel_id=1, source_target_pairs={{0,2},{2,0},{4,6},{6,4},{8,10},{10,8},{12,14},{14,12},{16,18},{18,... | collective-permute-start | bytes 208904 | tf_op jit(solution)/shard_map/ppermute | solution.py:265
  58.5 4.0 %collective-permute-start.30 = (f32[72,128]{1,0:T(8,128)S(1)}, f32[72,128]{1,0:T(8,128)S(1)}, u32[]{:S(2)}, u32[]{:S(2)}) collective-permute-start(f32[72,128]{1,0:T(8,128)S(1)} %get-tuple-element.49.refs_3_), channel_id=1, source_target_pairs={{0,1},{1,0},{2,3},{3,2},{4,5},{5,4},{6,7},{7,6},{8,9},{9,8},{10,11... | collective-permute-start | bytes 110600 | tf_op jit(solution)/shard_map/ppermute | solution.py:275
  62.8 1.2 %collective-permute-start.32 = (f32[8,128]{1,0:T(8,128)S(1)}, f32[8,128]{1,0:T(8,128)S(1)}, u32[]{:S(2)}, u32[]{:S(2)}) collective-permute-start(f32[8,128]{1,0:T(8,128)S(1)} %get-tuple-element.50), channel_id=1, source_target_pairs={{0,2},{2,0},{4,6},{6,4},{8,10},{10,8},{12,14},{14,12},{16,18},{18,... | collective-permute-start | bytes 12296 | tf_op jit(solution)/shard_map/ppermute | solution.py:265
  62.8 5.8 %collective-permute-start.31 = (f32[8,128]{1,0:T(8,128)S(1)}, f32[8,128]{1,0:T(8,128)S(1)}, u32[]{:S(2)}, u32[]{:S(2)}) collective-permute-start(f32[8,128]{1,0:T(8,128)S(1)} %get-tuple-element.50), channel_id=1, source_target_pairs={{0,4},{2,6},{4,0},{6,2},{8,12},{10,14},{12,8},{14,10},{16,20},{18,... | collective-permute-start | bytes 12296 | tf_op jit(solution)/shard_map/ppermute | solution.py:268
  63.9 5.4 %collective-permute-start.35 = (f32[8,128]{1,0:T(8,128)S(1)}, f32[8,128]{1,0:T(8,128)S(1)}, u32[]{:S(2)}, u32[]{:S(2)}) collective-permute-start(f32[8,128]{1,0:T(8,128)S(1)} %add.39), channel_id=1, source_target_pairs={{0,24},{2,30},{4,28},{6,26},{8,16},{10,22},{12,20},{14,18},{16,8},... | collective-permute-start | bytes 12296 | tf_op jit(solution)/shard_map/ppermute | solution.py:271
  66.1 4.5 %collective-permute-start.34 = (f32[8,128]{1,0:T(8,128)S(1)}, f32[8,128]{1,0:T(8,128)S(1)}, u32[]{:S(2)}, u32[]{:S(2)}) collective-permute-start(f32[8,128]{1,0:T(8,128)S(1)} %add.39), channel_id=1, source_target_pairs={{0,12},{2,22},{4,8},{6,18},{8,4},{10,30},{12,0},{14,26},{16,28},{1... | collective-permute-start | bytes 12296 | tf_op jit(solution)/shard_map/ppermute | solution.py:271
  66.5 4.1 %collective-permute-start.33 = (f32[8,128]{1,0:T(8,128)S(1)}, f32[8,128]{1,0:T(8,128)S(1)}, u32[]{:S(2)}, u32[]{:S(2)}) collective-permute-start(f32[8,128]{1,0:T(8,128)S(1)} %add.39), channel_id=1, source_target_pairs={{0,8},{2,18},{4,12},{6,22},{8,0},{10,26},{12,4},{14,30},{16,24},{1... | collective-permute-start | bytes 12296 | tf_op jit(solution)/shard_map/ppermute | solution.py:271
  70.6 1.2 %collective-permute-start.36 = (f32[8,128]{1,0:T(8,128)S(1)}, f32[8,128]{1,0:T(8,128)S(1)}, u32[]{:S(2)}, u32[]{:S(2)}) collective-permute-start(f32[8,128]{1,0:T(8,128)S(1)} %add_add_fusion.half), channel_id=1, source_target_pairs={{0,2},{2,0},{4,6},{6,4},{8,10},{10,8},{12,14},{14,12},{16,18},{18,... | collective-permute-start | bytes 12296 | tf_op jit(solution)/shard_map/ppermute | solution.py:265

commit v8 on v6

--- a/solution.py
+++ b/solution.py
@@ -248,7 +248,7 @@
 
 def chip_steps(chips):
     if chips == 8:
-        return (2, [(3, 4), (1, 5), (6, 7)]), (1, [(2, 4), (3, 5), (6, 7)])
+        return (2, [(1, 4), (3, 5), (6, 7)]), (1, [(2, 4), (3, 5), (6, 7)])
     steps = 1, [(m, m + 1) for m in range(2, chips, 2)]
     return steps, steps
 

time: 72.6 us -> 72.6 us (level)
  starting transfers between devices: 40.5 us -> 38.3 us
  waiting for transfers between devices: 19.8 us -> 22 us
    ppermute x12, waiting for transfers between devices: 6.33 us -> 9.69 us  [to_chips(): lax.ppermute(x, 'row', [(r, r ^ 2 * step[r % 2]) for r in range(n_row)])]
    ppermute x17, starting transfers between devices: 12.2 us -> 9.15 us  [swap(): return lax.ppermute(x, 'row', [(r, r ^ 1) for r in range(n_row)])]
    ppermute x4, starting transfers between devices: 3.08 us -> 4.43 us  [to_near(): return lax.ppermute(x, 'row', [(r, r ^ 2 * steps[0]) for r in range(n_row)])]
    ppermute x17, waiting for transfers between devices: 5.46 us -> 4.26 us  [swap(): return lax.ppermute(x, 'row', [(r, r ^ 1) for r in range(n_row)])]
where the time goes in v8:
time: 72.6 us; the launch traced here: 72.4 us
  starting transfers between devices  38.3 us (53%)
  waiting for transfers between devices  22 us (30%)
  Pallas kernels  11 us (15%)
  between operations  0.82 us (1%)
    ppermute x12, starting transfers between devices, to_chips(): lax.ppermute(x, 'row', [(r, r ^ 2 * step[r % 2]) for r in range(n_row)])  17.1 us
    ppermute x12, waiting for transfers between devices, to_chips(): lax.ppermute(x, 'row', [(r, r ^ 2 * step[r % 2]) for r in range(n_row)])  9.69 us
    ppermute x17, starting transfers between devices, swap(): return lax.ppermute(x, 'row', [(r, r ^ 1) for r in range(n_row)])  9.15 us
    pallas_call x12, Pallas kernels, call(): pl.pallas_call(body, out_shape=[jax.ShapeDtypeStruct(s, f32) for s in out...  8.09 us
    ppermute x4, waiting for transfers between devices, around_col(): lax.ppermute(x, 'col', [(i, (i - s) % n_col) for i in range(n_col)])  8.01 us
    ppermute x4, starting transfers between devices, around_col(): lax.ppermute(x, 'col', [(i, (i - s) % n_col) for i in range(n_col)])  7.65 us
    ppermute x4, starting transfers between devices, to_near(): return lax.ppermute(x, 'row', [(r, r ^ 2 * steps[0]) for r in range(n_row)])  4.43 us
    ppermute x17, waiting for transfers between devices, swap(): return lax.ppermute(x, 'row', [(r, r ^ 1) for r in range(n_row)])  4.26 us
  transfers between devices with their start and end apart: 37, of which 19 were waited for; matrix products, arithmetic and copies ran while one was open for 0% of the time, Pallas kernels for 6%

profile of v8, /device:TPU:0, one launch (start us, length us, event | category | flops | bytes accessed | tf_op | source)
XLA Modules:
  0.0 72.4 jit_solution(17227834024868115115)
XLA Ops:
  0.6 3.0 %collective-permute-start = (f32[248,128]{1,0:T(8,128)}, f32[248,128]{1,0:T(8,128)S(1)}, u32[]{:S(2)}, u32[]{:S(2)}) collective-permute-start(f32[248,128]{1,0:T(8,128)} %bitcast.7), channel_id=1, source_target_pairs={{0,1},{1,0},{2,3},{3,2},{4,5},{5,4},{6,7},{7,6},{8,9},{9,8},{10,11... | collective-permute-start | bytes 380936 | tf_op jit(solution)/shard_map/ppermute | solution.py:274
  3.7 2.9 %shard_map.59 = (bf16[16384,256]{1,0:T(8,128)(2,1)S(1)}, f32[8,128]{1,0:T(8,128)S(1)}, f32[128,128]{1,0:T(8,128)S(1)}, f32[248,128]{1,0:T(8,128)S(1)}) custom-call(f32[8192,128]{1,0:T(8,128)} %bitcast.6, s32[1,64]{1,0:T(1,128)} %bitcast.9, s32[1,64]{1,0:T(1,128)} %bitcast.10, f32[248,128]{1,0:T(8,128)} %bitcast.8, f32[8,128]{1,0:T(8,128)S(1)} %broadcast_in_dim.3.place), custom_call_target="tpu_custom_call" | custom-call | bytes 4194304 | tf_op jit(solution)/shard_map/pallas_call | solution.py:216
  6.6 0.7 collective-permute-done.refs_1_
  7.3 0.8 %shard_map.60 = (f32[512,128]{1,0:T(8,128)S(1)}, f32[72,128]{1,0:T(8,128)S(1)}) custom-call(bf16[16384,256]{1,0:T(8,128)(2,1)S(1)} %get-tuple-element.31.tiles.refs_0_, f32[248,128]{1,0:T(8,128)S(1)} %get-tuple-element.32.refs_0_, f32[248,128]{1,0:T(8,128)S(1)} %collective-permute-done.refs_1_, ...), custom_call_target="tpu_custom_call" | custom-call | tf_op jit(solution)/shard_map/pallas_call | solution.py:240
  8.1 1.9 %collective-permute-start.2 = (f32[144,128]{1,0:T(8,128)S(1)}, f32[144,128]{1,0:T(8,128)S(1)}, u32[]{:S(2)}, u32[]{:S(2)}) collective-permute-start(f32[144,128]{1,0:T(8,128)S(1)} %pad.10), channel_id=1, source_target_pairs={{0,8},{2,10},{4,12},{6,14},{8,0},{10,2},{12,4},{14,6},{16,24},{18,... | collective-permute-start | bytes 221192 | tf_op jit(solution)/shard_map/ppermute | solution.py:267
  10.1 3.2 %collective-permute-start.6 = (f32[136,128]{1,0:T(8,128)S(1)}, f32[136,128]{1,0:T(8,128)S(1)}, u32[]{:S(2)}, u32[]{:S(2)}) collective-permute-start(f32[136,128]{1,0:T(8,128)S(1)} %pad_maximum_fusion), channel_id=1, source_target_pairs={{0,24},{2,30},{4,28},{6,26},{8,16},{10,22},{12,20},{14,18},{16,8},... | collective-permute-start | bytes 208904 | tf_op jit(solution)/shard_map/ppermute | solution.py:270
  13.2 0.9 %collective-permute-start.4 = (f32[136,128]{1,0:T(8,128)S(1)}, f32[136,128]{1,0:T(8,128)S(1)}, u32[]{:S(2)}, u32[]{:S(2)}) collective-permute-start(f32[136,128]{1,0:T(8,128)S(1)} %pad_maximum_fusion), channel_id=1, source_target_pairs={{0,12},{2,22},{4,8},{6,18},{8,4},{10,30},{12,0},{14,26},{16,28},{1... | collective-permute-start | bytes 208904 | tf_op jit(solution)/shard_map/ppermute | solution.py:270
  14.2 0.5 collective-permute-start.8
  14.7 1.7 %collective-permute-start.3 = (f32[144,128]{1,0:T(8,128)S(1)}, f32[144,128]{1,0:T(8,128)S(1)}, u32[]{:S(2)}, u32[]{:S(2)}) collective-permute-start(f32[144,128]{1,0:T(8,128)S(1)} %collective-permute-done.2.refs_2_), channel_id=1, source_target_pairs={{0,2},{2,0},{4,6},{6,4},{8,10},{10,8},{12,14},{14,12},{16,18},{18,... | collective-permute-start | bytes 221192 | tf_op jit(solution)/shard_map/ppermute | solution.py:264
  17.0 1.5 %collective-permute-done.4.refs_4_ = f32[136,128]{1,0:T(8,128)S(1)} collective-permute-done((f32[136,128]{1,0:T(8,128)S(1)}, f32[136,128]{1,0:T(8,128)S(1)}, u32[]{:S(2)}, u32[]{:S(2)}) %collective-permute-start.4) | collective-permute-done | bytes 69664 | tf_op jit(solution)/shard_map/ppermute | solution.py:270
  18.5 1.8 %collective-permute-start.5 = (f32[136,128]{1,0:T(8,128)S(1)}, f32[136,128]{1,0:T(8,128)S(1)}, u32[]{:S(2)}, u32[]{:S(2)}) collective-permute-start(f32[136,128]{1,0:T(8,128)S(1)} %collective-permute-done.4.refs_4_), channel_id=1, source_target_pairs={{0,2},{2,0},{4,6},{6,4},{8,10},{10,8},{12,14},{14,12},{16,18},{18,... | collective-permute-start | bytes 208904 | tf_op jit(solution)/shard_map/ppermute | solution.py:264
  20.3 0.9 %collective-permute-done.5.refs_5_ = f32[136,128]{1,0:T(8,128)S(1)} collective-permute-done((f32[136,128]{1,0:T(8,128)S(1)}, f32[136,128]{1,0:T(8,128)S(1)}, u32[]{:S(2)}, u32[]{:S(2)}) %collective-permute-start.5) | collective-permute-done | bytes 69664 | tf_op jit(solution)/shard_map/ppermute | solution.py:264
  21.6 1.0 %shard_map.62 = (f32[512,128]{1,0:T(8,128)S(1)}, f32[72,128]{1,0:T(8,128)S(1)}, f32[8,128]{1,0:T(8,128)S(1)}) custom-call(bf16[16384,256]{1,0:T(8,128)(2,1)S(1)} %get-tuple-element.31.tiles.refs_0_, f32[520,128]{1,0:T(8,128)S(1)} %shard_map.61.refs_0_, f32[136,128]{1,0:T(8,128)S(1)} %collective-permute-done.8.refs_1_, ...), custom_call_target="tpu_custom_call" | custom-call | tf_op jit(solution)/shard_map/pallas_call | solution.py:240
  22.6 1.5 %collective-permute-start.10 = (f32[72,128]{1,0:T(8,128)S(1)}, f32[72,128]{1,0:T(8,128)S(1)}, u32[]{:S(2)}, u32[]{:S(2)}) collective-permute-start(f32[72,128]{1,0:T(8,128)S(1)} %get-tuple-element.37.refs_4_), channel_id=1, source_target_pairs={{0,1},{1,0},{2,3},{3,2},{4,5},{5,4},{6,7},{7,6},{8,9},{9,8},{10,11... | collective-permute-start | bytes 110600 | tf_op jit(solution)/shard_map/ppermute | solution.py:274
  24.2 2.4 %collective-permute-done.10.refs_5_ = f32[72,128]{1,0:T(8,128)S(1)} collective-permute-done((f32[72,128]{1,0:T(8,128)S(1)}, f32[72,128]{1,0:T(8,128)S(1)}, u32[]{:S(2)}, u32[]{:S(2)}) %collective-permute-start.10) | collective-permute-done | bytes 36896 | tf_op jit(solution)/shard_map/ppermute | solution.py:274
  26.6 1.0 %shard_map.63 = (f32[512,128]{1,0:T(8,128)S(1)}, f32[72,128]{1,0:T(8,128)S(1)}, f32[8,128]{1,0:T(8,128)S(1)}) custom-call(bf16[16384,256]{1,0:T(8,128)(2,1)S(1)} %get-tuple-element.31.tiles.refs_0_, f32[8,128]{1,0:T(8,128)S(1)} %get-tuple-element.30.refs_2_.refs_3_.refs_1_.refs_5_.refs_0_, f32[512,128]{1,0:T(8,128)S(1)} %get-tuple-element.34.refs_2_, ...), custom_call_target="tpu_custom_call" | custom-call | tf_op jit(solution)/shard_map/pallas_call | solution.py:240
  27.6 0.9 %collective-permute-start.12 = (f32[144,128]{1,0:T(8,128)S(1)}, f32[144,128]{1,0:T(8,128)S(1)}, u32[]{:S(2)}, u32[]{:S(2)}) collective-permute-start(f32[144,128]{1,0:T(8,128)S(1)} %pad.11), channel_id=1, source_target_pairs={{0,8},{2,10},{4,12},{6,14},{8,0},{10,2},{12,4},{14,6},{16,24},{18,... | collective-permute-start | bytes 221192 | tf_op jit(solution)/shard_map/ppermute | solution.py:267
  28.9 2.3 %collective-permute-start.16 = (f32[136,128]{1,0:T(8,128)S(1)}, f32[136,128]{1,0:T(8,128)S(1)}, u32[]{:S(2)}, u32[]{:S(2)}) collective-permute-start(f32[136,128]{1,0:T(8,128)S(1)} %pad_maximum_fusion.1), channel_id=1, source_target_pairs={{0,24},{2,30},{4,28},{6,26},{8,16},{10,22},{12,20},{14,18},{16,8},... | collective-permute-start | bytes 208904 | tf_op jit(solution)/shard_map/ppermute | solution.py:270
  31.2 0.6 collective-permute-start.14
  31.8 0.9 %collective-permute-start.18 = (f32[136,128]{1,0:T(8,128)S(1)}, f32[136,128]{1,0:T(8,128)S(1)}, u32[]{:S(2)}, u32[]{:S(2)}) collective-permute-start(f32[136,128]{1,0:T(8,128)S(1)} %pad_maximum_fusion.1), channel_id=1, source_target_pairs={{0,4},{2,18},{4,0},{6,22},{8,12},{10,26},{12,8},{14,30},{16,20},{1... | collective-permute-start | bytes 208904 | tf_op jit(solution)/shard_map/ppermute | solution.py:270
  32.7 1.7 %collective-permute-start.13 = (f32[144,128]{1,0:T(8,128)S(1)}, f32[144,128]{1,0:T(8,128)S(1)}, u32[]{:S(2)}, u32[]{:S(2)}) collective-permute-start(f32[144,128]{1,0:T(8,128)S(1)} %collective-permute-done.12.refs_2_), channel_id=1, source_target_pairs={{0,2},{2,0},{4,6},{6,4},{8,10},{10,8},{12,14},{14,12},{16,18},{18,... | collective-permute-start | bytes 221192 | tf_op jit(solution)/shard_map/ppermute | solution.py:264
  34.4 1.5 %collective-permute-done.16.refs_6_ = f32[136,128]{1,0:T(8,128)S(1)} collective-permute-done((f32[136,128]{1,0:T(8,128)S(1)}, f32[136,128]{1,0:T(8,128)S(1)}, u32[]{:S(2)}, u32[]{:S(2)}) %collective-permute-start.16) | collective-permute-done | bytes 69664 | tf_op jit(solution)/shard_map/ppermute | solution.py:270
  35.9 1.4 %collective-permute-done.14.refs_4_ = f32[136,128]{1,0:T(8,128)S(1)} collective-permute-done((f32[136,128]{1,0:T(8,128)S(1)}, f32[136,128]{1,0:T(8,128)S(1)}, u32[]{:S(2)}, u32[]{:S(2)}) %collective-permute-start.14) | collective-permute-done | bytes 69664 | tf_op jit(solution)/shard_map/ppermute | solution.py:270
  37.2 0.8 %collective-permute-start.15 = (f32[136,128]{1,0:T(8,128)S(1)}, f32[136,128]{1,0:T(8,128)S(1)}, u32[]{:S(2)}, u32[]{:S(2)}) collective-permute-start(f32[136,128]{1,0:T(8,128)S(1)} %collective-permute-done.14.refs_4_), channel_id=1, source_target_pairs={{0,2},{2,0},{4,6},{6,4},{8,10},{10,8},{12,14},{14,12},{16,18},{18,... | collective-permute-start | bytes 208904 | tf_op jit(solution)/shard_map/ppermute | solution.py:264
  38.3 0.7 collective-permute-done.15.refs_5_
  39.4 1.0 %shard_map.65 = (f32[512,128]{1,0:T(8,128)S(1)}, f32[72,128]{1,0:T(8,128)S(1)}, f32[8,128]{1,0:T(8,128)S(1)}) custom-call(bf16[16384,256]{1,0:T(8,128)(2,1)S(1)} %get-tuple-element.31.tiles.refs_0_, f32[520,128]{1,0:T(8,128)S(1)} %shard_map.64.refs_0_, f32[136,128]{1,0:T(8,128)S(1)} %collective-permute-done.18.refs_1_, ...), custom_call_target="tpu_custom_call" | custom-call | tf_op jit(solution)/shard_map/pallas_call | solution.py:240
  40.4 1.5 %collective-permute-start.20 = (f32[72,128]{1,0:T(8,128)S(1)}, f32[72,128]{1,0:T(8,128)S(1)}, u32[]{:S(2)}, u32[]{:S(2)}) collective-permute-start(f32[72,128]{1,0:T(8,128)S(1)} %get-tuple-element.43.refs_4_), channel_id=1, source_target_pairs={{0,1},{1,0},{2,3},{3,2},{4,5},{5,4},{6,7},{7,6},{8,9},{9,8},{10,11... | collective-permute-start | bytes 110600 | tf_op jit(solution)/shard_map/ppermute | solution.py:274
  42.0 2.4 %collective-permute-done.20.refs_5_ = f32[72,128]{1,0:T(8,128)S(1)} collective-permute-done((f32[72,128]{1,0:T(8,128)S(1)}, f32[72,128]{1,0:T(8,128)S(1)}, u32[]{:S(2)}, u32[]{:S(2)}) %collective-permute-start.20) | collective-permute-done | bytes 36896 | tf_op jit(solution)/shard_map/ppermute | solution.py:274
  44.4 1.0 %shard_map.66 = (f32[512,128]{1,0:T(8,128)S(1)}, f32[72,128]{1,0:T(8,128)S(1)}, f32[8,128]{1,0:T(8,128)S(1)}) custom-call(bf16[16384,256]{1,0:T(8,128)(2,1)S(1)} %get-tuple-element.31.tiles.refs_0_, f32[8,128]{1,0:T(8,128)S(1)} %get-tuple-element.30.refs_2_.refs_3_.refs_1_.refs_5_.refs_0_, f32[512,128]{1,0:T(8,128)S(1)} %get-tuple-element.38.refs_2_, ...), custom_call_target="tpu_custom_call" | custom-call | tf_op jit(solution)/shard_map/pallas_call | solution.py:240
  45.5 0.7 %collective-permute-start.22 = (f32[144,128]{1,0:T(8,128)S(1)}, f32[144,128]{1,0:T(8,128)S(1)}, u32[]{:S(2)}, u32[]{:S(2)}) collective-permute-start(f32[144,128]{1,0:T(8,128)S(1)} %pad.12), channel_id=1, source_target_pairs={{0,8},{2,10},{4,12},{6,14},{8,0},{10,2},{12,4},{14,6},{16,24},{18,... | collective-permute-start | bytes 221192 | tf_op jit(solution)/shard_map/ppermute | solution.py:267
  46.7 2.3 %collective-permute-start.26 = (f32[136,128]{1,0:T(8,128)S(1)}, f32[136,128]{1,0:T(8,128)S(1)}, u32[]{:S(2)}, u32[]{:S(2)}) collective-permute-start(f32[136,128]{1,0:T(8,128)S(1)} %pad_maximum_fusion.2), channel_id=1, source_target_pairs={{0,24},{2,30},{4,28},{6,26},{8,16},{10,22},{12,20},{14,18},{16,8},... | collective-permute-start | bytes 208904 | tf_op jit(solution)/shard_map/ppermute | solution.py:270
  49.0 0.6 collective-permute-start.24
  49.6 0.9 %collective-permute-start.28 = (f32[136,128]{1,0:T(8,128)S(1)}, f32[136,128]{1,0:T(8,128)S(1)}, u32[]{:S(2)}, u32[]{:S(2)}) collective-permute-start(f32[136,128]{1,0:T(8,128)S(1)} %pad_maximum_fusion.2), channel_id=1, source_target_pairs={{0,4},{2,18},{4,0},{6,22},{8,12},{10,26},{12,8},{14,30},{16,20},{1... | collective-permute-start | bytes 208904 | tf_op jit(solution)/shard_map/ppermute | solution.py:270
  50.5 1.7 %collective-permute-start.23 = (f32[144,128]{1,0:T(8,128)S(1)}, f32[144,128]{1,0:T(8,128)S(1)}, u32[]{:S(2)}, u32[]{:S(2)}) collective-permute-start(f32[144,128]{1,0:T(8,128)S(1)} %collective-permute-done.22.refs_2_), channel_id=1, source_target_pairs={{0,2},{2,0},{4,6},{6,4},{8,10},{10,8},{12,14},{14,12},{16,18},{18,... | collective-permute-start | bytes 221192 | tf_op jit(solution)/shard_map/ppermute | solution.py:264
  52.2 1.5 %collective-permute-done.26.refs_6_ = f32[136,128]{1,0:T(8,128)S(1)} collective-permute-done((f32[136,128]{1,0:T(8,128)S(1)}, f32[136,128]{1,0:T(8,128)S(1)}, u32[]{:S(2)}, u32[]{:S(2)}) %collective-permute-start.26) | collective-permute-done | bytes 69664 | tf_op jit(solution)/shard_map/ppermute | solution.py:270
  53.7 1.3 %collective-permute-done.24.refs_4_ = f32[136,128]{1,0:T(8,128)S(1)} collective-permute-done((f32[136,128]{1,0:T(8,128)S(1)}, f32[136,128]{1,0:T(8,128)S(1)}, u32[]{:S(2)}, u32[]{:S(2)}) %collective-permute-start.24) | collective-permute-done | bytes 69664 | tf_op jit(solution)/shard_map/ppermute | solution.py:270
  55.1 0.8 %collective-permute-start.25 = (f32[136,128]{1,0:T(8,128)S(1)}, f32[136,128]{1,0:T(8,128)S(1)}, u32[]{:S(2)}, u32[]{:S(2)}) collective-permute-start(f32[136,128]{1,0:T(8,128)S(1)} %collective-permute-done.24.refs_4_), channel_id=1, source_target_pairs={{0,2},{2,0},{4,6},{6,4},{8,10},{10,8},{12,14},{14,12},{16,18},{18,... | collective-permute-start | bytes 208904 | tf_op jit(solution)/shard_map/ppermute | solution.py:264
  56.1 0.7 collective-permute-done.25.refs_5_
  57.2 1.0 %shard_map.68 = (f32[512,128]{1,0:T(8,128)S(1)}, f32[72,128]{1,0:T(8,128)S(1)}, f32[8,128]{1,0:T(8,128)S(1)}) custom-call(bf16[16384,256]{1,0:T(8,128)(2,1)S(1)} %get-tuple-element.31.tiles.refs_0_, f32[520,128]{1,0:T(8,128)S(1)} %shard_map.67.refs_0_, f32[136,128]{1,0:T(8,128)S(1)} %collective-permute-done.28.refs_1_, ...), custom_call_target="tpu_custom_call" | custom-call | tf_op jit(solution)/shard_map/pallas_call | solution.py:240
  58.2 1.5 %collective-permute-start.30 = (f32[72,128]{1,0:T(8,128)S(1)}, f32[72,128]{1,0:T(8,128)S(1)}, u32[]{:S(2)}, u32[]{:S(2)}) collective-permute-start(f32[72,128]{1,0:T(8,128)S(1)} %get-tuple-element.49.refs_3_), channel_id=1, source_target_pairs={{0,1},{1,0},{2,3},{3,2},{4,5},{5,4},{6,7},{7,6},{8,9},{9,8},{10,11... | collective-permute-start | bytes 110600 | tf_op jit(solution)/shard_map/ppermute | solution.py:274
  59.8 2.4 %collective-permute-done.30.refs_4_ = f32[72,128]{1,0:T(8,128)S(1)} collective-permute-done((f32[72,128]{1,0:T(8,128)S(1)}, f32[72,128]{1,0:T(8,128)S(1)}, u32[]{:S(2)}, u32[]{:S(2)}) %collective-permute-start.30) | collective-permute-done | bytes 36896 | tf_op jit(solution)/shard_map/ppermute | solution.py:274
  62.6 1.0 %collective-permute-start.31 = (f32[8,128]{1,0:T(8,128)S(1)}, f32[8,128]{1,0:T(8,128)S(1)}, u32[]{:S(2)}, u32[]{:S(2)}) collective-permute-start(f32[8,128]{1,0:T(8,128)S(1)} %get-tuple-element.50), channel_id=1, source_target_pairs={{0,4},{2,6},{4,0},{6,2},{8,12},{10,14},{12,8},{14,10},{16,20},{18,... | collective-permute-start | bytes 12296 | tf_op jit(solution)/shard_map/ppermute | solution.py:267
  63.7 2.3 %collective-permute-start.35 = (f32[8,128]{1,0:T(8,128)S(1)}, f32[8,128]{1,0:T(8,128)S(1)}, u32[]{:S(2)}, u32[]{:S(2)}) collective-permute-start(f32[8,128]{1,0:T(8,128)S(1)} %add.39), channel_id=1, source_target_pairs={{0,24},{2,30},{4,28},{6,26},{8,16},{10,22},{12,20},{14,18},{16,8},... | collective-permute-start | bytes 12296 | tf_op jit(solution)/shard_map/ppermute | solution.py:270
  66.0 2.5 %collective-permute-start.33 = (f32[8,128]{1,0:T(8,128)S(1)}, f32[8,128]{1,0:T(8,128)S(1)}, u32[]{:S(2)}, u32[]{:S(2)}) collective-permute-start(f32[8,128]{1,0:T(8,128)S(1)} %add.39), channel_id=1, source_target_pairs={{0,8},{2,18},{4,12},{6,22},{8,0},{10,26},{12,4},{14,30},{16,24},{1... | collective-permute-start | bytes 12296 | tf_op jit(solution)/shard_map/ppermute | solution.py:270
  68.6 0.6 collective-permute-done.35
  69.2 1.4 %collective-permute-done.34 = f32[8,128]{1,0:T(8,128)S(1)} collective-permute-done((f32[8,128]{1,0:T(8,128)S(1)}, f32[8,128]{1,0:T(8,128)S(1)}, u32[]{:S(2)}, u32[]{:S(2)}) %collective-permute-start.34) | collective-permute-done | bytes 4128 | tf_op jit(solution)/shard_map/ppermute | solution.py:270
  70.8 1.0 %collective-permute-done.36.other = f32[8,128]{1,0:T(8,128)S(1)} collective-permute-done((f32[8,128]{1,0:T(8,128)S(1)}, f32[8,128]{1,0:T(8,128)S(1)}, u32[]{:S(2)}, u32[]{:S(2)}) %collective-permute-start.36) | collective-permute-done | bytes 4128 | tf_op jit(solution)/shard_map/ppermute | solution.py:264
  71.8 0.6 shard_map.71
  (62 shorter events, 4.1 us)
Async XLA Ops:
  0.6 6.7 %collective-permute-start = (f32[248,128]{1,0:T(8,128)}, f32[248,128]{1,0:T(8,128)S(1)}, u32[]{:S(2)}, u32[]{:S(2)}) collective-permute-start(f32[248,128]{1,0:T(8,128)} %bitcast.7), channel_id=1, source_target_pairs={{0,1},{1,0},{2,3},{3,2},{4,5},{5,4},{6,7},{7,6},{8,9},{9,8},{10,11... | collective-permute-start | bytes 380936 | tf_op jit(solution)/shard_map/ppermute | solution.py:274
  8.1 1.9 %collective-permute-start.1 = (f32[72,128]{1,0:T(8,128)S(1)}, f32[72,128]{1,0:T(8,128)S(1)}, u32[]{:S(2)}, u32[]{:S(2)}) collective-permute-start(f32[72,128]{1,0:T(8,128)S(1)} %get-tuple-element.35.refs_0_), channel_id=1, source_target_pairs={{0,2},{2,0},{4,6},{6,4},{8,10},{10,8},{12,14},{14,12},{16,18},{18,... | collective-permute-start | bytes 110600 | tf_op jit(solution)/shard_map/ppermute | solution.py:264
  8.1 6.6 %collective-permute-start.2 = (f32[144,128]{1,0:T(8,128)S(1)}, f32[144,128]{1,0:T(8,128)S(1)}, u32[]{:S(2)}, u32[]{:S(2)}) collective-permute-start(f32[144,128]{1,0:T(8,128)S(1)} %pad.10), channel_id=1, source_target_pairs={{0,8},{2,10},{4,12},{6,14},{8,0},{10,2},{12,4},{14,6},{16,24},{18,... | collective-permute-start | bytes 221192 | tf_op jit(solution)/shard_map/ppermute | solution.py:267
  10.1 6.8 %collective-permute-start.6 = (f32[136,128]{1,0:T(8,128)S(1)}, f32[136,128]{1,0:T(8,128)S(1)}, u32[]{:S(2)}, u32[]{:S(2)}) collective-permute-start(f32[136,128]{1,0:T(8,128)S(1)} %pad_maximum_fusion), channel_id=1, source_target_pairs={{0,24},{2,30},{4,28},{6,26},{8,16},{10,22},{12,20},{14,18},{16,8},... | collective-permute-start | bytes 208904 | tf_op jit(solution)/shard_map/ppermute | solution.py:270
  13.2 5.3 %collective-permute-start.4 = (f32[136,128]{1,0:T(8,128)S(1)}, f32[136,128]{1,0:T(8,128)S(1)}, u32[]{:S(2)}, u32[]{:S(2)}) collective-permute-start(f32[136,128]{1,0:T(8,128)S(1)} %pad_maximum_fusion), channel_id=1, source_target_pairs={{0,12},{2,22},{4,8},{6,18},{8,4},{10,30},{12,0},{14,26},{16,28},{1... | collective-permute-start | bytes 208904 | tf_op jit(solution)/shard_map/ppermute | solution.py:270
  14.2 6.1 %collective-permute-start.8 = (f32[136,128]{1,0:T(8,128)S(1)}, f32[136,128]{1,0:T(8,128)S(1)}, u32[]{:S(2)}, u32[]{:S(2)}) collective-permute-start(f32[136,128]{1,0:T(8,128)S(1)} %pad_maximum_fusion), channel_id=1, source_target_pairs={{0,4},{2,18},{4,0},{6,22},{8,12},{10,26},{12,8},{14,30},{16,20},{1... | collective-permute-start | bytes 208904 | tf_op jit(solution)/shard_map/ppermute | solution.py:270
  14.7 5.6 %collective-permute-start.3 = (f32[144,128]{1,0:T(8,128)S(1)}, f32[144,128]{1,0:T(8,128)S(1)}, u32[]{:S(2)}, u32[]{:S(2)}) collective-permute-start(f32[144,128]{1,0:T(8,128)S(1)} %collective-permute-done.2.refs_2_), channel_id=1, source_target_pairs={{0,2},{2,0},{4,6},{6,4},{8,10},{10,8},{12,14},{14,12},{16,18},{18,... | collective-permute-start | bytes 221192 | tf_op jit(solution)/shard_map/ppermute | solution.py:264
  16.9 3.4 %collective-permute-start.7 = (f32[136,128]{1,0:T(8,128)S(1)}, f32[136,128]{1,0:T(8,128)S(1)}, u32[]{:S(2)}, u32[]{:S(2)}) collective-permute-start(f32[136,128]{1,0:T(8,128)S(1)} %collective-permute-done.6.refs_6_), channel_id=1, source_target_pairs={{0,2},{2,0},{4,6},{6,4},{8,10},{10,8},{12,14},{14,12},{16,18},{18,... | collective-permute-start | bytes 208904 | tf_op jit(solution)/shard_map/ppermute | solution.py:264
  18.5 2.7 %collective-permute-start.5 = (f32[136,128]{1,0:T(8,128)S(1)}, f32[136,128]{1,0:T(8,128)S(1)}, u32[]{:S(2)}, u32[]{:S(2)}) collective-permute-start(f32[136,128]{1,0:T(8,128)S(1)} %collective-permute-done.4.refs_4_), channel_id=1, source_target_pairs={{0,2},{2,0},{4,6},{6,4},{8,10},{10,8},{12,14},{14,12},{16,18},{18,... | collective-permute-start | bytes 208904 | tf_op jit(solution)/shard_map/ppermute | solution.py:264
  20.3 1.3 %collective-permute-start.9 = (f32[136,128]{1,0:T(8,128)S(1)}, f32[136,128]{1,0:T(8,128)S(1)}, u32[]{:S(2)}, u32[]{:S(2)}) collective-permute-start(f32[136,128]{1,0:T(8,128)S(1)} %collective-permute-done.8.refs_1_), channel_id=1, source_target_pairs={{0,2},{2,0},{4,6},{6,4},{8,10},{10,8},{12,14},{14,12},{16,18},{18,... | collective-permute-start | bytes 208904 | tf_op jit(solution)/shard_map/ppermute | solution.py:264
  22.6 4.0 %collective-permute-start.10 = (f32[72,128]{1,0:T(8,128)S(1)}, f32[72,128]{1,0:T(8,128)S(1)}, u32[]{:S(2)}, u32[]{:S(2)}) collective-permute-start(f32[72,128]{1,0:T(8,128)S(1)} %get-tuple-element.37.refs_4_), channel_id=1, source_target_pairs={{0,1},{1,0},{2,3},{3,2},{4,5},{5,4},{6,7},{7,6},{8,9},{9,8},{10,11... | collective-permute-start | bytes 110600 | tf_op jit(solution)/shard_map/ppermute | solution.py:274
  27.6 1.2 %collective-permute-start.11 = (f32[72,128]{1,0:T(8,128)S(1)}, f32[72,128]{1,0:T(8,128)S(1)}, u32[]{:S(2)}, u32[]{:S(2)}) collective-permute-start(f32[72,128]{1,0:T(8,128)S(1)} %get-tuple-element.39.refs_0_), channel_id=1, source_target_pairs={{0,2},{2,0},{4,6},{6,4},{8,10},{10,8},{12,14},{14,12},{16,18},{18,... | collective-permute-start | bytes 110600 | tf_op jit(solution)/shard_map/ppermute | solution.py:264
  27.6 5.1 %collective-permute-start.12 = (f32[144,128]{1,0:T(8,128)S(1)}, f32[144,128]{1,0:T(8,128)S(1)}, u32[]{:S(2)}, u32[]{:S(2)}) collective-permute-start(f32[144,128]{1,0:T(8,128)S(1)} %pad.11), channel_id=1, source_target_pairs={{0,8},{2,10},{4,12},{6,14},{8,0},{10,2},{12,4},{14,6},{16,24},{18,... | collective-permute-start | bytes 221192 | tf_op jit(solution)/shard_map/ppermute | solution.py:267
  28.9 6.9 %collective-permute-start.16 = (f32[136,128]{1,0:T(8,128)S(1)}, f32[136,128]{1,0:T(8,128)S(1)}, u32[]{:S(2)}, u32[]{:S(2)}) collective-permute-start(f32[136,128]{1,0:T(8,128)S(1)} %pad_maximum_fusion.1), channel_id=1, source_target_pairs={{0,24},{2,30},{4,28},{6,26},{8,16},{10,22},{12,20},{14,18},{16,8},... | collective-permute-start | bytes 208904 | tf_op jit(solution)/shard_map/ppermute | solution.py:270
  31.2 6.0 %collective-permute-start.14 = (f32[136,128]{1,0:T(8,128)S(1)}, f32[136,128]{1,0:T(8,128)S(1)}, u32[]{:S(2)}, u32[]{:S(2)}) collective-permute-start(f32[136,128]{1,0:T(8,128)S(1)} %pad_maximum_fusion.1), channel_id=1, source_target_pairs={{0,12},{2,22},{4,8},{6,18},{8,4},{10,30},{12,0},{14,26},{16,28},{1... | collective-permute-start | bytes 208904 | tf_op jit(solution)/shard_map/ppermute | solution.py:270
  31.8 6.3 %collective-permute-start.18 = (f32[136,128]{1,0:T(8,128)S(1)}, f32[136,128]{1,0:T(8,128)S(1)}, u32[]{:S(2)}, u32[]{:S(2)}) collective-permute-start(f32[136,128]{1,0:T(8,128)S(1)} %pad_maximum_fusion.1), channel_id=1, source_target_pairs={{0,4},{2,18},{4,0},{6,22},{8,12},{10,26},{12,8},{14,30},{16,20},{1... | collective-permute-start | bytes 208904 | tf_op jit(solution)/shard_map/ppermute | solution.py:270
  32.7 5.6 %collective-permute-start.13 = (f32[144,128]{1,0:T(8,128)S(1)}, f32[144,128]{1,0:T(8,128)S(1)}, u32[]{:S(2)}, u32[]{:S(2)}) collective-permute-start(f32[144,128]{1,0:T(8,128)S(1)} %collective-permute-done.12.refs_2_), channel_id=1, source_target_pairs={{0,2},{2,0},{4,6},{6,4},{8,10},{10,8},{12,14},{14,12},{16,18},{18,... | collective-permute-start | bytes 221192 | tf_op jit(solution)/shard_map/ppermute | solution.py:264
  35.9 2.4 %collective-permute-start.17 = (f32[136,128]{1,0:T(8,128)S(1)}, f32[136,128]{1,0:T(8,128)S(1)}, u32[]{:S(2)}, u32[]{:S(2)}) collective-permute-start(f32[136,128]{1,0:T(8,128)S(1)} %collective-permute-done.16.refs_6_), channel_id=1, source_target_pairs={{0,2},{2,0},{4,6},{6,4},{8,10},{10,8},{12,14},{14,12},{16,18},{18,... | collective-permute-start | bytes 208904 | tf_op jit(solution)/shard_map/ppermute | solution.py:264
  37.2 1.7 %collective-permute-start.15 = (f32[136,128]{1,0:T(8,128)S(1)}, f32[136,128]{1,0:T(8,128)S(1)}, u32[]{:S(2)}, u32[]{:S(2)}) collective-permute-start(f32[136,128]{1,0:T(8,128)S(1)} %collective-permute-done.14.refs_4_), channel_id=1, source_target_pairs={{0,2},{2,0},{4,6},{6,4},{8,10},{10,8},{12,14},{14,12},{16,18},{18,... | collective-permute-start | bytes 208904 | tf_op jit(solution)/shard_map/ppermute | solution.py:264
  38.1 1.3 %collective-permute-start.19 = (f32[136,128]{1,0:T(8,128)S(1)}, f32[136,128]{1,0:T(8,128)S(1)}, u32[]{:S(2)}, u32[]{:S(2)}) collective-permute-start(f32[136,128]{1,0:T(8,128)S(1)} %collective-permute-done.18.refs_1_), channel_id=1, source_target_pairs={{0,2},{2,0},{4,6},{6,4},{8,10},{10,8},{12,14},{14,12},{16,18},{18,... | collective-permute-start | bytes 208904 | tf_op jit(solution)/shard_map/ppermute | solution.py:264
  40.4 4.0 %collective-permute-start.20 = (f32[72,128]{1,0:T(8,128)S(1)}, f32[72,128]{1,0:T(8,128)S(1)}, u32[]{:S(2)}, u32[]{:S(2)}) collective-permute-start(f32[72,128]{1,0:T(8,128)S(1)} %get-tuple-element.43.refs_4_), channel_id=1, source_target_pairs={{0,1},{1,0},{2,3},{3,2},{4,5},{5,4},{6,7},{7,6},{8,9},{9,8},{10,11... | collective-permute-start | bytes 110600 | tf_op jit(solution)/shard_map/ppermute | solution.py:274
  45.4 1.2 %collective-permute-start.21 = (f32[72,128]{1,0:T(8,128)S(1)}, f32[72,128]{1,0:T(8,128)S(1)}, u32[]{:S(2)}, u32[]{:S(2)}) collective-permute-start(f32[72,128]{1,0:T(8,128)S(1)} %get-tuple-element.45.refs_0_), channel_id=1, source_target_pairs={{0,2},{2,0},{4,6},{6,4},{8,10},{10,8},{12,14},{14,12},{16,18},{18,... | collective-permute-start | bytes 110600 | tf_op jit(solution)/shard_map/ppermute | solution.py:264
  45.5 5.1 %collective-permute-start.22 = (f32[144,128]{1,0:T(8,128)S(1)}, f32[144,128]{1,0:T(8,128)S(1)}, u32[]{:S(2)}, u32[]{:S(2)}) collective-permute-start(f32[144,128]{1,0:T(8,128)S(1)} %pad.12), channel_id=1, source_target_pairs={{0,8},{2,10},{4,12},{6,14},{8,0},{10,2},{12,4},{14,6},{16,24},{18,... | collective-permute-start | bytes 221192 | tf_op jit(solution)/shard_map/ppermute | solution.py:267
  46.7 7.0 %collective-permute-start.26 = (f32[136,128]{1,0:T(8,128)S(1)}, f32[136,128]{1,0:T(8,128)S(1)}, u32[]{:S(2)}, u32[]{:S(2)}) collective-permute-start(f32[136,128]{1,0:T(8,128)S(1)} %pad_maximum_fusion.2), channel_id=1, source_target_pairs={{0,24},{2,30},{4,28},{6,26},{8,16},{10,22},{12,20},{14,18},{16,8},... | collective-permute-start | bytes 208904 | tf_op jit(solution)/shard_map/ppermute | solution.py:270
  49.0 6.0 %collective-permute-start.24 = (f32[136,128]{1,0:T(8,128)S(1)}, f32[136,128]{1,0:T(8,128)S(1)}, u32[]{:S(2)}, u32[]{:S(2)}) collective-permute-start(f32[136,128]{1,0:T(8,128)S(1)} %pad_maximum_fusion.2), channel_id=1, source_target_pairs={{0,12},{2,22},{4,8},{6,18},{8,4},{10,30},{12,0},{14,26},{16,28},{1... | collective-permute-start | bytes 208904 | tf_op jit(solution)/shard_map/ppermute | solution.py:270
  49.6 6.3 %collective-permute-start.28 = (f32[136,128]{1,0:T(8,128)S(1)}, f32[136,128]{1,0:T(8,128)S(1)}, u32[]{:S(2)}, u32[]{:S(2)}) collective-permute-start(f32[136,128]{1,0:T(8,128)S(1)} %pad_maximum_fusion.2), channel_id=1, source_target_pairs={{0,4},{2,18},{4,0},{6,22},{8,12},{10,26},{12,8},{14,30},{16,20},{1... | collective-permute-start | bytes 208904 | tf_op jit(solution)/shard_map/ppermute | solution.py:270
  50.5 5.6 %collective-permute-start.23 = (f32[144,128]{1,0:T(8,128)S(1)}, f32[144,128]{1,0:T(8,128)S(1)}, u32[]{:S(2)}, u32[]{:S(2)}) collective-permute-start(f32[144,128]{1,0:T(8,128)S(1)} %collective-permute-done.22.refs_2_), channel_id=1, source_target_pairs={{0,2},{2,0},{4,6},{6,4},{8,10},{10,8},{12,14},{14,12},{16,18},{18,... | collective-permute-start | bytes 221192 | tf_op jit(solution)/shard_map/ppermute | solution.py:264
  53.7 2.4 %collective-permute-start.27 = (f32[136,128]{1,0:T(8,128)S(1)}, f32[136,128]{1,0:T(8,128)S(1)}, u32[]{:S(2)}, u32[]{:S(2)}) collective-permute-start(f32[136,128]{1,0:T(8,128)S(1)} %collective-permute-done.26.refs_6_), channel_id=1, source_target_pairs={{0,2},{2,0},{4,6},{6,4},{8,10},{10,8},{12,14},{14,12},{16,18},{18,... | collective-permute-start | bytes 208904 | tf_op jit(solution)/shard_map/ppermute | solution.py:264
  55.1 1.7 %collective-permute-start.25 = (f32[136,128]{1,0:T(8,128)S(1)}, f32[136,128]{1,0:T(8,128)S(1)}, u32[]{:S(2)}, u32[]{:S(2)}) collective-permute-start(f32[136,128]{1,0:T(8,128)S(1)} %collective-permute-done.24.refs_4_), channel_id=1, source_target_pairs={{0,2},{2,0},{4,6},{6,4},{8,10},{10,8},{12,14},{14,12},{16,18},{18,... | collective-permute-start | bytes 208904 | tf_op jit(solution)/shard_map/ppermute | solution.py:264
  55.9 1.3 %collective-permute-start.29 = (f32[136,128]{1,0:T(8,128)S(1)}, f32[136,128]{1,0:T(8,128)S(1)}, u32[]{:S(2)}, u32[]{:S(2)}) collective-permute-start(f32[136,128]{1,0:T(8,128)S(1)} %collective-permute-done.28.refs_1_), channel_id=1, source_target_pairs={{0,2},{2,0},{4,6},{6,4},{8,10},{10,8},{12,14},{14,12},{16,18},{18,... | collective-permute-start | bytes 208904 | tf_op jit(solution)/shard_map/ppermute | solution.py:264
  58.2 4.0 %collective-permute-start.30 = (f32[72,128]{1,0:T(8,128)S(1)}, f32[72,128]{1,0:T(8,128)S(1)}, u32[]{:S(2)}, u32[]{:S(2)}) collective-permute-start(f32[72,128]{1,0:T(8,128)S(1)} %get-tuple-element.49.refs_3_), channel_id=1, source_target_pairs={{0,1},{1,0},{2,3},{3,2},{4,5},{5,4},{6,7},{7,6},{8,9},{9,8},{10,11... | collective-permute-start | bytes 110600 | tf_op jit(solution)/shard_map/ppermute | solution.py:274
  62.5 1.2 %collective-permute-start.32 = (f32[8,128]{1,0:T(8,128)S(1)}, f32[8,128]{1,0:T(8,128)S(1)}, u32[]{:S(2)}, u32[]{:S(2)}) collective-permute-start(f32[8,128]{1,0:T(8,128)S(1)} %get-tuple-element.50), channel_id=1, source_target_pairs={{0,2},{2,0},{4,6},{6,4},{8,10},{10,8},{12,14},{14,12},{16,18},{18,... | collective-permute-start | bytes 12296 | tf_op jit(solution)/shard_map/ppermute | solution.py:264
  62.6 6.0 %collective-permute-start.31 = (f32[8,128]{1,0:T(8,128)S(1)}, f32[8,128]{1,0:T(8,128)S(1)}, u32[]{:S(2)}, u32[]{:S(2)}) collective-permute-start(f32[8,128]{1,0:T(8,128)S(1)} %get-tuple-element.50), channel_id=1, source_target_pairs={{0,4},{2,6},{4,0},{6,2},{8,12},{10,14},{12,8},{14,10},{16,20},{18,... | collective-permute-start | bytes 12296 | tf_op jit(solution)/shard_map/ppermute | solution.py:267
  63.7 5.4 %collective-permute-start.35 = (f32[8,128]{1,0:T(8,128)S(1)}, f32[8,128]{1,0:T(8,128)S(1)}, u32[]{:S(2)}, u32[]{:S(2)}) collective-permute-start(f32[8,128]{1,0:T(8,128)S(1)} %add.39), channel_id=1, source_target_pairs={{0,24},{2,30},{4,28},{6,26},{8,16},{10,22},{12,20},{14,18},{16,8},... | collective-permute-start | bytes 12296 | tf_op jit(solution)/shard_map/ppermute | solution.py:270
  66.0 4.5 %collective-permute-start.34 = (f32[8,128]{1,0:T(8,128)S(1)}, f32[8,128]{1,0:T(8,128)S(1)}, u32[]{:S(2)}, u32[]{:S(2)}) collective-permute-start(f32[8,128]{1,0:T(8,128)S(1)} %add.39), channel_id=1, source_target_pairs={{0,12},{2,22},{4,8},{6,18},{8,4},{10,30},{12,0},{14,26},{16,28},{1... | collective-permute-start | bytes 12296 | tf_op jit(solution)/shard_map/ppermute | solution.py:270
  66.0 4.5 %collective-permute-start.33 = (f32[8,128]{1,0:T(8,128)S(1)}, f32[8,128]{1,0:T(8,128)S(1)}, u32[]{:S(2)}, u32[]{:S(2)}) collective-permute-start(f32[8,128]{1,0:T(8,128)S(1)} %add.39), channel_id=1, source_target_pairs={{0,8},{2,18},{4,12},{6,22},{8,0},{10,26},{12,4},{14,30},{16,24},{1... | collective-permute-start | bytes 12296 | tf_op jit(solution)/shard_map/ppermute | solution.py:270
  70.5 1.2 %collective-permute-start.36 = (f32[8,128]{1,0:T(8,128)S(1)}, f32[8,128]{1,0:T(8,128)S(1)}, u32[]{:S(2)}, u32[]{:S(2)}) collective-permute-start(f32[8,128]{1,0:T(8,128)S(1)} %add_add_fusion.half), channel_id=1, source_target_pairs={{0,2},{2,0},{4,6},{6,4},{8,10},{10,8},{12,14},{14,12},{16,18},{18,... | collective-permute-start | bytes 12296 | tf_op jit(solution)/shard_map/ppermute | solution.py:264
